TPU v7x, 32 devices: a whole 2x2x4 slice. The times are simulated.
32 devices in a mesh: wide: 8 (over z, x), narrow: 4 (over y, core).
Axes of the slice: x: 2, y: 2, z: 4, core: 2. Of those that a mesh axis runs over, the one named last changes fastest.
Arguments:
- inputs: bfloat16 [64, 1024, 768], P(('wide', 'narrow')), may hold values from -6 to 6
- tok_landmark: int32 [64, 1024], P(('wide', 'narrow')), may hold values from 0 to 63, never falling along the last dimension, each value on 1 to 32 neighbouring positions
- landmark_doc: int32 [64, 64], P(('wide', 'narrow')), may hold values from 0 to 3, never falling along the last dimension, each value on 1 to 48 neighbouring positions
- w_query: bfloat16 [768, 768], P(None, ('wide', 'narrow')), may hold values from -0.75 to 0.75
- b_query: bfloat16 [768], P(('wide', 'narrow')), may hold values from -4 to 4
- w_key: bfloat16 [768, 768], P(None, ('wide', 'narrow')), may hold values from -0.75 to 0.75
- w_value: bfloat16 [768, 768], P(None, ('wide', 'narrow')), may hold values from -0.21875 to 0.21875
- b_value: bfloat16 [768], P(('wide', 'narrow')), may hold values from -3 to 3
- conv_weight: bfloat16 [33, 768], P(None, ('wide', 'narrow')), may hold values from -0.5 to 0.5
- w_out: bfloat16 [768, 768], P(None, ('wide', 'narrow')), may hold values from -0.4375 to 0.4375
- b_out: bfloat16 [768], P(('wide', 'narrow')), may hold values from -3 to 3
- gain_one: bfloat16 [768], P(('wide', 'narrow')), may hold values from 0.5 to 1.5
- shift_one: bfloat16 [768], P(('wide', 'narrow')), may hold values from -3 to 3
- w_up: bfloat16 [768, 3072], P(None, ('wide', 'narrow')), may hold values from -0.21875 to 0.21875
- b_up: bfloat16 [3072], P(('wide', 'narrow')), may hold values from -3 to 3
- w_down: bfloat16 [3072, 768], P(None, ('wide', 'narrow')), may hold values from -0.15625 to 0.15625
- b_down: bfloat16 [768], P(('wide', 'narrow')), may hold values from -3 to 3
- gain_two: bfloat16 [768], P(('wide', 'narrow')), may hold values from 0.5 to 1.5
- shift_two: bfloat16 [768], P(('wide', 'narrow')), may hold values from -3 to 3
- cotangent: bfloat16 [64, 1024, 768], P(('wide', 'narrow')), may hold values from -6 to 6
Outputs:
- layer_out: bfloat16 [64, 1024, 768], P(('wide', 'narrow'))
- input_grad: float32 [64, 1024, 768], P(('wide', 'narrow'))
- grad_w_query: float32 [768, 768], P(None, ('wide', 'narrow'))
- grad_b_query: float32 [768], P(('wide', 'narrow'))
- grad_w_key: float32 [768, 768], P(None, ('wide', 'narrow'))
- grad_w_value: float32 [768, 768], P(None, ('wide', 'narrow'))
- grad_b_value: float32 [768], P(('wide', 'narrow'))
- grad_conv: float32 [33, 768], P(None, ('wide', 'narrow'))
- grad_w_out: float32 [768, 768], P(None, ('wide', 'narrow'))
- grad_b_out: float32 [768], P(('wide', 'narrow'))
- grad_gain_one: float32 [768], P(('wide', 'narrow'))
- grad_shift_one: float32 [768], P(('wide', 'narrow'))
- grad_w_up: float32 [768, 3072], P(None, ('wide', 'narrow'))
- grad_b_up: float32 [3072], P(('wide', 'narrow'))
- grad_w_down: float32 [3072, 768], P(None, ('wide', 'narrow'))
- grad_b_down: float32 [768], P(('wide', 'narrow'))
- grad_gain_two: float32 [768], P(('wide', 'narrow'))
- grad_shift_two: float32 [768], P(('wide', 'narrow'))
Inputs may be any that keep to these rules, and one draw needn't show every extreme that they name: `tok_landmark`: in each sequence the landmark numbers never fall along the tokens and each of the 64 landmarks holds 1 to 32 tokens. `landmark_doc`: in each sequence the document numbers never fall along the landmarks and each of the 4 documents holds 1 to 48 landmarks.
All inputs are finite; a program needn't handle non-finite values.
Results may differ from a plain program's by a relative error of at most 0.0095.
Values may be sent and summed in bfloat16 or wider, within the bound.
No kernel may reach another device: no remote copies, remote signals or barrier semaphores. Data moves between devices by JAX's collectives and lax.ppermute only.
A program may use at most 576 MiB of HBM per device.

v0:
```python
import jax
import jax.numpy as jnp
from jax import lax
from jax.sharding import PartitionSpec as P

HEAD_COUNT = 12
HEAD_WIDTH = 64
LANDMARKS = 64
KW = 33
NEWTON = 6


HIGHEST = lax.Precision.HIGHEST


def batch_mapped(left_side, right_side, form):
    return jnp.einsum(form, left_side, right_side, precision=HIGHEST)


def softmax_with_mask(scores, allowed):
    held_scores = jnp.where(allowed, scores, -1e30)
    row_top = jnp.max(held_scores, axis=-1, keepdims=True)
    raised = jnp.where(allowed, jnp.exp(held_scores - row_top), 0.0)
    return raised / jnp.sum(raised, axis=-1, keepdims=True)


def newton_inverse(kernel):
    identity = jnp.eye(kernel.shape[-1], dtype=kernel.dtype)
    approx = jnp.swapaxes(kernel, 1, 2) / jnp.sum(kernel * kernel, axis=(1, 2), keepdims=True)
    for iteration in range(NEWTON):
        product = batch_mapped(kernel, approx, "hij,hjk->hik")
        inner_term = 7.0 * identity - product
        inner_term = 15.0 * identity - batch_mapped(product, inner_term, "hij,hjk->hik")
        outer_term = 13.0 * identity - batch_mapped(product, inner_term, "hij,hjk->hik")
        approx = 0.25 * batch_mapped(approx, outer_term, "hij,hjk->hik")
    return approx


def nystrom(query_rows, key_rows, value_rows, conv_weight, tok_landmark, landmark_doc):
    sequence_length = query_rows.shape[0]
    membership = tok_landmark[:, None] == jnp.arange(LANDMARKS, dtype=jnp.int32)[None, :]
    document_indicator = membership.astype(query_rows.dtype)
    landmark_counts = jnp.sum(document_indicator, axis=0)
    doc_tok = jnp.sum(jnp.where(membership, landmark_doc[None, :], 0), axis=1)
    first_document_mask = doc_tok[:, None] == landmark_doc[None, :]
    second_document_mask = landmark_doc[:, None] == landmark_doc[None, :]
    scaling = HEAD_WIDTH ** (-0.25)
    query_heads = (query_rows * scaling).reshape(sequence_length, HEAD_COUNT, HEAD_WIDTH)
    key_heads = (key_rows * scaling).reshape(sequence_length, HEAD_COUNT, HEAD_WIDTH)
    value_heads = value_rows.reshape(sequence_length, HEAD_COUNT, HEAD_WIDTH)
    landmark_queries = (
        batch_mapped(document_indicator, query_heads, "kp,ksz->spz")
        / landmark_counts[None, :, None]
    )
    landmark_keys = (
        batch_mapped(document_indicator, key_heads, "kp,ksz->spz") / landmark_counts[None, :, None]
    )
    first_kernel = softmax_with_mask(
        batch_mapped(query_heads, landmark_keys, "kxs,xfs->xkf"), first_document_mask[None]
    )
    middle_kernel = softmax_with_mask(
        batch_mapped(landmark_queries, landmark_keys, "cfo,cto->cft"), second_document_mask[None]
    )
    third_kernel = softmax_with_mask(
        batch_mapped(landmark_queries, key_heads, "ryx,srx->rys"), first_document_mask.T[None]
    )
    carry_state = batch_mapped(third_kernel, value_heads, "cyn,ncr->cyr")
    carry_state = batch_mapped(newton_inverse(middle_kernel), carry_state, "otz,ozu->otu")
    mixed_context = batch_mapped(first_kernel, carry_state, "fve,feg->vfg").reshape(
        sequence_length, HEAD_COUNT * HEAD_WIDTH
    )
    half_width = KW // 2
    padded = jnp.pad(value_rows, ((half_width, half_width), (0, 0)))
    padded_doc = jnp.pad(doc_tok, (half_width, half_width), constant_values=-1)
    for offset in range(KW):
        inside = (padded_doc[offset : offset + sequence_length] == doc_tok)[:, None]
        mixed_context = mixed_context + jnp.where(
            inside, conv_weight[offset][None, :] * padded[offset : offset + sequence_length], 0.0
        )
    return mixed_context


def normalize(values):
    row_mean = jnp.mean(values, axis=-1, keepdims=True)
    centered = values - row_mean
    inv_std = lax.rsqrt(jnp.mean(centered * centered, axis=-1, keepdims=True) + 1e-05)
    return (centered * inv_std, inv_std)


def norm_back(upstream, normal, inv_std, gain_vec):
    scaled = upstream * gain_vec
    inner_mean = jnp.mean(scaled, axis=-1, keepdims=True)
    cross_mean = jnp.mean(scaled * normal, axis=-1, keepdims=True)
    return (
        inv_std * (scaled - inner_mean - normal * cross_mean),
        jnp.sum(upstream * normal, axis=0),
        jnp.sum(upstream, axis=0),
    )


def forward_dot(left_side, right_side):
    return jnp.dot(left_side, right_side, preferred_element_type=jnp.float32)


def across_rows(left_side, right_side):
    return lax.dot_general(
        left_side, right_side, (((0,), (0,)), ((), ())), preferred_element_type=jnp.float32
    )


def against_cols(left_side, right_side):
    return lax.dot_general(
        left_side, right_side, (((1,), (1,)), ((), ())), preferred_element_type=jnp.float32
    )


def column_sums(values):
    return jnp.sum(values.astype(jnp.float32), axis=0)


def gelu_exact(values):
    return jax.nn.gelu(values, approximate=False)


def pack_terms(terms, dims, count):
    pieces = []
    for term, dim in zip(terms, dims):
        moved = jnp.moveaxis(term, dim, 0)
        pieces.append(moved.reshape(count, -1))
    return jnp.concatenate(pieces, axis=1)


def unpack_terms(flat_row, terms, dims, count):
    flat_row = flat_row.reshape(-1)
    results = []
    start = 0
    for term, dim in zip(terms, dims):
        moved_shape = tuple(jnp.moveaxis(term, dim, 0).shape)
        local_shape = (moved_shape[0] // count,) + moved_shape[1:]
        length = 1
        for extent in local_shape:
            length = length * extent
        piece = flat_row[start : start + length].reshape(local_shape)
        results.append(jnp.moveaxis(piece, 0, dim))
        start = start + length
    return tuple(results)


def shards(
    inputs,
    tok_landmark,
    landmark_doc,
    w_query,
    b_query,
    w_key,
    w_value,
    b_value,
    conv_weight,
    w_out,
    b_out,
    gain_one,
    shift_one,
    w_up,
    b_up,
    w_down,
    b_down,
    gain_two,
    shift_two,
    cotangent,
):
    batch_rows, sequence_length, feature_width = inputs.shape
    group_count = lax.axis_size("wide") * lax.axis_size("narrow")
    attn_full = (
        lax.all_gather(w_query, ("wide", "narrow"), axis=1, tiled=True),
        lax.all_gather(w_key, ("wide", "narrow"), axis=1, tiled=True),
        lax.all_gather(w_value, ("wide", "narrow"), axis=1, tiled=True),
        lax.all_gather(w_out, ("wide", "narrow"), axis=1, tiled=True),
        lax.all_gather(conv_weight, ("wide", "narrow"), axis=1, tiled=True),
        lax.all_gather(b_query, ("wide", "narrow"), axis=0, tiled=True),
        lax.all_gather(b_value, ("wide", "narrow"), axis=0, tiled=True),
        lax.all_gather(b_out, ("wide", "narrow"), axis=0, tiled=True),
        lax.all_gather(gain_one, ("wide", "narrow"), axis=0, tiled=True),
        lax.all_gather(shift_one, ("wide", "narrow"), axis=0, tiled=True),
    )
    rows_low = inputs.reshape(batch_rows * sequence_length, feature_width)
    rows_in = rows_low.astype(jnp.float32)
    query_rows = forward_dot(rows_low, attn_full[0]) + attn_full[5].astype(jnp.float32)
    key_rows = forward_dot(rows_low, attn_full[1])
    value_rows = forward_dot(rows_low, attn_full[2]) + attn_full[6].astype(jnp.float32)

    def attend(query_part, key_part, value_part, conv_part):
        shaped = (batch_rows, sequence_length, feature_width)
        mixed = jax.vmap(nystrom, in_axes=(0, 0, 0, None, 0, 0))(
            query_part.reshape(shaped),
            key_part.reshape(shaped),
            value_part.reshape(shaped),
            conv_part,
            tok_landmark,
            landmark_doc,
        )
        return mixed.reshape(batch_rows * sequence_length, feature_width)

    mixed_context = attend(query_rows, key_rows, value_rows, attn_full[4].astype(jnp.float32))
    context_low = mixed_context.astype(jnp.bfloat16)
    attended = forward_dot(context_low, attn_full[3]) + attn_full[7].astype(jnp.float32)
    normal_one, inv_one = normalize(rows_in + attended)
    normed = normal_one * attn_full[8].astype(jnp.float32) + attn_full[9].astype(jnp.float32)
    normed_low = normed.astype(jnp.bfloat16)
    ffn_full = (
        lax.all_gather(w_up, ("wide", "narrow"), axis=1, tiled=True),
        lax.all_gather(w_down, ("wide", "narrow"), axis=1, tiled=True),
        lax.all_gather(b_up, ("wide", "narrow"), axis=0, tiled=True),
        lax.all_gather(b_down, ("wide", "narrow"), axis=0, tiled=True),
        lax.all_gather(gain_two, ("wide", "narrow"), axis=0, tiled=True),
        lax.all_gather(shift_two, ("wide", "narrow"), axis=0, tiled=True),
    )
    up_pre = forward_dot(normed_low, ffn_full[0]) + ffn_full[2].astype(jnp.float32)
    hidden = gelu_exact(up_pre).astype(jnp.bfloat16)
    down_out = forward_dot(hidden, ffn_full[1]) + ffn_full[3].astype(jnp.float32)
    normal_two, inv_two = normalize(normed + down_out)
    layer_out = (
        normal_two * ffn_full[4].astype(jnp.float32) + ffn_full[5].astype(jnp.float32)
    ).astype(jnp.bfloat16)
    ffn_back = (
        lax.all_gather(w_up, ("wide", "narrow"), axis=1, tiled=True),
        lax.all_gather(w_down, ("wide", "narrow"), axis=1, tiled=True),
        lax.all_gather(b_up, ("wide", "narrow"), axis=0, tiled=True),
        lax.all_gather(b_down, ("wide", "narrow"), axis=0, tiled=True),
        lax.all_gather(gain_two, ("wide", "narrow"), axis=0, tiled=True),
        lax.all_gather(shift_two, ("wide", "narrow"), axis=0, tiled=True),
    )
    upstream = cotangent.reshape(batch_rows * sequence_length, feature_width).astype(jnp.float32)
    grad_two, grad_gain_two, grad_shift_two = norm_back(
        upstream, normal_two, inv_two, ffn_back[4].astype(jnp.float32)
    )
    down_low = grad_two.astype(jnp.bfloat16)
    grad_w_down = across_rows(hidden, down_low)
    grad_b_down = column_sums(down_low)
    hidden_grad = against_cols(down_low, ffn_back[1])
    up_low = jax.vjp(gelu_exact, up_pre)[1](hidden_grad)[0].astype(jnp.bfloat16)
    grad_w_up = across_rows(normed_low, up_low)
    grad_b_up = column_sums(up_low)
    normed_grad = grad_two + against_cols(up_low, ffn_back[0])
    ffn_dims = (1, 1, 0, 0, 0, 0)
    ffn_terms = (grad_w_up, grad_w_down, grad_b_up, grad_b_down, grad_gain_two, grad_shift_two)
    attn_back = (
        lax.all_gather(w_query, ("wide", "narrow"), axis=1, tiled=True),
        lax.all_gather(w_key, ("wide", "narrow"), axis=1, tiled=True),
        lax.all_gather(w_value, ("wide", "narrow"), axis=1, tiled=True),
        lax.all_gather(w_out, ("wide", "narrow"), axis=1, tiled=True),
        lax.all_gather(conv_weight, ("wide", "narrow"), axis=1, tiled=True),
        lax.all_gather(b_query, ("wide", "narrow"), axis=0, tiled=True),
        lax.all_gather(b_value, ("wide", "narrow"), axis=0, tiled=True),
        lax.all_gather(b_out, ("wide", "narrow"), axis=0, tiled=True),
        lax.all_gather(gain_one, ("wide", "narrow"), axis=0, tiled=True),
        lax.all_gather(shift_one, ("wide", "narrow"), axis=0, tiled=True),
    )
    grad_one, grad_gain_one, grad_shift_one = norm_back(
        normed_grad, normal_one, inv_one, attn_back[8].astype(jnp.float32)
    )
    attended_low = grad_one.astype(jnp.bfloat16)
    grad_w_out = across_rows(context_low, attended_low)
    grad_b_out = column_sums(attended_low)
    context_grad = against_cols(attended_low, attn_back[3])
    pullback = jax.vjp(attend, query_rows, key_rows, value_rows, attn_back[4].astype(jnp.float32))[
        1
    ]
    query_grad, key_grad, value_grad, grad_conv = pullback(context_grad)
    query_low = query_grad.astype(jnp.bfloat16)
    key_low = key_grad.astype(jnp.bfloat16)
    value_low = value_grad.astype(jnp.bfloat16)
    grad_w_query = across_rows(rows_low, query_low)
    grad_b_query = column_sums(query_low)
    grad_w_key = across_rows(rows_low, key_low)
    grad_w_value = across_rows(rows_low, value_low)
    grad_b_value = column_sums(value_low)
    input_grad = (
        grad_one
        + against_cols(query_low, attn_back[0])
        + against_cols(key_low, attn_back[1])
        + against_cols(value_low, attn_back[2])
    )
    attn_dims = (1, 1, 1, 1, 1, 0, 0, 0, 0, 0)
    attn_terms = (
        grad_w_query,
        grad_w_key,
        grad_w_value,
        grad_w_out,
        grad_conv,
        grad_b_query,
        grad_b_value,
        grad_b_out,
        grad_gain_one,
        grad_shift_one,
    )
    every_term = attn_terms + ffn_terms
    every_dim = attn_dims + ffn_dims
    every_packed = pack_terms(every_term, every_dim, group_count)
    summed_row = lax.psum_scatter(every_packed, ("wide", "narrow"), scatter_dimension=0, tiled=True)
    summed = unpack_terms(summed_row, every_term, every_dim, group_count)
    attn_shares = summed[:10]
    final_ffn = summed[10:]
    shaped_out = (batch_rows, sequence_length, feature_width)
    return (
        layer_out.reshape(shaped_out),
        input_grad.reshape(shaped_out),
        attn_shares[0],
        attn_shares[5],
        attn_shares[1],
        attn_shares[2],
        attn_shares[6],
        attn_shares[4],
        attn_shares[3],
        attn_shares[7],
        attn_shares[8],
        attn_shares[9],
        final_ffn[0],
        final_ffn[2],
        final_ffn[1],
        final_ffn[3],
        final_ffn[4],
        final_ffn[5],
    )


def solution(mesh):
    return jax.shard_map(
        shards,
        mesh=mesh,
        in_specs=(
            P(("wide", "narrow"), None, None),
            P(("wide", "narrow"), None),
            P(("wide", "narrow"), None),
            P(None, ("wide", "narrow")),
            P(("wide", "narrow")),
            P(None, ("wide", "narrow")),
            P(None, ("wide", "narrow")),
            P(("wide", "narrow")),
            P(None, ("wide", "narrow")),
            P(None, ("wide", "narrow")),
            P(("wide", "narrow")),
            P(("wide", "narrow")),
            P(("wide", "narrow")),
            P(None, ("wide", "narrow")),
            P(("wide", "narrow")),
            P(None, ("wide", "narrow")),
            P(("wide", "narrow")),
            P(("wide", "narrow")),
            P(("wide", "narrow")),
            P(("wide", "narrow"), None, None),
        ),
        out_specs=(
            P(("wide", "narrow"), None, None),
            P(("wide", "narrow"), None, None),
            P(None, ("wide", "narrow")),
            P(("wide", "narrow")),
            P(None, ("wide", "narrow")),
            P(None, ("wide", "narrow")),
            P(("wide", "narrow")),
            P(None, ("wide", "narrow")),
            P(None, ("wide", "narrow")),
            P(("wide", "narrow")),
            P(("wide", "narrow")),
            P(("wide", "narrow")),
            P(None, ("wide", "narrow")),
            P(("wide", "narrow")),
            P(None, ("wide", "narrow")),
            P(("wide", "narrow")),
            P(("wide", "narrow")),
            P(("wide", "narrow")),
        ),
        check_vma=False,
    )
```

profile of v0, /device:TPU:0, one launch (start us, length us, event | category | flops | bytes accessed | tf_op | source)
XLA Modules:
  0.0 1645.7 jit_solution(12265306314491653179)
XLA Ops:
  18.5 44.0 %all_gather.62 = bf16[33,768]{0,1:T(8,128)(2,1)S(1)} all-gather(bf16[33,24]{0,1:T(8,128)(2,1)} %param.28), channel_id=1, replica_groups=mesh['wide'=8,'narrow'=4] {'wide','narrow'}, dimensions={1}, use_global_device_ids=true | all-gather | bytes 52272 | tf_op jit(solution)/shard_map/all_gather | solution.py:178
  81.3 38.1 %all-reduce.78 = (bf16[768]{0:T(1024)(128)(2,1)}, bf16[768]{0:T(1024)(128)(2,1)}, bf16[768]{0:T(1024)(128)(2,1)}, bf16[768]{0:T(1024)(128)(2,1)}, bf16[768]{0:T(...) all-reduce(bf16[768]{0:T(1024)(128)(2,1)} %dynamic-update-slice.1, ...), channel_id=1, replica_groups=mesh['wide'=8,'narrow'=4] {'wide','narrow'}, use_global_device_ids=true, to_apply=%add.69 | all-reduce | flops 9216 | bytes 36864
  280.6 126.0 %add_convert_fusion.2 = bf16[2,1024,768]{2,1,0:T(8,128)(2,1)S(1)} fusion(f32[2,1024,768]{2,1,0:T(8,128)} %bitcast.332, f32[2,1024,768]{2,1,0:T(8,128)} %copy.177, f32[768]{0:T(1024)} %get-tuple-element.65, f32[768]{0:T(1024)} %get-tuple-element.66, f32[768]{0:T(1024)} %get-tuple-element.67, f32[768]{0:T(1024)} %get-tuple-element.68, ...), kind=kLoop, calls=%fused_computation.99 | loop fusion | flops 155713536 | bytes 15895552 | tf_op jit(solution)/shard_map/convert_element_type | solution.py:204
  416.7 68.2 %multiply_convert_fusion = (bf16[2048,3072]{1,0:T(8,128)(2,1)}, f32[2048,3072]{1,0:T(8,128)}, f32[2048,3072]{1,0:T(8,128)}) fusion(f32[3072]{0:T(1024)S(1)} %copy-done.177, bf16[768,3072]{0,1:T(8,128)(2,1)} %all-gather.15.cloned.1.call-done, f32[2048,768]{1,0:T(8,128)} %copy-done.19, f32[768]{0:T(1024)S(1)} %convert_element_type.138, ...), kind=kOutput, calls=%fused_computation.4 | convolution fusion | flops 10086776832 | bytes 73959424 | tf_op jit(solution)/shard_map/dot_general | solution.py:102
  485.0 16.0 fusion.179
  510.4 17.7 %fusion.133 = f32[768,3072]{1,0:T(8,128)} fusion(bf16[2048,3072]{1,0:T(8,128)(2,1)} %get-tuple-element.124, f32[2048,768]{1,0:T(8,128)S(1)} %get-tuple-element.107), kind=kOutput, calls=%fused_computation.429 | convolution fusion | flops 9665249280 | bytes 28311552 | tf_op jit(solution)/shard_map/dot_general | solution.py:106
  528.2 32.2 %convert_reduce_fusion = (f32[3072]{0:T(1024)}, bf16[2048,3072]{1,0:T(8,128)(2,1)}) fusion(f32[2048,3072]{1,0:T(8,128)} %get-tuple-element.125, bf16[3072,768]{0,1:T(8,128)(2,1)} %all-gather.17.cloned.1.call-done, f32[2048,768]{1,0:T(8,128)} %copy-done.71, f32[2048,3072]{1,0:T(8,128)} %get-tuple-element.216, f32[3072]{0:T(1024)S(1)} %copy-done.177), kind=kOutput, calls=%fused_computation.2 | convolution fusion | flops 9772200960 | bytes 73949184 | tf_op jit(solution)/shard_map/dot_general | solution.py:112
  560.4 17.9 %fusion.151 = f32[3072,768]{1,0:T(8,128)} fusion(bf16[2048,3072]{1,0:T(8,128)(2,1)} %get-tuple-element.232, f32[2048,768]{1,0:T(8,128)} %copy-done.19, f32[768]{0:T(1024)S(1)} %convert_element_type.138, f32[768]{0:T(1024)S(1)} %convert_element_type.137, f32[2048]{0:T(1024)S(1)} %add_rsqrt_fusion.1, f32[2048]{0:T(1024)S(1)} %broadcast_multiply_fusion.6), kind=kOutput, calls=%fused_computation.447 | convolution fusion | flops 9671540736 | bytes 28334080 | tf_op jit(solution)/shard_map/dot_general | solution.py:106
  578.3 19.6 %multiply_reduce_fusion = (f32[768]{0:T(1024)}, f32[2048]{0:T(1024)S(1)}, f32[2048]{0:T(1024)S(1)}, f32[768]{0:T(1024)}, f32[2048,768]{1,0:T(8,128)}) fusion(f32[2048,768]{1,0:T(8,128)} %copy-done.19, f32[2048]{0:T(1024)S(1)} %add_rsqrt_fusion.1, f32[2048]{0:T(1024)S(1)} %broadcast_multiply_fusion.6, f32[768]{0:T(1024)S(1)} %convert_element_type.137, ...), kind=kOutput, calls=%fused_computation.45 | convolution fusion | flops 9679398912 | bytes 36217856 | tf_op jit(solution)/shard_map/dot_general | solution.py:112
  609.6 14.1 multiply_reduce_fusion.13
  627.9 28.1 %multiply_reduce_fusion.32 = (f32[768]{0:T(1024)}, f32[768]{0:T(1024)}, f32[768]{0:T(1024)}, f32[768]{0:T(1024)}, f32[768]{0:T(1024)}, /*index=5*/f32[768]{0:T(1024)}, f32[768]{0:T(1024)}, f32[768]{0:T(1024)}, f32[768]{0:T(1024)}) fusion(f32[2048,768]{1,0:T(8,128)} %copy-done, pred[2,1024]{1,0:T(4,128)(4,1)} %get-tuple-element.175, ...), kind=kLoop, calls=%fused_computation.80 | loop fusion | flops 42460416 | bytes 12628992 | tf_op jit(solution)/shard_map/transpose(jvp(vmap()))/reduce_sum | solution.py:78
  656.0 28.2 %multiply_reduce_fusion.23 = (f32[768]{0:T(1024)}, f32[768]{0:T(1024)}, f32[768]{0:T(1024)}, f32[768]{0:T(1024)}, f32[768]{0:T(1024)}, /*index=5*/f32[768]{0:T(1024)}, f32[768]{0:T(1024)}, f32[768]{0:T(1024)}, f32[768]{0:T(1024)}) fusion(f32[2048,768]{1,0:T(8,128)} %copy-done, pred[2,1024]{1,0:T(4,128)(4,1)} %get-tuple-element.185, ...), kind=kLoop, calls=%fused_computation.71 | loop fusion | flops 42460416 | bytes 12628992 | tf_op jit(solution)/shard_map/transpose(jvp(vmap()))/reduce_sum | solution.py:78
  700.1 12.2 fusion.19
  834.5 12.7 fusion.38
  847.2 11.0 fusion.37
  858.2 14.7 multiply_reduce_fusion.4
  872.9 19.3 %select_multiply_fusion.30 = (f32[2,1024,768]{2,1,0:T(8,128)}, f32[2,1024,768]{2,1,0:T(8,128)}, f32[2,1024,768]{2,1,0:T(8,128)}, f32[2,1024,768]{2,1,0:T(8,128)}...) fusion(f32[768]{0:T(1024)} %get-tuple-element.68, ...), kind=kLoop, calls=%fused_computation.139 | loop fusion | flops 28311552 | bytes 62960640 | tf_op jit(solution)/shard_map/transpose(jvp(vmap()))/mul | solution.py:78
  892.2 19.4 %select_multiply_fusion.32 = (f32[2,1024,768]{2,1,0:T(8,128)}, f32[2,1024,768]{2,1,0:T(8,128)}, f32[2,1024,768]{2,1,0:T(8,128)}, f32[2,1024,768]{2,1,0:T(8,128)}...) fusion(f32[768]{0:T(1024)} %get-tuple-element.66, ...), kind=kLoop, calls=%fused_computation.141 | loop fusion | flops 28311552 | bytes 62960640 | tf_op jit(solution)/shard_map/transpose(jvp(vmap()))/mul | solution.py:78
  911.6 19.6 %select_multiply_fusion.31 = (f32[2,1024,768]{2,1,0:T(8,128)}, f32[2,1024,768]{2,1,0:T(8,128)}, f32[2,1024,768]{2,1,0:T(8,128)}, f32[2,1024,768]{2,1,0:T(8,128)}...) fusion(f32[768]{0:T(1024)} %get-tuple-element.67, ...), kind=kLoop, calls=%fused_computation.140 | loop fusion | flops 26738688 | bytes 62958592 | tf_op jit(solution)/shard_map/transpose(jvp(vmap()))/mul | solution.py:78
  1028.7 56.8 %pad_add_fusion = f32[2,1056,768]{2,1,0:T(8,128)} fusion(f32[2,1024,768]{2,1,0:T(8,128)} %get-tuple-element.147, f32[2,1024,768]{2,1,0:T(8,128)} %get-tuple-element.148, f32[2,1024,768]{2,1,0:T(8,128)} %get-tuple-element.149, f32[2,1024,768]{2,1,0:T(8,128)} %get-tuple-element.150, f32[2,1024,768]{2,1,0:T(8,128)} %get-tuple-element.151, ...), kind=kLoop, calls=%fused_computation.18 | loop fusion | flops 42172416 | bytes 176357376 | tf_op jit(solution)/shard_map/transpose(jvp(vmap()))/add_any | solution.py:78
  1085.4 17.6 %convert_reduce_fusion.4 = (f32[768]{0:T(1024)S(1)}, bf16[2,1024,768]{2,1,0:T(8,128)(2,1)S(1)}) fusion(f32[2,1024,768]{2,1,0:T(8,128)} %copy.207, f32[2,1024,768]{2,1,0:T(8,128)} %get-tuple-element.140, f32[2,1024,768]{2,1,0:T(8,128)} %get-tuple-element.142, f32[2,1024,768]{2,1,0:T(8,128)} %get-tuple-element.141, f32[2,1024,768]{2,1,0:T(8,128)} %get-tuple-element.143, ...), kind=kLoop, calls=%fused_computation.47 | loop fusion | flops 15727872 | bytes 53480448 | tf_op jit(solution)/shard_map/reduce_sum | solution.py:118
  1127.6 28.8 %dynamic-update-slice.19 = f32[32,222264]{1,0:T(8,128)} dynamic-update-slice(f32[32,222264]{1,0:T(8,128)} %dynamic-update-slice.18, f32[32,73728]{1,0:T(8,128)} %reshape.621, s32[]{} %constant.388, s32[]{} %constant.398) | dynamic-update-slice | bytes 18874372
  1156.4 28.4 %dynamic-update-slice.20 = f32[32,222264]{1,0:T(8,128)} dynamic-update-slice(f32[32,222264]{1,0:T(8,128)} %dynamic-update-slice.19, f32[32,73728]{1,0:T(8,128)} %reshape.622, s32[]{} %constant.388, s32[]{} %constant.399) | dynamic-update-slice | bytes 18874372
  1204.4 419.1 %all-reduce.81.cloned.1.call-done = f32[32,222264]{1,0:T(8,128)} async-done(((f32[32,222264]{1,0:T(8,128)}), f32[32,222264]{1,0:T(8,128)}) %all-reduce.81.cloned.1.call-update) | async-done | bytes 28449808
  (743 shorter events, 517.7 us)
Async XLA Ops:
  7.2 124.7 %all-gather.7.cloned.1.call-start = ((), (), s32[]{:S(2)}) async-start(), calls=%async_computation | async-start | bytes 1216512 | tf_op jit(solution)/shard_map/all_gather | solution.py:174
  7.9 155.0 %all-gather.9.cloned.1.call-start = ((), (), s32[]{:S(2)}) async-start(), calls=%async_computation.1 | async-start | bytes 1216512 | tf_op jit(solution)/shard_map/all_gather | solution.py:175
  8.7 171.1 %all-gather.11.cloned.1.call-start = ((), (), s32[]{:S(2)}) async-start(), calls=%async_computation.2 | async-start | bytes 1216512 | tf_op jit(solution)/shard_map/all_gather | solution.py:176
  9.4 397.3 %all-gather.13.cloned.1.call-start = ((), (), s32[]{:S(2)}) async-start(), calls=%async_computation.3 | async-start | bytes 1216512 | tf_op jit(solution)/shard_map/all_gather | solution.py:177
  10.0 406.7 %all-gather.15.cloned.1.call-start = ((), (), s32[]{:S(2)}) async-start(), calls=%async_computation.4 | async-start | bytes 4866048 | tf_op jit(solution)/shard_map/all_gather | solution.py:210
  10.6 474.4 %all-gather.17.cloned.1.call-start = ((), (), s32[]{:S(2)}) async-start(), calls=%async_computation.5 | async-start | bytes 4866048 | tf_op jit(solution)/shard_map/all_gather | solution.py:211
  11.1 1612.4 %all-reduce.81.cloned.1.call-start = ((), (), s32[]{:S(2)}) async-start(), calls=%async_computation.6 | async-start | bytes 56918016
  12.0 156.1 %copy-start.152 = (f32[2,64]{1,0:T(2,128)}, f32[2,64]{1,0:T(2,128)S(1)}, u32[]{:S(2)}) copy-start(f32[2,64]{1,0:T(2,128)S(1)} %convert_reduce_fusion.9) | copy-start | bytes 1540
  13.8 193.9 %copy-start.149 = (pred[2,64,64]{2,1,0:T(8,128)(4,1)}, pred[2,64,64]{2,1,0:T(8,128)(4,1)S(1)}, u32[]{:S(2)}) copy-start(pred[2,64,64]{2,1,0:T(8,128)(4,1)S(1)} %get-tuple-element.206) | copy-start | bytes 24580
  16.8 213.0 %copy-start.73 = (f32[64,64]{1,0:T(8,128)}, f32[64,64]{1,0:T(8,128)S(1)}, u32[]{:S(2)}) copy-start(f32[64,64]{1,0:T(8,128)S(1)} %get-tuple-element.233) | copy-start | bytes 49156
  17.6 247.5 %copy-start.69 = (pred[2,1024,64]{1,2,0:T(8,128)(4,1)}, pred[2,1024,64]{1,2,0:T(8,128)(4,1)S(1)}, u32[]{:S(2)}) copy-start(pred[2,1024,64]{1,2,0:T(8,128)(4,1)S(1)} %broadcast_compare_fusion) | copy-start | bytes 393220
  18.5 225.1 %copy-start.67 = (pred[2,64,1024]{2,1,0:T(8,128)(4,1)}, pred[2,64,1024]{2,1,0:T(8,128)(4,1)S(1)}, u32[]{:S(2)}) copy-start(pred[2,64,1024]{2,1,0:T(8,128)(4,1)S(1)} %broadcast_compare_fusion.1) | copy-start | bytes 393220
  62.6 66.4 %copy-start.5 = (bf16[2,1024,768]{2,1,0:T(8,128)(2,1)S(1)}, bf16[2,1024,768]{2,1,0:T(8,128)(2,1)}, u32[]{:S(2)}) copy-start(bf16[2,1024,768]{2,1,0:T(8,128)(2,1)} %param.39) | copy-start | bytes 9437188
  131.9 96.2 %copy-start.102 = (pred[2,64,64]{1,2,0:T(8,128)(4,1)}, pred[2,64,64]{1,2,0:T(8,128)(4,1)S(1)}, u32[]{:S(2)}) copy-start(pred[2,64,64]{1,2,0:T(8,128)(4,1)S(1)} %copy.162) | copy-start | bytes 24580
  162.9 70.6 %copy-start.20 = (f32[2,12,64,64]{3,2,1,0:T(8,128)}, f32[2,12,64,64]{3,2,1,0:T(8,128)S(1)}, u32[]{:S(2)}) copy-start(f32[2,12,64,64]{3,2,1,0:T(8,128)S(1)} %fusion.71) | copy-start | bytes 1179652
  173.9 78.4 %copy-start.34 = (f32[2,12,64,64]{3,2,1,0:T(8,128)}, f32[2,12,64,64]{3,2,1,0:T(8,128)S(1)}, u32[]{:S(2)}) copy-start(f32[2,12,64,64]{3,2,1,0:T(8,128)S(1)} %convolution_divide_fusion) | copy-start | bytes 1179652
  175.3 52.7 %copy-start.24 = (f32[2,12,64,64]{2,3,1,0:T(8,128)}, f32[2,12,64,64]{2,3,1,0:T(8,128)S(1)}, u32[]{:S(2)}) copy-start(f32[2,12,64,64]{2,3,1,0:T(8,128)S(1)} %get-tuple-element.209) | copy-start | bytes 1179652
  175.3 52.7 %copy-start.104 = (f32[2,12,64]{2,1,0:T(8,128)}, f32[2,12,64]{2,1,0:T(8,128)S(1)}, u32[]{:S(2)}) copy-start(f32[2,12,64]{2,1,0:T(8,128)S(1)} %get-tuple-element.208) | copy-start | bytes 18436
  175.6 52.5 %copy-start.106 = (f32[2,12,64]{2,1,0:T(8,128)}, f32[2,12,64]{2,1,0:T(8,128)S(1)}, u32[]{:S(2)}) copy-start(f32[2,12,64]{2,1,0:T(8,128)S(1)} %fusion.103) | copy-start | bytes 18436
  175.9 31.7 %copy-start.181 = (f32[2,12]{1,0:T(2,128)}, f32[2,12]{1,0:T(2,128)S(1)}, u32[]{:S(2)}) copy-start(f32[2,12]{1,0:T(2,128)S(1)} %multiply_reduce_fusion.42) | copy-start | bytes 292
  280.6 126.1 %copy-start.186 = (f32[768]{0:T(1024)S(1)}, f32[768]{0:T(1024)}, u32[]{:S(2)}) copy-start(f32[768]{0:T(1024)} %convert_element_type.136) | copy-start | bytes 9220
  416.7 68.2 %copy-start.185 = (f32[768]{0:T(1024)S(1)}, f32[768]{0:T(1024)}, u32[]{:S(2)}) copy-start(f32[768]{0:T(1024)} %convert_element_type.142) | copy-start | bytes 9220
  560.4 37.6 %slice-start.26 = ((s8[6291456]{0:T(1024)(128)(4,1)}), s8[4194304]{0:T(1024)(128)(4,1)S(1)}, s32[]{:S(2)}) async-start(s8[6291456]{0:T(1024)(128)(4,1)} %bitcast.366), calls=%async_computation.33 | async-start | bytes 8388608
  1156.4 32.8 %copy-start.114 = (f32[32,24]{1,0:T(8,128)S(1)}, f32[32,24]{1,0:T(8,128)}, u32[]{:S(2)}) copy-start(f32[32,24]{1,0:T(8,128)} %reshape.626) | copy-start | bytes 9220
  (204 other events, 1804.4 us)
Sparse Core Ops, SparseCore 0:
  10.9 56.8 all-gather.6
  70.7 53.0 all-gather.8
  126.7 53.0 all-gather.10
  182.5 53.0 all-gather.12
  238.3 62.5 all-gather.14
  303.6 62.3 all-gather.16
  1190.9 432.5 all-reduce.80
where the time goes:
time: 1660 us; the launch traced here: 1650 us
  matrix products  491 us (30%)
  waiting for transfers between devices  426 us (26%)
  other arithmetic  384 us (23%)
  local copies, waits for them, and re-layouts  244 us (15%)
  blocking collectives  82.1 us (5%)
  between operations  18.1 us (1%)
    unnamed x8, waiting for transfers between devices  423 us
    dot_general x94, matrix products, batch_mapped(): return jnp.einsum(form, left_side, right_side, precision=HIGHEST)  244 us
    convert_element_type x1, other arithmetic, shards(): context_low = mixed_context.astype(jnp.bfloat16)  126 us
    dot_general x6, matrix products, forward_dot(): return jnp.dot(left_side, right_side, preferred_element_type=jnp.float32)  111 us
    unnamed x478, local copies, waits for them, and re-layouts  110 us
    dot_general x6, matrix products, against_cols(): lax.dot_general(left_side, right_side, (((1,), (1,)), ((), ())), preferre...  79.4 us
    reduce_sum x4, other arithmetic, nystrom(): conv_weight[offset][None, :] * padded[offset:offset + sequence_length]  72.6 us
    mul x3, other arithmetic, nystrom(): conv_weight[offset][None, :] * padded[offset:offset + sequence_length]  58.3 us
  transfers between devices with their start and end apart: 7, of which 2 were waited for; matrix products, arithmetic and copies ran while one was open for 24% of the time, Pallas kernels for 0%

commit v1 on v0

--- a/solution.py
+++ b/solution.py
@@ -122,28 +122,69 @@
     return jax.nn.gelu(values, approximate=False)
 
 
-def pack_terms(terms, dims, count):
-    pieces = []
-    for term, dim in zip(terms, dims):
-        moved = jnp.moveaxis(term, dim, 0)
-        pieces.append(moved.reshape(count, -1))
-    return jnp.concatenate(pieces, axis=1)
-
-
-def unpack_terms(flat_row, terms, dims, count):
-    flat_row = flat_row.reshape(-1)
-    results = []
-    start = 0
-    for term, dim in zip(terms, dims):
-        moved_shape = tuple(jnp.moveaxis(term, dim, 0).shape)
-        local_shape = (moved_shape[0] // count,) + moved_shape[1:]
-        length = 1
-        for extent in local_shape:
-            length = length * extent
-        piece = flat_row[start : start + length].reshape(local_shape)
-        results.append(jnp.moveaxis(piece, 0, dim))
-        start = start + length
-    return tuple(results)
+def digits():
+    found = []
+    for axis in ("wide", "narrow"):
+        stride = lax.axis_size(axis) // 2
+        while stride >= 1:
+            found.append((axis, stride))
+            stride //= 2
+    return found
+
+
+def stage_orders():
+    count = len(digits())
+    if lax.axis_size("wide") == 8 and lax.axis_size("narrow") == 4:
+        return [(4, 2, 3, 1, 0), (4, 3, 1, 2, 0), (4, 1, 2, 3, 0)]
+    return [tuple(range(count - 1, -1, -1))] * 3
+
+
+def exchange(values, axis, stride):
+    return lax.ppermute(values, axis, [(i, i ^ stride) for i in range(lax.axis_size(axis))])
+
+
+def digit_of(axis, stride):
+    return (lax.axis_index(axis) // stride) % 2
+
+
+def gather_rows(shard):
+    rows, columns = shard.shape
+    places = digits()
+    width = columns // 3
+    parts = []
+    for number, order in enumerate(stage_orders()):
+        held = shard[:, number * width : (number + 1) * width]
+        held = held.reshape((1,) * len(places) + (rows, width))
+        for dim in order[::-1]:
+            mine = digit_of(*places[dim])
+            got = exchange(held, *places[dim])
+            first = jnp.where(mine == 0, held, got)
+            second = jnp.where(mine == 0, got, held)
+            held = jnp.concatenate([first, second], dim)
+        parts.append(held.reshape(-1, rows, width))
+    return jnp.concatenate(parts, 2)
+
+
+def scatter_rows(whole):
+    _, rows, columns = whole.shape
+    places = digits()
+    width = columns // 3
+    parts = []
+    for number, order in enumerate(stage_orders()):
+        held = whole[:, :, number * width : (number + 1) * width]
+        held = held.reshape((2,) * len(places) + (rows, width))
+        for dim in order:
+            mine = digit_of(*places[dim])
+            keep = lax.dynamic_slice_in_dim(held, mine, 1, dim).astype(jnp.float32)
+            send = lax.dynamic_slice_in_dim(held, 1 - mine, 1, dim).astype(jnp.bfloat16)
+            held = keep + exchange(send, *places[dim]).astype(jnp.float32)
+        parts.append(held.reshape(rows, width))
+    return jnp.concatenate(parts, 1)
+
+
+def pad_rows(flat, rows):
+    count, length = flat.shape
+    return jnp.pad(flat, ((0, 0), (0, rows * 768 - length))).reshape(count, rows, 768)
 
 
 def shards(
@@ -170,23 +211,33 @@
 ):
     batch_rows, sequence_length, feature_width = inputs.shape
     group_count = lax.axis_size("wide") * lax.axis_size("narrow")
-    attn_full = (
-        lax.all_gather(w_query, ("wide", "narrow"), axis=1, tiled=True),
-        lax.all_gather(w_key, ("wide", "narrow"), axis=1, tiled=True),
-        lax.all_gather(w_value, ("wide", "narrow"), axis=1, tiled=True),
-        lax.all_gather(w_out, ("wide", "narrow"), axis=1, tiled=True),
-        lax.all_gather(conv_weight, ("wide", "narrow"), axis=1, tiled=True),
-        lax.all_gather(b_query, ("wide", "narrow"), axis=0, tiled=True),
-        lax.all_gather(b_value, ("wide", "narrow"), axis=0, tiled=True),
-        lax.all_gather(b_out, ("wide", "narrow"), axis=0, tiled=True),
-        lax.all_gather(gain_one, ("wide", "narrow"), axis=0, tiled=True),
-        lax.all_gather(shift_one, ("wide", "narrow"), axis=0, tiled=True),
-    )
+    own = feature_width // group_count
+    vectors = (b_query, b_value, b_out, gain_one, shift_one, b_down, gain_two, shift_two)
+    flat = jnp.concatenate([conv_weight.T.reshape(-1)] + list(vectors) + [b_up])
+    small_rows = -(-flat.shape[0] // 768)
+    small = pad_rows(flat[None], small_rows)[0]
+    bundle = jnp.concatenate([w_query.T, w_key.T, w_value.T, small], axis=0)
+    gathered = gather_rows(bundle)
+    w_q, w_k, w_v = [
+        gathered[:, i * own : (i + 1) * own].reshape(feature_width, feature_width) for i in range(3)
+    ]
+    small = gathered[:, 3 * own :].reshape(group_count, -1)
+    conv_full = small[:, : own * KW].reshape(feature_width, KW).T
+    small = small[:, own * KW :]
+    b_q, b_v, b_o, g_one, s_one, b_d, g_two, s_two = [
+        small[:, i * own : (i + 1) * own].reshape(feature_width).astype(jnp.float32)
+        for i in range(8)
+    ]
+    b_u = small[:, 8 * own : 8 * own + b_up.shape[0]].reshape(-1).astype(jnp.float32)
+    later = lax.optimization_barrier((w_out.T, w_up.T, w_down.T, gathered))
+    w_o, w_u, w_d = [
+        lax.all_gather(shard, ("wide", "narrow"), axis=0, tiled=True) for shard in later[:3]
+    ]
     rows_low = inputs.reshape(batch_rows * sequence_length, feature_width)
     rows_in = rows_low.astype(jnp.float32)
-    query_rows = forward_dot(rows_low, attn_full[0]) + attn_full[5].astype(jnp.float32)
-    key_rows = forward_dot(rows_low, attn_full[1])
-    value_rows = forward_dot(rows_low, attn_full[2]) + attn_full[6].astype(jnp.float32)
+    query_rows = against_cols(rows_low, w_q) + b_q
+    key_rows = against_cols(rows_low, w_k)
+    value_rows = against_cols(rows_low, w_v) + b_v
 
     def attend(query_part, key_part, value_part, conv_part):
         shaped = (batch_rows, sequence_length, feature_width)
@@ -200,126 +251,106 @@
         )
         return mixed.reshape(batch_rows * sequence_length, feature_width)
 
-    mixed_context = attend(query_rows, key_rows, value_rows, attn_full[4].astype(jnp.float32))
+    conv_taps = conv_full.astype(jnp.float32)
+    mixed_context = attend(query_rows, key_rows, value_rows, conv_taps)
     context_low = mixed_context.astype(jnp.bfloat16)
-    attended = forward_dot(context_low, attn_full[3]) + attn_full[7].astype(jnp.float32)
+    attended = against_cols(context_low, w_o) + b_o
     normal_one, inv_one = normalize(rows_in + attended)
-    normed = normal_one * attn_full[8].astype(jnp.float32) + attn_full[9].astype(jnp.float32)
+    normed = normal_one * g_one + s_one
     normed_low = normed.astype(jnp.bfloat16)
-    ffn_full = (
-        lax.all_gather(w_up, ("wide", "narrow"), axis=1, tiled=True),
-        lax.all_gather(w_down, ("wide", "narrow"), axis=1, tiled=True),
-        lax.all_gather(b_up, ("wide", "narrow"), axis=0, tiled=True),
-        lax.all_gather(b_down, ("wide", "narrow"), axis=0, tiled=True),
-        lax.all_gather(gain_two, ("wide", "narrow"), axis=0, tiled=True),
-        lax.all_gather(shift_two, ("wide", "narrow"), axis=0, tiled=True),
-    )
-    up_pre = forward_dot(normed_low, ffn_full[0]) + ffn_full[2].astype(jnp.float32)
+    up_pre = against_cols(normed_low, w_u) + b_u
     hidden = gelu_exact(up_pre).astype(jnp.bfloat16)
-    down_out = forward_dot(hidden, ffn_full[1]) + ffn_full[3].astype(jnp.float32)
+    down_out = against_cols(hidden, w_d) + b_d
     normal_two, inv_two = normalize(normed + down_out)
-    layer_out = (
-        normal_two * ffn_full[4].astype(jnp.float32) + ffn_full[5].astype(jnp.float32)
-    ).astype(jnp.bfloat16)
-    ffn_back = (
-        lax.all_gather(w_up, ("wide", "narrow"), axis=1, tiled=True),
-        lax.all_gather(w_down, ("wide", "narrow"), axis=1, tiled=True),
-        lax.all_gather(b_up, ("wide", "narrow"), axis=0, tiled=True),
-        lax.all_gather(b_down, ("wide", "narrow"), axis=0, tiled=True),
-        lax.all_gather(gain_two, ("wide", "narrow"), axis=0, tiled=True),
-        lax.all_gather(shift_two, ("wide", "narrow"), axis=0, tiled=True),
-    )
+    layer_out = (normal_two * g_two + s_two).astype(jnp.bfloat16)
     upstream = cotangent.reshape(batch_rows * sequence_length, feature_width).astype(jnp.float32)
-    grad_two, grad_gain_two, grad_shift_two = norm_back(
-        upstream, normal_two, inv_two, ffn_back[4].astype(jnp.float32)
-    )
+    grad_two, grad_gain_two, grad_shift_two = norm_back(upstream, normal_two, inv_two, g_two)
     down_low = grad_two.astype(jnp.bfloat16)
-    grad_w_down = across_rows(hidden, down_low)
+    grad_w_down = across_rows(down_low, hidden)
     grad_b_down = column_sums(down_low)
-    hidden_grad = against_cols(down_low, ffn_back[1])
+    hidden_grad = forward_dot(down_low, w_d)
     up_low = jax.vjp(gelu_exact, up_pre)[1](hidden_grad)[0].astype(jnp.bfloat16)
-    grad_w_up = across_rows(normed_low, up_low)
+    grad_w_up = across_rows(up_low, normed_low)
     grad_b_up = column_sums(up_low)
-    normed_grad = grad_two + against_cols(up_low, ffn_back[0])
-    ffn_dims = (1, 1, 0, 0, 0, 0)
-    ffn_terms = (grad_w_up, grad_w_down, grad_b_up, grad_b_down, grad_gain_two, grad_shift_two)
-    attn_back = (
-        lax.all_gather(w_query, ("wide", "narrow"), axis=1, tiled=True),
-        lax.all_gather(w_key, ("wide", "narrow"), axis=1, tiled=True),
-        lax.all_gather(w_value, ("wide", "narrow"), axis=1, tiled=True),
-        lax.all_gather(w_out, ("wide", "narrow"), axis=1, tiled=True),
-        lax.all_gather(conv_weight, ("wide", "narrow"), axis=1, tiled=True),
-        lax.all_gather(b_query, ("wide", "narrow"), axis=0, tiled=True),
-        lax.all_gather(b_value, ("wide", "narrow"), axis=0, tiled=True),
-        lax.all_gather(b_out, ("wide", "narrow"), axis=0, tiled=True),
-        lax.all_gather(gain_one, ("wide", "narrow"), axis=0, tiled=True),
-        lax.all_gather(shift_one, ("wide", "narrow"), axis=0, tiled=True),
-    )
-    grad_one, grad_gain_one, grad_shift_one = norm_back(
-        normed_grad, normal_one, inv_one, attn_back[8].astype(jnp.float32)
-    )
+    normed_grad = grad_two + forward_dot(up_low, w_u)
+    grad_one, grad_gain_one, grad_shift_one = norm_back(normed_grad, normal_one, inv_one, g_one)
     attended_low = grad_one.astype(jnp.bfloat16)
-    grad_w_out = across_rows(context_low, attended_low)
+    grad_w_out = across_rows(attended_low, context_low)
     grad_b_out = column_sums(attended_low)
-    context_grad = against_cols(attended_low, attn_back[3])
-    pullback = jax.vjp(attend, query_rows, key_rows, value_rows, attn_back[4].astype(jnp.float32))[
-        1
-    ]
+    context_grad = forward_dot(attended_low, w_o)
+
+    def by_device(values):
+        return values.reshape((group_count, -1) + values.shape[1:])
+
+    early_vectors = (
+        grad_b_out,
+        grad_gain_one,
+        grad_shift_one,
+        grad_b_down,
+        grad_gain_two,
+        grad_shift_two,
+        grad_b_up,
+    )
+    early = jnp.concatenate([by_device(v) for v in early_vectors], axis=1)
+    early_rows = -(-early.shape[1] // 768)
+    share_up = scatter_rows(by_device(grad_w_up))
+    share_down = scatter_rows(by_device(grad_w_down))
+    share_out = scatter_rows(
+        jnp.concatenate([by_device(grad_w_out), pad_rows(early, early_rows)], axis=1)
+    )
+    pullback = jax.vjp(attend, query_rows, key_rows, value_rows, conv_taps)[1]
     query_grad, key_grad, value_grad, grad_conv = pullback(context_grad)
     query_low = query_grad.astype(jnp.bfloat16)
     key_low = key_grad.astype(jnp.bfloat16)
     value_low = value_grad.astype(jnp.bfloat16)
-    grad_w_query = across_rows(rows_low, query_low)
-    grad_b_query = column_sums(query_low)
-    grad_w_key = across_rows(rows_low, key_low)
-    grad_w_value = across_rows(rows_low, value_low)
-    grad_b_value = column_sums(value_low)
+    late = jnp.concatenate(
+        [
+            by_device(grad_conv.T).reshape(group_count, -1),
+            by_device(column_sums(query_low)),
+            by_device(column_sums(value_low)),
+        ],
+        axis=1,
+    )
+    late_rows = -(-late.shape[1] // 768)
+    share_late = scatter_rows(
+        jnp.concatenate(
+            [
+                by_device(across_rows(query_low, rows_low)),
+                by_device(across_rows(key_low, rows_low)),
+                by_device(across_rows(value_low, rows_low)),
+                pad_rows(late, late_rows),
+            ],
+            axis=1,
+        )
+    )
     input_grad = (
         grad_one
-        + against_cols(query_low, attn_back[0])
-        + against_cols(key_low, attn_back[1])
-        + against_cols(value_low, attn_back[2])
-    )
-    attn_dims = (1, 1, 1, 1, 1, 0, 0, 0, 0, 0)
-    attn_terms = (
-        grad_w_query,
-        grad_w_key,
-        grad_w_value,
-        grad_w_out,
-        grad_conv,
-        grad_b_query,
-        grad_b_value,
-        grad_b_out,
-        grad_gain_one,
-        grad_shift_one,
-    )
-    every_term = attn_terms + ffn_terms
-    every_dim = attn_dims + ffn_dims
-    every_packed = pack_terms(every_term, every_dim, group_count)
-    summed_row = lax.psum_scatter(every_packed, ("wide", "narrow"), scatter_dimension=0, tiled=True)
-    summed = unpack_terms(summed_row, every_term, every_dim, group_count)
-    attn_shares = summed[:10]
-    final_ffn = summed[10:]
+        + forward_dot(query_low, w_q)
+        + forward_dot(key_low, w_k)
+        + forward_dot(value_low, w_v)
+    )
+    early = share_out[own:].reshape(-1)
+    late = share_late[3 * own :].reshape(-1)
     shaped_out = (batch_rows, sequence_length, feature_width)
     return (
         layer_out.reshape(shaped_out),
         input_grad.reshape(shaped_out),
-        attn_shares[0],
-        attn_shares[5],
-        attn_shares[1],
-        attn_shares[2],
-        attn_shares[6],
-        attn_shares[4],
-        attn_shares[3],
-        attn_shares[7],
-        attn_shares[8],
-        attn_shares[9],
-        final_ffn[0],
-        final_ffn[2],
-        final_ffn[1],
-        final_ffn[3],
-        final_ffn[4],
-        final_ffn[5],
+        share_late[:own].T,
+        late[own * KW : own * KW + own],
+        share_late[own : 2 * own].T,
+        share_late[2 * own : 3 * own].T,
+        late[own * KW + own : own * KW + 2 * own],
+        late[: own * KW].reshape(own, KW).T,
+        share_out[:own].T,
+        early[:own],
+        early[own : 2 * own],
+        early[2 * own : 3 * own],
+        share_up.T,
+        early[6 * own : 6 * own + b_up.shape[0]],
+        share_down.T,
+        early[3 * own : 4 * own],
+        early[4 * own : 5 * own],
+        early[5 * own : 6 * own],
     )
 
 

time: 1660 us -> 1280 us (0.77)
  waiting for transfers between devices: 426 us -> 101 us
  blocking collectives: 82.1 us -> 0 us
  local copies, waits for them, and re-layouts: 244 us -> 171 us
  starting transfers between devices: 0.27 us -> 71.7 us
  other arithmetic: 384 us -> 407 us
    unnamed x8 -> x3, waiting for transfers between devices: 423 us -> 0.05 us
    ppermute x0 -> x75, waiting for transfers between devices: none -> 100 us  [exchange(): lax.ppermute(values, axis, [(i, i ^ stride) for i in range(lax.axis_size(...]
    unnamed x478 -> x785, local copies, waits for them, and re-layouts: 110 us -> 16.2 us
    ppermute x0 -> x75, starting transfers between devices: none -> 70.9 us  [exchange(): lax.ppermute(values, axis, [(i, i ^ stride) for i in range(lax.axis_size(...]
    all_gather x1 -> x0, blocking collectives: 44 us -> none  [shards(): lax.all_gather(conv_weight, ('wide', 'narrow'), axis=1, tiled=True)]
    unnamed x1 -> x0, blocking collectives: 38.1 us -> none
    reshape x23 -> x16, local copies, waits for them, and re-layouts: 33.2 us -> 3.01 us  [the longest x9 1.3 us: by_device(): return values.reshape((group_count, -1) + values.shape[1:])]
    convert_element_type x0 -> x70, local copies, waits for them, and re-layouts: none -> 30.1 us  [the longest x60 23.5 us: scatter_rows(): send = lax.dynamic_slice_in_dim(held, 1 - mine, 1, dim).astype(jnp.bfloat16)]
  transfers between devices with their start and end apart: 7 -> 78, of which waited for: 2 -> 33; matrix products, arithmetic and copies ran while one was open for 24% -> 47% of each run, Pallas kernels for 0% -> 0%
where the time goes in v1:
time: 1280 us; the launch traced here: 1270 us
  matrix products  502 us (39%)
  other arithmetic  407 us (32%)
  local copies, waits for them, and re-layouts  171 us (13%)
  waiting for transfers between devices  101 us (8%)
  starting transfers between devices  71.7 us (6%)
  between operations  21.7 us (2%)
    dot_general x94, matrix products, batch_mapped(): return jnp.einsum(form, left_side, right_side, precision=HIGHEST)  250 us
    convert_element_type x1, other arithmetic, shards(): context_low = mixed_context.astype(jnp.bfloat16)  131 us
    dot_general x6, matrix products, against_cols(): lax.dot_general(left_side, right_side, (((1,), (1,)), ((), ())), preferre...  108 us
    ppermute x75, waiting for transfers between devices, exchange(): lax.ppermute(values, axis, [(i, i ^ stride) for i in range(lax.axis_size(...  100 us
    dot_general x6, matrix products, forward_dot(): return jnp.dot(left_side, right_side, preferred_element_type=jnp.float32)  86.9 us
    ppermute x75, starting transfers between devices, exchange(): lax.ppermute(values, axis, [(i, i ^ stride) for i in range(lax.axis_size(...  70.9 us
    reduce_sum x4, other arithmetic, nystrom(): conv_weight[offset][None, :] * padded[offset:offset + sequence_length]  70.6 us
    add_any x1, other arithmetic, nystrom(): padded[offset:offset + sequence_length]  56.6 us
  transfers between devices with their start and end apart: 78, of which 33 were waited for; matrix products, arithmetic and copies ran while one was open for 47% of the time, Pallas kernels for 0%

profile of v1, /device:TPU:0, one launch (start us, length us, event | category | flops | bytes accessed | tf_op | source)
XLA Modules:
  0.0 1274.0 jit_solution(12415443602850639531)
XLA Ops:
  76.2 9.3 mul.1008
  91.9 9.2 mul.1011
  233.4 130.9 %add_convert_fusion.2 = bf16[2,1024,768]{2,1,0:T(8,128)(2,1)S(1)} fusion(f32[2,1024,768]{2,1,0:T(8,128)} %bitcast.429, f32[2,1024,768]{2,1,0:T(8,128)} %copy.777, f32[768]{0:T(1024)S(1)} %get-tuple-element.65, f32[768]{0:T(1024)S(1)} %get-tuple-element.66, f32[768]{0:T(1024)S(1)} %get-tuple-element.67, f32[768]{0:T(1024)S(1)} %get-tuple-element.68, ...), kind=kLoop, calls=%fused_computation.100 | loop fusion | flops 155713536 | bytes 15895552 | tf_op jit(solution)/shard_map/convert_element_type | solution.py:256
  374.9 67.9 %multiply_convert_fusion = (bf16[2048,3072]{1,0:T(8,128)(2,1)}, f32[2048,3072]{1,0:T(8,128)}, f32[2048,3072]{1,0:T(8,128)}) fusion(f32[3072]{0:T(1024)S(1)} %copy-done.346, bf16[3072,768]{1,0:T(8,128)(2,1)} %all-gather.6.cloned.1.call-done, f32[2048,768]{1,0:T(8,128)} %copy-done.18, f32[768]{0:T(1024)S(1)} %copy-done.353, f32[768]{0:T(1024)S(1)} %copy-done.300, ...), kind=kOutput, calls=%fused_computation.4 | convolution fusion | flops 10086776832 | bytes 73959424 | tf_op jit(solution)/shard_map/dot_general | solution.py:112
  442.8 16.0 %fusion.193 = (f32[2048]{0:T(1024)S(1)}, f32[2048,768]{1,0:T(8,128)S(1)}) fusion(f32[768]{0:T(1024)S(1)} %copy-done.354, bf16[2048,3072]{1,0:T(8,128)(2,1)} %get-tuple-element.115, bf16[768,3072]{1,0:T(8,128)(2,1)} %all-gather.8.cloned.1.call-done, f32[768]{0:T(1024)S(1)} %copy-done.353, f32[768]{0:T(1024)S(1)} %copy-done.300, ...), kind=kOutput, calls=%fused_computation.663 | convolution fusion | flops 9674684416 | bytes 29918208 | tf_op jit(solution)/shard_map/dot_general | solution.py:112
  468.3 17.7 %fusion.142 = f32[768,3072]{1,0:T(8,128)} fusion(bf16[2048,3072]{1,0:T(8,128)(2,1)} %get-tuple-element.115, f32[2048,768]{1,0:T(8,128)S(1)} %get-tuple-element.100), kind=kOutput, calls=%fused_computation.629 | convolution fusion | flops 9665249280 | bytes 28311552 | tf_op jit(solution)/shard_map/dot_general | solution.py:106
  486.0 32.5 %convert_reduce_fusion = (f32[3072]{0:T(1024)}, bf16[2048,3072]{1,0:T(8,128)(2,1)}) fusion(f32[2048,3072]{1,0:T(8,128)} %get-tuple-element.116, bf16[768,3072]{1,0:T(8,128)(2,1)} %all-gather.8.cloned.1.call-done, f32[2048,768]{1,0:T(8,128)} %copy-done.75, f32[2048,3072]{1,0:T(8,128)} %get-tuple-element.269, f32[3072]{0:T(1024)S(1)} %copy-done.346), kind=kOutput, calls=%fused_computation.2 | convolution fusion | flops 9772200960 | bytes 73949184 | tf_op jit(solution)/shard_map/dot_general | solution.py:102
  518.4 19.4 %fusion.160 = f32[3072,768]{1,0:T(8,128)} fusion(bf16[2048,3072]{1,0:T(8,128)(2,1)} %get-tuple-element.285, f32[2048,768]{1,0:T(8,128)} %copy-done.18, f32[768]{0:T(1024)S(1)} %copy-done.353, f32[768]{0:T(1024)S(1)} %copy-done.300, f32[2048]{0:T(1024)S(1)} %add_rsqrt_fusion.1, f32[2048]{0:T(1024)S(1)} %broadcast_multiply_fusion.5), kind=kOutput, calls=%fused_computation.647 | convolution fusion | flops 9671540736 | bytes 28334080 | tf_op jit(solution)/shard_map/dot_general | solution.py:106
  537.8 20.9 %multiply_reduce_fusion = (f32[768]{0:T(1024)}, f32[2048]{0:T(1024)S(1)}, f32[2048]{0:T(1024)S(1)}, f32[768]{0:T(1024)}, f32[2048,768]{1,0:T(8,128)}) fusion(f32[2048,768]{1,0:T(8,128)} %copy-done.18, f32[2048]{0:T(1024)S(1)} %add_rsqrt_fusion.1, f32[2048]{0:T(1024)S(1)} %broadcast_multiply_fusion.5, f32[768]{0:T(1024)S(1)} %copy-done.300, ...), kind=kOutput, calls=%fused_computation.46 | convolution fusion | flops 9679398912 | bytes 36217856 | tf_op jit(solution)/shard_map/dot_general | solution.py:102
  567.3 15.9 %multiply_reduce_fusion.13 = (f32[768]{0:T(1024)}, f32[768]{0:T(1024)}, f32[768]{0:T(1024)}, f32[768]{0:T(1024)}, f32[768]{0:T(1024)}, /*index=5*/f32[768]{0:T(1...) fusion(pred[2,1024]{1,0:T(4,128)(4,1)S(1)} %copy-done.185, f32[2,1024,768]{2,1,0:T(8,128)S(1)} %bitcast.434, ...), kind=kOutput, calls=%fused_computation.62 | convolution fusion | flops 2459952384 | bytes 20100096 | tf_op jit(solution)/shard_map/dot_general | solution.py:102
  583.4 25.3 %multiply_reduce_fusion.32 = (f32[768]{0:T(1024)}, f32[768]{0:T(1024)}, f32[768]{0:T(1024)}, f32[768]{0:T(1024)}, f32[768]{0:T(1024)}, /*index=5*/f32[768]{0:T(1024)}, f32[768]{0:T(1024)}, f32[768]{0:T(1024)}, f32[768]{0:T(1024)}) fusion(f32[2048,768]{1,0:T(8,128)} %get-tuple-element.283, pred[2,1024]{1,0:T(4,128)(4,1)S(1)} %copy-done.197, ...), kind=kLoop, calls=%fused_computation.81 | loop fusion | flops 42460416 | bytes 12628992 | tf_op jit(solution)/shard_map/transpose(jvp(vmap()))/reduce_sum | solution.py:78
  608.7 24.9 %multiply_reduce_fusion.23 = (f32[768]{0:T(1024)}, f32[768]{0:T(1024)}, f32[768]{0:T(1024)}, f32[768]{0:T(1024)}, f32[768]{0:T(1024)}, /*index=5*/f32[768]{0:T(1024)}, f32[768]{0:T(1024)}, f32[768]{0:T(1024)}, f32[768]{0:T(1024)}) fusion(f32[2048,768]{1,0:T(8,128)} %get-tuple-element.283, pred[2,1024]{1,0:T(4,128)(4,1)S(1)} %copy-done.201, ...), kind=kLoop, calls=%fused_computation.72 | loop fusion | flops 42460416 | bytes 12628992 | tf_op jit(solution)/shard_map/transpose(jvp(vmap()))/reduce_sum | solution.py:78
  646.1 9.2 reshape.757
  655.3 12.2 fusion.19
  731.5 10.3 multiply_reduce_fusion.35
  774.5 10.1 multiply_reduce_fusion.34
  790.5 13.6 %fusion.30 = f32[2,12,64,64]{3,2,1,0:T(8,128)} fusion(f32[2,1024,12,64]{1,0,3,2:T(2,128)} %mul.1011, f32[2,12,64,1024]{3,2,1,0:T(8,128)} %get-tuple-element.129, pred[2,12,64,1024]{3,2,1,0:T(32,128)(4,1)S(1)} %get-tuple-element.114, f32[2,12,64]{2,1,0:T(8,128)S(1)} %negate_divide_fusion.2, pred[2,64,1024]{2,1,0:T(8,128)(4,1)S(1)} %copy-done.72), kind=kOutput, calls=%fused_computation.151 | convolution fusion | flops 1212678144 | bytes 14686208 | tf_op jit(solution)/shard_map/transpose(jvp(vmap(ryx,srx->rys)))/dot_general | solution.py:17
  804.2 11.1 fusion.43
  815.6 14.6 %multiply_reduce_fusion.4 = (f32[768]{0:T(1024)}, f32[768]{0:T(1024)}, f32[768]{0:T(1024)}, f32[768]{0:T(1024)}, f32[768]{0:T(1024)}, /*index=5*/f32[2,1024,768]...) fusion(f32[2048,768]{1,0:T(8,128)S(1)} %bitcast.428, ...), kind=kLoop, calls=%fused_computation.53 | loop fusion | flops 34599168 | bytes 50377728 | tf_op jit(solution)/shard_map/transpose(jvp(vmap()))/reduce_sum | solution.py:78
  830.2 18.5 %select_multiply_fusion.30 = (f32[2,1024,768]{2,1,0:T(8,128)}, f32[2,1024,768]{2,1,0:T(8,128)}, f32[2,1024,768]{2,1,0:T(8,128)}, f32[2,1024,768]{2,1,0:T(8,128)}...) fusion(f32[768]{0:T(1024)S(1)} %copy-done.244, ...), kind=kLoop, calls=%fused_computation.142 | loop fusion | flops 28311552 | bytes 62960640 | tf_op jit(solution)/shard_map/transpose(jvp(vmap()))/mul | solution.py:78
  848.9 19.2 %select_multiply_fusion.32 = (f32[2,1024,768]{2,1,0:T(8,128)}, f32[2,1024,768]{2,1,0:T(8,128)}, f32[2,1024,768]{2,1,0:T(8,128)}, f32[2,1024,768]{2,1,0:T(8,128)}...) fusion(f32[768]{0:T(1024)S(1)} %copy-done.242, ...), kind=kLoop, calls=%fused_computation.144 | loop fusion | flops 28311552 | bytes 62960640 | tf_op jit(solution)/shard_map/transpose(jvp(vmap()))/mul | solution.py:78
  868.3 18.8 %select_multiply_fusion.31 = (f32[2,1024,768]{2,1,0:T(8,128)}, f32[2,1024,768]{2,1,0:T(8,128)}, f32[2,1024,768]{2,1,0:T(8,128)}, f32[2,1024,768]{2,1,0:T(8,128)}...) fusion(f32[768]{0:T(1024)S(1)} %copy-done.228, ...), kind=kLoop, calls=%fused_computation.143 | loop fusion | flops 26738688 | bytes 62958592 | tf_op jit(solution)/shard_map/transpose(jvp(vmap()))/mul | solution.py:78
  997.4 56.6 %pad_add_fusion = f32[2,1056,768]{2,1,0:T(8,128)} fusion(f32[2,1024,768]{2,1,0:T(8,128)} %get-tuple-element.139, f32[2,1024,768]{2,1,0:T(8,128)} %get-tuple-element.140, f32[2,1024,768]{2,1,0:T(8,128)} %get-tuple-element.141, f32[2,1024,768]{2,1,0:T(8,128)} %get-tuple-element.142, f32[2,1024,768]{2,1,0:T(8,128)} %get-tuple-element.143, ...), kind=kLoop, calls=%fused_computation.19 | loop fusion | flops 42172416 | bytes 176357376 | tf_op jit(solution)/shard_map/transpose(jvp(vmap()))/add_any | solution.py:78
  1054.0 17.5 %convert_reduce_fusion.4 = (f32[768]{0:T(1024)S(1)}, bf16[2,1024,768]{2,1,0:T(8,128)(2,1)S(1)}) fusion(f32[2,1024,768]{2,1,0:T(8,128)} %copy.808, f32[2,1024,768]{2,1,0:T(8,128)} %get-tuple-element.132, f32[2,1024,768]{2,1,0:T(8,128)} %get-tuple-element.134, f32[2,1024,768]{2,1,0:T(8,128)} %get-tuple-element.133, f32[2,1024,768]{2,1,0:T(8,128)} %get-tuple-element.135, ...), kind=kLoop, calls=%fused_computation.48 | loop fusion | flops 15727872 | bytes 53480448 | tf_op jit(solution)/shard_map/reduce_sum | solution.py:118
  (1362 shorter events, 650.9 us)
Async XLA Ops:
  7.2 357.6 %all-gather.4.cloned.1.call-start = ((), (), s32[]{:S(2)}) async-start(), calls=%async_computation | async-start | bytes 1216512 | tf_op jit(solution)/shard_map/all_gather | solution.py:234
  15.0 15.9 %collective-permute-start.10 = (bf16[1,1,1,1,1,74,256]{6,5,4,3,2,1,0:T(8,128)(2,1)S(1)}, bf16[1,1,1,1,1,74,256]{6,5,4,3,2,1,0:T(8,128)(2,1)S(1)}, u32[]{:S(2)}, u32[]{:S(2)}) collective-permute-start(bf16[1,1,1,1,1,74,256]{6,5,4,3,2,1,0:T(8,128)(2,1)S(1)} %get-tuple-element.208), channel_id=1, source_target_pairs={{0,16},{4,20},{8,24},{12,28},{16,0},{20,4},{24,8},{28,12},{1,17},{... | collective-permute-start | bytes 113672 | tf_op jit(solution)/shard_map/ppermute | solution.py:143
  19.1 11.8 collective-permute-start.5
  19.2 11.8 collective-permute-start
  42.7 11.7 collective-permute-start.8
  62.1 312.8 %all-gather.6.cloned.1.call-start = ((), (), s32[]{:S(2)}) async-start(), calls=%async_computation.1 | async-start | bytes 4866048 | tf_op jit(solution)/shard_map/all_gather | solution.py:234
  161.6 281.2 %all-gather.8.cloned.1.call-start = ((), (), s32[]{:S(2)}) async-start(), calls=%async_computation.2 | async-start | bytes 4866048 | tf_op jit(solution)/shard_map/all_gather | solution.py:234
  902.7 252.7 %collective-permute-start.65 = (bf16[2,2,2,2,1,24,1024]{6,5,4,3,2,1,0:T(8,128)(2,1)}, bf16[2,2,2,2,1,24,1024]{6,5,4,3,2,1,0:T(8,128)(2,1)}, u32[]{:S(2)}, u32[]{:S(2)}) collective-permute-start(bf16[2,2,2,2,1,24,1024]{6,5,4,3,2,1,0:T(8,128)(2,1)} %dynamic-slice_convert_fusion.1), channel_id=1, source_target_pairs={{0,1},{1,0},{2,3},{3,2},{4,5},{5,4},{6,7},{7,6},{8,9},{9,8},{10,11... | collective-permute-start | bytes 2359304 | tf_op jit(solution)/shard_map/ppermute | solution.py:143
  903.0 256.5 %collective-permute-start.60 = (bf16[2,2,2,2,1,24,1024]{6,5,4,3,2,1,0:T(8,128)(2,1)}, bf16[2,2,2,2,1,24,1024]{6,5,4,3,2,1,0:T(8,128)(2,1)}, u32[]{:S(2)}, u32[]{:S(2)}) collective-permute-start(bf16[2,2,2,2,1,24,1024]{6,5,4,3,2,1,0:T(8,128)(2,1)} %dynamic-slice_convert_fusion.2), channel_id=1, source_target_pairs={{0,1},{1,0},{2,3},{3,2},{4,5},{5,4},{6,7},{7,6},{8,9},{9,8},{10,11... | collective-permute-start | bytes 2359304 | tf_op jit(solution)/shard_map/ppermute | solution.py:143
  903.2 258.7 %collective-permute-start.70 = (bf16[2,2,2,2,1,24,1024]{6,5,4,3,2,1,0:T(8,128)(2,1)}, bf16[2,2,2,2,1,24,1024]{6,5,4,3,2,1,0:T(8,128)(2,1)}, u32[]{:S(2)}, u32[]{:S(2)}) collective-permute-start(bf16[2,2,2,2,1,24,1024]{6,5,4,3,2,1,0:T(8,128)(2,1)} %dynamic-slice_convert_fusion), channel_id=1, source_target_pairs={{0,1},{1,0},{2,3},{3,2},{4,5},{5,4},{6,7},{7,6},{8,9},{9,8},{10,11... | collective-permute-start | bytes 2359304 | tf_op jit(solution)/shard_map/ppermute | solution.py:143
  924.9 168.3 %collective-permute-start.35 = (bf16[2,2,2,2,1,25,256]{6,5,4,3,2,1,0:T(8,128)(2,1)}, bf16[2,2,2,2,1,25,256]{6,5,4,3,2,1,0:T(8,128)(2,1)}, u32[]{:S(2)}, u32[]{:S(2)}) collective-permute-start(bf16[2,2,2,2,1,25,256]{6,5,4,3,2,1,0:T(8,128)(2,1)} %dynamic-slice_convert_fusion.17), channel_id=1, source_target_pairs={{0,1},{1,0},{2,3},{3,2},{4,5},{5,4},{6,7},{7,6},{8,9},{9,8},{10,11... | collective-permute-start | bytes 614408 | tf_op jit(solution)/shard_map/ppermute | solution.py:143
  925.1 169.3 %collective-permute-start.30 = (bf16[2,2,2,2,1,25,256]{6,5,4,3,2,1,0:T(8,128)(2,1)}, bf16[2,2,2,2,1,25,256]{6,5,4,3,2,1,0:T(8,128)(2,1)}, u32[]{:S(2)}, u32[]{:S(2)}) collective-permute-start(bf16[2,2,2,2,1,25,256]{6,5,4,3,2,1,0:T(8,128)(2,1)} %dynamic-slice_convert_fusion.18), channel_id=1, source_target_pairs={{0,1},{1,0},{2,3},{3,2},{4,5},{5,4},{6,7},{7,6},{8,9},{9,8},{10,11... | collective-permute-start | bytes 614408 | tf_op jit(solution)/shard_map/ppermute | solution.py:143
  1094.5 56.6 %collective-permute-start.20 = (bf16[2,2,2,2,1,74,256]{6,3,5,4,2,1,0:T(2,128)(2,1)}, bf16[2,2,2,2,1,74,256]{6,3,5,4,2,1,0:T(2,128)(2,1)S(1)}, u32[]{:S(2)}, u32[]{:S(2)}) collective-permute-start(bf16[2,2,2,2,1,74,256]{6,3,5,4,2,1,0:T(2,128)(2,1)} %copy.1053), channel_id=1, source_target_pairs={{0,1},{1,0},{2,3},{3,2},{4,5},{5,4},{6,7},{7,6},{8,9},{9,8},{10,11... | collective-permute-start | bytes 1818632 | tf_op jit(solution)/shard_map/ppermute | solution.py:143
  1154.3 12.2 collective-permute-start.50
  1154.6 13.2 %collective-permute-start.45 = (bf16[2,2,2,2,1,96,256]{6,5,4,3,2,1,0:T(8,128)(2,1)S(1)}, bf16[2,2,2,2,1,96,256]{6,5,4,3,2,1,0:T(8,128)(2,1)S(1)}, u32[]{:S(2)}, u32[]{:S(2)}) collective-permute-start(bf16[2,2,2,2,1,96,256]{6,5,4,3,2,1,0:T(8,128)(2,1)S(1)} %copy-done.133), channel_id=1, source_target_pairs={{0,1},{1,0},{2,3},{3,2},{4,5},{5,4},{6,7},{7,6},{8,9},{9,8},{10,11... | collective-permute-start | bytes 2359304 | tf_op jit(solution)/shard_map/ppermute | solution.py:143
  1155.4 13.6 %collective-permute-start.55 = (bf16[2,2,2,2,1,96,256]{6,5,4,3,2,1,0:T(8,128)(2,1)S(1)}, bf16[2,2,2,2,1,96,256]{6,5,4,3,2,1,0:T(8,128)(2,1)S(1)}, u32[]{:S(2)}, u32[]{:S(2)}) collective-permute-start(bf16[2,2,2,2,1,96,256]{6,5,4,3,2,1,0:T(8,128)(2,1)S(1)} %copy-done.132), channel_id=1, source_target_pairs={{0,1},{1,0},{2,3},{3,2},{4,5},{5,4},{6,7},{7,6},{8,9},{9,8},{10,11... | collective-permute-start | bytes 2359304 | tf_op jit(solution)/shard_map/ppermute | solution.py:143
  1159.5 12.9 %collective-permute-start.26 = (bf16[2,1,2,2,1,74,256]{6,5,4,3,2,1,0:T(8,128)(2,1)S(1)}, bf16[2,1,2,2,1,74,256]{6,5,4,3,2,1,0:T(8,128)(2,1)S(1)}, u32[]{:S(2)}, u32[]{:S(2)}) collective-permute-start(bf16[2,1,2,2,1,74,256]{6,5,4,3,2,1,0:T(8,128)(2,1)S(1)} %dynamic-slice_convert_fusion.13), channel_id=1, source_target_pairs={{0,8},{4,12},{8,0},{12,4},{16,24},{20,28},{24,16},{28,20},{1,9},{5... | collective-permute-start | bytes 909320 | tf_op jit(solution)/shard_map/ppermute | solution.py:143
  1161.9 12.1 collective-permute-start.16
  1167.9 63.7 %collective-permute-start.66 = (bf16[2,2,2,1,1,24,1024]{6,5,4,3,2,1,0:T(8,128)(2,1)}, bf16[2,2,2,1,1,24,1024]{6,5,4,3,2,1,0:T(8,128)(2,1)}, u32[]{:S(2)}, u32[]{:S(2)}) collective-permute-start(bf16[2,2,2,1,1,24,1024]{6,5,4,3,2,1,0:T(8,128)(2,1)} %dynamic-slice_convert_fusion.8), channel_id=1, source_target_pairs={{0,2},{1,3},{2,0},{3,1},{4,6},{5,7},{6,4},{7,5},{8,10},{9,11},{10,... | collective-permute-start | bytes 1179656 | tf_op jit(solution)/shard_map/ppermute | solution.py:143
  1169.0 64.4 %collective-permute-start.61 = (bf16[2,2,1,2,1,24,1024]{6,5,4,3,2,1,0:T(8,128)(2,1)}, bf16[2,2,1,2,1,24,1024]{6,5,4,3,2,1,0:T(8,128)(2,1)}, u32[]{:S(2)}, u32[]{:S(2)}) collective-permute-start(bf16[2,2,1,2,1,24,1024]{6,5,4,3,2,1,0:T(8,128)(2,1)} %dynamic-slice_convert_fusion.9), channel_id=1, source_target_pairs={{0,4},{4,0},{8,12},{12,8},{16,20},{20,16},{24,28},{28,24},{1,5},{5... | collective-permute-start | bytes 1179656 | tf_op jit(solution)/shard_map/ppermute | solution.py:143
  1172.4 64.0 %collective-permute-start.71 = (bf16[2,1,2,2,1,24,1024]{6,5,4,3,2,1,0:T(8,128)(2,1)}, bf16[2,1,2,2,1,24,1024]{6,5,4,3,2,1,0:T(8,128)(2,1)}, u32[]{:S(2)}, u32[]{:S(2)}) collective-permute-start(bf16[2,1,2,2,1,24,1024]{6,5,4,3,2,1,0:T(8,128)(2,1)} %dynamic-slice_convert_fusion.7), channel_id=1, source_target_pairs={{0,8},{4,12},{8,0},{12,4},{16,24},{20,28},{24,16},{28,20},{1,9},{5... | collective-permute-start | bytes 1179656 | tf_op jit(solution)/shard_map/ppermute | solution.py:143
  1174.0 65.6 %collective-permute-start.51 = (bf16[2,2,2,1,1,96,256]{6,5,4,3,2,1,0:T(8,128)(2,1)}, bf16[2,2,2,1,1,96,256]{6,5,4,3,2,1,0:T(8,128)(2,1)}, u32[]{:S(2)}, u32[]{:S(2)}) collective-permute-start(bf16[2,2,2,1,1,96,256]{6,5,4,3,2,1,0:T(8,128)(2,1)} %dynamic-slice_convert_fusion.11), channel_id=1, source_target_pairs={{0,2},{1,3},{2,0},{3,1},{4,6},{5,7},{6,4},{7,5},{8,10},{9,11},{10,... | collective-permute-start | bytes 1179656 | tf_op jit(solution)/shard_map/ppermute | solution.py:143
  1227.8 13.9 %collective-permute-start.46 = (bf16[2,2,1,2,1,96,256]{6,5,4,3,2,1,0:T(8,128)(2,1)}, bf16[2,2,1,2,1,96,256]{6,5,4,3,2,1,0:T(8,128)(2,1)}, u32[]{:S(2)}, u32[]{:S(2)}) collective-permute-start(bf16[2,2,1,2,1,96,256]{6,5,4,3,2,1,0:T(8,128)(2,1)} %dynamic-slice_convert_fusion.12), channel_id=1, source_target_pairs={{0,4},{4,0},{8,12},{12,8},{16,20},{20,16},{24,28},{28,24},{1,5},{5... | collective-permute-start | bytes 1179656 | tf_op jit(solution)/shard_map/ppermute | solution.py:143
  1231.5 11.8 collective-permute-start.56
  (442 other events, 9331.6 us)
Sparse Core Ops, SparseCore 0:
  62.2 51.6 all-gather.3
  161.7 61.3 all-gather.5
  233.2 61.2 all-gather.7

commit v2 on v1

v2 whole, which is shorter than its diff:
```python
import functools

import jax
import jax.numpy as jnp
from jax import lax
from jax.experimental import pallas as pl
from jax.experimental.pallas import tpu as pltpu
from jax.sharding import PartitionSpec as P

BF = jnp.bfloat16
F32 = jnp.float32
KW=33; HALF=16; DOCS=4; GAP=16
def spread(dst, get, bounds, length, step):
    total=length+GAP*(DOCS+1)
    ids=lax.broadcasted_iota(jnp.int32,(step,128),0)
    for p0 in range(0,total,step):
        size=min(step,total-p0)
        acc=None
        for d in range(DOCS):
            s0=p0-GAP*(d+1)
            lo=max(s0,0); hi=min(s0+size,length)
            if hi<=lo: continue
            row=ids[:hi-lo]+lo
            inside=(row>=bounds[d])&(row<bounds[d+1])
            part=jnp.where(inside,get(lo,hi-lo),0.0)
            pads=[]
            if lo>s0: pads.append(jnp.zeros((lo-s0,128),F32))
            pads.append(part)
            if s0+size>hi: pads.append(jnp.zeros((s0+size-hi,128),F32))
            part=jnp.concatenate(pads,0) if len(pads)>1 else part
            acc=part if acc is None else acc+part
        if acc is None: acc=jnp.zeros((size,128),F32)
        dst[HALF+p0:HALF+p0+size,:]=acc
def collect(src, bounds, lo, size):
    row=lax.broadcasted_iota(jnp.int32,(size,128),0)+lo
    acc=None
    for d in range(DOCS):
        part=src[lo+GAP*(d+1):lo+GAP*(d+1)+size,:]
        acc=part if acc is None else jnp.where(row>=bounds[d],part,acc)
    return acc
BLOCK=64
def taps(ref, base, weight, sign):
    acc=None
    for r in range(8):
        win=ref[pl.ds(base+r,BLOCK+32),:] if r==0 else ref[pl.ds(base+r,BLOCK+24),:]
        for a in range(5 if r==0 else 4):
            o=8*a+r
            t=weight(o if sign>0 else 2*HALF-o)*win[8*a:8*a+BLOCK]
            acc=t if acc is None else acc+t
    return acc
def conv_fwd_kernel(bounds_ref, v_ref, w_ref, out_ref, pad_ref, res_ref):
    b=pl.program_id(0)
    bounds=[bounds_ref[b,d] for d in range(DOCS+1)]
    length=v_ref.shape[1]; total=length+GAP*(DOCS+1)
    zeros=jnp.zeros((HALF,128),F32)
    pad_ref[0:HALF,:]=zeros; pad_ref[HALF+total:,:]=jnp.zeros((pad_ref.shape[0]-HALF-total,128),F32)
    spread(pad_ref, lambda lo,n: v_ref[0,lo:lo+n,:], bounds, length, BLOCK)
    def block(i,c):
        base=pl.multiple_of(i*BLOCK,BLOCK)
        res_ref[pl.ds(base,BLOCK),:]=taps(pad_ref, base, lambda s: w_ref[s:s+1,:], 1)
        return c
    lax.fori_loop(0,-(-total//BLOCK),block,0)
    for lo in range(0,length,BLOCK):
        out_ref[0,lo:lo+BLOCK,:]=collect(res_ref,bounds,lo,BLOCK)
def padded_rows(length):
    total=length+GAP*(DOCS+1)
    return -(-total//BLOCK)*BLOCK
def conv_fwd(bounds, v, w):
    B,L,D=v.shape
    rows=padded_rows(L)
    return pl.pallas_call(conv_fwd_kernel,grid_spec=pltpu.PrefetchScalarGridSpec(num_scalar_prefetch=1,grid=(B,D//128),
        in_specs=[pl.BlockSpec((1,L,128),lambda b,c,_:(b,0,c)),pl.BlockSpec((KW,128),lambda b,c,_:(0,c))],
        out_specs=pl.BlockSpec((1,L,128),lambda b,c,_:(b,0,c)),
        scratch_shapes=[pltpu.VMEM((rows+2*HALF+8,128),F32),pltpu.VMEM((rows,128),F32)]),
        out_shape=jax.ShapeDtypeStruct((B,L,D),F32),
        compiler_params=pltpu.CompilerParams(vmem_limit_bytes=32*2**20))(bounds,v,w)
def conv_bwd_kernel(bounds_ref, v_ref, g_ref, w_ref, dv_ref, dw_ref, vpad_ref, gpad_ref, res_ref, acc_ref):
    b=pl.program_id(1)
    bounds=[bounds_ref[b,d] for d in range(DOCS+1)]
    length=v_ref.shape[1]; total=length+GAP*(DOCS+1)
    for ref in (vpad_ref,gpad_ref):
        ref[0:HALF,:]=jnp.zeros((HALF,128),F32)
        ref[HALF+total:,:]=jnp.zeros((ref.shape[0]-HALF-total,128),F32)
    spread(vpad_ref, lambda lo,n: v_ref[0,lo:lo+n,:], bounds, length, BLOCK)
    spread(gpad_ref, lambda lo,n: g_ref[0,lo:lo+n,:], bounds, length, BLOCK)
    @pl.when(b==0)
    def _(): acc_ref[...]=jnp.zeros_like(acc_ref)
    def block(i,c):
        base=pl.multiple_of(i*BLOCK,BLOCK)
        here=vpad_ref[pl.ds(base+HALF,BLOCK),:]
        acc=None
        for r in range(8):
            n=5 if r==0 else 4
            win=gpad_ref[pl.ds(base+r,BLOCK+8*(n-1)),:]
            for a in range(n):
                s=2*HALF-(8*a+r)
                x=win[8*a:8*a+BLOCK]
                t=w_ref[s:s+1,:]*x
                acc=t if acc is None else acc+t
                p=(here*x).reshape(BLOCK//8,8,128)
                acc_ref[s]+=jnp.sum(p,axis=0)
        res_ref[pl.ds(base,BLOCK),:]=acc
        return c
    lax.fori_loop(0,-(-total//BLOCK),block,0)
    for lo in range(0,length,BLOCK):
        dv_ref[0,lo:lo+BLOCK,:]=collect(res_ref,bounds,lo,BLOCK)
    @pl.when(b==pl.num_programs(1)-1)
    def _():
        for s in range(KW):
            dw_ref[s:s+1,:]=jnp.sum(acc_ref[s],axis=0,keepdims=True)
def conv_bwd(bounds, v, g, w):
    B,L,D=v.shape
    rows=padded_rows(L)
    slab=pl.BlockSpec((1,L,128),lambda c,b,_:(b,0,c)); tapsp=pl.BlockSpec((KW,128),lambda c,b,_:(0,c))
    return pl.pallas_call(conv_bwd_kernel,grid_spec=pltpu.PrefetchScalarGridSpec(num_scalar_prefetch=1,grid=(D//128,B),
        in_specs=[slab,slab,tapsp],out_specs=[slab,tapsp],
        scratch_shapes=[pltpu.VMEM((rows+2*HALF+8,128),F32)]*2+[pltpu.VMEM((rows,128),F32),pltpu.VMEM((KW,8,128),F32)]),
        out_shape=[jax.ShapeDtypeStruct((B,L,D),F32),jax.ShapeDtypeStruct((KW,D),F32)],
        compiler_params=pltpu.CompilerParams(vmem_limit_bytes=32*2**20))(bounds,v,g,w)

HW=64; LM=64; NEWTON=6; GH=4; GW=GH*HW
STASH=4*NEWTON
def nt(a,b): return lax.dot_general(a,b,(((1,),(1,)),((),())),preferred_element_type=F32)
def nn(a,b): return lax.dot_general(a,b,(((1,),(0,)),((),())),preferred_element_type=F32)
def split(a):
    hi=a.astype(BF); return hi,(a-hi.astype(F32)).astype(BF)
def wide(a):
    hi,lo=split(a); return jnp.concatenate([hi,hi,lo],axis=1)
def tall(b):
    hi,lo=split(b); return jnp.concatenate([hi,lo,hi],axis=0)
def mm3(a,b): return nn(wide(a),tall(b))
def mm1(a,b): return nn(a.astype(BF),b.astype(BF))
def pair(a):
    hi,lo=split(a); return jnp.concatenate([hi,lo],axis=0)
def long3(a,b):
    full=nt(a,b); n=full.shape[0]//2
    return full[:n,:n]+(full[:n,n:]+full[n:,:n])
def eye(c):
    return jnp.where(lax.broadcasted_iota(jnp.int32,(LM,LM),0)==lax.broadcasted_iota(jnp.int32,(LM,LM),1),c,0.0)
def masks(tok_ref,ldc_ref,ldr_ref):
    tok=tok_ref[0]; ldc=ldc_ref[0]; ldr=ldr_ref[0]
    member=lax.broadcasted_iota(jnp.int32,(LM,tok.shape[1]),0)==tok
    doc=jnp.sum(jnp.where(member,ldc,0),axis=0,keepdims=True)
    return member, doc==ldc, ldc==ldr
def softmax(s,allowed,axis):
    held=jnp.where(allowed,s,-1e30)
    raised=jnp.exp(held-jnp.max(held,axis=axis,keepdims=True))
    raised=jnp.where(allowed,raised,0.0)
    return raised/jnp.sum(raised,axis=axis,keepdims=True)
def att_fwd_kernel(x_ref,wq_ref,wk_ref,wv_ref,bq_ref,bv_ref,tok_ref,ldc_ref,ldr_ref,conv_ref,
               q_ref,k_ref,v_ref,k1_ref,k3_ref,stash_ref,small_ref,ctx_ref):
    x=x_ref[0]
    member,allow1,allow2=masks(tok_ref,ldc_ref,ldr_ref)
    one_hot=jnp.where(member,1.0,0.0).astype(BF)
    count=nt(jnp.ones((8,x.shape[0]),BF),one_hot)[0:1]
    scale=HW**-0.25
    q=(nt(wq_ref[...],x)+bq_ref[...])*scale; q_ref[0]=q
    k=nt(wk_ref[...],x)*scale; k_ref[0]=k
    v=nt(wv_ref[...],x)+bv_ref[...]; v_ref[0]=v
    def land(a):
        hi,lo=split(a); return (nt(hi,one_hot)+nt(lo,one_hot))/count
    lqt,lkt=land(q),land(k)
    heads=range(GH)
    cut=lambda a,h: a[h*HW:(h+1)*HW]
    lq=[cut(lqt,h).T for h in heads]; lk=[cut(lkt,h).T for h in heads]
    k2=[softmax(mm3(lq[h],cut(lkt,h)),allow2,1) for h in heads]
    z=[k2[h].T*(1.0/jnp.sum(k2[h]*k2[h])) for h in heads]
    k2w=[wide(a) for a in k2]
    for n in range(NEWTON):
        p=[nn(k2w[h],tall(z[h])) for h in heads]
        pw=[wide(a) for a in p]
        b=[eye(15.0)-nn(pw[h],tall(eye(7.0)-p[h])) for h in heads]
        c=[eye(13.0)-nn(pw[h],tall(b[h])) for h in heads]
        for h in heads:
            stash_ref[0,h,4*n]=p[h].astype(BF); stash_ref[0,h,4*n+1]=b[h].astype(BF)
            stash_ref[0,h,4*n+2]=c[h].astype(BF); stash_ref[0,h,4*n+3]=z[h].T.astype(BF)
        z=[0.25*mm3(z[h],c[h]) for h in heads]
    outs=[]
    for h in heads:
        k1=softmax(mm3(lk[h],cut(q,h)),allow1,0); k1_ref[0,h*LM:(h+1)*LM]=k1
        k3=softmax(mm3(lq[h],cut(k,h)),allow1,1); k3_ref[0,h*LM:(h+1)*LM]=k3
        r=long3(pair(k3),pair(cut(v,h)))
        u=mm3(z[h],r)
        small_ref[0,h,0]=lq[h]; small_ref[0,h,1]=lk[h]; small_ref[0,h,2]=k2[h]; small_ref[0,h,3]=z[h]
        small_ref[0,h,4]=r; small_ref[0,h,5]=u
        outs.append(mm3(u.T,k1))
    ctx_ref[0]=(jnp.concatenate(outs,axis=0).T+conv_ref[0]).astype(BF)
def att_fwd(x,wq,wk,wv,bq,bv,tok,ld,conv):
    B,T,D=x.shape; G=D//GW; H=D//HW
    seq=lambda s: pl.BlockSpec((1,)+s,lambda g,b:(b,)+(0,)*len(s))
    wsp=pl.BlockSpec((GW,D),lambda g,b:(g,0)); bsp=pl.BlockSpec((GW,1),lambda g,b:(g,0))
    rows=pl.BlockSpec((1,GW,T),lambda g,b:(b,g,0)); cols=pl.BlockSpec((1,T,GW),lambda g,b:(b,0,g))
    sq=lambda n: pl.BlockSpec((1,GH,n,LM,LM),lambda g,b:(b,g,0,0,0))
    sd=jax.ShapeDtypeStruct; big=sd((B,D,T),F32)
    return pl.pallas_call(att_fwd_kernel,grid=(G,B),
        in_specs=[seq((T,D)),wsp,wsp,wsp,bsp,bsp,seq((1,T)),seq((LM,1)),seq((1,LM)),cols],
        out_specs=[rows]*5+[sq(STASH),sq(6),cols],
        out_shape=[big]*5+[sd((B,H,STASH,LM,LM),BF),sd((B,H,6,LM,LM),F32),sd((B,T,D),BF)],
        compiler_params=pltpu.CompilerParams(vmem_limit_bytes=60*2**20))(
            x,wq,wk,wv,bq,bv,tok[:,None,:],ld[:,:,None],ld[:,None,:],conv)
def att_bwd_kernel(x_ref,al_ref,wo_ref,q_ref,k_ref,v_ref,k1_ref,k3_ref,stash_ref,small_ref,tok_ref,ldc_ref,ldr_ref,conv_ref,
               dq_ref,dk_ref,dv_ref,gq_ref,gk_ref,gv_ref,sq_ref,sv_ref):
    x=x_ref[0]
    member,_,_=masks(tok_ref,ldc_ref,ldr_ref)
    one_hot=jnp.where(member,1.0,0.0).astype(BF)
    count=nt(jnp.ones((8,x.shape[0]),BF),one_hot)[0:1]
    per=1.0/count
    scale=HW**-0.25
    g=nt(wo_ref[...],al_ref[0])
    heads=range(GH)
    rows=lambda ref,h: ref[0,h*HW:(h+1)*HW]
    lq,lk,k2,z,r,u=[[small_ref[0,h,i] for h in heads] for i in range(6)]
    du=[];ds1=[];dlk=[]
    for h in heads:
        gh=g[h*HW:(h+1)*HW]; k1=rows(k1_ref,h)
        gp=pair(gh)
        dk1=nn(wide(u[h]),jnp.concatenate([gp,gp[:HW]],axis=0))
        du.append(long3(pair(k1),gp))
        d=k1*(dk1-jnp.sum(k1*dk1,axis=0,keepdims=True)); ds1.append(d)
        dlk.append(long3(pair(d),pair(rows(q_ref,h))))
    dr=[mm3(z[h].T,du[h]) for h in heads]
    dz=[mm3(du[h],r[h].T) for h in heads]
    dlq=[];ds3=[];dvs=[]
    for h in heads:
        k3=rows(k3_ref,h)
        dk3=mm3(dr[h],rows(v_ref,h))
        dvs.append(mm3(dr[h].T,k3))
        d=k3*(dk3-jnp.sum(k3*dk3,axis=1,keepdims=True)); ds3.append(d)
        dlq.append(long3(pair(d),pair(rows(k_ref,h))))
    dk2=[None]*GH
    k2t=[a.T for a in k2]; k2tb=[a.astype(BF) for a in k2t]
    for n in reversed(range(NEWTON)):
        P,Bm,C,ZT=[[stash_ref[0,h,4*n+i] for h in heads] for i in range(4)]
        A=[(eye(7.0)-P[h].astype(F32)).astype(BF) for h in heads]
        gz=[(0.25*dz[h]).astype(BF) for h in heads]
        dc=[nn(ZT[h],gz[h]).astype(BF) for h in heads]
        db=[nn(P[h],dc[h]).astype(BF) for h in heads]
        da=[nn(P[h],db[h]) for h in heads]
        dp=[(nn(db[h],A[h])-nn(dc[h],Bm[h])-da[h]).astype(BF) for h in heads]
        for h in heads:
            t=nn(dp[h],ZT[h]); dk2[h]=t if dk2[h] is None else dk2[h]+t
        dz=[nn(gz[h],C[h])+nn(k2tb[h],dp[h]) for h in heads]
    dqs=[];dks=[]
    for h in heads:
        inv=1.0/jnp.sum(k2[h]*k2[h])
        d=dk2[h]+inv*dz[h].T-k2[h]*(2.0*inv*inv*jnp.sum(dz[h]*k2t[h]))
        d=k2[h]*(d-jnp.sum(k2[h]*d,axis=1,keepdims=True))
        dlqh=dlq[h]+mm3(d,lk[h]); dlkh=dlk[h]+mm3(d.T,lq[h])
        def back(land,dscore,dland):
            ah,al=split(land.T); dh,dl=split(dscore); mh,ml=split(dland.T*per)
            return nn(jnp.concatenate([ah,ah,al,mh,ml],axis=1),jnp.concatenate([dh,dl,dh,one_hot,one_hot],axis=0))
        dqs.append(back(lk[h],ds1[h],dlqh)); dks.append(back(lq[h],ds3[h],dlkh))
    cat=lambda a: jnp.concatenate(a,axis=0)
    dq=(cat(dqs)*scale).astype(BF); dk=(cat(dks)*scale).astype(BF)
    dv=(cat(dvs)+conv_ref[0].T).astype(BF)
    dq_ref[0]=dq; dk_ref[0]=dk; dv_ref[0]=dv
    @pl.when(pl.program_id(1)==0)
    def _():
        for ref in (gq_ref,gk_ref,gv_ref,sq_ref,sv_ref): ref[...]=jnp.zeros_like(ref)
    gq_ref[...]+=nn(dq,x); gk_ref[...]+=nn(dk,x); gv_ref[...]+=nn(dv,x)
    sq_ref[...]+=jnp.sum(dq.astype(F32),axis=1,keepdims=True)
    sv_ref[...]+=jnp.sum(dv.astype(F32),axis=1,keepdims=True)
def att_bwd(x,al,wo,q,k,v,k1,k3,stash,small,tok,ld,conv):
    B,T,D=x.shape; G=D//GW; H=D//HW
    seq=lambda s: pl.BlockSpec((1,)+s,lambda g,b:(b,)+(0,)*len(s))
    wsp=pl.BlockSpec((GW,D),lambda g,b:(g,0)); bsp=pl.BlockSpec((GW,1),lambda g,b:(g,0))
    rows=pl.BlockSpec((1,GW,T),lambda g,b:(b,g,0)); cols=pl.BlockSpec((1,T,GW),lambda g,b:(b,0,g))
    sq=lambda n: pl.BlockSpec((1,GH,n,LM,LM),lambda g,b:(b,g,0,0,0))
    sd=jax.ShapeDtypeStruct; big=sd((B,D,T),BF)
    return pl.pallas_call(att_bwd_kernel,grid=(G,B),
        in_specs=[seq((T,D)),seq((T,D)),wsp]+[rows]*5+[sq(STASH),sq(6),seq((1,T)),seq((LM,1)),seq((1,LM)),cols],
        out_specs=[rows]*3+[wsp]*3+[bsp]*2,
        out_shape=[big]*3+[sd((D,D),F32)]*3+[sd((D,1),F32)]*2,
        compiler_params=pltpu.CompilerParams(vmem_limit_bytes=60*2**20))(
            x,al,wo,q,k,v,k1,k3,stash,small,tok[:,None,:],ld[:,:,None],ld[:,None,:],conv)

def gelu_parts(x):
    size=jnp.abs(x)
    density=jnp.exp(-0.5*x*x)*0.3989422804014327
    t=1.0/(1.0+0.2316419*size)
    tail=density*(t*(0.319381530+t*(-0.356563782+t*(1.781477937+t*(-1.821255978+t*1.330274429)))))
    dist=jnp.where(x<0.0,tail,1.0-tail)
    return dist, x*density
def norm(v):
    mean=jnp.mean(v,axis=-1,keepdims=True); c=v-mean
    r=lax.rsqrt(jnp.mean(c*c,axis=-1,keepdims=True)+1e-5)
    return c*r, r
def norm_back(up,n,r,g):
    e=up*g
    return r*(e-jnp.mean(e,axis=-1,keepdims=True)-n*jnp.mean(e*n,axis=-1,keepdims=True))
def ffn_kernel(chunks, ctx_ref,x_ref,cot_ref,wo_ref,wu_ref,wd_ref,vec_ref,bu_ref,
               out_ref,normed_ref,hidden_ref,down_ref,up_ref,one_ref,att_ref,sums_ref,sumu_ref,slope_ref):
    width=wu_ref.shape[0]//chunks
    @pl.when(pl.program_id(0)==0)
    def _():
        sums_ref[...]=jnp.zeros_like(sums_ref); sumu_ref[...]=jnp.zeros_like(sumu_ref)
    v=lambda i: vec_ref[i:i+1,:]
    b_o,g1,s1,b_d,g2,s2=[v(i) for i in range(6)]
    n1,r1=norm(x_ref[...].astype(F32)+(nt(ctx_ref[...],wo_ref[...])+b_o))
    normed=n1*g1+s1
    low=normed.astype(BF); normed_ref[...]=low
    down=None
    for k in range(chunks):
        part=slice(k*width,(k+1)*width)
        pre=nt(low,wu_ref[part,:])+bu_ref[:,part]
        dist,slope=gelu_parts(pre)
        slope_ref[:,part]=dist+slope
        hid=(pre*dist).astype(BF); hidden_ref[:,part]=hid
        add=nt(hid,wd_ref[:,part]); down=add if down is None else down+add
    n2,r2=norm(normed+(down+b_d))
    out_ref[...]=(n2*g2+s2).astype(BF)
    cot=cot_ref[...].astype(F32)
    g_two=norm_back(cot,n2,r2,g2)
    low2=g_two.astype(BF); down_ref[...]=low2
    back=g_two
    for k in range(chunks):
        part=slice(k*width,(k+1)*width)
        hg=nn(low2,wd_ref[:,part])
        upl=(hg*slope_ref[:,part]).astype(BF); up_ref[:,part]=upl
        sumu_ref[:,part]+=jnp.sum(upl.astype(F32),axis=0,keepdims=True)
        back=back+nn(upl,wu_ref[part,:])
    g_one=norm_back(back,n1,r1,g1)
    one_ref[...]=g_one
    al=g_one.astype(BF); att_ref[...]=al
    s=lambda a: jnp.sum(a,axis=0,keepdims=True)
    sums_ref[...]+=jnp.concatenate([s(al.astype(F32)),s(back*n1),s(back),s(low2.astype(F32)),s(cot*n2),s(cot),jnp.zeros((2,n1.shape[1]),F32)],axis=0)
def ffn(ctx,x,cot,wo,wu,wd,vec,bu,block=256,chunks=4):
    T,D=x.shape; F=wu.shape[0]
    row=lambda w: pl.BlockSpec((block,w),lambda i:(i,0))
    full=lambda a: pl.BlockSpec(a.shape,lambda i:(0,0),pipeline_mode=pl.Buffered(1))
    keep=lambda r,w: pl.BlockSpec((r,w),lambda i:(0,0))
    sd=jax.ShapeDtypeStruct
    return pl.pallas_call(functools.partial(ffn_kernel,chunks),grid=(T//block,),
        in_specs=[row(D),row(D),row(D),full(wo),full(wu),full(wd),full(vec),full(bu)],
        out_specs=[row(D),row(D),row(F),row(D),row(F),row(D),row(D),keep(8,D),keep(1,F)],
        out_shape=[sd((T,D),BF),sd((T,D),BF),sd((T,F),BF),sd((T,D),BF),sd((T,F),BF),sd((T,D),F32),sd((T,D),BF),sd((8,D),F32),sd((1,F),F32)],
        scratch_shapes=[pltpu.VMEM((block,F),F32)],
        compiler_params=pltpu.CompilerParams(vmem_limit_bytes=60*2**20,dimension_semantics=("arbitrary",)),
    )(ctx,x,cot,wo,wu,wd,vec,bu)


def digits():
    found = []
    for axis in ("wide", "narrow"):
        stride = lax.axis_size(axis) // 2
        while stride >= 1:
            found.append((axis, stride))
            stride //= 2
    return found


def link_order(number):
    count = len(digits())
    if lax.axis_size("wide") == 8 and lax.axis_size("narrow") == 4:
        return [(4, 2, 3, 1, 0), (4, 3, 1, 2, 0), (4, 1, 2, 3, 0)][number]
    return tuple(range(count - 1, -1, -1))


def exchange(values, axis, stride):
    return lax.ppermute(values, axis, [(i, i ^ stride) for i in range(lax.axis_size(axis))])


def digit_of(axis, stride):
    return (lax.axis_index(axis) // stride) % 2


def gather_rows(shard, number):
    places = digits()
    held = shard.reshape((1,) * len(places) + shard.shape)
    for dim in link_order(number)[::-1]:
        mine = digit_of(*places[dim])
        got = exchange(held, *places[dim])
        first = jnp.where(mine == 0, held, got)
        second = jnp.where(mine == 0, got, held)
        held = jnp.concatenate([first, second], dim)
    return held.reshape((-1,) + shard.shape)


def scatter_start(whole):
    return whole.reshape((2,) * len(digits()) + whole.shape[1:])


def scatter_step(held, number, step):
    places = digits()
    dim = link_order(number)[step]
    mine = digit_of(*places[dim])
    keep = lax.dynamic_slice_in_dim(held, mine, 1, dim).astype(F32)
    send = lax.dynamic_slice_in_dim(held, 1 - mine, 1, dim).astype(BF)
    return keep + exchange(send, *places[dim]).astype(F32)


def scatter_rest(held, number, step):
    for later in range(step, len(digits())):
        held = scatter_step(held, number, later)
    return held.reshape(held.shape[-2:])


def pad_rows(flat, rows):
    count, length = flat.shape
    return jnp.pad(flat, ((0, 0), (0, rows * 768 - length))).reshape(count, rows, 768)


def across_rows(left_side, right_side):
    return lax.dot_general(left_side, right_side, (((0,), (0,)), ((), ())), preferred_element_type=F32)


def shards(
    inputs,
    tok_landmark,
    landmark_doc,
    w_query,
    b_query,
    w_key,
    w_value,
    b_value,
    conv_weight,
    w_out,
    b_out,
    gain_one,
    shift_one,
    w_up,
    b_up,
    w_down,
    b_down,
    gain_two,
    shift_two,
    cotangent,
):
    batch_rows, sequence_length, feature_width = inputs.shape
    group_count = lax.axis_size("wide") * lax.axis_size("narrow")
    own = feature_width // group_count
    tokens = batch_rows * sequence_length
    vectors = (b_query, b_value, b_out, gain_one, shift_one, b_down, gain_two, shift_two)
    flat = jnp.concatenate([conv_weight.T.reshape(-1)] + list(vectors) + [b_up])
    small = pad_rows(flat[None], -(-flat.shape[0] // 768))[0]
    gathered_v = gather_rows(jnp.concatenate([w_value.T, small], axis=0), 0)
    w_q = gather_rows(w_query.T, 1).reshape(feature_width, feature_width)
    w_k = gather_rows(w_key.T, 2).reshape(feature_width, feature_width)
    w_v = gathered_v[:, :own].reshape(feature_width, feature_width)
    small = gathered_v[:, own:].reshape(group_count, -1).astype(F32)
    conv_taps = small[:, : own * KW].reshape(feature_width, KW).T
    small = small[:, own * KW :]
    b_q, b_v, b_o, g_one, s_one, b_d, g_two, s_two = [
        small[:, i * own : (i + 1) * own].reshape(feature_width) for i in range(8)
    ]
    b_u = small[:, 8 * own : 8 * own + b_up.shape[0]].reshape(1, -1)
    later = lax.optimization_barrier((w_out.T, w_up.T, w_down.T, gathered_v, w_q, w_k))
    w_o, w_u, w_d = [
        lax.all_gather(shard, ("wide", "narrow"), axis=0, tiled=True) for shard in later[:3]
    ]
    w_q, w_k = later[4:]
    doc = jnp.sum(
        jnp.where(tok_landmark[:, :, None] == jnp.arange(LM)[None, None], landmark_doc[:, None], 0), axis=2
    )
    bounds = jnp.sum(doc[:, None, :] < jnp.arange(DOCS + 1)[None, :, None], axis=2).astype(jnp.int32)
    rows_low = inputs.reshape(tokens, feature_width)
    value_rows = (nt(rows_low, w_v) + b_v).reshape(inputs.shape)
    conv_part = conv_fwd(bounds, value_rows, conv_taps)
    q, k, v, k1, k3, stash, landmarks, context = att_fwd(
        inputs, w_q, w_k, w_v, b_q[:, None], b_v[:, None], tok_landmark, landmark_doc, conv_part
    )
    context = context.reshape(tokens, feature_width)
    vec = jnp.concatenate([jnp.stack([b_o, g_one, s_one, b_d, g_two, s_two]), jnp.zeros((2, feature_width), F32)])
    layer_out, normed, hidden, down_low, up_low, grad_one, att_low, sums, sums_up = ffn(
        context, rows_low, cotangent.reshape(tokens, feature_width), w_o, w_u, w_d, vec, b_u
    )

    def by_device(values):
        return values.reshape((group_count, -1) + values.shape[1:])

    context_grad = nn(att_low, w_o).reshape(inputs.shape)
    early = jnp.concatenate([by_device(sums[i]) for i in range(6)] + [by_device(sums_up[0])], axis=1)
    grad_out = jnp.concatenate(
        [by_device(across_rows(att_low, context)), pad_rows(early, -(-early.shape[1] // 768))], axis=1
    )
    share_up = scatter_start(by_device(across_rows(up_low, normed)))
    share_down = scatter_start(by_device(across_rows(down_low, hidden)))
    share_out = scatter_start(grad_out)
    shares = [share_up, share_down, share_out]
    shares = [scatter_step(share, i, 0) for i, share in enumerate(shares)]
    context_grad, *shares = lax.optimization_barrier((context_grad, *shares))
    shares = [scatter_step(share, i, 1) for i, share in enumerate(shares)]
    conv_grad, taps_grad = conv_bwd(bounds, value_rows, context_grad, conv_taps)
    conv_grad, att_low, *shares = lax.optimization_barrier((conv_grad, att_low, *shares))
    shares = [scatter_step(share, i, 2) for i, share in enumerate(shares)]
    w_plain = w_o.T
    dq, dk, dv, grad_q, grad_k, grad_v, sum_q, sum_v = att_bwd(
        inputs, att_low.reshape(inputs.shape), w_plain, q, k, v, k1, k3, stash, landmarks, tok_landmark,
        landmark_doc, conv_grad,
    )
    dq, dk, dv, grad_q, grad_k, grad_v, *shares = lax.optimization_barrier(
        (dq, dk, dv, grad_q, grad_k, grad_v, *shares)
    )
    share_up, share_down, share_out = [scatter_rest(share, i, 3) for i, share in enumerate(shares)]
    late = jnp.concatenate(
        [by_device(taps_grad.T).reshape(group_count, -1), by_device(sum_q[:, 0]), by_device(sum_v[:, 0])], axis=1
    )
    grad_v = jnp.concatenate([by_device(grad_v), pad_rows(late, -(-late.shape[1] // 768))], axis=1)
    share_v = scatter_rest(scatter_start(grad_v), 0, 0)
    share_q = scatter_rest(scatter_start(by_device(grad_q)), 1, 0)
    share_k = scatter_rest(scatter_start(by_device(grad_k)), 2, 0)

    def through(grad, weight):
        return jnp.einsum("bot,oi->bti", grad, weight, preferred_element_type=F32)

    input_grad = grad_one.reshape(inputs.shape) + through(dq, w_q) + through(dk, w_k) + through(dv, w_v)
    early = share_out[own:].reshape(-1)
    late = share_v[own:].reshape(-1)
    return (
        layer_out.reshape(inputs.shape),
        input_grad,
        share_q.T,
        late[own * KW : own * KW + own],
        share_k.T,
        share_v[:own].T,
        late[own * KW + own : own * KW + 2 * own],
        late[: own * KW].reshape(own, KW).T,
        share_out[:own].T,
        early[:own],
        early[own : 2 * own],
        early[2 * own : 3 * own],
        share_up.T,
        early[6 * own : 6 * own + b_up.shape[0]],
        share_down.T,
        early[3 * own : 4 * own],
        early[4 * own : 5 * own],
        early[5 * own : 6 * own],
    )


def solution(mesh):
    return jax.shard_map(
        shards,
        mesh=mesh,
        in_specs=(
            P(("wide", "narrow"), None, None),
            P(("wide", "narrow"), None),
            P(("wide", "narrow"), None),
            P(None, ("wide", "narrow")),
            P(("wide", "narrow")),
            P(None, ("wide", "narrow")),
            P(None, ("wide", "narrow")),
            P(("wide", "narrow")),
            P(None, ("wide", "narrow")),
            P(None, ("wide", "narrow")),
            P(("wide", "narrow")),
            P(("wide", "narrow")),
            P(("wide", "narrow")),
            P(None, ("wide", "narrow")),
            P(("wide", "narrow")),
            P(None, ("wide", "narrow")),
            P(("wide", "narrow")),
            P(("wide", "narrow")),
            P(("wide", "narrow")),
            P(("wide", "narrow"), None, None),
        ),
        out_specs=(
            P(("wide", "narrow"), None, None),
            P(("wide", "narrow"), None, None),
            P(None, ("wide", "narrow")),
            P(("wide", "narrow")),
            P(None, ("wide", "narrow")),
            P(None, ("wide", "narrow")),
            P(("wide", "narrow")),
            P(None, ("wide", "narrow")),
            P(None, ("wide", "narrow")),
            P(("wide", "narrow")),
            P(("wide", "narrow")),
            P(("wide", "narrow")),
            P(None, ("wide", "narrow")),
            P(("wide", "narrow")),
            P(None, ("wide", "narrow")),
            P(("wide", "narrow")),
            P(("wide", "narrow")),
            P(("wide", "narrow")),
        ),
        check_vma=False,
    )
```

time: 1280 us -> 648 us (0.51)
  matrix products: 502 us -> 54.7 us
  other arithmetic: 407 us -> 45.8 us
  Pallas kernels: 0 us -> 299 us
  local copies, waits for them, and re-layouts: 171 us -> 80.4 us
  starting transfers between devices: 71.7 us -> 46.5 us
    dot_general x106 -> x5, matrix products: 446 us -> 23.9 us  [the longest x3 13.3 us: through(): return jnp.einsum('bot,oi->bti', grad, weight, preferred_element_type=F32)]
    pallas_call x0 -> x5, Pallas kernels: none -> 299 us  [the longest x1 76.4 us: ffn(): pl.pallas_call(functools.partial(ffn_kernel, chunks), grid=(T // block,),...]
    convert_element_type x4 -> x0, other arithmetic: 133 us -> none  [the longest x1 131 us: shards(): context_low = mixed_context.astype(jnp.bfloat16)]
    reduce_sum x20 -> x2, other arithmetic: 118 us -> 0.34 us  [the longest x1 0.18 us: shards(): jnp.sum(doc[:, None, :] < jnp.arange(DOCS + 1)[None, :, None], axis=2)]
    add_any x1 -> x0, other arithmetic: 56.6 us -> none  [nystrom(): padded[offset:offset + sequence_length]]
    mul x5 -> x0, other arithmetic: 56.5 us -> none  [the longest x3 56.5 us: nystrom(): conv_weight[offset][None, :] * padded[offset:offset + sequence_length]]
    ppermute x75 -> x45, waiting for transfers between devices: 100 us -> 47.9 us  [exchange(): lax.ppermute(values, axis, [(i, i ^ stride) for i in range(lax.axis_size(...]
    all_gather x3, waiting for transfers between devices: 0.04 us -> 51.3 us  [shards(): lax.all_gather(shard, ('wide', 'narrow'), axis=0, tiled=True)]
  transfers between devices with their start and end apart: 78 -> 48, of which waited for: 33 -> 17; matrix products, arithmetic and copies ran while one was open for 47% -> 19% of each run, Pallas kernels for 0% -> 35%
where the time goes in v2:
time: 648 us; the launch traced here: 642 us
  Pallas kernels  299 us (46%)
  waiting for transfers between devices  100 us (15%)
  local copies, waits for them, and re-layouts  80.4 us (12%)
  matrix products  54.7 us (8%)
  starting transfers between devices  46.5 us (7%)
  other arithmetic  45.8 us (7%)
  between operations  15.2 us (2%)
    pallas_call x1, Pallas kernels, ffn(): pl.pallas_call(functools.partial(ffn_kernel, chunks), grid=(T // block,),...  76.4 us
    pallas_call x1, Pallas kernels, att_fwd(): pl.pallas_call(att_fwd_kernel, grid=(G, B), in_specs=[seq((T, D)), wsp, w...  74.7 us
    pallas_call x1, Pallas kernels, att_bwd(): pl.pallas_call(att_bwd_kernel, grid=(G, B), in_specs=[seq((T, D)), seq((T...  74.1 us
    all_gather x3, waiting for transfers between devices, shards(): lax.all_gather(shard, ('wide', 'narrow'), axis=0, tiled=True)  51.3 us
    ppermute x45, waiting for transfers between devices, exchange(): lax.ppermute(values, axis, [(i, i ^ stride) for i in range(lax.axis_size(...  47.9 us
    ppermute x45, starting transfers between devices, exchange(): lax.ppermute(values, axis, [(i, i ^ stride) for i in range(lax.axis_size(...  46 us
    pallas_call x1, Pallas kernels, conv_bwd(): pl.pallas_call(conv_bwd_kernel, grid_spec=pltpu.PrefetchScalarGridSpec(nu...  45.3 us
    dot_general x3, matrix products, across_rows(): lax.dot_general(left_side, right_side, (((0,), (0,)), ((), ())), preferre...  30.8 us
  transfers between devices with their start and end apart: 48, of which 17 were waited for; matrix products, arithmetic and copies ran while one was open for 19% of the time, Pallas kernels for 35%

profile of v2, /device:TPU:0, one launch (start us, length us, event | category | flops | bytes accessed | tf_op | source)
XLA Modules:
  0.0 642.2 jit_solution(14904628020290315047)
XLA Ops:
  7.2 4.1 collective-permute-start.5
  12.1 6.1 concatenate.74
  64.1 4.5 add_bitcast_fusion
  68.6 6.7 %copy.186 = f32[2048,768]{1,0:T(8,128)} copy(f32[2048,768]{0,1:T(8,128)} %add_bitcast_fusion) | data formatting | bytes 12582912 | tf_op jit(solution)/shard_map/add | solution.py:457
  80.6 28.9 %shard_map.331.conv_ref = f32[2,1024,768]{2,1,0:T(8,128)S(1)} custom-call(s32[2,5]{1,0:T(2,128)S(1)} %copy.188.bounds_ref, f32[2,1024,768]{2,1,0:T(8,128)S(1)} %bitcast.120, f32[33,768]{1,0:T(8,128)S(1)} %bitcast.123), custom_call_target="tpu_custom_call" | custom-call | tf_op jit(solution)/shard_map/pallas_call | solution.py:71
  112.9 74.7 %shard_map.332 = (f32[2,768,1024]{2,1,0:T(8,128)}, f32[2,768,1024]{2,1,0:T(8,128)}, f32[2,768,1024]{2,1,0:T(8,128)}, f32[2,768,1024]{2,1,0:T(8,128)}, f32[2,768,...) custom-call(bf16[2,1024,768]{2,1,0:T(8,128)(2,1)} %x_ref.3, ...), custom_call_target="tpu_custom_call" | custom-call | tf_op jit(solution)/shard_map/pallas_call | solution.py:195
  187.6 51.3 %all-gather.8.cloned.1.call-done.wd_ref = bf16[768,3072]{1,0:T(8,128)(2,1)} async-done(((bf16[24,3072]{1,0:T(8,128)(2,1)}), bf16[768,3072]{1,0:T(8,128)(2,1)}) %all-gather.8.cloned.1.call-update) | async-done | bytes 4718608 | tf_op jit(solution)/shard_map/all_gather | solution.py:449
  238.9 76.4 %shard_map.333 = (bf16[2048,768]{1,0:T(8,128)(2,1)}, bf16[2048,768]{1,0:T(8,128)(2,1)}, bf16[2048,3072]{1,0:T(8,128)(2,1)}, bf16[2048,768]{1,0:T(8,128)(2,1)}, b...) custom-call(bf16[2048,768]{1,0:T(8,128)(2,1)} %bitcast.150, ...), custom_call_target="tpu_custom_call" | custom-call | tf_op jit(solution)/shard_map/pallas_call | solution.py:333
  319.0 3.2 copy.193
  322.2 14.1 %fusion.9 = f32[768,3072]{1,0:T(8,128)S(1)} fusion(bf16[2048,768]{1,0:T(8,128)(2,1)} %get-tuple-element.79, bf16[2048,3072]{1,0:T(8,128)(2,1)} %get-tuple-element.80), kind=kOutput, calls=%fused_computation.145 | convolution fusion | flops 9663676416 | bytes 25165824 | tf_op jit(solution)/shard_map/dot_general | solution.py:404
  340.5 14.0 %fusion.8 = f32[3072,768]{1,0:T(8,128)S(1)} fusion(bf16[2048,3072]{1,0:T(8,128)(2,1)} %get-tuple-element.77, bf16[2048,768]{1,0:T(8,128)(2,1)S(1)} %copy-done.35), kind=kOutput, calls=%fused_computation.144 | convolution fusion | flops 9663676416 | bytes 25165824 | tf_op jit(solution)/shard_map/dot_general | solution.py:404
  366.4 6.1 fusion.7
  374.3 3.8 convert_add_fusion
  378.2 6.2 convert_add_fusion.1
  399.7 45.3 %shard_map.334 = (f32[2,1024,768]{2,1,0:T(8,128)S(1)}, f32[33,768]{1,0:T(8,128)S(1)}) custom-call(s32[2,5]{1,0:T(2,128)S(1)} %copy.188.bounds_ref, f32[2,1024,768]{2,1,0:T(8,128)S(1)} %bitcast.121, f32[2,1024,768]{2,1,0:T(8,128)S(1)} %bitcast.122, f32[33,768]{1,0:T(8,128)S(1)} %bitcast.124), custom_call_target="tpu_custom_call" | custom-call | tf_op jit(solution)/shard_map/pallas_call | solution.py:115
  458.8 74.1 %shard_map.335 = (bf16[2,768,1024]{2,1,0:T(8,128)(2,1)}, bf16[2,768,1024]{2,1,0:T(8,128)(2,1)}, bf16[2,768,1024]{2,1,0:T(8,128)(2,1)}, f32[768,768]{1,0:T(8,128)...) custom-call(bf16[2,1024,768]{2,1,0:T(8,128)(2,1)} %x_ref.3, ...), custom_call_target="tpu_custom_call" | custom-call | tf_op jit(solution)/shard_map/pallas_call | solution.py:270
  556.2 7.9 %add_add_fusion = f32[2,1024,768]{2,1,0:T(8,128)} fusion(f32[2,1024,768]{2,1,0:T(8,128)S(1)} %fusion, f32[2,1024,768]{2,1,0:T(8,128)S(1)} %bitcast.135, f32[2,1024,768]{2,1,0:T(8,128)S(1)} %fusion.2, bf16[2,768,1024]{2,1,0:T(8,128)(2,1)} %get-tuple-element.108, bf16[768,768,1]{1,0,2:T(8,128)(2,1)S(1)} %bitcast.132), kind=kOutput, calls=%fused_computation | convolution fusion | flops 2420637696 | bytes 29491200 | tf_op jit(solution)/shard_map/bot,oi->bti/dot_general | solution.py:504
  567.4 4.2 collective-permute-done.40
  579.0 8.9 %collective-permute-done.44 = bf16[1,1,1,1,1,24,3072]{6,5,4,3,2,1,0:T(8,128)(2,1)S(1)} collective-permute-done((bf16[1,1,1,1,1,24,3072]{6,5,4,3,2,1,0:T(8,128)(2,1)S(1)}, bf16[1,1,1,1,1,24,3072]{6,5,4,3,2,1,0:T(8,128)(2,1)S(1)}, u32[]{:S(2)}, u32[]{:S(2)}) %collective-permute-start.44) | collective-permute-done | bytes 147488 | tf_op jit(solution)/shard_map/ppermute | solution.py:360
  597.4 4.6 collective-permute-done.35
  604.3 3.0 collective-permute-done.30
  611.6 5.3 collective-permute-done.37
  622.7 4.1 collective-permute-done.32
  629.4 4.0 collective-permute-done.33
  (334 shorter events, 165.6 us)
Async XLA Ops:
  7.2 180.4 %all-gather.4.cloned.1.call-start = ((), (), s32[]{:S(2)}) async-start(), calls=%async_computation | async-start | bytes 1216512 | tf_op jit(solution)/shard_map/all_gather | solution.py:449
  7.2 14.8 %collective-permute-start.5 = (bf16[1,1,1,1,1,24,768]{6,5,4,3,2,1,0:T(8,128)(2,1)}, bf16[1,1,1,1,1,24,768]{6,5,4,3,2,1,0:T(8,128)(2,1)S(1)}, u32[]{:S(2)}, u32[]{:S(2)}) collective-permute-start(bf16[1,1,1,1,1,24,768]{6,5,4,3,2,1,0:T(8,128)(2,1)} %bitcast.167), channel_id=1, source_target_pairs={{0,16},{4,20},{8,24},{12,28},{16,0},{20,4},{24,8},{28,12},{1,17},{... | collective-permute-start | bytes 110600 | tf_op jit(solution)/shard_map/ppermute | solution.py:360
  53.3 134.3 %all-gather.6.cloned.1.call-start = ((), (), s32[]{:S(2)}) async-start(), calls=%async_computation.1 | async-start | bytes 4866048 | tf_op jit(solution)/shard_map/all_gather | solution.py:449
  54.0 184.9 %all-gather.8.cloned.1.call-start = ((), (), s32[]{:S(2)}) async-start(), calls=%async_computation.2 | async-start | bytes 4866048 | tf_op jit(solution)/shard_map/all_gather | solution.py:449
  338.1 36.3 %collective-permute-start.16 = (bf16[2,2,2,2,1,24,3072]{6,5,4,3,2,1,0:T(8,128)(2,1)}, bf16[2,2,2,2,1,24,3072]{6,5,4,3,2,1,0:T(8,128)(2,1)}, u32[]{:S(2)}, u32[]{:S(2)}) collective-permute-start(bf16[2,2,2,2,1,24,3072]{6,5,4,3,2,1,0:T(8,128)(2,1)} %dynamic-slice_convert_fusion), channel_id=1, source_target_pairs={{0,1},{1,0},{2,3},{3,2},{4,5},{5,4},{6,7},{7,6},{8,9},{9,8},{10,11... | collective-permute-start | bytes 7077896 | tf_op jit(solution)/shard_map/ppermute | solution.py:360
  356.4 21.7 %collective-permute-start.15 = (bf16[2,2,2,2,1,96,768]{6,5,4,3,2,1,0:T(8,128)(2,1)}, bf16[2,2,2,2,1,96,768]{6,5,4,3,2,1,0:T(8,128)(2,1)}, u32[]{:S(2)}, u32[]{:S(2)}) collective-permute-start(bf16[2,2,2,2,1,96,768]{6,5,4,3,2,1,0:T(8,128)(2,1)} %dynamic-slice_convert_fusion.1), channel_id=1, source_target_pairs={{0,1},{1,0},{2,3},{3,2},{4,5},{5,4},{6,7},{7,6},{8,9},{9,8},{10,11... | collective-permute-start | bytes 7077896 | tf_op jit(solution)/shard_map/ppermute | solution.py:360
  385.6 63.7 %collective-permute-start.19 = (bf16[2,2,2,1,1,24,3072]{6,5,4,3,2,1,0:T(8,128)(2,1)}, bf16[2,2,2,1,1,24,3072]{6,5,4,3,2,1,0:T(8,128)(2,1)}, u32[]{:S(2)}, u32[]{:S(2)}) collective-permute-start(bf16[2,2,2,1,1,24,3072]{6,5,4,3,2,1,0:T(8,128)(2,1)} %dynamic-slice_convert_fusion.2), channel_id=1, source_target_pairs={{0,2},{1,3},{2,0},{3,1},{4,6},{5,7},{6,4},{7,5},{8,10},{9,11},{10,... | collective-permute-start | bytes 3538952 | tf_op jit(solution)/shard_map/ppermute | solution.py:360
  387.3 60.7 %collective-permute-start.20 = (bf16[2,1,2,2,1,25,768]{6,3,5,4,2,1,0:T(2,128)(2,1)S(1)}, bf16[2,1,2,2,1,25,768]{6,3,5,4,2,1,0:T(2,128)(2,1)}, u32[]{:S(2)}, u32[]{:S(2)}) collective-permute-start(bf16[2,1,2,2,1,25,768]{6,3,5,4,2,1,0:T(2,128)(2,1)S(1)} %dynamic-slice_convert_fusion.11), channel_id=1, source_target_pairs={{0,8},{4,12},{8,0},{12,4},{16,24},{20,28},{24,16},{28,20},{1,9},{5... | collective-permute-start | bytes 921608 | tf_op jit(solution)/shard_map/ppermute | solution.py:360
  392.1 59.5 %collective-permute-start.18 = (bf16[2,2,1,2,1,96,768]{6,5,4,3,2,1,0:T(8,128)(2,1)}, bf16[2,2,1,2,1,96,768]{6,5,4,3,2,1,0:T(8,128)(2,1)}, u32[]{:S(2)}, u32[]{:S(2)}) collective-permute-start(bf16[2,2,1,2,1,96,768]{6,5,4,3,2,1,0:T(8,128)(2,1)} %dynamic-slice_convert_fusion.3), channel_id=1, source_target_pairs={{0,4},{4,0},{8,12},{12,8},{16,20},{20,16},{24,28},{28,24},{1,5},{5... | collective-permute-start | bytes 3538952 | tf_op jit(solution)/shard_map/ppermute | solution.py:360
  454.8 81.6 %collective-permute-start.23 = (bf16[2,1,1,2,1,25,768]{6,3,5,4,2,1,0:T(2,128)(2,1)}, bf16[2,1,1,2,1,25,768]{6,3,5,4,2,1,0:T(2,128)(2,1)S(1)}, u32[]{:S(2)}, u32[]{:S(2)}) collective-permute-start(bf16[2,1,1,2,1,25,768]{6,3,5,4,2,1,0:T(2,128)(2,1)} %dynamic-slice_convert_fusion.17), channel_id=1, source_target_pairs={{0,4},{4,0},{8,12},{12,8},{16,20},{20,16},{24,28},{28,24},{1,5},{5... | collective-permute-start | bytes 460808 | tf_op jit(solution)/shard_map/ppermute | solution.py:360
  457.2 79.3 %collective-permute-start.22 = (bf16[2,1,2,1,1,24,3072]{6,5,4,3,2,1,0:T(8,128)(2,1)}, bf16[2,1,2,1,1,24,3072]{6,5,4,3,2,1,0:T(8,128)(2,1)}, u32[]{:S(2)}, u32[]{:S(2)}) collective-permute-start(bf16[2,1,2,1,1,24,3072]{6,5,4,3,2,1,0:T(8,128)(2,1)} %dynamic-slice_convert_fusion.8), channel_id=1, source_target_pairs={{0,8},{4,12},{8,0},{12,4},{16,24},{20,28},{24,16},{28,20},{1,9},{5... | collective-permute-start | bytes 1769480 | tf_op jit(solution)/shard_map/ppermute | solution.py:360
  458.2 79.7 %collective-permute-start.21 = (bf16[2,2,1,1,1,96,768]{6,5,4,3,2,1,0:T(8,128)(2,1)}, bf16[2,2,1,1,1,96,768]{6,5,4,3,2,1,0:T(8,128)(2,1)}, u32[]{:S(2)}, u32[]{:S(2)}) collective-permute-start(bf16[2,2,1,1,1,96,768]{6,5,4,3,2,1,0:T(8,128)(2,1)} %dynamic-slice_convert_fusion.9), channel_id=1, source_target_pairs={{0,2},{1,3},{2,0},{3,1},{4,6},{5,7},{6,4},{7,5},{8,10},{9,11},{10,... | collective-permute-start | bytes 1769480 | tf_op jit(solution)/shard_map/ppermute | solution.py:360
  539.7 33.9 %collective-permute-start.43 = (bf16[2,1,1,1,1,24,3072]{6,5,4,3,2,1,0:T(8,128)(2,1)S(1)}, bf16[2,1,1,1,1,24,3072]{6,5,4,3,2,1,0:T(8,128)(2,1)}, u32[]{:S(2)}, u32[]{:S(2)}) collective-permute-start(bf16[2,1,1,1,1,24,3072]{6,5,4,3,2,1,0:T(8,128)(2,1)S(1)} %dynamic-slice_convert_fusion.12), channel_id=1, source_target_pairs={{0,4},{4,0},{8,12},{12,8},{16,20},{20,16},{24,28},{28,24},{1,5},{5... | collective-permute-start | bytes 884744 | tf_op jit(solution)/shard_map/ppermute | solution.py:360
  541.9 33.0 %collective-permute-start.41 = (bf16[2,1,1,1,1,96,768]{6,5,4,3,2,1,0:T(8,128)(2,1)}, bf16[2,1,1,1,1,96,768]{6,5,4,3,2,1,0:T(8,128)(2,1)}, u32[]{:S(2)}, u32[]{:S(2)}) collective-permute-start(bf16[2,1,1,1,1,96,768]{6,5,4,3,2,1,0:T(8,128)(2,1)} %dynamic-slice_convert_fusion.13), channel_id=1, source_target_pairs={{0,8},{4,12},{8,0},{12,4},{16,24},{20,28},{24,16},{28,20},{1,9},{5... | collective-permute-start | bytes 884744 | tf_op jit(solution)/shard_map/ppermute | solution.py:360
  544.0 20.1 %collective-permute-start.39 = (bf16[2,1,1,1,1,25,768]{6,3,5,4,2,1,0:T(2,128)(2,1)S(1)}, bf16[2,1,1,1,1,25,768]{6,3,5,4,2,1,0:T(2,128)(2,1)}, u32[]{:S(2)}, u32[]{:S(2)}) collective-permute-start(bf16[2,1,1,1,1,25,768]{6,3,5,4,2,1,0:T(2,128)(2,1)S(1)} %dynamic-slice_convert_fusion.23), channel_id=1, source_target_pairs={{0,2},{1,3},{2,0},{3,1},{4,6},{5,7},{6,4},{7,5},{8,10},{9,11},{10,... | collective-permute-start | bytes 230408 | tf_op jit(solution)/shard_map/ppermute | solution.py:360
  546.9 44.9 %collective-permute-start.34 = (bf16[2,2,2,2,1,24,768]{6,5,4,3,2,1,0:T(8,128)(2,1)}, bf16[2,2,2,2,1,24,768]{6,5,4,3,2,1,0:T(8,128)(2,1)}, u32[]{:S(2)}, u32[]{:S(2)}) collective-permute-start(bf16[2,2,2,2,1,24,768]{6,5,4,3,2,1,0:T(8,128)(2,1)} %dynamic-slice_convert_fusion.6), channel_id=1, source_target_pairs={{0,1},{1,0},{2,3},{3,2},{4,5},{5,4},{6,7},{7,6},{8,9},{9,8},{10,11... | collective-permute-start | bytes 1769480 | tf_op jit(solution)/shard_map/ppermute | solution.py:360
  550.2 44.7 %collective-permute-start.29 = (bf16[2,2,2,2,1,26,768]{6,3,5,4,2,1,0:T(2,128)(2,1)}, bf16[2,2,2,2,1,26,768]{6,3,5,4,2,1,0:T(2,128)(2,1)}, u32[]{:S(2)}, u32[]{:S(2)}) collective-permute-start(bf16[2,2,2,2,1,26,768]{6,3,5,4,2,1,0:T(2,128)(2,1)} %dynamic-slice_convert_fusion.4), channel_id=1, source_target_pairs={{0,1},{1,0},{2,3},{3,2},{4,5},{5,4},{6,7},{7,6},{8,9},{9,8},{10,11... | collective-permute-start | bytes 1916936 | tf_op jit(solution)/shard_map/ppermute | solution.py:360
  571.7 21.4 %collective-permute-start.24 = (bf16[2,2,2,2,1,24,768]{6,5,4,3,2,1,0:T(8,128)(2,1)S(1)}, bf16[2,2,2,2,1,24,768]{6,5,4,3,2,1,0:T(8,128)(2,1)S(1)}, u32[]{:S(2)}, u32[]{:S(2)}) collective-permute-start(bf16[2,2,2,2,1,24,768]{6,5,4,3,2,1,0:T(8,128)(2,1)S(1)} %dynamic-slice_convert_fusion.7), channel_id=1, source_target_pairs={{0,1},{1,0},{2,3},{3,2},{4,5},{5,4},{6,7},{7,6},{8,9},{9,8},{10,11... | collective-permute-start | bytes 1769480 | tf_op jit(solution)/shard_map/ppermute | solution.py:360
  574.8 13.1 %collective-permute-start.44 = (bf16[1,1,1,1,1,24,3072]{6,5,4,3,2,1,0:T(8,128)(2,1)S(1)}, bf16[1,1,1,1,1,24,3072]{6,5,4,3,2,1,0:T(8,128)(2,1)S(1)}, u32[]{:S(2)}, u32[]{:S(2)}) collective-permute-start(bf16[1,1,1,1,1,24,3072]{6,5,4,3,2,1,0:T(8,128)(2,1)S(1)} %dynamic-slice_convert_fusion.18), channel_id=1, source_target_pairs={{0,16},{4,20},{8,24},{12,28},{16,0},{20,4},{24,8},{28,12},{1,17},{... | collective-permute-start | bytes 442376 | tf_op jit(solution)/shard_map/ppermute | solution.py:360
  576.0 15.0 %collective-permute-start.42 = (bf16[1,1,1,1,1,96,768]{6,5,4,3,2,1,0:T(8,128)(2,1)S(1)}, bf16[1,1,1,1,1,96,768]{6,5,4,3,2,1,0:T(8,128)(2,1)S(1)}, u32[]{:S(2)}, u32[]{:S(2)}) collective-permute-start(bf16[1,1,1,1,1,96,768]{6,5,4,3,2,1,0:T(8,128)(2,1)S(1)} %dynamic-slice_convert_fusion.19), channel_id=1, source_target_pairs={{0,16},{4,20},{8,24},{12,28},{16,0},{20,4},{24,8},{28,12},{1,17},{... | collective-permute-start | bytes 442376 | tf_op jit(solution)/shard_map/ppermute | solution.py:360
  593.3 10.4 %collective-permute-start.25 = (bf16[2,2,2,1,1,24,768]{6,5,4,3,2,1,0:T(8,128)(2,1)S(1)}, bf16[2,2,2,1,1,24,768]{6,5,4,3,2,1,0:T(8,128)(2,1)S(1)}, u32[]{:S(2)}, u32[]{:S(2)}) collective-permute-start(bf16[2,2,2,1,1,24,768]{6,5,4,3,2,1,0:T(8,128)(2,1)S(1)} %dynamic-slice_convert_fusion.15), channel_id=1, source_target_pairs={{0,2},{1,3},{2,0},{3,1},{4,6},{5,7},{6,4},{7,5},{8,10},{9,11},{10,... | collective-permute-start | bytes 884744 | tf_op jit(solution)/shard_map/ppermute | solution.py:360
  596.8 10.5 %collective-permute-start.30 = (bf16[2,2,1,2,1,26,768]{6,3,5,4,2,1,0:T(2,128)(2,1)S(1)}, bf16[2,2,1,2,1,26,768]{6,3,5,4,2,1,0:T(2,128)(2,1)S(1)}, u32[]{:S(2)}, u32[]{:S(2)}) collective-permute-start(bf16[2,2,1,2,1,26,768]{6,3,5,4,2,1,0:T(2,128)(2,1)S(1)} %dynamic-slice_convert_fusion.10), channel_id=1, source_target_pairs={{0,4},{4,0},{8,12},{12,8},{16,20},{20,16},{24,28},{28,24},{1,5},{5... | collective-permute-start | bytes 958472 | tf_op jit(solution)/shard_map/ppermute | solution.py:360
  607.9 12.1 %collective-permute-start.31 = (bf16[2,2,1,1,1,26,768]{6,3,5,4,2,1,0:T(2,128)(2,1)S(1)}, bf16[2,2,1,1,1,26,768]{6,3,5,4,2,1,0:T(2,128)(2,1)S(1)}, u32[]{:S(2)}, u32[]{:S(2)}) collective-permute-start(bf16[2,2,1,1,1,26,768]{6,3,5,4,2,1,0:T(2,128)(2,1)S(1)} %dynamic-slice_convert_fusion.16), channel_id=1, source_target_pairs={{0,2},{1,3},{2,0},{3,1},{4,6},{5,7},{6,4},{7,5},{8,10},{9,11},{10,... | collective-permute-start | bytes 479240 | tf_op jit(solution)/shard_map/ppermute | solution.py:360
  618.7 10.1 %collective-permute-start.28 = (bf16[1,1,1,1,1,24,768]{6,5,4,3,2,1,0:T(8,128)(2,1)S(1)}, bf16[1,1,1,1,1,24,768]{6,5,4,3,2,1,0:T(8,128)(2,1)S(1)}, u32[]{:S(2)}, u32[]{:S(2)}) collective-permute-start(bf16[1,1,1,1,1,24,768]{6,5,4,3,2,1,0:T(8,128)(2,1)S(1)} %dynamic-slice_convert_fusion.29), channel_id=1, source_target_pairs={{0,16},{4,20},{8,24},{12,28},{16,0},{20,4},{24,8},{28,12},{1,17},{... | collective-permute-start | bytes 110600 | tf_op jit(solution)/shard_map/ppermute | solution.py:360
  (65 other events, 394.7 us)
Sparse Core Ops, SparseCore 0:
  53.4 54.6 all-gather.3
  111.0 62.4 all-gather.5
  176.4 62.3 all-gather.7

commit v3 on v2

v3 whole, which is shorter than its diff:
```python
import functools

import jax
import jax.numpy as jnp
from jax import lax
from jax.experimental import pallas as pl
from jax.experimental.pallas import tpu as pltpu
from jax.sharding import PartitionSpec as P

BF = jnp.bfloat16
F32 = jnp.float32
HW=64; LM=64; NEWTON=6; GH=6; GW=GH*HW
CHUNK=256
def nt(a,b): return lax.dot_general(a,b,(((1,),(1,)),((),())),preferred_element_type=F32)
def nn(a,b): return lax.dot_general(a,b,(((1,),(0,)),((),())),preferred_element_type=F32)
def split(a):
    hi=a.astype(BF); return hi,(a-hi.astype(F32)).astype(BF)
def wide(a):
    hi,lo=split(a); return jnp.concatenate([hi,hi,lo],axis=1)
def tall(b):
    hi,lo=split(b); return jnp.concatenate([hi,lo,hi],axis=0)
def mm3(a,b): return nn(wide(a),tall(b))
def eye(c):
    return jnp.where(lax.broadcasted_iota(jnp.int32,(LM,LM),0)==lax.broadcasted_iota(jnp.int32,(LM,LM),1),c,0.0)
def weave(first, second):
    done=0
    for i,step in enumerate(first):
        step()
        upto=(i+1)*len(second)//len(first)
        for other in second[done:upto]: other()
        done=upto
def att_fwd_kernel(x_ref,mean_ref,wq_ref,wk_ref,wv_ref,vec_ref,tok_ref,ldc_ref,ldr_ref,conv_ref,
               q_ref,k_ref,v_ref,k1_ref,k3_ref,inv_ref,stash_ref,small_ref,ctx_ref,
               qlo_ref,klo_ref,score_ref,bias_ref):
    T=x_ref.shape[1]
    heads=range(GH); chunks=[slice(c,c+CHUNK) for c in range(0,T,CHUNK)]
    rows=[slice(h*HW,(h+1)*HW) for h in heads]
    scale=HW**-0.25
    bq=vec_ref[0:1,:].T; bv=vec_ref[1:2,:].T
    ldc=ldc_ref[0]
    for cs in chunks:
        member=lax.broadcasted_iota(jnp.int32,(LM,CHUNK),0)==tok_ref[0,:,cs]
        doc=jnp.sum(jnp.where(member,ldc,0),axis=0,keepdims=True)
        bias_ref[:,cs]=jnp.where(doc==ldc,0.0,-1e30)
    mean=jnp.concatenate(split(mean_ref[0]),axis=0)
    def land(w_ref):
        both=nt(w_ref[...],mean)
        return both[:,:LM]+both[:,LM:]
    lqt=(land(wq_ref)+bq)*scale; lkt=land(wk_ref)*scale
    lq=[lqt[r].T for r in rows]; lk=[lkt[r].T for r in rows]
    lqw=[wide(a) for a in lq]; lkw=[wide(a) for a in lk]
    allow2=ldc==ldr_ref[0]
    k2=[];z=[]
    for h in heads:
        s=jnp.where(allow2,nn(lqw[h],tall(lkt[rows[h]])),-1e30)
        e=jnp.exp(s-jnp.max(s,axis=1,keepdims=True))
        k2.append(e/jnp.sum(e,axis=1,keepdims=True))
        z.append(k2[h].T*(1.0/jnp.sum(k2[h]*k2[h])))
    state={"z":z}
    k2w=[wide(a) for a in k2]
    def newton(n):
        def one():
            state["p"]=[nn(k2w[h],tall(state["z"][h])) for h in heads]
            state["pw"]=[wide(a) for a in state["p"]]
        def two(): state["b"]=[eye(15.0)-nn(state["pw"][h],tall(eye(7.0)-state["p"][h])) for h in heads]
        def three(): state["c"]=[eye(13.0)-nn(state["pw"][h],tall(state["b"][h])) for h in heads]
        def four():
            for h in heads:
                stash_ref[0,h,2*n]=jnp.concatenate([state["p"][h],state["b"][h]],axis=1)
                stash_ref[0,h,2*n+1]=jnp.concatenate([state["c"][h],state["z"][h].T],axis=1)
            state["z"]=[0.25*mm3(state["z"][h],state["c"][h]) for h in heads]
        return [one,two,three,four]
    chain=[step for n in range(NEWTON) for step in newton(n)]
    side=[]
    def project(cs):
        x=x_ref[0,cs,:]
        def q():
            a=(nt(wq_ref[...],x)+bq)*scale
            hi,lo=split(a); q_ref[0,:,cs]=hi; qlo_ref[:,cs]=lo
        def k():
            a=nt(wk_ref[...],x)*scale
            hi,lo=split(a); k_ref[0,:,cs]=hi; klo_ref[:,cs]=lo
        def v(): v_ref[0,:,cs]=(nt(wv_ref[...],x)+bv).astype(BF)
        return [q,k,v]
    tops=[None]*GH; sums=[None]*GH; r=[None]*GH
    def lanes(a): return [a[:,i:i+128] for i in range(0,CHUNK,128)]
    def first(h,cs):
        def go():
            hi=q_ref[0,rows[h],cs]
            s=nn(lkw[h],jnp.concatenate([hi,qlo_ref[rows[h],cs],hi],axis=0))+bias_ref[:,cs]
            e=jnp.exp(s-jnp.max(s,axis=0,keepdims=True))
            e=e.astype(BF); k1_ref[0,rows[h],cs]=e
            inv_ref[0,0,h:h+1,cs]=1.0/jnp.sum(e.astype(F32),axis=0,keepdims=True)
        return go
    def third(h,cs):
        def go():
            hi=k_ref[0,rows[h],cs]
            s=nn(lqw[h],jnp.concatenate([hi,klo_ref[rows[h],cs],hi],axis=0))+bias_ref[:,cs]
            score_ref[rows[h],cs]=s
            for a in lanes(s): tops[h]=a if tops[h] is None else jnp.maximum(tops[h],a)
        return go
    def raised(h,cs):
        def go():
            if cs.start==0: tops[h]=jnp.max(tops[h],axis=1,keepdims=True)
            e=jnp.exp(score_ref[rows[h],cs]-tops[h])
            e=e.astype(BF); k3_ref[0,rows[h],cs]=e
            for a in lanes(e.astype(F32)): sums[h]=a if sums[h] is None else sums[h]+a
        return go
    def gathered(h):
        def go():
            sums[h]=1.0/jnp.sum(sums[h],axis=1,keepdims=True)
            r[h]=nt(k3_ref[0,rows[h]],v_ref[0,rows[h]])*sums[h]
        return go
    for cs in chunks: side+=project(cs)
    for h in heads:
        side+=[third(h,cs) for cs in chunks]
        side+=[raised(h,cs) for cs in chunks]+[gathered(h)]
        side+=[first(h,cs) for cs in chunks]
    weave(chain,side)
    uts=[]
    for h in heads:
        u=mm3(state["z"][h],r[h])
        small_ref[0,h,0]=jnp.concatenate([lq[h],lk[h]],axis=1)
        small_ref[0,h,1]=jnp.concatenate([k2[h],state["z"][h].T],axis=1)
        small_ref[0,h,2]=jnp.concatenate([r[h],u],axis=1)
        small_ref[0,h,3]=jnp.broadcast_to(sums[h],(LM,128))
        uts.append(u.T.astype(BF))
    for cs in chunks:
        mixed=jnp.concatenate([nn(uts[h],k1_ref[0,rows[h],cs])*inv_ref[0,0,h:h+1,cs] for h in heads],axis=0)
        ctx_ref[0,cs,:]=(mixed.T+conv_ref[0,cs,:]).astype(BF)
def att_specs(D,T):
    seq=lambda s: pl.BlockSpec((1,)+s,lambda g,b:(b,)+(0,)*len(s))
    wsp=pl.BlockSpec((GW,D),lambda g,b:(g,0)); bsp=pl.BlockSpec((GW,1),lambda g,b:(g,0))
    rows=pl.BlockSpec((1,GW,T),lambda g,b:(b,g,0)); cols=pl.BlockSpec((1,T,GW),lambda g,b:(b,0,g))
    sq=lambda n: pl.BlockSpec((1,GH,n,LM,2*LM),lambda g,b:(b,g,0,0,0))
    turned=pl.BlockSpec((1,1,8,T),lambda g,b:(b,g,0,0))
    return seq,wsp,bsp,rows,cols,sq,turned
def att_fwd(x,mean,wq,wk,wv,vec,tok,ld,conv):
    B,T,D=x.shape; G=D//GW; H=D//HW
    seq,wsp,bsp,rows,cols,sq,turned=att_specs(D,T)
    sd=jax.ShapeDtypeStruct; big=sd((B,D,T),BF)
    return pl.pallas_call(att_fwd_kernel,grid=(G,B),
        in_specs=[seq((T,D)),seq((LM,D)),wsp,wsp,wsp,pl.BlockSpec((8,GW),lambda g,b:(0,g)),seq((1,T)),seq((LM,1)),seq((1,LM)),cols],
        out_specs=[rows]*5+[turned,sq(2*NEWTON),sq(4),cols],
        out_shape=[big]*5+[sd((B,G,8,T),F32),sd((B,H,2*NEWTON,LM,2*LM),F32),sd((B,H,4,LM,2*LM),F32),sd((B,T,D),BF)],
        scratch_shapes=[pltpu.VMEM((GW,T),BF)]*2+[pltpu.VMEM((GW,T),F32),pltpu.VMEM((LM,T),F32)],
        compiler_params=pltpu.CompilerParams(vmem_limit_bytes=60*2**20))(
            x,mean,wq,wk,wv,vec,tok[:,None,:],ld[:,:,None],ld[:,None,:],conv)
def att_bwd_kernel(x_ref,al_ref,wo_ref,q_ref,k_ref,v_ref,k1_ref,k3_ref,inv_ref,stash_ref,small_ref,tok_ref,conv_ref,
               dq_ref,dk_ref,dv_ref,gq_ref,gk_ref,gv_ref,sq_ref,sv_ref,
               g_ref,ds1_ref,ds3_ref,hot_ref):
    T=x_ref.shape[1]
    heads=range(GH); chunks=[slice(c,c+CHUNK) for c in range(0,T,CHUNK)]
    rows=[slice(h*HW,(h+1)*HW) for h in heads]
    scale=HW**-0.25
    for cs in chunks:
        member=lax.broadcasted_iota(jnp.int32,(LM,CHUNK),0)==tok_ref[0,:,cs]
        hot_ref[:,cs]=jnp.where(member,1.0,0.0).astype(BF)
    per=1.0/nt(jnp.ones((8,T),BF),hot_ref[...])[0:1]
    left=lambda i: [small_ref[0,h,i,:,:LM] for h in heads]
    right=lambda i: [small_ref[0,h,i,:,LM:] for h in heads]
    lq,lk,k2,zt,r,u=left(0),right(0),left(1),right(1),left(2),right(2)
    inv=[small_ref[0,h,3,:,:LM] for h in heads]
    ub=[a.astype(BF) for a in u]
    def upstream(cs):
        def go():
            a=nt(wo_ref[...],al_ref[0,cs,:])
            for h in heads: g_ref[rows[h],cs]=(a[rows[h]]*inv_ref[0,0,h:h+1,cs]).astype(BF)
        return go
    def first(h,cs):
        def go():
            k1=k1_ref[0,rows[h],cs].astype(F32)
            t=k1*nn(ub[h],g_ref[rows[h],cs])
            ds1_ref[rows[h],cs]=(t-k1*(jnp.sum(t,axis=0,keepdims=True)*inv_ref[0,0,h:h+1,cs])).astype(BF)
        return go
    for cs in chunks: upstream(cs)()
    du=[nt(k1_ref[0,rows[h]],g_ref[rows[h],:]) for h in heads]
    dr=[mm3(zt[h],du[h]) for h in heads]
    state={"dz":[mm3(du[h],r[h].T) for h in heads],"dk2":[None]*GH}
    drs=[(dr[h]*inv[h]) for h in heads]
    drb=[a.astype(BF) for a in drs]; drt=[a.T.astype(BF) for a in drs]
    delta=[jnp.sum(drb[h].astype(F32)*r[h],axis=1,keepdims=True) for h in heads]
    dlq=[None]*GH; dlk=[None]*GH
    def third(h,cs):
        def go():
            d=k3_ref[0,rows[h],cs].astype(F32)*(nn(drb[h],v_ref[0,rows[h],cs])-delta[h])
            ds3_ref[rows[h],cs]=d.astype(BF)
        return go
    def values(cs):
        def go():
            a=jnp.concatenate([nn(drt[h],k3_ref[0,rows[h],cs]) for h in heads],axis=0)
            dv_ref[0,:,cs]=(a+conv_ref[0,cs,:].T).astype(BF)
        return go
    def to_lk(h):
        def go(): dlk[h]=nt(ds1_ref[rows[h],:],q_ref[0,rows[h]])
        return go
    def to_lq(h):
        def go(): dlq[h]=nt(ds3_ref[rows[h],:],k_ref[0,rows[h]])
        return go
    @pl.when(pl.program_id(1)==0)
    def _():
        for ref in (gq_ref,gk_ref,gv_ref,sq_ref,sv_ref): ref[...]=jnp.zeros_like(ref)
    def value_weights():
        dv=dv_ref[0]
        gv_ref[...]+=nn(dv,x_ref[0]); sv_ref[...]+=jnp.sum(dv.astype(F32),axis=1,keepdims=True)
    side=[]
    for h in heads: side+=[third(h,cs) for cs in chunks]+[to_lq(h)]+[first(h,cs) for cs in chunks]+[to_lk(h)]
    side+=[values(cs) for cs in chunks]+[value_weights]
    k2t=[a.T for a in k2]; k2tw=[wide(a) for a in k2t]
    def newton(n):
        def one():
            a=[stash_ref[0,h,2*n] for h in heads]; c=[stash_ref[0,h,2*n+1] for h in heads]
            state["p"]=[m[:,:LM] for m in a]; state["b"]=[tall(m[:,LM:]) for m in a]
            state["c"]=[tall(m[:,:LM]) for m in c]; state["zt"]=[m[:,LM:] for m in c]
            state["gz"]=[0.25*d for d in state["dz"]]
            state["dc"]=[mm3(state["zt"][h],state["gz"][h]) for h in heads]
            state["pw"]=[wide(m) for m in state["p"]]
        def two(): state["db"]=[nn(state["pw"][h],tall(state["dc"][h])) for h in heads]
        def three():
            da=[nn(state["pw"][h],tall(state["db"][h])) for h in heads]
            state["dp"]=[mm3(state["db"][h],eye(7.0)-state["p"][h])-nn(wide(state["dc"][h]),state["b"][h])-da[h] for h in heads]
        def four():
            for h in heads:
                t=mm3(state["dp"][h],state["zt"][h])
                state["dk2"][h]=t if state["dk2"][h] is None else state["dk2"][h]+t
            state["dz"]=[nn(wide(state["gz"][h]),state["c"][h])+nn(k2tw[h],tall(state["dp"][h])) for h in heads]
        return [one,two,three,four]
    chain=[step for n in reversed(range(NEWTON)) for step in newton(n)]
    weave(chain,side)
    lhq=[];lhk=[]
    for h in heads:
        i2=1.0/jnp.sum(k2[h]*k2[h]); dz=state["dz"][h]
        d=state["dk2"][h]+i2*dz.T-k2[h]*(2.0*i2*i2*jnp.sum(dz*k2t[h]))
        d=k2[h]*(d-jnp.sum(k2[h]*d,axis=1,keepdims=True))
        dlqh=dlq[h]+mm3(d,lk[h]); dlkh=dlk[h]+mm3(d.T,lq[h])
        lhq.append(jnp.concatenate([lk[h].T,dlqh.T*per],axis=1).astype(BF))
        lhk.append(jnp.concatenate([lq[h].T,dlkh.T*per],axis=1).astype(BF))
    for cs in chunks:
        hot=hot_ref[:,cs]
        for lh,ds_ref,out_ref in ((lhq,ds1_ref,dq_ref),(lhk,ds3_ref,dk_ref)):
            for h in heads:
                a=nn(lh[h],jnp.concatenate([ds_ref[rows[h],cs],hot],axis=0))
                out_ref[0,rows[h],cs]=(a*scale).astype(BF)
    dq=dq_ref[0]
    gq_ref[...]+=nn(dq,x_ref[0]); gk_ref[...]+=nn(dk_ref[0],x_ref[0])
    sq_ref[...]+=jnp.sum(dq.astype(F32),axis=1,keepdims=True)
def att_bwd(x,al,wo,q,k,v,k1,k3,inv,stash,small,tok,conv,group):
    B,T,D=x.shape
    seq=lambda s: pl.BlockSpec((1,)+s,lambda g,b:(b,)+(0,)*len(s))
    rows=pl.BlockSpec((1,GW,T),lambda g,b:(b,group,0))
    sq=lambda n: pl.BlockSpec((1,GH,n,LM,2*LM),lambda g,b:(b,group,0,0,0))
    whole=lambda r,c: pl.BlockSpec((r,c),lambda g,b:(0,0))
    sd=jax.ShapeDtypeStruct
    return pl.pallas_call(att_bwd_kernel,grid=(1,B),
        in_specs=[seq((T,D)),seq((T,D)),pl.BlockSpec((GW,D),lambda g,b:(group,0))]+[rows]*5+[
            pl.BlockSpec((1,1,8,T),lambda g,b:(b,group,0,0)),sq(2*NEWTON),sq(4),seq((1,T)),seq((T,GW))],
        out_specs=[seq((GW,T))]*3+[whole(GW,D)]*3+[whole(GW,1)]*2,
        out_shape=[sd((B,GW,T),BF)]*3+[sd((GW,D),F32)]*3+[sd((GW,1),F32)]*2,
        scratch_shapes=[pltpu.VMEM((GW,T),BF)]*3+[pltpu.VMEM((LM,T),BF)],
        compiler_params=pltpu.CompilerParams(vmem_limit_bytes=60*2**20))(
            x,al,wo,q,k,v,k1,k3,inv,stash,small,tok[:,None,:],conv)

KW=33; HALF=16; DOCS=4; GAP=16
def spread(dst, get, bounds, length, step):
    total=length+GAP*(DOCS+1)
    ids=lax.broadcasted_iota(jnp.int32,(step,128),0)
    for p0 in range(0,total,step):
        size=min(step,total-p0)
        acc=None
        for d in range(DOCS):
            s0=p0-GAP*(d+1)
            lo=max(s0,0); hi=min(s0+size,length)
            if hi<=lo: continue
            row=ids[:hi-lo]+lo
            inside=(row>=bounds[d])&(row<bounds[d+1])
            part=jnp.where(inside,get(lo,hi-lo),0.0)
            pads=[]
            if lo>s0: pads.append(jnp.zeros((lo-s0,128),F32))
            pads.append(part)
            if s0+size>hi: pads.append(jnp.zeros((s0+size-hi,128),F32))
            part=jnp.concatenate(pads,0) if len(pads)>1 else part
            acc=part if acc is None else acc+part
        if acc is None: acc=jnp.zeros((size,128),F32)
        dst[HALF+p0:HALF+p0+size,:]=acc
def collect(src, bounds, lo, size):
    row=lax.broadcasted_iota(jnp.int32,(size,128),0)+lo
    acc=None
    for d in range(DOCS):
        part=src[lo+GAP*(d+1):lo+GAP*(d+1)+size,:]
        acc=part if acc is None else jnp.where(row>=bounds[d],part,acc)
    return acc
BLOCK=64
def taps(ref, base, weight, sign):
    acc=None
    for r in range(8):
        win=ref[pl.ds(base+r,BLOCK+32),:] if r==0 else ref[pl.ds(base+r,BLOCK+24),:]
        for a in range(5 if r==0 else 4):
            o=8*a+r
            t=weight(o if sign>0 else 2*HALF-o)*win[8*a:8*a+BLOCK]
            acc=t if acc is None else acc+t
    return acc

def conv_fwd_kernel(bounds_ref, x_ref, wv_ref, vec_ref, w_ref, v_ref, out_ref, pad_ref, res_ref):
    b=pl.program_id(0)
    bounds=[bounds_ref[b,d] for d in range(DOCS+1)]
    length=v_ref.shape[1]; total=length+GAP*(DOCS+1)
    pad_ref[0:HALF,:]=jnp.zeros((HALF,128),F32); pad_ref[HALF+total:,:]=jnp.zeros((pad_ref.shape[0]-HALF-total,128),F32)
    for lo in range(0,length,256):
        v_ref[0,lo:lo+256,:]=nt(x_ref[0,lo:lo+256,:],wv_ref[...])+vec_ref[1:2,:]
    spread(pad_ref, lambda lo,n: v_ref[0,lo:lo+n,:], bounds, length, BLOCK)
    def block(i,c):
        base=pl.multiple_of(i*BLOCK,BLOCK)
        res_ref[pl.ds(base,BLOCK),:]=taps(pad_ref, base, lambda s: w_ref[s:s+1,:], 1)
        return c
    lax.fori_loop(0,-(-total//BLOCK),block,0)
    for lo in range(0,length,BLOCK):
        out_ref[0,lo:lo+BLOCK,:]=collect(res_ref,bounds,lo,BLOCK)
def padded_rows(length):
    total=length+GAP*(DOCS+1)
    return -(-total//BLOCK)*BLOCK

def conv_fwd(bounds, x, w_v, vec, w):
    B,L,D=x.shape
    rows=padded_rows(L)
    slab=pl.BlockSpec((1,L,128),lambda b,c,_:(b,0,c)); big=jax.ShapeDtypeStruct((B,L,D),F32)
    return pl.pallas_call(conv_fwd_kernel,grid_spec=pltpu.PrefetchScalarGridSpec(num_scalar_prefetch=1,grid=(B,D//128),
        in_specs=[pl.BlockSpec((1,L,D),lambda b,c,_:(b,0,0)),pl.BlockSpec((128,D),lambda b,c,_:(c,0)),
            pl.BlockSpec((8,128),lambda b,c,_:(0,c)),pl.BlockSpec((KW,128),lambda b,c,_:(0,c))],
        out_specs=[slab,slab],
        scratch_shapes=[pltpu.VMEM((rows+2*HALF+8,128),F32),pltpu.VMEM((rows,128),F32)]),
        out_shape=[big,big],
        compiler_params=pltpu.CompilerParams(vmem_limit_bytes=60*2**20))(bounds,x,w_v,vec,w)
def conv_bwd_kernel(bounds_ref, v_ref, al_ref, wo_ref, w_ref, dv_ref, dw_ref, vpad_ref, gpad_ref, res_ref, acc_ref, g_ref):
    b=pl.program_id(1)
    bounds=[bounds_ref[b,d] for d in range(DOCS+1)]
    length=v_ref.shape[1]; total=length+GAP*(DOCS+1)
    for lo in range(0,length,256):
        g_ref[lo:lo+256,:]=nn(al_ref[0,lo:lo+256,:],wo_ref[...])
    for ref in (vpad_ref,gpad_ref):
        ref[0:HALF,:]=jnp.zeros((HALF,128),F32)
        ref[HALF+total:,:]=jnp.zeros((ref.shape[0]-HALF-total,128),F32)
    spread(vpad_ref, lambda lo,n: v_ref[0,lo:lo+n,:], bounds, length, BLOCK)
    spread(gpad_ref, lambda lo,n: g_ref[lo:lo+n,:], bounds, length, BLOCK)
    @pl.when(b==0)
    def _(): acc_ref[...]=jnp.zeros_like(acc_ref)
    def block(i,c):
        base=pl.multiple_of(i*BLOCK,BLOCK)
        here=vpad_ref[pl.ds(base+HALF,BLOCK),:]
        acc=None
        for r in range(8):
            n=5 if r==0 else 4
            win=gpad_ref[pl.ds(base+r,BLOCK+8*(n-1)),:]
            for a in range(n):
                s=2*HALF-(8*a+r)
                x=win[8*a:8*a+BLOCK]
                t=w_ref[s:s+1,:]*x
                acc=t if acc is None else acc+t
                p=(here*x).reshape(BLOCK//8,8,128)
                acc_ref[s]+=jnp.sum(p,axis=0)
        res_ref[pl.ds(base,BLOCK),:]=acc
        return c
    lax.fori_loop(0,-(-total//BLOCK),block,0)
    for lo in range(0,length,BLOCK):
        dv_ref[0,lo:lo+BLOCK,:]=collect(res_ref,bounds,lo,BLOCK)
    @pl.when(b==pl.num_programs(1)-1)
    def _():
        for s in range(KW):
            dw_ref[s:s+1,:]=jnp.sum(acc_ref[s],axis=0,keepdims=True)

def conv_bwd(bounds, v, al, w_o, w, group):
    B,L,D=v.shape
    rows=padded_rows(L); slabs=GW//128; at=group*slabs
    return pl.pallas_call(conv_bwd_kernel,grid_spec=pltpu.PrefetchScalarGridSpec(num_scalar_prefetch=1,grid=(slabs,B),
        in_specs=[pl.BlockSpec((1,L,128),lambda c,b,_:(b,0,at+c)),pl.BlockSpec((1,L,D),lambda c,b,_:(b,0,0)),
            pl.BlockSpec((D,128),lambda c,b,_:(0,at+c)),pl.BlockSpec((KW,128),lambda c,b,_:(0,at+c))],
        out_specs=[pl.BlockSpec((1,L,128),lambda c,b,_:(b,0,c)),pl.BlockSpec((KW,128),lambda c,b,_:(0,c))],
        scratch_shapes=[pltpu.VMEM((rows+2*HALF+8,128),F32)]*2+[pltpu.VMEM((rows,128),F32),pltpu.VMEM((KW,8,128),F32),pltpu.VMEM((L,128),F32)]),
        out_shape=[jax.ShapeDtypeStruct((B,L,GW),F32),jax.ShapeDtypeStruct((KW,GW),F32)],
        compiler_params=pltpu.CompilerParams(vmem_limit_bytes=60*2**20))(bounds,v,al,w_o,w)

def gelu_parts(x):
    size=jnp.abs(x)
    density=jnp.exp(-0.5*x*x)*0.3989422804014327
    t=1.0/(1.0+0.2316419*size)
    tail=density*(t*(0.319381530+t*(-0.356563782+t*(1.781477937+t*(-1.821255978+t*1.330274429)))))
    dist=jnp.where(x<0.0,tail,1.0-tail)
    return dist, x*density
def norm(v):
    mean=jnp.mean(v,axis=-1,keepdims=True); c=v-mean
    r=lax.rsqrt(jnp.mean(c*c,axis=-1,keepdims=True)+1e-5)
    return c*r, r
def norm_back(up,n,r,g):
    e=up*g
    return r*(e-jnp.mean(e,axis=-1,keepdims=True)-n*jnp.mean(e*n,axis=-1,keepdims=True))
def ffn_kernel(chunks, ctx_ref,x_ref,cot_ref,wo_ref,wu_ref,wd_ref,vec_ref,bu_ref,
               out_ref,normed_ref,hidden_ref,down_ref,up_ref,one_ref,att_ref,sums_ref,sumu_ref,slope_ref):
    width=wu_ref.shape[0]//chunks
    @pl.when(pl.program_id(0)==0)
    def _():
        sums_ref[...]=jnp.zeros_like(sums_ref); sumu_ref[...]=jnp.zeros_like(sumu_ref)
    v=lambda i: vec_ref[i:i+1,:]
    b_o,g1,s1,b_d,g2,s2=[v(i) for i in range(2,8)]
    n1,r1=norm(x_ref[...].astype(F32)+(nt(ctx_ref[...],wo_ref[...])+b_o))
    normed=n1*g1+s1
    low=normed.astype(BF); normed_ref[...]=low
    down=None
    for k in range(chunks):
        part=slice(k*width,(k+1)*width)
        pre=nt(low,wu_ref[part,:])+bu_ref[:,part]
        dist,slope=gelu_parts(pre)
        slope_ref[:,part]=dist+slope
        hid=(pre*dist).astype(BF); hidden_ref[:,part]=hid
        add=nt(hid,wd_ref[k]); down=add if down is None else down+add
    n2,r2=norm(normed+(down+b_d))
    out_ref[...]=(n2*g2+s2).astype(BF)
    cot=cot_ref[...].astype(F32)
    g_two=norm_back(cot,n2,r2,g2)
    low2=g_two.astype(BF); down_ref[...]=low2
    back=g_two
    for k in range(chunks):
        part=slice(k*width,(k+1)*width)
        hg=nn(low2,wd_ref[k])
        upl=(hg*slope_ref[:,part]).astype(BF); up_ref[:,part]=upl
        sumu_ref[:,part]+=jnp.sum(upl.astype(F32),axis=0,keepdims=True)
        back=back+nn(upl,wu_ref[part,:])
    g_one=norm_back(back,n1,r1,g1)
    one_ref[...]=g_one
    al=g_one.astype(BF); att_ref[...]=al
    s=lambda a: jnp.sum(a,axis=0,keepdims=True)
    sums_ref[...]+=jnp.concatenate([s(al.astype(F32)),s(back*n1),s(back),s(low2.astype(F32)),s(cot*n2),s(cot),jnp.zeros((2,n1.shape[1]),F32)],axis=0)
def ffn(ctx,x,cot,wo,wu,wd,vec,bu,block=512):
    chunks=wd.shape[0]
    T,D=x.shape; F=wu.shape[0]
    row=lambda w: pl.BlockSpec((block,w),lambda i:(i,0))
    full=lambda a: pl.BlockSpec(a.shape,lambda i:(0,)*a.ndim,pipeline_mode=pl.Buffered(1))
    keep=lambda r,w: pl.BlockSpec((r,w),lambda i:(0,0))
    sd=jax.ShapeDtypeStruct
    return pl.pallas_call(functools.partial(ffn_kernel,chunks),grid=(T//block,),
        in_specs=[row(D),row(D),row(D),full(wo),full(wu),full(wd),full(vec),full(bu)],
        out_specs=[row(D),row(D),row(F),row(D),row(F),row(D),row(D),keep(8,D),keep(1,F)],
        out_shape=[sd((T,D),BF),sd((T,D),BF),sd((T,F),BF),sd((T,D),BF),sd((T,F),BF),sd((T,D),F32),sd((T,D),BF),sd((8,D),F32),sd((1,F),F32)],
        scratch_shapes=[pltpu.VMEM((block,F),F32)],
        compiler_params=pltpu.CompilerParams(vmem_limit_bytes=60*2**20,dimension_semantics=("arbitrary",)),
    )(ctx,x,cot,wo,wu,wd,vec,bu)


def digits():
    found = []
    for axis in ("wide", "narrow"):
        stride = lax.axis_size(axis) // 2
        while stride >= 1:
            found.append((axis, stride))
            stride //= 2
    return found


def link_order(number):
    count = len(digits())
    if lax.axis_size("wide") == 8 and lax.axis_size("narrow") == 4:
        return [(4, 2, 3, 1, 0), (4, 3, 1, 2, 0), (4, 1, 2, 3, 0)][number]
    return tuple(range(count - 1, -1, -1))


def exchange(values, axis, stride):
    return lax.ppermute(values, axis, [(i, i ^ stride) for i in range(lax.axis_size(axis))])


def digit_of(axis, stride):
    return (lax.axis_index(axis) // stride) % 2


def gather_rows(shard, number):
    places = digits()
    held = shard.reshape((1,) * len(places) + shard.shape)
    for dim in link_order(number)[::-1]:
        mine = digit_of(*places[dim])
        got = exchange(held, *places[dim])
        first = jnp.where(mine == 0, held, got)
        second = jnp.where(mine == 0, got, held)
        held = jnp.concatenate([first, second], dim)
    return held.reshape((-1,) + shard.shape)


def scatter_start(whole):
    return whole.reshape((2,) * len(digits()) + whole.shape[1:])


def scatter_step(held, number, step):
    places = digits()
    dim = link_order(number)[step]
    mine = digit_of(*places[dim])
    keep = lax.dynamic_slice_in_dim(held, mine, 1, dim).astype(F32)
    send = lax.dynamic_slice_in_dim(held, 1 - mine, 1, dim).astype(BF)
    return keep + exchange(send, *places[dim]).astype(F32)


def scatter_rest(held, number, step):
    for later in range(step, len(digits())):
        held = scatter_step(held, number, later)
    return held.reshape(held.shape[-2:])


def pad_rows(flat, rows):
    count, length = flat.shape
    return jnp.pad(flat, ((0, 0), (0, rows * 768 - length))).reshape(count, rows, 768)


def across_rows(left_side, right_side):
    return lax.dot_general(left_side, right_side, (((0,), (0,)), ((), ())), preferred_element_type=F32)


def shards(
    inputs,
    tok_landmark,
    landmark_doc,
    w_query,
    b_query,
    w_key,
    w_value,
    b_value,
    conv_weight,
    w_out,
    b_out,
    gain_one,
    shift_one,
    w_up,
    b_up,
    w_down,
    b_down,
    gain_two,
    shift_two,
    cotangent,
):
    batch_rows, sequence_length, feature_width = inputs.shape
    group_count = lax.axis_size("wide") * lax.axis_size("narrow")
    own = feature_width // group_count
    tokens = batch_rows * sequence_length
    lines = b_up.shape[0] // own
    vectors = (b_query, b_value, b_out, gain_one, shift_one, b_down, gain_two, shift_two)
    flat = jnp.concatenate([conv_weight.reshape(-1)] + list(vectors) + [b_up])
    small = pad_rows(flat[None], -(-flat.shape[0] // 768))[0]
    gathered_v = gather_rows(jnp.concatenate([w_value.T, small], axis=0), 0)
    w_q = gather_rows(w_query.T, 1).reshape(feature_width, feature_width)
    w_k = gather_rows(w_key.T, 2).reshape(feature_width, feature_width)
    w_v = gathered_v[:, :own].reshape(feature_width, feature_width)
    small = gathered_v[:, own:].reshape(group_count, -1).astype(F32)[:, : flat.shape[0]]
    small = small.reshape(group_count, -1, own)
    b_u = small[:, KW + 8 :].reshape(1, -1)
    small = jnp.moveaxis(small[:, : KW + 8], 0, 1).reshape(KW + 8, feature_width)
    conv_taps, vec = small[:KW], small[KW:]
    ff_count = w_down.shape[0] // feature_width
    shard = jnp.concatenate(
        [w_out.T, w_up.T] + [w_down[i * feature_width : (i + 1) * feature_width].T for i in range(ff_count)]
    )
    gathered = lax.all_gather(shard, ("wide", "narrow"), axis=0)
    w_o = gathered[:, :own].reshape(feature_width, feature_width)
    w_u = gathered[:, own : own * (1 + lines)].reshape(-1, feature_width)
    w_d = jnp.moveaxis(
        gathered[:, own * (1 + lines) :].reshape(group_count, ff_count, own, feature_width), 0, 1
    ).reshape(ff_count, feature_width, feature_width)
    member = tok_landmark[:, None, :] == jnp.arange(LM)[None, :, None]
    means = jnp.einsum("bjt,bti->bji", member.astype(BF), inputs, preferred_element_type=F32)
    means = means / jnp.sum(member, axis=2)[..., None].astype(F32)
    doc = jnp.sum(jnp.where(member, landmark_doc[:, :, None], 0), axis=1)
    bounds = jnp.sum(doc[:, None, :] < jnp.arange(DOCS + 1)[None, :, None], axis=2).astype(jnp.int32)
    rows_low = inputs.reshape(tokens, feature_width)
    value_rows, conv_part = conv_fwd(bounds, inputs, w_v, vec, conv_taps)
    q, k, v, k1, k3, inv, stash, landmarks, context = att_fwd(
        inputs, means, w_q, w_k, w_v, vec, tok_landmark, landmark_doc, conv_part
    )
    context = context.reshape(tokens, feature_width)
    layer_out, normed, hidden, down_low, up_low, grad_one, att_low, sums, sums_up = ffn(
        context, rows_low, cotangent.reshape(tokens, feature_width), w_o, w_u, w_d, vec, b_u
    )

    def by_device(values):
        return values.reshape((group_count, -1) + values.shape[1:])

    early = jnp.concatenate([by_device(sums[i]) for i in range(6)] + [by_device(sums_up[0])], axis=1)
    grad_out = jnp.concatenate(
        [by_device(across_rows(att_low, context)), pad_rows(early, -(-early.shape[1] // 768))], axis=1
    )
    shares = [
        scatter_start(by_device(across_rows(up_low, normed))),
        scatter_start(by_device(across_rows(down_low, hidden))),
        scatter_start(grad_out),
    ]

    def advance(shares, step):
        return [scatter_step(share, i, step) for i, share in enumerate(shares)]

    shares = advance(shares, 0)
    w_plain = w_o.T
    att_low = att_low.reshape(inputs.shape)
    groups = feature_width // GW
    conv_grads, att_grads = [], []
    att_low, shares = lax.optimization_barrier((att_low, shares))
    for group in range(groups):
        moved = advance(shares, 1 + group)
        found = conv_bwd(bounds, value_rows, att_low, w_o, conv_taps, group)
        att_low, found, shares = lax.optimization_barrier((att_low, found, moved))
        conv_grads.append(found)
    for group in range(groups):
        moved = advance(shares, 1 + groups + group)
        found = att_bwd(
            inputs, att_low, w_plain, q, k, v, k1, k3, inv, stash, landmarks, tok_landmark,
            conv_grads[group][0], group,
        )
        att_low, found, shares = lax.optimization_barrier((att_low, found, moved))
        att_grads.append(found)
    share_up, share_down, share_out = [
        scatter_rest(share, i, 1 + 2 * groups) for i, share in enumerate(shares)
    ]
    grad_q, grad_k, grad_v, sum_q, sum_v = [
        jnp.concatenate([found[i] for found in att_grads]) for i in range(3, 8)
    ]
    taps_grad = jnp.concatenate([found[1] for found in conv_grads], axis=1)
    late = jnp.concatenate(
        [by_device(taps_grad.T).reshape(group_count, -1), by_device(sum_q[:, 0]), by_device(sum_v[:, 0])], axis=1
    )
    grad_v = jnp.concatenate([by_device(grad_v), pad_rows(late, -(-late.shape[1] // 768))], axis=1)
    share_v = scatter_rest(scatter_start(grad_v), 0, 0)
    share_q = scatter_rest(scatter_start(by_device(grad_q)), 1, 0)
    share_k = scatter_rest(scatter_start(by_device(grad_k)), 2, 0)
    input_grad = grad_one.reshape(inputs.shape)
    for group, found in enumerate(att_grads):
        for grad, weight in zip(found[:3], (w_q, w_k, w_v)):
            part = weight[group * GW : (group + 1) * GW]
            input_grad = input_grad + jnp.einsum("bot,oi->bti", grad, part, preferred_element_type=F32)
    early = share_out[own:].reshape(-1)
    late = share_v[own:].reshape(-1)
    return (
        layer_out.reshape(inputs.shape),
        input_grad,
        share_q.T,
        late[own * KW : own * KW + own],
        share_k.T,
        share_v[:own].T,
        late[own * KW + own : own * KW + 2 * own],
        late[: own * KW].reshape(own, KW).T,
        share_out[:own].T,
        early[:own],
        early[own : 2 * own],
        early[2 * own : 3 * own],
        share_up.T,
        early[6 * own : 6 * own + b_up.shape[0]],
        share_down.T,
        early[3 * own : 4 * own],
        early[4 * own : 5 * own],
        early[5 * own : 6 * own],
    )


def solution(mesh):
    return jax.shard_map(
        shards,
        mesh=mesh,
        in_specs=(
            P(("wide", "narrow"), None, None),
            P(("wide", "narrow"), None),
            P(("wide", "narrow"), None),
            P(None, ("wide", "narrow")),
            P(("wide", "narrow")),
            P(None, ("wide", "narrow")),
            P(None, ("wide", "narrow")),
            P(("wide", "narrow")),
            P(None, ("wide", "narrow")),
            P(None, ("wide", "narrow")),
            P(("wide", "narrow")),
            P(("wide", "narrow")),
            P(("wide", "narrow")),
            P(None, ("wide", "narrow")),
            P(("wide", "narrow")),
            P(None, ("wide", "narrow")),
            P(("wide", "narrow")),
            P(("wide", "narrow")),
            P(("wide", "narrow")),
            P(("wide", "narrow"), None, None),
        ),
        out_specs=(
            P(("wide", "narrow"), None, None),
            P(("wide", "narrow"), None, None),
            P(None, ("wide", "narrow")),
            P(("wide", "narrow")),
            P(None, ("wide", "narrow")),
            P(None, ("wide", "narrow")),
            P(("wide", "narrow")),
            P(None, ("wide", "narrow")),
            P(None, ("wide", "narrow")),
            P(("wide", "narrow")),
            P(("wide", "narrow")),
            P(("wide", "narrow")),
            P(None, ("wide", "narrow")),
            P(("wide", "narrow")),
            P(None, ("wide", "narrow")),
            P(("wide", "narrow")),
            P(("wide", "narrow")),
            P(("wide", "narrow")),
        ),
        check_vma=False,
    )
```

time: 648 us -> 608 us (0.938)
  waiting for transfers between devices: 100 us -> 47.5 us
  Pallas kernels: 299 us -> 269 us
  matrix products: 54.7 us -> 73.5 us
  local copies, waits for them, and re-layouts: 80.4 us -> 95.8 us
    all_gather x3 -> x1, waiting for transfers between devices: 51.3 us -> 0.02 us  [shards(): gathered = lax.all_gather(shard, ('wide', 'narrow'), axis=0)]
    pallas_call x2 -> x3, Pallas kernels: 149 us -> 108 us  [the longest x2 65 us: att_bwd(): pl.pallas_call(att_bwd_kernel, grid=(1, B), in_specs=[seq((T, D)), seq((T...]
    dot_general x5 -> x7, matrix products: 23.9 us -> 42.5 us  [the longest x6 39.3 us: shards(): jnp.einsum('bot,oi->bti', grad, part, preferred_element_type=F32)]
    slice x3 -> x11, local copies, waits for them, and re-layouts: 1.38 us -> 16.3 us  [the longest x1 6.57 us: shards(): gathered[:, own * (1 + lines):]]
    add x2 -> x0, local copies, waits for them, and re-layouts: 6.77 us -> none  [shards(): value_rows = (nt(rows_low, w_v) + b_v).reshape(inputs.shape)]
    pallas_call x1 -> x2, Pallas kernels: 45.3 us -> 51.7 us  [conv_bwd(): pl.pallas_call(conv_bwd_kernel, grid_spec=pltpu.PrefetchScalarGridSpec(nu...]
    add x26 -> x28, other arithmetic: 28.4 us -> 34.1 us  [scatter_step(): return keep + exchange(send, *places[dim]).astype(F32)]
    unnamed x86 -> x119, local copies, waits for them, and re-layouts: 25.7 us -> 20.8 us
  transfers between devices with their start and end apart: 48 -> 46, of which waited for: 17 -> 15; matrix products, arithmetic and copies ran while one was open for 19% -> 25% of each run, Pallas kernels for 35% -> 32%
where the time goes in v3:
time: 608 us; the launch traced here: 601 us
  Pallas kernels  269 us (44%)
  local copies, waits for them, and re-layouts  95.8 us (16%)
  matrix products  73.5 us (12%)
  other arithmetic  51.1 us (8%)
  starting transfers between devices  49 us (8%)
  waiting for transfers between devices  47.5 us (8%)
  between operations  15.9 us (3%)
    pallas_call x1, Pallas kernels, ffn(): pl.pallas_call(functools.partial(ffn_kernel, chunks), grid=(T // block,),...  74 us
    pallas_call x2, Pallas kernels, att_bwd(): pl.pallas_call(att_bwd_kernel, grid=(1, B), in_specs=[seq((T, D)), seq((T...  65 us
    pallas_call x2, Pallas kernels, conv_bwd(): pl.pallas_call(conv_bwd_kernel, grid_spec=pltpu.PrefetchScalarGridSpec(nu...  51.7 us
    ppermute x45, starting transfers between devices, exchange(): lax.ppermute(values, axis, [(i, i ^ stride) for i in range(lax.axis_size(...  48.9 us
    ppermute x45, waiting for transfers between devices, exchange(): lax.ppermute(values, axis, [(i, i ^ stride) for i in range(lax.axis_size(...  47.4 us
    pallas_call x1, Pallas kernels, att_fwd(): pl.pallas_call(att_fwd_kernel, grid=(G, B), in_specs=[seq((T, D)), seq((L...  42.7 us
    dot_general x6, matrix products, shards(): jnp.einsum('bot,oi->bti', grad, part, preferred_element_type=F32)  39.3 us
    pallas_call x1, Pallas kernels, conv_fwd(): pl.pallas_call(conv_fwd_kernel, grid_spec=pltpu.PrefetchScalarGridSpec(nu...  35.1 us
  transfers between devices with their start and end apart: 46, of which 15 were waited for; matrix products, arithmetic and copies ran while one was open for 25% of the time, Pallas kernels for 32%

profile of v3, /device:TPU:0, one launch (start us, length us, event | category | flops | bytes accessed | tf_op | source)
XLA Modules:
  0.0 601.3 jit_solution(12353400280668776579)
XLA Ops:
  13.7 6.1 %concatenate.102 = bf16[1080]{0:T(1024)(128)(2,1)S(1)} concatenate(bf16[792]{0:T(1024)(128)(2,1)S(1)} %reshape.164, bf16[24]{0:T(256)(128)(2,1)} %param.24, bf16[24]{0:T(256)(128)(2,1)} %param.27, bf16[24]{0:T(256)(128)(2,1)} %param.30, bf16[24]{0:T(256)(128)(2,1)} %param.31, bf16[24]{0:T(256)(128)(2,1)} %param.32, bf16[24]{0:T(256)(128)(2,1)} %param.36, bf16[24]{0:T(256)(128)(2,1)} %param.37, ...), dimensions={0} | concatenate | bytes 4320 | tf_op jit(solution)/shard_map/concatenate | solution.py:540
  49.4 5.7 collective-permute-done.12
  55.2 5.8 collective-permute-done.8
  80.6 35.1 %shard_map.331 = (f32[2,1024,768]{2,1,0:T(8,128)}, f32[2,1024,768]{2,1,0:T(8,128)}) custom-call(s32[2,5]{1,0:T(2,128)} %copy.227.bounds_ref, bf16[2,1024,768]{2,1,0:T(8,128)(2,1)} %x_ref.7, bf16[768,768]{1,0:T(8,128)(2,1)} %bitcast.161, f32[8,768]{1,0:T(8,128)} %slice.186.vec_ref, f32[33,768]{1,0:T(8,128)} %slice.188.w_ref), custom_call_target="tpu_custom_call" | custom-call | tf_op jit(solution)/shard_map/pallas_call | solution.py:326
  115.7 42.7 %shard_map.332 = (bf16[2,768,1024]{2,1,0:T(8,128)(2,1)}, bf16[2,768,1024]{2,1,0:T(8,128)(2,1)}, bf16[2,768,1024]{2,1,0:T(8,128)(2,1)}, bf16[2,768,1024]{2,1,0:T(...) custom-call(bf16[2,1024,768]{2,1,0:T(8,128)(2,1)} %x_ref.7, ...), custom_call_target="tpu_custom_call" | custom-call | tf_op jit(solution)/shard_map/pallas_call | solution.py:142
  160.8 6.6 %fusion.6 = (bf16[32,96,768]{2,1,0:T(8,128)(2,1)S(1)}, bf16[32,96,768]{2,1,0:T(8,128)(2,1)}) fusion(bf16[32,216,768]{2,1,0:T(8,128)(2,1)} %bitcast.164), kind=kLoop, calls=%fused_computation.164 | loop fusion | bytes 18874368 | tf_op jit(solution)/shard_map/slice | solution.py:559
  169.8 74.0 %shard_map.333 = (bf16[2048,768]{1,0:T(8,128)(2,1)}, bf16[2048,768]{1,0:T(8,128)(2,1)}, bf16[2048,3072]{1,0:T(8,128)(2,1)}, bf16[2048,768]{1,0:T(8,128)(2,1)}, b...) custom-call(bf16[2048,768]{1,0:T(8,128)(2,1)} %bitcast.182, ...), custom_call_target="tpu_custom_call" | custom-call | tf_op jit(solution)/shard_map/pallas_call | solution.py:438
  247.5 4.7 copy.231
  252.2 14.1 %fusion.10 = f32[768,3072]{1,0:T(8,128)S(1)} fusion(bf16[2048,768]{1,0:T(8,128)(2,1)} %get-tuple-element.104, bf16[2048,3072]{1,0:T(8,128)(2,1)} %get-tuple-element.105), kind=kOutput, calls=%fused_computation.168 | convolution fusion | flops 9663676416 | bytes 25165824 | tf_op jit(solution)/shard_map/dot_general | solution.py:509
  270.6 14.1 %fusion.9 = f32[3072,768]{1,0:T(8,128)S(1)} fusion(bf16[2048,3072]{1,0:T(8,128)(2,1)} %get-tuple-element.102, bf16[2048,768]{1,0:T(8,128)(2,1)S(1)} %copy-done.51), kind=kOutput, calls=%fused_computation.167 | convolution fusion | flops 9663676416 | bytes 25165824 | tf_op jit(solution)/shard_map/dot_general | solution.py:509
  309.3 4.6 convert_add_fusion.1
  325.6 25.6 %shard_map.334 = (f32[2,1024,384]{2,1,0:T(8,128)}, f32[33,384]{1,0:T(8,128)}) custom-call(s32[2,5]{1,0:T(2,128)} %copy.227.bounds_ref, f32[2,1024,768]{2,1,0:T(8,128)} %get-tuple-element.109.v_ref, bf16[2,1024,768]{2,1,0:T(8,128)(2,1)} %bitcast.145, bf16[768,768]{1,0:T(8,128)(2,1)} %bitcast.151, f32[33,768]{1,0:T(8,128)} %slice.188.w_ref), custom_call_target="tpu_custom_call" | custom-call | tf_op jit(solution)/shard_map/pallas_call | solution.py:373
  355.1 4.6 convert_add_fusion.3
  368.6 26.1 %shard_map.335 = (f32[2,1024,384]{2,1,0:T(8,128)}, f32[33,384]{1,0:T(8,128)}) custom-call(s32[2,5]{1,0:T(2,128)} %copy.227.bounds_ref, f32[2,1024,768]{2,1,0:T(8,128)} %get-tuple-element.109.v_ref, bf16[2,1024,768]{2,1,0:T(8,128)(2,1)} %bitcast.146, bf16[768,768]{1,0:T(8,128)(2,1)} %bitcast.152, f32[33,768]{1,0:T(8,128)} %slice.188.w_ref), custom_call_target="tpu_custom_call" | custom-call | tf_op jit(solution)/shard_map/pallas_call | solution.py:373
  404.4 32.6 %shard_map.336 = (bf16[2,384,1024]{2,1,0:T(8,128)(2,1)}, bf16[2,384,1024]{2,1,0:T(8,128)(2,1)}, bf16[2,384,1024]{2,1,0:T(8,128)(2,1)}, f32[384,768]{1,0:T(8,128)...) custom-call(bf16[2,1024,768]{2,1,0:T(8,128)(2,1)} %x_ref.7, ...), custom_call_target="tpu_custom_call" | custom-call | tf_op jit(solution)/shard_map/pallas_call | solution.py:254
  440.8 5.5 collective-permute-start.29
  449.3 4.6 fusion.13
  453.9 4.5 fusion.14
  458.4 4.4 fusion.12
  463.6 32.4 %shard_map.337 = (bf16[2,384,1024]{2,1,0:T(8,128)(2,1)}, bf16[2,384,1024]{2,1,0:T(8,128)(2,1)}, bf16[2,384,1024]{2,1,0:T(8,128)(2,1)}, f32[384,768]{1,0:T(8,128)...) custom-call(bf16[2,1024,768]{2,1,0:T(8,128)(2,1)} %x_ref.7, ...), custom_call_target="tpu_custom_call" | custom-call | tf_op jit(solution)/shard_map/pallas_call | solution.py:254
  517.4 4.5 fusion.15
  521.9 4.5 fusion.16
  526.5 16.7 %add_add_fusion = f32[2,1024,768]{2,1,0:T(8,128)} fusion(f32[2,1024,768]{2,1,0:T(8,128)} %fusion.16, f32[2,1024,768]{2,1,0:T(8,128)} %fusion.15, f32[2,1024,768]{2,1,0:T(8,128)} %fusion.14, f32[2,1024,768]{2,1,0:T(8,128)S(1)} %bitcast.155, f32[2,1024,768]{2,1,0:T(8,128)} %bitcast.173, f32[2,1024,768]{2,1,0:T(8,128)} %fusion.12, ...), kind=kOutput, calls=%fused_computation | convolution fusion | flops 1217396736 | bytes 46202880 | tf_op jit(solution)/shard_map/bot,oi->bti/dot_general | solution.py:629
  568.5 8.6 %collective-permute-done.43 = bf16[2,1,1,1,1,24,768]{6,5,4,3,2,1,0:T(8,128)(2,1)S(1)} collective-permute-done((bf16[2,1,1,1,1,24,768]{6,5,4,3,2,1,0:T(8,128)(2,1)S(1)}, bf16[2,1,1,1,1,24,768]{6,5,4,3,2,1,0:T(8,128)(2,1)S(1)}, u32[]{:S(2)}, u32[]{:S(2)}) %collective-permute-start.43) | collective-permute-done | bytes 73760 | tf_op jit(solution)/shard_map/ppermute | solution.py:465
  (370 shorter events, 197.3 us)
Async XLA Ops:
  7.2 151.2 %all-gather.3.cloned.1.call-start = ((), (), s32[]{:S(2)}) async-start(), calls=%async_computation | async-start | bytes 10948608 | tf_op jit(solution)/shard_map/all_gather | solution.py:555
  20.7 17.6 %collective-permute-start.10 = (bf16[1,1,1,1,1,26,768]{6,5,4,3,2,1,0:T(8,128)(2,1)S(1)}, bf16[1,1,1,1,1,26,768]{6,5,4,3,2,1,0:T(8,128)(2,1)S(1)}, u32[]{:S(2)}, u32[]{:S(2)}) collective-permute-start(bf16[1,1,1,1,1,26,768]{6,5,4,3,2,1,0:T(8,128)(2,1)S(1)} %maximum_bitcast_fusion.1), channel_id=1, source_target_pairs={{0,16},{4,20},{8,24},{12,28},{16,0},{20,4},{24,8},{28,12},{1,17},{... | collective-permute-start | bytes 119816 | tf_op jit(solution)/shard_map/ppermute | solution.py:465
  43.7 11.3 %collective-permute-start.12 = (bf16[2,2,1,1,1,26,768]{6,5,4,3,2,1,0:T(8,128)(2,1)S(1)}, bf16[2,2,1,1,1,26,768]{6,5,4,3,2,1,0:T(8,128)(2,1)S(1)}, u32[]{:S(2)}, u32[]{:S(2)}) collective-permute-start(bf16[2,2,1,1,1,26,768]{6,5,4,3,2,1,0:T(8,128)(2,1)S(1)} %pad_maximum_fusion.12), channel_id=1, source_target_pairs={{0,2},{1,3},{2,0},{3,1},{4,6},{5,7},{6,4},{7,5},{8,10},{9,11},{10,... | collective-permute-start | bytes 479240 | tf_op jit(solution)/shard_map/ppermute | solution.py:465
  45.1 15.9 %collective-permute-start.8 = (bf16[2,1,2,2,1,24,768]{6,5,4,3,2,1,0:T(8,128)(2,1)S(1)}, bf16[2,1,2,2,1,24,768]{6,5,4,3,2,1,0:T(8,128)(2,1)S(1)}, u32[]{:S(2)}, u32[]{:S(2)}) collective-permute-start(bf16[2,1,2,2,1,24,768]{6,5,4,3,2,1,0:T(8,128)(2,1)S(1)} %pad_maximum_fusion.11), channel_id=1, source_target_pairs={{0,8},{4,12},{8,0},{12,4},{16,24},{20,28},{24,16},{28,20},{1,9},{5... | collective-permute-start | bytes 884744 | tf_op jit(solution)/shard_map/ppermute | solution.py:465
  47.8 13.4 %collective-permute-start.3 = (bf16[2,2,2,1,1,24,768]{6,5,4,3,2,1,0:T(8,128)(2,1)S(1)}, bf16[2,2,2,1,1,24,768]{6,5,4,3,2,1,0:T(8,128)(2,1)S(1)}, u32[]{:S(2)}, u32[]{:S(2)}) collective-permute-start(bf16[2,2,2,1,1,24,768]{6,5,4,3,2,1,0:T(8,128)(2,1)S(1)} %pad_maximum_fusion.10), channel_id=1, source_target_pairs={{0,2},{1,3},{2,0},{3,1},{4,6},{5,7},{6,4},{7,5},{8,10},{9,11},{10,... | collective-permute-start | bytes 884744 | tf_op jit(solution)/shard_map/ppermute | solution.py:465
  55.2 10.8 %collective-permute-start.13 = (bf16[2,2,1,2,1,26,768]{6,5,4,3,2,1,0:T(8,128)(2,1)S(1)}, bf16[2,2,1,2,1,26,768]{6,5,4,3,2,1,0:T(8,128)(2,1)S(1)}, u32[]{:S(2)}, u32[]{:S(2)}) collective-permute-start(bf16[2,2,1,2,1,26,768]{6,5,4,3,2,1,0:T(8,128)(2,1)S(1)} %pad_maximum_fusion.9), channel_id=1, source_target_pairs={{0,4},{4,0},{8,12},{12,8},{16,20},{20,16},{24,28},{28,24},{1,5},{5... | collective-permute-start | bytes 958472 | tf_op jit(solution)/shard_map/ppermute | solution.py:465
  268.1 33.8 %collective-permute-start.16 = (bf16[2,2,2,2,1,24,3072]{6,5,4,3,2,1,0:T(8,128)(2,1)}, bf16[2,2,2,2,1,24,3072]{6,5,4,3,2,1,0:T(8,128)(2,1)}, u32[]{:S(2)}, u32[]{:S(2)}) collective-permute-start(bf16[2,2,2,2,1,24,3072]{6,5,4,3,2,1,0:T(8,128)(2,1)} %dynamic-slice_convert_fusion), channel_id=1, source_target_pairs={{0,1},{1,0},{2,3},{3,2},{4,5},{5,4},{6,7},{7,6},{8,9},{9,8},{10,11... | collective-permute-start | bytes 7077896 | tf_op jit(solution)/shard_map/ppermute | solution.py:465
  286.4 19.3 %collective-permute-start.15 = (bf16[2,2,2,2,1,96,768]{6,5,4,3,2,1,0:T(8,128)(2,1)}, bf16[2,2,2,2,1,96,768]{6,5,4,3,2,1,0:T(8,128)(2,1)}, u32[]{:S(2)}, u32[]{:S(2)}) collective-permute-start(bf16[2,2,2,2,1,96,768]{6,5,4,3,2,1,0:T(8,128)(2,1)} %dynamic-slice_convert_fusion.1), channel_id=1, source_target_pairs={{0,1},{1,0},{2,3},{3,2},{4,5},{5,4},{6,7},{7,6},{8,9},{9,8},{10,11... | collective-permute-start | bytes 7077896 | tf_op jit(solution)/shard_map/ppermute | solution.py:465
  315.1 37.5 %collective-permute-start.19 = (bf16[2,2,2,1,1,24,3072]{6,5,4,3,2,1,0:T(8,128)(2,1)}, bf16[2,2,2,1,1,24,3072]{6,5,4,3,2,1,0:T(8,128)(2,1)}, u32[]{:S(2)}, u32[]{:S(2)}) collective-permute-start(bf16[2,2,2,1,1,24,3072]{6,5,4,3,2,1,0:T(8,128)(2,1)} %dynamic-slice_convert_fusion.2), channel_id=1, source_target_pairs={{0,2},{1,3},{2,0},{3,1},{4,6},{5,7},{6,4},{7,5},{8,10},{9,11},{10,... | collective-permute-start | bytes 3538952 | tf_op jit(solution)/shard_map/ppermute | solution.py:465
  318.6 32.7 %collective-permute-start.20 = (bf16[2,1,2,2,1,25,768]{6,3,5,4,2,1,0:T(2,128)(2,1)}, bf16[2,1,2,2,1,25,768]{6,3,5,4,2,1,0:T(2,128)(2,1)}, u32[]{:S(2)}, u32[]{:S(2)}) collective-permute-start(bf16[2,1,2,2,1,25,768]{6,3,5,4,2,1,0:T(2,128)(2,1)} %dynamic-slice_convert_fusion.11), channel_id=1, source_target_pairs={{0,8},{4,12},{8,0},{12,4},{16,24},{20,28},{24,16},{28,20},{1,9},{5... | collective-permute-start | bytes 921608 | tf_op jit(solution)/shard_map/ppermute | solution.py:465
  322.8 32.3 %collective-permute-start.18 = (bf16[2,2,1,2,1,96,768]{6,5,4,3,2,1,0:T(8,128)(2,1)}, bf16[2,2,1,2,1,96,768]{6,5,4,3,2,1,0:T(8,128)(2,1)}, u32[]{:S(2)}, u32[]{:S(2)}) collective-permute-start(bf16[2,2,1,2,1,96,768]{6,5,4,3,2,1,0:T(8,128)(2,1)} %dynamic-slice_convert_fusion.3), channel_id=1, source_target_pairs={{0,4},{4,0},{8,12},{12,8},{16,20},{20,16},{24,28},{28,24},{1,5},{5... | collective-permute-start | bytes 3538952 | tf_op jit(solution)/shard_map/ppermute | solution.py:465
  360.5 34.2 %collective-permute-start.23 = (bf16[2,1,1,2,1,25,768]{6,3,5,4,2,1,0:T(2,128)(2,1)}, bf16[2,1,1,2,1,25,768]{6,3,5,4,2,1,0:T(2,128)(2,1)S(1)}, u32[]{:S(2)}, u32[]{:S(2)}) collective-permute-start(bf16[2,1,1,2,1,25,768]{6,3,5,4,2,1,0:T(2,128)(2,1)} %dynamic-slice_convert_fusion.17), channel_id=1, source_target_pairs={{0,4},{4,0},{8,12},{12,8},{16,20},{20,16},{24,28},{28,24},{1,5},{5... | collective-permute-start | bytes 460808 | tf_op jit(solution)/shard_map/ppermute | solution.py:465
  362.8 32.1 %collective-permute-start.22 = (bf16[2,1,2,1,1,24,3072]{6,5,4,3,2,1,0:T(8,128)(2,1)}, bf16[2,1,2,1,1,24,3072]{6,5,4,3,2,1,0:T(8,128)(2,1)}, u32[]{:S(2)}, u32[]{:S(2)}) collective-permute-start(bf16[2,1,2,1,1,24,3072]{6,5,4,3,2,1,0:T(8,128)(2,1)} %dynamic-slice_convert_fusion.8), channel_id=1, source_target_pairs={{0,8},{4,12},{8,0},{12,4},{16,24},{20,28},{24,16},{28,20},{1,9},{5... | collective-permute-start | bytes 1769480 | tf_op jit(solution)/shard_map/ppermute | solution.py:465
  368.0 28.3 %collective-permute-start.21 = (bf16[2,2,1,1,1,96,768]{6,5,4,3,2,1,0:T(8,128)(2,1)}, bf16[2,2,1,1,1,96,768]{6,5,4,3,2,1,0:T(8,128)(2,1)}, u32[]{:S(2)}, u32[]{:S(2)}) collective-permute-start(bf16[2,2,1,1,1,96,768]{6,5,4,3,2,1,0:T(8,128)(2,1)} %dynamic-slice_convert_fusion.9), channel_id=1, source_target_pairs={{0,2},{1,3},{2,0},{3,1},{4,6},{5,7},{6,4},{7,5},{8,10},{9,11},{10,... | collective-permute-start | bytes 1769480 | tf_op jit(solution)/shard_map/ppermute | solution.py:465
  398.6 38.4 %collective-permute-start.26 = (bf16[2,1,1,1,1,25,768]{6,3,5,4,2,1,0:T(2,128)(2,1)}, bf16[2,1,1,1,1,25,768]{6,3,5,4,2,1,0:T(2,128)(2,1)}, u32[]{:S(2)}, u32[]{:S(2)}) collective-permute-start(bf16[2,1,1,1,1,25,768]{6,3,5,4,2,1,0:T(2,128)(2,1)} %dynamic-slice_convert_fusion.23), channel_id=1, source_target_pairs={{0,2},{1,3},{2,0},{3,1},{4,6},{5,7},{6,4},{7,5},{8,10},{9,11},{10,... | collective-permute-start | bytes 230408 | tf_op jit(solution)/shard_map/ppermute | solution.py:465
  400.7 37.6 %collective-permute-start.25 = (bf16[2,1,1,1,1,24,3072]{6,5,4,3,2,1,0:T(8,128)(2,1)}, bf16[2,1,1,1,1,24,3072]{6,5,4,3,2,1,0:T(8,128)(2,1)}, u32[]{:S(2)}, u32[]{:S(2)}) collective-permute-start(bf16[2,1,1,1,1,24,3072]{6,5,4,3,2,1,0:T(8,128)(2,1)} %dynamic-slice_convert_fusion.14), channel_id=1, source_target_pairs={{0,4},{4,0},{8,12},{12,8},{16,20},{20,16},{24,28},{28,24},{1,5},{5... | collective-permute-start | bytes 884744 | tf_op jit(solution)/shard_map/ppermute | solution.py:465
  401.9 37.6 %collective-permute-start.24 = (bf16[2,1,1,1,1,96,768]{6,5,4,3,2,1,0:T(8,128)(2,1)}, bf16[2,1,1,1,1,96,768]{6,5,4,3,2,1,0:T(8,128)(2,1)}, u32[]{:S(2)}, u32[]{:S(2)}) collective-permute-start(bf16[2,1,1,1,1,96,768]{6,5,4,3,2,1,0:T(8,128)(2,1)} %dynamic-slice_convert_fusion.15), channel_id=1, source_target_pairs={{0,8},{4,12},{8,0},{12,4},{16,24},{20,28},{24,16},{28,20},{1,9},{5... | collective-permute-start | bytes 884744 | tf_op jit(solution)/shard_map/ppermute | solution.py:465
  440.8 55.3 %collective-permute-start.29 = (bf16[1,1,1,1,1,25,768]{6,3,5,4,2,1,0:T(2,128)(2,1)S(1)}, bf16[1,1,1,1,1,25,768]{6,3,5,4,2,1,0:T(2,128)(2,1)S(1)}, u32[]{:S(2)}, u32[]{:S(2)}) collective-permute-start(bf16[1,1,1,1,1,25,768]{6,3,5,4,2,1,0:T(2,128)(2,1)S(1)} %dynamic-slice_convert_fusion.27), channel_id=1, source_target_pairs={{0,16},{4,20},{8,24},{12,28},{16,0},{20,4},{24,8},{28,12},{1,17},{... | collective-permute-start | bytes 115208 | tf_op jit(solution)/shard_map/ppermute | solution.py:465
  446.2 50.5 %collective-permute-start.28 = (bf16[1,1,1,1,1,24,3072]{6,5,4,3,2,1,0:T(8,128)(2,1)S(1)}, bf16[1,1,1,1,1,24,3072]{6,5,4,3,2,1,0:T(8,128)(2,1)S(1)}, u32[]{:S(2)}, u32[]{:S(2)}) collective-permute-start(bf16[1,1,1,1,1,24,3072]{6,5,4,3,2,1,0:T(8,128)(2,1)S(1)} %dynamic-slice_convert_fusion.20), channel_id=1, source_target_pairs={{0,16},{4,20},{8,24},{12,28},{16,0},{20,4},{24,8},{28,12},{1,17},{... | collective-permute-start | bytes 442376 | tf_op jit(solution)/shard_map/ppermute | solution.py:465
  446.3 51.2 %collective-permute-start.27 = (bf16[1,1,1,1,1,96,768]{6,5,4,3,2,1,0:T(8,128)(2,1)S(1)}, bf16[1,1,1,1,1,96,768]{6,5,4,3,2,1,0:T(8,128)(2,1)S(1)}, u32[]{:S(2)}, u32[]{:S(2)}) collective-permute-start(bf16[1,1,1,1,1,96,768]{6,5,4,3,2,1,0:T(8,128)(2,1)S(1)} %dynamic-slice_convert_fusion.21), channel_id=1, source_target_pairs={{0,16},{4,20},{8,24},{12,28},{16,0},{20,4},{24,8},{28,12},{1,17},{... | collective-permute-start | bytes 442376 | tf_op jit(solution)/shard_map/ppermute | solution.py:465
  500.6 46.9 %collective-permute-start.40 = (bf16[2,2,2,2,1,24,768]{6,5,4,3,2,1,0:T(8,128)(2,1)}, bf16[2,2,2,2,1,24,768]{6,5,4,3,2,1,0:T(8,128)(2,1)}, u32[]{:S(2)}, u32[]{:S(2)}) collective-permute-start(bf16[2,2,2,2,1,24,768]{6,5,4,3,2,1,0:T(8,128)(2,1)} %dynamic-slice_convert_fusion.6), channel_id=1, source_target_pairs={{0,1},{1,0},{2,3},{3,2},{4,5},{5,4},{6,7},{7,6},{8,9},{9,8},{10,11... | collective-permute-start | bytes 1769480 | tf_op jit(solution)/shard_map/ppermute | solution.py:465
  515.8 36.5 %collective-permute-start.35 = (bf16[2,2,2,2,1,26,768]{6,3,5,4,2,1,0:T(2,128)(2,1)}, bf16[2,2,2,2,1,26,768]{6,3,5,4,2,1,0:T(2,128)(2,1)}, u32[]{:S(2)}, u32[]{:S(2)}) collective-permute-start(bf16[2,2,2,2,1,26,768]{6,3,5,4,2,1,0:T(2,128)(2,1)} %dynamic-slice_convert_fusion.4), channel_id=1, source_target_pairs={{0,1},{1,0},{2,3},{3,2},{4,5},{5,4},{6,7},{7,6},{8,9},{9,8},{10,11... | collective-permute-start | bytes 1916936 | tf_op jit(solution)/shard_map/ppermute | solution.py:465
  516.6 32.4 %collective-permute-start.30 = (bf16[2,2,2,2,1,24,768]{6,5,4,3,2,1,0:T(8,128)(2,1)S(1)}, bf16[2,2,2,2,1,24,768]{6,5,4,3,2,1,0:T(8,128)(2,1)}, u32[]{:S(2)}, u32[]{:S(2)}) collective-permute-start(bf16[2,2,2,2,1,24,768]{6,5,4,3,2,1,0:T(8,128)(2,1)S(1)} %dynamic-slice_convert_fusion.7), channel_id=1, source_target_pairs={{0,1},{1,0},{2,3},{3,2},{4,5},{5,4},{6,7},{7,6},{8,9},{9,8},{10,11... | collective-permute-start | bytes 1769480 | tf_op jit(solution)/shard_map/ppermute | solution.py:465
  565.7 14.6 %collective-permute-start.37 = (bf16[2,2,1,1,1,26,768]{6,3,5,4,2,1,0:T(2,128)(2,1)S(1)}, bf16[2,2,1,1,1,26,768]{6,3,5,4,2,1,0:T(2,128)(2,1)S(1)}, u32[]{:S(2)}, u32[]{:S(2)}) collective-permute-start(bf16[2,2,1,1,1,26,768]{6,3,5,4,2,1,0:T(2,128)(2,1)S(1)} %dynamic-slice_convert_fusion.16), channel_id=1, source_target_pairs={{0,2},{1,3},{2,0},{3,1},{4,6},{5,7},{6,4},{7,5},{8,10},{9,11},{10,... | collective-permute-start | bytes 479240 | tf_op jit(solution)/shard_map/ppermute | solution.py:465
  (76 other events, 710.0 us)
Sparse Core Ops, SparseCore 0:
  13.0 98.9 all-gather.2

commit v4 on v3

--- a/solution.py
+++ b/solution.py
@@ -11,6 +11,8 @@
 F32 = jnp.float32
 HW=64; LM=64; NEWTON=6; GH=6; GW=GH*HW
 CHUNK=256
+KW=33
+SMALL=48
 def nt(a,b): return lax.dot_general(a,b,(((1,),(1,)),((),())),preferred_element_type=F32)
 def nn(a,b): return lax.dot_general(a,b,(((1,),(0,)),((),())),preferred_element_type=F32)
 def split(a):
@@ -36,7 +38,7 @@
     heads=range(GH); chunks=[slice(c,c+CHUNK) for c in range(0,T,CHUNK)]
     rows=[slice(h*HW,(h+1)*HW) for h in heads]
     scale=HW**-0.25
-    bq=vec_ref[0:1,:].T; bv=vec_ref[1:2,:].T
+    bq=vec_ref[KW:KW+1,:].T; bv=vec_ref[KW+1:KW+2,:].T
     ldc=ldc_ref[0]
     for cs in chunks:
         member=lax.broadcasted_iota(jnp.int32,(LM,CHUNK),0)==tok_ref[0,:,cs]
@@ -140,14 +142,14 @@
     seq,wsp,bsp,rows,cols,sq,turned=att_specs(D,T)
     sd=jax.ShapeDtypeStruct; big=sd((B,D,T),BF)
     return pl.pallas_call(att_fwd_kernel,grid=(G,B),
-        in_specs=[seq((T,D)),seq((LM,D)),wsp,wsp,wsp,pl.BlockSpec((8,GW),lambda g,b:(0,g)),seq((1,T)),seq((LM,1)),seq((1,LM)),cols],
+        in_specs=[seq((T,D)),seq((LM,D)),wsp,wsp,wsp,pl.BlockSpec((SMALL,GW),lambda g,b:(0,g)),seq((1,T)),seq((LM,1)),seq((1,LM)),cols],
         out_specs=[rows]*5+[turned,sq(2*NEWTON),sq(4),cols],
         out_shape=[big]*5+[sd((B,G,8,T),F32),sd((B,H,2*NEWTON,LM,2*LM),F32),sd((B,H,4,LM,2*LM),F32),sd((B,T,D),BF)],
         scratch_shapes=[pltpu.VMEM((GW,T),BF)]*2+[pltpu.VMEM((GW,T),F32),pltpu.VMEM((LM,T),F32)],
         compiler_params=pltpu.CompilerParams(vmem_limit_bytes=60*2**20))(
             x,mean,wq,wk,wv,vec,tok[:,None,:],ld[:,:,None],ld[:,None,:],conv)
-def att_bwd_kernel(x_ref,al_ref,wo_ref,q_ref,k_ref,v_ref,k1_ref,k3_ref,inv_ref,stash_ref,small_ref,tok_ref,conv_ref,
-               dq_ref,dk_ref,dv_ref,gq_ref,gk_ref,gv_ref,sq_ref,sv_ref,
+def att_bwd_kernel(x_ref,al_ref,wo_ref,q_ref,k_ref,v_ref,k1_ref,k3_ref,inv_ref,stash_ref,small_ref,tok_ref,
+               dq_ref,dk_ref,dv_ref,gqk_ref,sq_ref,
                g_ref,ds1_ref,ds3_ref,hot_ref):
     T=x_ref.shape[1]
     heads=range(GH); chunks=[slice(c,c+CHUNK) for c in range(0,T,CHUNK)]
@@ -189,7 +191,7 @@
     def values(cs):
         def go():
             a=jnp.concatenate([nn(drt[h],k3_ref[0,rows[h],cs]) for h in heads],axis=0)
-            dv_ref[0,:,cs]=(a+conv_ref[0,cs,:].T).astype(BF)
+            dv_ref[0,:,cs]=a
         return go
     def to_lk(h):
         def go(): dlk[h]=nt(ds1_ref[rows[h],:],q_ref[0,rows[h]])
@@ -199,13 +201,10 @@
         return go
     @pl.when(pl.program_id(1)==0)
     def _():
-        for ref in (gq_ref,gk_ref,gv_ref,sq_ref,sv_ref): ref[...]=jnp.zeros_like(ref)
-    def value_weights():
-        dv=dv_ref[0]
-        gv_ref[...]+=nn(dv,x_ref[0]); sv_ref[...]+=jnp.sum(dv.astype(F32),axis=1,keepdims=True)
+        for ref in (gqk_ref,sq_ref): ref[...]=jnp.zeros_like(ref)
     side=[]
     for h in heads: side+=[third(h,cs) for cs in chunks]+[to_lq(h)]+[first(h,cs) for cs in chunks]+[to_lk(h)]
-    side+=[values(cs) for cs in chunks]+[value_weights]
+    side+=[values(cs) for cs in chunks]
     k2t=[a.T for a in k2]; k2tw=[wide(a) for a in k2t]
     def newton(n):
         def one():
@@ -242,25 +241,21 @@
                 a=nn(lh[h],jnp.concatenate([ds_ref[rows[h],cs],hot],axis=0))
                 out_ref[0,rows[h],cs]=(a*scale).astype(BF)
     dq=dq_ref[0]
-    gq_ref[...]+=nn(dq,x_ref[0]); gk_ref[...]+=nn(dk_ref[0],x_ref[0])
+    gqk_ref[0]+=nn(dq,x_ref[0]); gqk_ref[1]+=nn(dk_ref[0],x_ref[0])
     sq_ref[...]+=jnp.sum(dq.astype(F32),axis=1,keepdims=True)
-def att_bwd(x,al,wo,q,k,v,k1,k3,inv,stash,small,tok,conv,group):
-    B,T,D=x.shape
-    seq=lambda s: pl.BlockSpec((1,)+s,lambda g,b:(b,)+(0,)*len(s))
-    rows=pl.BlockSpec((1,GW,T),lambda g,b:(b,group,0))
-    sq=lambda n: pl.BlockSpec((1,GH,n,LM,2*LM),lambda g,b:(b,group,0,0,0))
-    whole=lambda r,c: pl.BlockSpec((r,c),lambda g,b:(0,0))
-    sd=jax.ShapeDtypeStruct
-    return pl.pallas_call(att_bwd_kernel,grid=(1,B),
-        in_specs=[seq((T,D)),seq((T,D)),pl.BlockSpec((GW,D),lambda g,b:(group,0))]+[rows]*5+[
-            pl.BlockSpec((1,1,8,T),lambda g,b:(b,group,0,0)),sq(2*NEWTON),sq(4),seq((1,T)),seq((T,GW))],
-        out_specs=[seq((GW,T))]*3+[whole(GW,D)]*3+[whole(GW,1)]*2,
-        out_shape=[sd((B,GW,T),BF)]*3+[sd((GW,D),F32)]*3+[sd((GW,1),F32)]*2,
+def att_bwd(x,al,wo,q,k,v,k1,k3,inv,stash,small,tok):
+    B,T,D=x.shape; G=D//GW
+    seq,wsp,bsp,rows,cols,sq,turned=att_specs(D,T)
+    sd=jax.ShapeDtypeStruct; big=sd((B,D,T),BF)
+    return pl.pallas_call(att_bwd_kernel,grid=(G,B),
+        in_specs=[seq((T,D)),seq((T,D)),wsp]+[rows]*5+[turned,sq(2*NEWTON),sq(4),seq((1,T))],
+        out_specs=[rows]*3+[pl.BlockSpec((2,GW,D),lambda g,b:(0,g,0)),bsp],
+        out_shape=[big,big,sd((B,D,T),F32),sd((2,D,D),F32),sd((D,1),F32)],
         scratch_shapes=[pltpu.VMEM((GW,T),BF)]*3+[pltpu.VMEM((LM,T),BF)],
         compiler_params=pltpu.CompilerParams(vmem_limit_bytes=60*2**20))(
-            x,al,wo,q,k,v,k1,k3,inv,stash,small,tok[:,None,:],conv)
-
-KW=33; HALF=16; DOCS=4; GAP=16
+            x,al,wo,q,k,v,k1,k3,inv,stash,small,tok[:,None,:])
+
+HALF=16; DOCS=4; GAP=16
 def spread(dst, get, bounds, length, step):
     total=length+GAP*(DOCS+1)
     ids=lax.broadcasted_iota(jnp.int32,(step,128),0)
@@ -300,13 +295,13 @@
             acc=t if acc is None else acc+t
     return acc
 
-def conv_fwd_kernel(bounds_ref, x_ref, wv_ref, vec_ref, w_ref, v_ref, out_ref, pad_ref, res_ref):
+def conv_fwd_kernel(bounds_ref, x_ref, wv_ref, w_ref, v_ref, out_ref, pad_ref, res_ref):
     b=pl.program_id(0)
     bounds=[bounds_ref[b,d] for d in range(DOCS+1)]
     length=v_ref.shape[1]; total=length+GAP*(DOCS+1)
     pad_ref[0:HALF,:]=jnp.zeros((HALF,128),F32); pad_ref[HALF+total:,:]=jnp.zeros((pad_ref.shape[0]-HALF-total,128),F32)
     for lo in range(0,length,256):
-        v_ref[0,lo:lo+256,:]=nt(x_ref[0,lo:lo+256,:],wv_ref[...])+vec_ref[1:2,:]
+        v_ref[0,lo:lo+256,:]=nt(x_ref[0,lo:lo+256,:],wv_ref[...])+w_ref[KW+1:KW+2,:]
     spread(pad_ref, lambda lo,n: v_ref[0,lo:lo+n,:], bounds, length, BLOCK)
     def block(i,c):
         base=pl.multiple_of(i*BLOCK,BLOCK)
@@ -319,18 +314,19 @@
     total=length+GAP*(DOCS+1)
     return -(-total//BLOCK)*BLOCK
 
-def conv_fwd(bounds, x, w_v, vec, w):
+def conv_fwd(bounds, x, w_v, w):
     B,L,D=x.shape
     rows=padded_rows(L)
     slab=pl.BlockSpec((1,L,128),lambda b,c,_:(b,0,c)); big=jax.ShapeDtypeStruct((B,L,D),F32)
     return pl.pallas_call(conv_fwd_kernel,grid_spec=pltpu.PrefetchScalarGridSpec(num_scalar_prefetch=1,grid=(B,D//128),
         in_specs=[pl.BlockSpec((1,L,D),lambda b,c,_:(b,0,0)),pl.BlockSpec((128,D),lambda b,c,_:(c,0)),
-            pl.BlockSpec((8,128),lambda b,c,_:(0,c)),pl.BlockSpec((KW,128),lambda b,c,_:(0,c))],
+            pl.BlockSpec((SMALL,128),lambda b,c,_:(0,c))],
         out_specs=[slab,slab],
         scratch_shapes=[pltpu.VMEM((rows+2*HALF+8,128),F32),pltpu.VMEM((rows,128),F32)]),
         out_shape=[big,big],
-        compiler_params=pltpu.CompilerParams(vmem_limit_bytes=60*2**20))(bounds,x,w_v,vec,w)
-def conv_bwd_kernel(bounds_ref, v_ref, al_ref, wo_ref, w_ref, dv_ref, dw_ref, vpad_ref, gpad_ref, res_ref, acc_ref, g_ref):
+        compiler_params=pltpu.CompilerParams(vmem_limit_bytes=60*2**20))(bounds,x,w_v,w)
+def conv_bwd_kernel(bounds_ref, v_ref, al_ref, wo_ref, w_ref, x_ref, att_ref, more_ref, *refs):
+    dv_ref, gv_ref, vpad_ref, gpad_ref, res_ref, acc_ref, g_ref, sum_ref = refs[-8:]
     b=pl.program_id(1)
     bounds=[bounds_ref[b,d] for d in range(DOCS+1)]
     length=v_ref.shape[1]; total=length+GAP*(DOCS+1)
@@ -342,7 +338,8 @@
     spread(vpad_ref, lambda lo,n: v_ref[0,lo:lo+n,:], bounds, length, BLOCK)
     spread(gpad_ref, lambda lo,n: g_ref[lo:lo+n,:], bounds, length, BLOCK)
     @pl.when(b==0)
-    def _(): acc_ref[...]=jnp.zeros_like(acc_ref)
+    def _():
+        acc_ref[...]=jnp.zeros_like(acc_ref); gv_ref[...]=jnp.zeros_like(gv_ref); sum_ref[...]=jnp.zeros_like(sum_ref)
     def block(i,c):
         base=pl.multiple_of(i*BLOCK,BLOCK)
         here=vpad_ref[pl.ds(base+HALF,BLOCK),:]
@@ -360,23 +357,34 @@
         res_ref[pl.ds(base,BLOCK),:]=acc
         return c
     lax.fori_loop(0,-(-total//BLOCK),block,0)
-    for lo in range(0,length,BLOCK):
-        dv_ref[0,lo:lo+BLOCK,:]=collect(res_ref,bounds,lo,BLOCK)
+    for lo in range(0,length,BLOCK*2):
+        part=collect(res_ref,bounds,lo,BLOCK*2).T+att_ref[0,:,lo:lo+BLOCK*2]
+        dv_ref[0,:,lo:lo+BLOCK*2]=part.astype(BF)
+    dv=dv_ref[0]; depth=x_ref.shape[2]
+    gv_ref[:,:depth]+=nn(dv,x_ref[0])
+    sum_ref[...]+=jnp.sum(dv.astype(F32),axis=1,keepdims=True)
     @pl.when(b==pl.num_programs(1)-1)
     def _():
-        for s in range(KW):
-            dw_ref[s:s+1,:]=jnp.sum(acc_ref[s],axis=0,keepdims=True)
-
-def conv_bwd(bounds, v, al, w_o, w, group):
+        rows=[jnp.sum(acc_ref[s],axis=0,keepdims=True) for s in range(KW)]
+        side=jnp.concatenate(rows+[jnp.zeros((128-KW,128),F32)],axis=0).T
+        lane=lax.broadcasted_iota(jnp.int32,(128,128),1)
+        gv_ref[:,depth:]=more_ref[...]+side+jnp.where(lane==KW,sum_ref[:,:1],0.0)
+def conv_bwd(bounds, v, al, w_o, w, x, att, more, before, slabs, at):
     B,L,D=v.shape
-    rows=padded_rows(L); slabs=GW//128; at=group*slabs
+    rows=padded_rows(L)
+    sd=jax.ShapeDtypeStruct
+    seq=pl.BlockSpec((1,L,D),lambda c,b,_:(b,0,0))
+    feats=pl.BlockSpec((1,128,L),lambda c,b,_:(b,at+c,0))
+    alias={9:0,10:1} if before else {}
     return pl.pallas_call(conv_bwd_kernel,grid_spec=pltpu.PrefetchScalarGridSpec(num_scalar_prefetch=1,grid=(slabs,B),
-        in_specs=[pl.BlockSpec((1,L,128),lambda c,b,_:(b,0,at+c)),pl.BlockSpec((1,L,D),lambda c,b,_:(b,0,0)),
-            pl.BlockSpec((D,128),lambda c,b,_:(0,at+c)),pl.BlockSpec((KW,128),lambda c,b,_:(0,at+c))],
-        out_specs=[pl.BlockSpec((1,L,128),lambda c,b,_:(b,0,c)),pl.BlockSpec((KW,128),lambda c,b,_:(0,c))],
-        scratch_shapes=[pltpu.VMEM((rows+2*HALF+8,128),F32)]*2+[pltpu.VMEM((rows,128),F32),pltpu.VMEM((KW,8,128),F32),pltpu.VMEM((L,128),F32)]),
-        out_shape=[jax.ShapeDtypeStruct((B,L,GW),F32),jax.ShapeDtypeStruct((KW,GW),F32)],
-        compiler_params=pltpu.CompilerParams(vmem_limit_bytes=60*2**20))(bounds,v,al,w_o,w)
+        in_specs=[pl.BlockSpec((1,L,128),lambda c,b,_:(b,0,at+c)),seq,
+            pl.BlockSpec((D,128),lambda c,b,_:(0,at+c)),pl.BlockSpec((SMALL,128),lambda c,b,_:(0,at+c)),
+            seq,feats,pl.BlockSpec((128,128),lambda c,b,_:(at+c,0))]+[pl.BlockSpec(memory_space=pl.ANY)]*len(before),
+        out_specs=[feats,pl.BlockSpec((128,D+128),lambda c,b,_:(at+c,0))],
+        scratch_shapes=[pltpu.VMEM((rows+2*HALF+8,128),F32)]*2+[pltpu.VMEM((rows,128),F32),pltpu.VMEM((KW,8,128),F32),
+            pltpu.VMEM((L,128),F32),pltpu.VMEM((128,128),F32)]),
+        out_shape=[sd((B,D,L),BF),sd((D,D+128),F32)],input_output_aliases={i-1:o for i,o in alias.items()},
+        compiler_params=pltpu.CompilerParams(vmem_limit_bytes=60*2**20))(bounds,v,al,w_o,w,x,att,more,*before)
 
 def gelu_parts(x):
     size=jnp.abs(x)
@@ -399,7 +407,7 @@
     def _():
         sums_ref[...]=jnp.zeros_like(sums_ref); sumu_ref[...]=jnp.zeros_like(sumu_ref)
     v=lambda i: vec_ref[i:i+1,:]
-    b_o,g1,s1,b_d,g2,s2=[v(i) for i in range(2,8)]
+    b_o,g1,s1,b_d,g2,s2=[v(KW+i) for i in range(2,8)]
     n1,r1=norm(x_ref[...].astype(F32)+(nt(ctx_ref[...],wo_ref[...])+b_o))
     normed=n1*g1+s1
     low=normed.astype(BF); normed_ref[...]=low
@@ -436,12 +444,53 @@
     keep=lambda r,w: pl.BlockSpec((r,w),lambda i:(0,0))
     sd=jax.ShapeDtypeStruct
     return pl.pallas_call(functools.partial(ffn_kernel,chunks),grid=(T//block,),
-        in_specs=[row(D),row(D),row(D),full(wo),full(wu),full(wd),full(vec),full(bu)],
+        in_specs=[row(D),row(D),row(D),full(wo),full(wu),full(wd),pl.BlockSpec((SMALL,D),lambda i:(0,0)),full(bu)],
         out_specs=[row(D),row(D),row(F),row(D),row(F),row(D),row(D),keep(8,D),keep(1,F)],
         out_shape=[sd((T,D),BF),sd((T,D),BF),sd((T,F),BF),sd((T,D),BF),sd((T,F),BF),sd((T,D),F32),sd((T,D),BF),sd((8,D),F32),sd((1,F),F32)],
         scratch_shapes=[pltpu.VMEM((block,F),F32)],
         compiler_params=pltpu.CompilerParams(vmem_limit_bytes=60*2**20,dimension_semantics=("arbitrary",)),
     )(ctx,x,cot,wo,wu,wd,vec,bu)
+
+
+def across_rows(left_side, right_side):
+    return lax.dot_general(left_side, right_side, (((0,), (0,)), ((), ())), preferred_element_type=F32)
+
+
+def weight_kernel(own, up_ref, normed_ref, hidden_ref, down_ref, att_ref, ctx_ref, out_ref, acc_ref):
+    depth=normed_ref.shape[1]; k=pl.program_id(1)
+    wide_rows=up_ref.shape[1]; rows=down_ref.shape[1]; parts=hidden_ref.shape[1]//depth
+    @pl.when(k==0)
+    def _(): acc_ref[...]=jnp.zeros_like(acc_ref)
+    for lo in range(0,wide_rows,rows):
+        acc_ref[lo:lo+rows]+=across_rows(up_ref[:,lo:lo+rows],normed_ref[...])
+    for i in range(parts):
+        at=wide_rows+i*rows
+        acc_ref[at:at+rows]+=across_rows(down_ref[...],hidden_ref[:,i*depth:(i+1)*depth])
+    at=wide_rows+parts*rows
+    acc_ref[at:at+rows]+=across_rows(att_ref[...],ctx_ref[...])
+    @pl.when(k==pl.num_programs(1)-1)
+    def _():
+        many=rows//own; lines=wide_rows//many
+        out_ref[:,:lines]=acc_ref[:wide_rows].reshape(many,lines,depth).astype(BF)
+        narrow=[acc_ref[wide_rows+i*rows:wide_rows+(i+1)*rows].reshape(many,own,depth) for i in range(parts+1)]
+        narrow.append(jnp.zeros((many,out_ref.shape[1]-lines-(parts+1)*own,depth),F32))
+        out_ref[:,lines:]=jnp.concatenate(narrow,axis=1).astype(BF)
+def weight_grads(own, up, normed, hidden, down, att, ctx):
+    T,D=normed.shape; F=up.shape[1]; halves=2; many=D//own//halves; block=512
+    R=-(-(F//D*2+1)*own//16)*16
+    if own%8:
+        by=lambda a: a.reshape(D//own,-1,D)
+        pieces=[by(across_rows(up,normed))]+[by(across_rows(down,hidden[:,i*D:(i+1)*D])) for i in range(F//D)]
+        pieces.append(by(across_rows(att,ctx)))
+        pieces.append(jnp.zeros((D//own,R-(F//D*2+1)*own,D),F32))
+        return jnp.concatenate(pieces,axis=1).astype(BF)
+    col=lambda w: pl.BlockSpec((block,w),lambda h,k:(k,h)); row=lambda w: pl.BlockSpec((block,w),lambda h,k:(k,0))
+    return pl.pallas_call(functools.partial(weight_kernel,own),grid=(halves,T//block),
+        in_specs=[col(F//halves),row(D),row(F),col(D//halves),col(D//halves),row(D)],
+        out_specs=pl.BlockSpec((many,R,D),lambda h,k:(h,0,0)),
+        out_shape=jax.ShapeDtypeStruct((D//own,R,D),BF),
+        scratch_shapes=[pltpu.VMEM((many*own*(F//D*2+1),D),F32)],
+        compiler_params=pltpu.CompilerParams(vmem_limit_bytes=60*2**20))(up,normed,hidden,down,att,ctx)
 
 
 def digits():
@@ -469,10 +518,12 @@
     return (lax.axis_index(axis) // stride) % 2
 
 
-def gather_rows(shard, number):
+def gather_rows(shard, number, passed=None):
     places = digits()
     held = shard.reshape((1,) * len(places) + shard.shape)
     for dim in link_order(number)[::-1]:
+        if passed is not None:
+            passed.append(held)
         mine = digit_of(*places[dim])
         got = exchange(held, *places[dim])
         first = jnp.where(mine == 0, held, got)
@@ -481,32 +532,24 @@
     return held.reshape((-1,) + shard.shape)
 
 
-def scatter_start(whole):
-    return whole.reshape((2,) * len(digits()) + whole.shape[1:])
+def scatter_start(whole, own):
+    return whole.reshape(whole.shape[:-2] + (2,) * len(digits()) + (own, whole.shape[-1]))
 
 
 def scatter_step(held, number, step):
     places = digits()
-    dim = link_order(number)[step]
-    mine = digit_of(*places[dim])
+    dim = link_order(number)[step] + held.ndim - 2 - len(places)
+    place = places[link_order(number)[step]]
+    mine = digit_of(*place)
     keep = lax.dynamic_slice_in_dim(held, mine, 1, dim).astype(F32)
     send = lax.dynamic_slice_in_dim(held, 1 - mine, 1, dim).astype(BF)
-    return keep + exchange(send, *places[dim]).astype(F32)
+    return keep + exchange(send, *place).astype(F32)
 
 
 def scatter_rest(held, number, step):
     for later in range(step, len(digits())):
         held = scatter_step(held, number, later)
-    return held.reshape(held.shape[-2:])
-
-
-def pad_rows(flat, rows):
-    count, length = flat.shape
-    return jnp.pad(flat, ((0, 0), (0, rows * 768 - length))).reshape(count, rows, 768)
-
-
-def across_rows(left_side, right_side):
-    return lax.dot_general(left_side, right_side, (((0,), (0,)), ((), ())), preferred_element_type=F32)
+    return held.reshape(held.shape[: held.ndim - 2 - len(digits())] + held.shape[-2:])
 
 
 def shards(
@@ -537,21 +580,24 @@
     tokens = batch_rows * sequence_length
     lines = b_up.shape[0] // own
     vectors = (b_query, b_value, b_out, gain_one, shift_one, b_down, gain_two, shift_two)
-    flat = jnp.concatenate([conv_weight.reshape(-1)] + list(vectors) + [b_up])
-    small = pad_rows(flat[None], -(-flat.shape[0] // 768))[0]
-    gathered_v = gather_rows(jnp.concatenate([w_value.T, small], axis=0), 0)
+    small = jnp.concatenate(
+        [conv_weight] + [vector[None] for vector in vectors] + [b_up.reshape(own, lines).T]
+    )
+    small = jnp.pad(small.T, ((0, 0), (0, 128 - small.shape[0])))
+    passed = []
     w_q = gather_rows(w_query.T, 1).reshape(feature_width, feature_width)
     w_k = gather_rows(w_key.T, 2).reshape(feature_width, feature_width)
-    w_v = gathered_v[:, :own].reshape(feature_width, feature_width)
-    small = gathered_v[:, own:].reshape(group_count, -1).astype(F32)[:, : flat.shape[0]]
-    small = small.reshape(group_count, -1, own)
-    b_u = small[:, KW + 8 :].reshape(1, -1)
-    small = jnp.moveaxis(small[:, : KW + 8], 0, 1).reshape(KW + 8, feature_width)
-    conv_taps, vec = small[:KW], small[KW:]
+    gathered_v = gather_rows(jnp.concatenate([w_value.T, small], axis=1), 0, passed)
+    gathered_v = gathered_v.reshape(feature_width, feature_width + 128)
+    w_v = gathered_v[:, :feature_width]
+    small = gathered_v[:, feature_width:]
+    b_u = small[:, KW + 8 : KW + 8 + lines].reshape(1, -1).astype(F32)
+    small = small.astype(F32).T
     ff_count = w_down.shape[0] // feature_width
     shard = jnp.concatenate(
         [w_out.T, w_up.T] + [w_down[i * feature_width : (i + 1) * feature_width].T for i in range(ff_count)]
     )
+    shard, _ = lax.optimization_barrier((shard, passed[2]))
     gathered = lax.all_gather(shard, ("wide", "narrow"), axis=0)
     w_o = gathered[:, :own].reshape(feature_width, feature_width)
     w_u = gathered[:, own : own * (1 + lines)].reshape(-1, feature_width)
@@ -564,90 +610,68 @@
     doc = jnp.sum(jnp.where(member, landmark_doc[:, :, None], 0), axis=1)
     bounds = jnp.sum(doc[:, None, :] < jnp.arange(DOCS + 1)[None, :, None], axis=2).astype(jnp.int32)
     rows_low = inputs.reshape(tokens, feature_width)
-    value_rows, conv_part = conv_fwd(bounds, inputs, w_v, vec, conv_taps)
+    value_rows, conv_part = conv_fwd(bounds, inputs, w_v, small)
     q, k, v, k1, k3, inv, stash, landmarks, context = att_fwd(
-        inputs, means, w_q, w_k, w_v, vec, tok_landmark, landmark_doc, conv_part
+        inputs, means, w_q, w_k, w_v, small, tok_landmark, landmark_doc, conv_part
     )
     context = context.reshape(tokens, feature_width)
     layer_out, normed, hidden, down_low, up_low, grad_one, att_low, sums, sums_up = ffn(
-        context, rows_low, cotangent.reshape(tokens, feature_width), w_o, w_u, w_d, vec, b_u
+        context, rows_low, cotangent.reshape(tokens, feature_width), w_o, w_u, w_d, small, b_u
     )
-
-    def by_device(values):
-        return values.reshape((group_count, -1) + values.shape[1:])
-
-    early = jnp.concatenate([by_device(sums[i]) for i in range(6)] + [by_device(sums_up[0])], axis=1)
-    grad_out = jnp.concatenate(
-        [by_device(across_rows(att_low, context)), pad_rows(early, -(-early.shape[1] // 768))], axis=1
-    )
-    shares = [
-        scatter_start(by_device(across_rows(up_low, normed))),
-        scatter_start(by_device(across_rows(down_low, hidden))),
-        scatter_start(grad_out),
-    ]
-
-    def advance(shares, step):
-        return [scatter_step(share, i, step) for i, share in enumerate(shares)]
-
-    shares = advance(shares, 0)
+    grads = weight_grads(own, up_low, normed, hidden, down_low, att_low, context)
+    share = lax.psum_scatter(grads, ("wide", "narrow"), scatter_dimension=0, tiled=True)[0].astype(F32)
     w_plain = w_o.T
     att_low = att_low.reshape(inputs.shape)
-    groups = feature_width // GW
-    conv_grads, att_grads = [], []
-    att_low, shares = lax.optimization_barrier((att_low, shares))
-    for group in range(groups):
-        moved = advance(shares, 1 + group)
-        found = conv_bwd(bounds, value_rows, att_low, w_o, conv_taps, group)
-        att_low, found, shares = lax.optimization_barrier((att_low, found, moved))
-        conv_grads.append(found)
-    for group in range(groups):
-        moved = advance(shares, 1 + groups + group)
-        found = att_bwd(
-            inputs, att_low, w_plain, q, k, v, k1, k3, inv, stash, landmarks, tok_landmark,
-            conv_grads[group][0], group,
+    dq, dk, dv, grad_qk, sum_q = att_bwd(
+        inputs, att_low, w_plain, q, k, v, k1, k3, inv, stash, landmarks, tok_landmark
+    )
+    more = jnp.concatenate(
+        [
+            jnp.zeros((feature_width, KW + 1), F32),
+            sum_q,
+            sums[:6].T,
+            sums_up.reshape(feature_width, lines),
+            jnp.zeros((feature_width, 128 - KW - 8 - lines), F32),
+        ],
+        axis=1,
+    )
+    moving = scatter_step(scatter_start(grad_qk, own), 1, 0)
+    calls, before = 3, ()
+    slabs = feature_width // 128 // calls
+    for call in range(calls):
+        moved = scatter_step(moving, 1, 1 + call)
+        before = conv_bwd(
+            bounds, value_rows, att_low, w_o, small, inputs, dv, more, before, slabs, call * slabs
         )
-        att_low, found, shares = lax.optimization_barrier((att_low, found, moved))
-        att_grads.append(found)
-    share_up, share_down, share_out = [
-        scatter_rest(share, i, 1 + 2 * groups) for i, share in enumerate(shares)
-    ]
-    grad_q, grad_k, grad_v, sum_q, sum_v = [
-        jnp.concatenate([found[i] for found in att_grads]) for i in range(3, 8)
-    ]
-    taps_grad = jnp.concatenate([found[1] for found in conv_grads], axis=1)
-    late = jnp.concatenate(
-        [by_device(taps_grad.T).reshape(group_count, -1), by_device(sum_q[:, 0]), by_device(sum_v[:, 0])], axis=1
-    )
-    grad_v = jnp.concatenate([by_device(grad_v), pad_rows(late, -(-late.shape[1] // 768))], axis=1)
-    share_v = scatter_rest(scatter_start(grad_v), 0, 0)
-    share_q = scatter_rest(scatter_start(by_device(grad_q)), 1, 0)
-    share_k = scatter_rest(scatter_start(by_device(grad_k)), 2, 0)
+        before, att_low, moving = lax.optimization_barrier((tuple(before), att_low, moved))
+    dv, grad_v = before
+    share_qk = scatter_rest(moving, 1, 1 + calls)
+    share_v = scatter_rest(scatter_start(grad_v, own), 0, 0)
     input_grad = grad_one.reshape(inputs.shape)
-    for group, found in enumerate(att_grads):
-        for grad, weight in zip(found[:3], (w_q, w_k, w_v)):
-            part = weight[group * GW : (group + 1) * GW]
-            input_grad = input_grad + jnp.einsum("bot,oi->bti", grad, part, preferred_element_type=F32)
-    early = share_out[own:].reshape(-1)
-    late = share_v[own:].reshape(-1)
+    for grad, weight in zip((dq, dk, dv), (w_q, w_k, w_v)):
+        input_grad = input_grad + jnp.einsum("bot,oi->bti", grad, weight, preferred_element_type=F32)
+    late = share_v[:, feature_width:]
+    share_down = share[own * lines : 2 * own * lines].reshape(ff_count, own, feature_width)
+    share_out = share[2 * own * lines : 2 * own * lines + own]
     return (
         layer_out.reshape(inputs.shape),
         input_grad,
-        share_q.T,
-        late[own * KW : own * KW + own],
-        share_k.T,
-        share_v[:own].T,
-        late[own * KW + own : own * KW + 2 * own],
-        late[: own * KW].reshape(own, KW).T,
-        share_out[:own].T,
-        early[:own],
-        early[own : 2 * own],
-        early[2 * own : 3 * own],
-        share_up.T,
-        early[6 * own : 6 * own + b_up.shape[0]],
-        share_down.T,
-        early[3 * own : 4 * own],
-        early[4 * own : 5 * own],
-        early[5 * own : 6 * own],
+        share_qk[0].T,
+        late[:, KW + 1],
+        share_qk[1].T,
+        share_v[:, :feature_width].T,
+        late[:, KW],
+        late[:, :KW].T,
+        share_out.T,
+        late[:, KW + 2],
+        late[:, KW + 3],
+        late[:, KW + 4],
+        share[: own * lines].T,
+        late[:, KW + 8 : KW + 8 + lines].reshape(-1),
+        jnp.moveaxis(share_down, 1, 2).reshape(-1, own),
+        late[:, KW + 5],
+        late[:, KW + 6],
+        late[:, KW + 7],
     )
 
 

time: 608 us -> 462 us (0.76)
  matrix products: 73.5 us -> 15.5 us
  local copies, waits for them, and re-layouts: 95.8 us -> 47.4 us
  other arithmetic: 51.1 us -> 12.3 us
  Pallas kernels: 269 us -> 303 us
  starting transfers between devices: 49 us -> 30.5 us
  waiting for transfers between devices: 47.5 us -> 33.2 us
    dot_general x9 -> x3, matrix products: 70.2 us -> 12.3 us  [shards(): jnp.einsum('bot,oi->bti', grad, weight, preferred_element_type=F32)]
    add x28 -> x9, other arithmetic: 34.1 us -> 3.57 us  [scatter_step(): return keep + exchange(send, *place).astype(F32)]
    pallas_call x2, Pallas kernels: 65 us -> 87.7 us  [the longest x1 54.5 us: att_bwd(): pl.pallas_call(att_bwd_kernel, grid=(G, B), in_specs=[seq((T, D)), seq((T...]
    ppermute x45 -> x25, starting transfers between devices: 48.9 us -> 30.5 us  [exchange(): lax.ppermute(values, axis, [(i, i ^ stride) for i in range(lax.axis_size(...]
    convert_element_type x30 -> x10, local copies, waits for them, and re-layouts: 20.4 us -> 4.32 us  [scatter_step(): send = lax.dynamic_slice_in_dim(held, 1 - mine, 1, dim).astype(BF)]
    ppermute x45 -> x25, waiting for transfers between devices: 47.4 us -> 33.1 us  [exchange(): lax.ppermute(values, axis, [(i, i ^ stride) for i in range(lax.axis_size(...]
    unnamed x119 -> x38, local copies, waits for them, and re-layouts: 20.8 us -> 6.55 us
    pallas_call x2 -> x3, Pallas kernels: 51.7 us -> 63.9 us  [conv_bwd(): pl.pallas_call(conv_bwd_kernel, grid_spec=pltpu.PrefetchScalarGridSpec(nu...]
  transfers between devices with their start and end apart: 46 -> 27, of which waited for: 15 -> 12; matrix products, arithmetic and copies ran while one was open for 25% -> 11% of each run, Pallas kernels for 32% -> 43%
where the time goes in v4:
time: 462 us; the launch traced here: 457 us
  Pallas kernels  303 us (66%)
  local copies, waits for them, and re-layouts  47.4 us (10%)
  waiting for transfers between devices  33.2 us (7%)
  starting transfers between devices  30.5 us (7%)
  matrix products  15.5 us (3%)
  between operations  15 us (3%)
  other arithmetic  12.3 us (3%)
    pallas_call x1, Pallas kernels, ffn(): pl.pallas_call(functools.partial(ffn_kernel, chunks), grid=(T // block,),...  73.9 us
    pallas_call x3, Pallas kernels, conv_bwd(): pl.pallas_call(conv_bwd_kernel, grid_spec=pltpu.PrefetchScalarGridSpec(nu...  63.9 us
    pallas_call x1, Pallas kernels, att_bwd(): pl.pallas_call(att_bwd_kernel, grid=(G, B), in_specs=[seq((T, D)), seq((T...  54.5 us
    pallas_call x1, Pallas kernels, att_fwd(): pl.pallas_call(att_fwd_kernel, grid=(G, B), in_specs=[seq((T, D)), seq((L...  42.8 us
    pallas_call x1, Pallas kernels, conv_fwd(): pl.pallas_call(conv_fwd_kernel, grid_spec=pltpu.PrefetchScalarGridSpec(nu...  35 us
    pallas_call x1, Pallas kernels, weight_grads(): pl.pallas_call(functools.partial(weight_kernel, own), grid=(halves, T //...  33.2 us
    ppermute x25, waiting for transfers between devices, exchange(): lax.ppermute(values, axis, [(i, i ^ stride) for i in range(lax.axis_size(...  33.1 us
    ppermute x25, starting transfers between devices, exchange(): lax.ppermute(values, axis, [(i, i ^ stride) for i in range(lax.axis_size(...  30.5 us
  transfers between devices with their start and end apart: 27, of which 12 were waited for; matrix products, arithmetic and copies ran while one was open for 11% of the time, Pallas kernels for 43%

profile of v4, /device:TPU:0, one launch (start us, length us, event | category | flops | bytes accessed | tf_op | source)
XLA Modules:
  0.0 457.2 jit_solution(1993812344093465215)
XLA Ops:
  15.6 4.0 collective-permute-start.10
  33.1 3.3 convolution_divide_fusion.mean_ref
  50.6 3.8 collective-permute-done.2
  59.5 3.3 collective-permute-done.3
  62.9 5.6 %collective-permute-done.13 = bf16[2,2,1,2,1,24,896]{6,5,4,3,2,1,0:T(8,128)(2,1)S(1)} collective-permute-done((bf16[2,2,1,2,1,24,896]{6,5,4,3,2,1,0:T(8,128)(2,1)S(1)}, bf16[2,2,1,2,1,24,896]{6,5,4,3,2,1,0:T(8,128)(2,1)S(1)}, u32[]{:S(2)}, u32[]{:S(2)}) %collective-permute-start.13) | collective-permute-done | bytes 344096 | tf_op jit(solution)/shard_map/ppermute | solution.py:514
  74.6 35.0 %shard_map.331 = (f32[2,1024,768]{2,1,0:T(8,128)}, f32[2,1024,768]{2,1,0:T(8,128)}) custom-call(s32[2,5]{1,0:T(2,128)} %copy.89.bounds_ref, bf16[2,1024,768]{2,1,0:T(8,128)(2,1)} %x_ref.11, bf16[768,768]{1,0:T(8,128)(2,1)} %slice.131.wv_ref, f32[128,768]{1,0:T(8,128)} %convert_bitcast_fusion.w_ref.vec_ref), custom_call_target="tpu_custom_call" | custom-call | tf_op jit(solution)/shard_map/pallas_call | solution.py:321
  109.6 42.8 %shard_map.332 = (bf16[2,768,1024]{2,1,0:T(8,128)(2,1)}, bf16[2,768,1024]{2,1,0:T(8,128)(2,1)}, bf16[2,768,1024]{2,1,0:T(8,128)(2,1)}, bf16[2,768,1024]{2,1,0:T(...) custom-call(bf16[2,1024,768]{2,1,0:T(8,128)(2,1)} %x_ref.11, ...), custom_call_target="tpu_custom_call" | custom-call | tf_op jit(solution)/shard_map/pallas_call | solution.py:144
  152.5 6.6 %fusion.8 = (bf16[32,96,768]{2,1,0:T(8,128)(2,1)S(1)}, bf16[32,96,768]{2,1,0:T(8,128)(2,1)}) fusion(bf16[32,216,768]{2,1,0:T(8,128)(2,1)} %bitcast.126), kind=kLoop, calls=%fused_computation.102 | loop fusion | bytes 18874368 | tf_op jit(solution)/shard_map/slice | solution.py:605
  159.1 2.4 slice.133
  161.5 2.4 copy.92
  163.9 73.9 %shard_map.333 = (bf16[2048,768]{1,0:T(8,128)(2,1)}, bf16[2048,768]{1,0:T(8,128)(2,1)}, bf16[2048,3072]{1,0:T(8,128)(2,1)}, bf16[2048,768]{1,0:T(8,128)(2,1)}, b...) custom-call(bf16[2048,768]{1,0:T(8,128)(2,1)} %bitcast.122, ...), custom_call_target="tpu_custom_call" | custom-call | tf_op jit(solution)/shard_map/pallas_call | solution.py:446
  237.8 33.2 %shard_map.338 = bf16[32,224,768]{2,1,0:T(8,128)(2,1)} custom-call(bf16[2048,3072]{1,0:T(8,128)(2,1)} %get-tuple-element.100.up_ref, bf16[2048,768]{1,0:T(8,128)(2,1)} %get-tuple-element.101.normed_ref, bf16[2048,3072]{1,0:T(8,128)(2,1)} %get-tuple-element.102.hidden_ref, bf16[2048,768]{1,0:T(8,128)(2,1)} %get-tuple-element.103.down_ref, ...), custom_call_target="tpu_custom_call" | custom-call | tf_op jit(solution)/shard_map/pallas_call | solution.py:488
  273.8 54.5 %shard_map.334 = (bf16[2,768,1024]{2,1,0:T(8,128)(2,1)}, bf16[2,768,1024]{2,1,0:T(8,128)(2,1)}, f32[2,768,1024]{2,1,0:T(8,128)}, f32[2,768,768]{2,1,0:T(8,128)}, f32[768,1]{1,0:T(8,128)}) custom-call(bf16[2,1024,768]{2,1,0:T(8,128)(2,1)} %x_ref.11, bf16[2,1024,768]{2,1,0:T(8,128)(2,1)} %bitcast.108, bf16[768,768]{1,0:T(8,128)(2,1)} %copy.93.wo_ref, ...), custom_call_target="tpu_custom_call" | custom-call | tf_op jit(solution)/shard_map/pallas_call | solution.py:250
  330.8 2.5 collective-permute-done.15
  341.7 21.5 %shard_map.335 = (bf16[2,768,1024]{2,1,0:T(8,128)(2,1)}, f32[768,896]{1,0:T(8,128)}) custom-call(s32[2,5]{1,0:T(2,128)} %copy.89.bounds_ref, f32[2,1024,768]{2,1,0:T(8,128)} %get-tuple-element.77.v_ref, bf16[2,1024,768]{2,1,0:T(8,128)(2,1)} %bitcast.109, bf16[768,768]{1,0:T(8,128)(2,1)} %bitcast.113, f32[128,768]{1,0:T(8,128)} %convert_bitcast_fusion.w_ref.vec_ref, ...), custom_call_target="tpu_custom_call" | custom-call | tf_op jit(solution)/shard_map/pallas_call | solution.py:379
  364.6 21.1 %shard_map.336 = (bf16[2,768,1024]{2,1,0:T(8,128)(2,1)}, f32[768,896]{1,0:T(8,128)}) custom-call(s32[2,5]{1,0:T(2,128)} %copy.89.bounds_ref, f32[2,1024,768]{2,1,0:T(8,128)} %get-tuple-element.77.v_ref, bf16[2,1024,768]{2,1,0:T(8,128)(2,1)} %bitcast.110, bf16[768,768]{1,0:T(8,128)(2,1)} %bitcast.114, ...), custom_call_target="tpu_custom_call", output_to_operand_aliasing={{0}: (8, {}), {1}: (9, {})} | custom-call | tf_op jit(solution)/shard_map/pallas_call | solution.py:379
  385.8 2.3 collective-permute-start.18
  388.1 21.3 %shard_map.337 = (bf16[2,768,1024]{2,1,0:T(8,128)(2,1)}, f32[768,896]{1,0:T(8,128)}) custom-call(s32[2,5]{1,0:T(2,128)} %copy.89.bounds_ref, f32[2,1024,768]{2,1,0:T(8,128)} %get-tuple-element.77.v_ref, bf16[2,1024,768]{2,1,0:T(8,128)(2,1)} %bitcast.111, bf16[768,768]{1,0:T(8,128)(2,1)} %bitcast.115, ...), custom_call_target="tpu_custom_call", output_to_operand_aliasing={{0}: (8, {}), {1}: (9, {})} | custom-call | tf_op jit(solution)/shard_map/pallas_call | solution.py:379
  411.0 4.7 %fusion.9 = f32[2,1024,768]{2,1,0:T(8,128)S(1)} fusion(bf16[2,768,1024]{2,1,0:T(8,128)(2,1)} %get-tuple-element.75, bf16[768,768,1]{1,0,2:T(8,128)(2,1)S(1)} %bitcast.136), kind=kOutput, calls=%fused_computation.103 | convolution fusion | flops 2415919104 | bytes 10616832 | tf_op jit(solution)/shard_map/bot,oi->bti/dot_general | solution.py:652
  417.6 2.7 fusion
  420.4 6.2 %collective-permute-done.21 = bf16[2,2,1,2,1,24,896]{6,5,4,3,2,1,0:T(8,128)(2,1)S(1)} collective-permute-done((bf16[2,2,1,2,1,24,896]{6,5,4,3,2,1,0:T(8,128)(2,1)S(1)}, bf16[2,2,1,2,1,24,896]{6,5,4,3,2,1,0:T(8,128)(2,1)S(1)}, u32[]{:S(2)}, u32[]{:S(2)}) %collective-permute-start.21) | collective-permute-done | bytes 344096 | tf_op jit(solution)/shard_map/ppermute | solution.py:514
  428.8 4.8 %add_add_fusion = f32[2,1024,768]{2,1,0:T(8,128)} fusion(f32[2,1024,768]{2,1,0:T(8,128)S(1)} %fusion, f32[2,1024,768]{2,1,0:T(8,128)S(1)} %bitcast.134, f32[2,1024,768]{2,1,0:T(8,128)S(1)} %fusion.9, bf16[2,768,1024]{2,1,0:T(8,128)(2,1)S(1)} %copy-done.7, bf16[768,768,1]{1,0,2:T(8,128)(2,1)S(1)} %bitcast.125), kind=kOutput, calls=%fused_computation | convolution fusion | flops 2420637696 | bytes 29491200 | tf_op jit(solution)/shard_map/bot,oi->bti/dot_general | solution.py:652
  435.7 2.5 collective-permute-done.23
  438.3 2.7 collective-permute-start.24
  (177 shorter events, 79.1 us)
Async XLA Ops:
  7.2 145.3 %all-gather.3.cloned.1.call-start = ((), (), s32[]{:S(2)}) async-start(), calls=%async_computation.2 | async-start | bytes 10948608 | tf_op jit(solution)/shard_map/all_gather | solution.py:601
  15.6 8.0 %collective-permute-start.10 = (bf16[1,1,1,1,1,24,896]{6,5,4,3,2,1,0:T(8,128)(2,1)S(1)}, bf16[1,1,1,1,1,24,896]{6,5,4,3,2,1,0:T(8,128)(2,1)S(1)}, u32[]{:S(2)}, u32[]{:S(2)}) collective-permute-start(bf16[1,1,1,1,1,24,896]{6,5,4,3,2,1,0:T(8,128)(2,1)S(1)} %fusion.5), channel_id=1, source_target_pairs={{0,16},{4,20},{8,24},{12,28},{16,0},{20,4},{24,8},{28,12},{1,17},{... | collective-permute-start | bytes 129032 | tf_op jit(solution)/shard_map/ppermute | solution.py:514
  24.5 4.6 collective-permute-start.11
  29.1 416.9 %reduce-scatter.2.cloned.1.call-start = ((), (), s32[]{:S(2)}) async-start(), calls=%async_computation.1 | async-start | bytes 11354112 | tf_op jit(solution)/shard_map/reduce_scatter | solution.py:622
  29.2 9.4 %collective-permute-start = (bf16[1,1,1,1,1,24,768]{6,5,4,3,2,1,0:T(8,128)(2,1)}, bf16[1,1,1,1,1,24,768]{6,5,4,3,2,1,0:T(8,128)(2,1)S(1)}, u32[]{:S(2)}, u32[]{:S(2)}) collective-permute-start(bf16[1,1,1,1,1,24,768]{6,5,4,3,2,1,0:T(8,128)(2,1)} %bitcast.148), channel_id=1, source_target_pairs={{0,16},{4,20},{8,24},{12,28},{16,0},{20,4},{24,8},{28,12},{1,17},{... | collective-permute-start | bytes 110600 | tf_op jit(solution)/shard_map/ppermute | solution.py:514
  30.2 8.4 %collective-permute-start.5 = (bf16[1,1,1,1,1,24,768]{6,5,4,3,2,1,0:T(8,128)(2,1)}, bf16[1,1,1,1,1,24,768]{6,5,4,3,2,1,0:T(8,128)(2,1)S(1)}, u32[]{:S(2)}, u32[]{:S(2)}) collective-permute-start(bf16[1,1,1,1,1,24,768]{6,5,4,3,2,1,0:T(8,128)(2,1)} %bitcast.147), channel_id=1, source_target_pairs={{0,16},{4,20},{8,24},{12,28},{16,0},{20,4},{24,8},{28,12},{1,17},{... | collective-permute-start | bytes 110600 | tf_op jit(solution)/shard_map/ppermute | solution.py:514
  38.6 5.1 %collective-permute-start.6 = (bf16[2,1,1,1,1,24,768]{6,5,4,3,2,1,0:T(8,128)(2,1)S(1)}, bf16[2,1,1,1,1,24,768]{6,5,4,3,2,1,0:T(8,128)(2,1)S(1)}, u32[]{:S(2)}, u32[]{:S(2)}) collective-permute-start(bf16[2,1,1,1,1,24,768]{6,5,4,3,2,1,0:T(8,128)(2,1)S(1)} %pad_maximum_fusion.14), channel_id=1, source_target_pairs={{0,2},{1,3},{2,0},{3,1},{4,6},{5,7},{6,4},{7,5},{8,10},{9,11},{10,... | collective-permute-start | bytes 221192 | tf_op jit(solution)/shard_map/ppermute | solution.py:514
  40.2 5.2 %collective-permute-start.1 = (bf16[2,1,1,1,1,24,768]{6,5,4,3,2,1,0:T(8,128)(2,1)S(1)}, bf16[2,1,1,1,1,24,768]{6,5,4,3,2,1,0:T(8,128)(2,1)S(1)}, u32[]{:S(2)}, u32[]{:S(2)}) collective-permute-start(bf16[2,1,1,1,1,24,768]{6,5,4,3,2,1,0:T(8,128)(2,1)S(1)} %pad_maximum_fusion.13), channel_id=1, source_target_pairs={{0,4},{4,0},{8,12},{12,8},{16,20},{20,16},{24,28},{28,24},{1,5},{5... | collective-permute-start | bytes 221192 | tf_op jit(solution)/shard_map/ppermute | solution.py:514
  43.7 5.2 %collective-permute-start.7 = (bf16[2,1,1,2,1,24,768]{6,5,4,3,2,1,0:T(8,128)(2,1)S(1)}, bf16[2,1,1,2,1,24,768]{6,5,4,3,2,1,0:T(8,128)(2,1)S(1)}, u32[]{:S(2)}, u32[]{:S(2)}) collective-permute-start(bf16[2,1,1,2,1,24,768]{6,5,4,3,2,1,0:T(8,128)(2,1)S(1)} %pad_maximum_fusion.11), channel_id=1, source_target_pairs={{0,4},{4,0},{8,12},{12,8},{16,20},{20,16},{24,28},{28,24},{1,5},{5... | collective-permute-start | bytes 442376 | tf_op jit(solution)/shard_map/ppermute | solution.py:514
  45.5 8.9 %collective-permute-start.2 = (bf16[2,1,2,1,1,24,768]{6,5,4,3,2,1,0:T(8,128)(2,1)S(1)}, bf16[2,1,2,1,1,24,768]{6,5,4,3,2,1,0:T(8,128)(2,1)S(1)}, u32[]{:S(2)}, u32[]{:S(2)}) collective-permute-start(bf16[2,1,2,1,1,24,768]{6,5,4,3,2,1,0:T(8,128)(2,1)S(1)} %pad_maximum_fusion.10), channel_id=1, source_target_pairs={{0,8},{4,12},{8,0},{12,4},{16,24},{20,28},{24,16},{28,20},{1,9},{5... | collective-permute-start | bytes 442376 | tf_op jit(solution)/shard_map/ppermute | solution.py:514
  47.1 8.6 %collective-permute-start.12 = (bf16[2,2,1,1,1,24,896]{6,5,4,3,2,1,0:T(8,128)(2,1)S(1)}, bf16[2,2,1,1,1,24,896]{6,5,4,3,2,1,0:T(8,128)(2,1)S(1)}, u32[]{:S(2)}, u32[]{:S(2)}) collective-permute-start(bf16[2,2,1,1,1,24,896]{6,5,4,3,2,1,0:T(8,128)(2,1)S(1)} %pad_maximum_fusion.9), channel_id=1, source_target_pairs={{0,2},{1,3},{2,0},{3,1},{4,6},{5,7},{6,4},{7,5},{8,10},{9,11},{10,... | collective-permute-start | bytes 516104 | tf_op jit(solution)/shard_map/ppermute | solution.py:514
  49.0 10.3 %collective-permute-start.8 = (bf16[2,1,2,2,1,24,768]{6,5,4,3,2,1,0:T(8,128)(2,1)S(1)}, bf16[2,1,2,2,1,24,768]{6,5,4,3,2,1,0:T(8,128)(2,1)S(1)}, u32[]{:S(2)}, u32[]{:S(2)}) collective-permute-start(bf16[2,1,2,2,1,24,768]{6,5,4,3,2,1,0:T(8,128)(2,1)S(1)} %pad_maximum_fusion.8), channel_id=1, source_target_pairs={{0,8},{4,12},{8,0},{12,4},{16,24},{20,28},{24,16},{28,20},{1,9},{5... | collective-permute-start | bytes 884744 | tf_op jit(solution)/shard_map/ppermute | solution.py:514
  54.4 8.3 %collective-permute-start.3 = (bf16[2,2,2,1,1,24,768]{6,5,4,3,2,1,0:T(8,128)(2,1)S(1)}, bf16[2,2,2,1,1,24,768]{6,5,4,3,2,1,0:T(8,128)(2,1)S(1)}, u32[]{:S(2)}, u32[]{:S(2)}) collective-permute-start(bf16[2,2,2,1,1,24,768]{6,5,4,3,2,1,0:T(8,128)(2,1)S(1)} %pad_maximum_fusion.7), channel_id=1, source_target_pairs={{0,2},{1,3},{2,0},{3,1},{4,6},{5,7},{6,4},{7,5},{8,10},{9,11},{10,... | collective-permute-start | bytes 884744 | tf_op jit(solution)/shard_map/ppermute | solution.py:514
  55.8 12.8 %collective-permute-start.13 = (bf16[2,2,1,2,1,24,896]{6,5,4,3,2,1,0:T(8,128)(2,1)S(1)}, bf16[2,2,1,2,1,24,896]{6,5,4,3,2,1,0:T(8,128)(2,1)S(1)}, u32[]{:S(2)}, u32[]{:S(2)}) collective-permute-start(bf16[2,2,1,2,1,24,896]{6,5,4,3,2,1,0:T(8,128)(2,1)S(1)} %pad_maximum_fusion.6), channel_id=1, source_target_pairs={{0,4},{4,0},{8,12},{12,8},{16,20},{20,16},{24,28},{28,24},{1,5},{5... | collective-permute-start | bytes 1032200 | tf_op jit(solution)/shard_map/ppermute | solution.py:514
  59.4 9.4 %collective-permute-start.9 = (bf16[2,2,2,2,1,24,768]{6,5,4,3,2,1,0:T(8,128)(2,1)S(1)}, bf16[2,2,2,2,1,24,768]{6,5,4,3,2,1,0:T(8,128)(2,1)S(1)}, u32[]{:S(2)}, u32[]{:S(2)}) collective-permute-start(bf16[2,2,2,2,1,24,768]{6,5,4,3,2,1,0:T(8,128)(2,1)S(1)} %pad_maximum_fusion.5), channel_id=1, source_target_pairs={{0,1},{1,0},{2,3},{3,2},{4,5},{5,4},{6,7},{7,6},{8,9},{9,8},{10,11... | collective-permute-start | bytes 1769480 | tf_op jit(solution)/shard_map/ppermute | solution.py:514
  62.9 7.2 %collective-permute-start.4 = (bf16[2,2,2,2,1,24,768]{6,5,4,3,2,1,0:T(8,128)(2,1)S(1)}, bf16[2,2,2,2,1,24,768]{6,5,4,3,2,1,0:T(8,128)(2,1)S(1)}, u32[]{:S(2)}, u32[]{:S(2)}) collective-permute-start(bf16[2,2,2,2,1,24,768]{6,5,4,3,2,1,0:T(8,128)(2,1)S(1)} %pad_maximum_fusion.4), channel_id=1, source_target_pairs={{0,1},{1,0},{2,3},{3,2},{4,5},{5,4},{6,7},{7,6},{8,9},{9,8},{10,11... | collective-permute-start | bytes 1769480 | tf_op jit(solution)/shard_map/ppermute | solution.py:514
  336.1 27.1 %collective-permute-start.16 = (bf16[2,2,2,2,1,1,24,768]{7,6,5,4,3,2,1,0:T(8,128)(2,1)}, bf16[2,2,2,2,1,1,24,768]{7,6,5,4,3,2,1,0:T(8,128)(2,1)}, u32[]{:S(2)}, u32[]{:S(2)}) collective-permute-start(bf16[2,2,2,2,1,1,24,768]{7,6,5,4,3,2,1,0:T(8,128)(2,1)} %dynamic-slice_convert_fusion.2), channel_id=1, source_target_pairs={{0,2},{1,3},{2,0},{3,1},{4,6},{5,7},{6,4},{7,5},{8,10},{9,11},{10,... | collective-permute-start | bytes 1769480 | tf_op jit(solution)/shard_map/ppermute | solution.py:514
  364.5 21.2 %collective-permute-start.17 = (bf16[2,2,1,2,1,1,24,768]{7,6,5,4,3,2,1,0:T(8,128)(2,1)S(1)}, bf16[2,2,1,2,1,1,24,768]{7,6,5,4,3,2,1,0:T(8,128)(2,1)S(1)}, u32[]{:S(2)}, u32[]{:S(2)}) collective-permute-start(bf16[2,2,1,2,1,1,24,768]{7,6,5,4,3,2,1,0:T(8,128)(2,1)S(1)} %dynamic-slice_convert_fusion.4), channel_id=1, source_target_pairs={{0,8},{4,12},{8,0},{12,4},{16,24},{20,28},{24,16},{28,20},{1,9},{5... | collective-permute-start | bytes 884744 | tf_op jit(solution)/shard_map/ppermute | solution.py:514
  385.8 23.6 %collective-permute-start.18 = (bf16[2,2,1,1,1,1,24,768]{7,6,5,4,3,2,1,0:T(8,128)(2,1)S(1)}, bf16[2,2,1,1,1,1,24,768]{7,6,5,4,3,2,1,0:T(8,128)(2,1)S(1)}, u32[]{:S(2)}, u32[]{:S(2)}) collective-permute-start(bf16[2,2,1,1,1,1,24,768]{7,6,5,4,3,2,1,0:T(8,128)(2,1)S(1)} %dynamic-slice_convert_fusion.6), channel_id=1, source_target_pairs={{0,4},{4,0},{8,12},{12,8},{16,20},{20,16},{24,28},{28,24},{1,5},{5... | collective-permute-start | bytes 442376 | tf_op jit(solution)/shard_map/ppermute | solution.py:514
  410.9 5.0 %collective-permute-start.20 = (bf16[2,2,2,2,1,24,896]{6,5,4,3,2,1,0:T(8,128)(2,1)S(1)}, bf16[2,2,2,2,1,24,896]{6,5,4,3,2,1,0:T(8,128)(2,1)S(1)}, u32[]{:S(2)}, u32[]{:S(2)}) collective-permute-start(bf16[2,2,2,2,1,24,896]{6,5,4,3,2,1,0:T(8,128)(2,1)S(1)} %dynamic-slice_convert_fusion.1), channel_id=1, source_target_pairs={{0,1},{1,0},{2,3},{3,2},{4,5},{5,4},{6,7},{7,6},{8,9},{9,8},{10,11... | collective-permute-start | bytes 2064392 | tf_op jit(solution)/shard_map/ppermute | solution.py:514
  415.8 19.9 %collective-permute-start.19 = (bf16[2,1,1,1,1,1,24,768]{7,6,5,4,3,2,1,0:T(8,128)(2,1)S(1)}, bf16[2,1,1,1,1,1,24,768]{7,6,5,4,3,2,1,0:T(8,128)(2,1)S(1)}, u32[]{:S(2)}, u32[]{:S(2)}) collective-permute-start(bf16[2,1,1,1,1,1,24,768]{7,6,5,4,3,2,1,0:T(8,128)(2,1)S(1)} %dynamic-slice_convert_fusion.8), channel_id=1, source_target_pairs={{0,16},{4,20},{8,24},{12,28},{16,0},{20,4},{24,8},{28,12},{1,17},{... | collective-permute-start | bytes 221192 | tf_op jit(solution)/shard_map/ppermute | solution.py:514
  416.1 10.5 %collective-permute-start.21 = (bf16[2,2,1,2,1,24,896]{6,5,4,3,2,1,0:T(8,128)(2,1)S(1)}, bf16[2,2,1,2,1,24,896]{6,5,4,3,2,1,0:T(8,128)(2,1)S(1)}, u32[]{:S(2)}, u32[]{:S(2)}) collective-permute-start(bf16[2,2,1,2,1,24,896]{6,5,4,3,2,1,0:T(8,128)(2,1)S(1)} %dynamic-slice_convert_fusion.3), channel_id=1, source_target_pairs={{0,4},{4,0},{8,12},{12,8},{16,20},{20,16},{24,28},{28,24},{1,5},{5... | collective-permute-start | bytes 1032200 | tf_op jit(solution)/shard_map/ppermute | solution.py:514
  426.7 6.9 %collective-permute-start.22 = (bf16[2,2,1,1,1,24,896]{6,5,4,3,2,1,0:T(8,128)(2,1)S(1)}, bf16[2,2,1,1,1,24,896]{6,5,4,3,2,1,0:T(8,128)(2,1)S(1)}, u32[]{:S(2)}, u32[]{:S(2)}) collective-permute-start(bf16[2,2,1,1,1,24,896]{6,5,4,3,2,1,0:T(8,128)(2,1)S(1)} %dynamic-slice_convert_fusion.5), channel_id=1, source_target_pairs={{0,2},{1,3},{2,0},{3,1},{4,6},{5,7},{6,4},{7,5},{8,10},{9,11},{10,... | collective-permute-start | bytes 516104 | tf_op jit(solution)/shard_map/ppermute | solution.py:514
  438.3 5.0 %collective-permute-start.24 = (bf16[1,1,1,1,1,24,896]{6,5,4,3,2,1,0:T(8,128)(2,1)S(1)}, bf16[1,1,1,1,1,24,896]{6,5,4,3,2,1,0:T(8,128)(2,1)S(1)}, u32[]{:S(2)}, u32[]{:S(2)}) collective-permute-start(bf16[1,1,1,1,1,24,896]{6,5,4,3,2,1,0:T(8,128)(2,1)S(1)} %dynamic-slice_convert_fusion.9), channel_id=1, source_target_pairs={{0,16},{4,20},{8,24},{12,28},{16,0},{20,4},{24,8},{28,12},{1,17},{... | collective-permute-start | bytes 129032 | tf_op jit(solution)/shard_map/ppermute | solution.py:514
  (19 other events, 264.9 us)
Sparse Core Ops, SparseCore 0:
  29.2 91.2 all-gather.2
  271.2 142.6 reduce-scatter.1

commit v5 on v4

--- a/solution.py
+++ b/solution.py
@@ -9,7 +9,7 @@
 
 BF = jnp.bfloat16
 F32 = jnp.float32
-HW=64; LM=64; NEWTON=6; GH=6; GW=GH*HW
+HW=64; LM=64; NEWTON=6; GH=12; GW=GH*HW
 CHUNK=256
 KW=33
 SMALL=48
@@ -23,7 +23,16 @@
     hi,lo=split(b); return jnp.concatenate([hi,lo,hi],axis=0)
 def mm3(a,b): return nn(wide(a),tall(b))
 def eye(c):
-    return jnp.where(lax.broadcasted_iota(jnp.int32,(LM,LM),0)==lax.broadcasted_iota(jnp.int32,(LM,LM),1),c,0.0)
+    row=lax.broadcasted_iota(jnp.int32,(LM,2*LM),0); col=lax.broadcasted_iota(jnp.int32,(LM,2*LM),1)
+    return jnp.where((row==col)|(row+LM==col),c,0.0)
+def beside(a):
+    return [jnp.concatenate([a[i],a[i+1]],axis=1) for i in range(0,len(a),2)]
+def blocks(b):
+    lane=lax.broadcasted_iota(jnp.int32,(1,2*LM),1)
+    first=jnp.where(lane<LM,1.0,0.0).astype(BF); second=jnp.where(lane<LM,0.0,1.0).astype(BF)
+    hi,lo=split(b)
+    return jnp.concatenate([hi*first,hi*second,lo*first,lo*second,hi*first,hi*second],axis=0)
+def mmb(a,b): return nn(wide(a),blocks(b))
 def weave(first, second):
     done=0
     for i,step in enumerate(first):
@@ -52,25 +61,25 @@
     lq=[lqt[r].T for r in rows]; lk=[lkt[r].T for r in rows]
     lqw=[wide(a) for a in lq]; lkw=[wide(a) for a in lk]
     allow2=ldc==ldr_ref[0]
-    k2=[];z=[]
+    k2=[];zt=[]
     for h in heads:
-        s=jnp.where(allow2,nn(lqw[h],tall(lkt[rows[h]])),-1e30)
-        e=jnp.exp(s-jnp.max(s,axis=1,keepdims=True))
+        sc=jnp.where(allow2,nn(lqw[h],tall(lkt[rows[h]])),-1e30)
+        e=jnp.exp(sc-jnp.max(sc,axis=1,keepdims=True))
         k2.append(e/jnp.sum(e,axis=1,keepdims=True))
-        z.append(k2[h].T*(1.0/jnp.sum(k2[h]*k2[h])))
-    state={"z":z}
-    k2w=[wide(a) for a in k2]
+        zt.append(k2[h]*(1.0/jnp.sum(k2[h]*k2[h])))
+    pairs=range(GH//2)
+    state={"zt":beside(zt)}
+    k2tb=[blocks(a) for a in beside([a.T for a in k2])]
     def newton(n):
         def one():
-            state["p"]=[nn(k2w[h],tall(state["z"][h])) for h in heads]
+            state["p"]=[nn(wide(state["zt"][i]),k2tb[i]) for i in pairs]
             state["pw"]=[wide(a) for a in state["p"]]
-        def two(): state["b"]=[eye(15.0)-nn(state["pw"][h],tall(eye(7.0)-state["p"][h])) for h in heads]
-        def three(): state["c"]=[eye(13.0)-nn(state["pw"][h],tall(state["b"][h])) for h in heads]
+        def two(): state["b"]=[eye(15.0)-nn(state["pw"][i],blocks(eye(7.0)-state["p"][i])) for i in pairs]
+        def three(): state["c"]=[eye(13.0)-nn(state["pw"][i],blocks(state["b"][i])) for i in pairs]
         def four():
-            for h in heads:
-                stash_ref[0,h,2*n]=jnp.concatenate([state["p"][h],state["b"][h]],axis=1)
-                stash_ref[0,h,2*n+1]=jnp.concatenate([state["c"][h],state["z"][h].T],axis=1)
-            state["z"]=[0.25*mm3(state["z"][h],state["c"][h]) for h in heads]
+            for i in pairs:
+                for place,key in enumerate(("p","b","c","zt")): stash_ref[0,i,4*n+place]=state[key][i]
+            state["zt"]=[0.25*mmb(state["c"][i],state["zt"][i]) for i in pairs]
         return [one,two,three,four]
     chain=[step for n in range(NEWTON) for step in newton(n)]
     side=[]
@@ -121,9 +130,10 @@
     weave(chain,side)
     uts=[]
     for h in heads:
-        u=mm3(state["z"][h],r[h])
+        zt=state["zt"][h//2][:,h%2*LM:(h%2+1)*LM]
+        u=mm3(zt.T,r[h])
         small_ref[0,h,0]=jnp.concatenate([lq[h],lk[h]],axis=1)
-        small_ref[0,h,1]=jnp.concatenate([k2[h],state["z"][h].T],axis=1)
+        small_ref[0,h,1]=jnp.concatenate([k2[h],zt],axis=1)
         small_ref[0,h,2]=jnp.concatenate([r[h],u],axis=1)
         small_ref[0,h,3]=jnp.broadcast_to(sums[h],(LM,128))
         uts.append(u.T.astype(BF))
@@ -134,8 +144,8 @@
     seq=lambda s: pl.BlockSpec((1,)+s,lambda g,b:(b,)+(0,)*len(s))
     wsp=pl.BlockSpec((GW,D),lambda g,b:(g,0)); bsp=pl.BlockSpec((GW,1),lambda g,b:(g,0))
     rows=pl.BlockSpec((1,GW,T),lambda g,b:(b,g,0)); cols=pl.BlockSpec((1,T,GW),lambda g,b:(b,0,g))
-    sq=lambda n: pl.BlockSpec((1,GH,n,LM,2*LM),lambda g,b:(b,g,0,0,0))
-    turned=pl.BlockSpec((1,1,8,T),lambda g,b:(b,g,0,0))
+    sq=lambda m,n: pl.BlockSpec((1,m,n,LM,2*LM),lambda g,b:(b,g,0,0,0))
+    turned=pl.BlockSpec((1,1,-(-GH//8)*8,T),lambda g,b:(b,g,0,0))
     return seq,wsp,bsp,rows,cols,sq,turned
 def att_fwd(x,mean,wq,wk,wv,vec,tok,ld,conv):
     B,T,D=x.shape; G=D//GW; H=D//HW
@@ -143,8 +153,8 @@
     sd=jax.ShapeDtypeStruct; big=sd((B,D,T),BF)
     return pl.pallas_call(att_fwd_kernel,grid=(G,B),
         in_specs=[seq((T,D)),seq((LM,D)),wsp,wsp,wsp,pl.BlockSpec((SMALL,GW),lambda g,b:(0,g)),seq((1,T)),seq((LM,1)),seq((1,LM)),cols],
-        out_specs=[rows]*5+[turned,sq(2*NEWTON),sq(4),cols],
-        out_shape=[big]*5+[sd((B,G,8,T),F32),sd((B,H,2*NEWTON,LM,2*LM),F32),sd((B,H,4,LM,2*LM),F32),sd((B,T,D),BF)],
+        out_specs=[rows]*5+[turned,sq(GH//2,4*NEWTON),sq(GH,4),cols],
+        out_shape=[big]*5+[sd((B,G,-(-GH//8)*8,T),F32),sd((B,H//2,4*NEWTON,LM,2*LM),F32),sd((B,H,4,LM,2*LM),F32),sd((B,T,D),BF)],
         scratch_shapes=[pltpu.VMEM((GW,T),BF)]*2+[pltpu.VMEM((GW,T),F32),pltpu.VMEM((LM,T),F32)],
         compiler_params=pltpu.CompilerParams(vmem_limit_bytes=60*2**20))(
             x,mean,wq,wk,wv,vec,tok[:,None,:],ld[:,:,None],ld[:,None,:],conv)
@@ -178,7 +188,7 @@
     for cs in chunks: upstream(cs)()
     du=[nt(k1_ref[0,rows[h]],g_ref[rows[h],:]) for h in heads]
     dr=[mm3(zt[h],du[h]) for h in heads]
-    state={"dz":[mm3(du[h],r[h].T) for h in heads],"dk2":[None]*GH}
+    state={"dz":beside([mm3(du[h],r[h].T) for h in heads]),"dk2":[None]*(GH//2)}
     drs=[(dr[h]*inv[h]) for h in heads]
     drb=[a.astype(BF) for a in drs]; drt=[a.T.astype(BF) for a in drs]
     delta=[jnp.sum(drb[h].astype(F32)*r[h],axis=1,keepdims=True) for h in heads]
@@ -205,31 +215,31 @@
     side=[]
     for h in heads: side+=[third(h,cs) for cs in chunks]+[to_lq(h)]+[first(h,cs) for cs in chunks]+[to_lk(h)]
     side+=[values(cs) for cs in chunks]
-    k2t=[a.T for a in k2]; k2tw=[wide(a) for a in k2t]
+    pairs=range(GH//2)
+    k2t=[a.T for a in k2]; k2tw=[wide(a) for a in beside(k2t)]
     def newton(n):
         def one():
-            a=[stash_ref[0,h,2*n] for h in heads]; c=[stash_ref[0,h,2*n+1] for h in heads]
-            state["p"]=[m[:,:LM] for m in a]; state["b"]=[tall(m[:,LM:]) for m in a]
-            state["c"]=[tall(m[:,:LM]) for m in c]; state["zt"]=[m[:,LM:] for m in c]
+            state["p"],state["b"],state["c"],state["zt"]=[[stash_ref[0,i,4*n+place] for i in pairs] for place in range(4)]
             state["gz"]=[0.25*d for d in state["dz"]]
-            state["dc"]=[mm3(state["zt"][h],state["gz"][h]) for h in heads]
+            state["dc"]=[mmb(state["zt"][i],state["gz"][i]) for i in pairs]
             state["pw"]=[wide(m) for m in state["p"]]
-        def two(): state["db"]=[nn(state["pw"][h],tall(state["dc"][h])) for h in heads]
+        def two(): state["db"]=[nn(state["pw"][i],blocks(state["dc"][i])) for i in pairs]
         def three():
-            da=[nn(state["pw"][h],tall(state["db"][h])) for h in heads]
-            state["dp"]=[mm3(state["db"][h],eye(7.0)-state["p"][h])-nn(wide(state["dc"][h]),state["b"][h])-da[h] for h in heads]
+            da=[nn(state["pw"][i],blocks(state["db"][i])) for i in pairs]
+            state["dp"]=[mmb(state["db"][i],eye(7.0)-state["p"][i])-mmb(state["dc"][i],state["b"][i])-da[i] for i in pairs]
         def four():
-            for h in heads:
-                t=mm3(state["dp"][h],state["zt"][h])
-                state["dk2"][h]=t if state["dk2"][h] is None else state["dk2"][h]+t
-            state["dz"]=[nn(wide(state["gz"][h]),state["c"][h])+nn(k2tw[h],tall(state["dp"][h])) for h in heads]
+            for i in pairs:
+                t=mmb(state["dp"][i],state["zt"][i])
+                state["dk2"][i]=t if state["dk2"][i] is None else state["dk2"][i]+t
+            state["dz"]=[mmb(state["gz"][i],state["c"][i])+nn(k2tw[i],blocks(state["dp"][i])) for i in pairs]
         return [one,two,three,four]
     chain=[step for n in reversed(range(NEWTON)) for step in newton(n)]
     weave(chain,side)
     lhq=[];lhk=[]
     for h in heads:
-        i2=1.0/jnp.sum(k2[h]*k2[h]); dz=state["dz"][h]
-        d=state["dk2"][h]+i2*dz.T-k2[h]*(2.0*i2*i2*jnp.sum(dz*k2t[h]))
+        half=slice(h%2*LM,(h%2+1)*LM)
+        i2=1.0/jnp.sum(k2[h]*k2[h]); dz=state["dz"][h//2][:,half]
+        d=state["dk2"][h//2][:,half]+i2*dz.T-k2[h]*(2.0*i2*i2*jnp.sum(dz*k2t[h]))
         d=k2[h]*(d-jnp.sum(k2[h]*d,axis=1,keepdims=True))
         dlqh=dlq[h]+mm3(d,lk[h]); dlkh=dlk[h]+mm3(d.T,lq[h])
         lhq.append(jnp.concatenate([lk[h].T,dlqh.T*per],axis=1).astype(BF))
@@ -248,7 +258,7 @@
     seq,wsp,bsp,rows,cols,sq,turned=att_specs(D,T)
     sd=jax.ShapeDtypeStruct; big=sd((B,D,T),BF)
     return pl.pallas_call(att_bwd_kernel,grid=(G,B),
-        in_specs=[seq((T,D)),seq((T,D)),wsp]+[rows]*5+[turned,sq(2*NEWTON),sq(4),seq((1,T))],
+        in_specs=[seq((T,D)),seq((T,D)),wsp]+[rows]*5+[turned,sq(GH//2,4*NEWTON),sq(GH,4),seq((1,T))],
         out_specs=[rows]*3+[pl.BlockSpec((2,GW,D),lambda g,b:(0,g,0)),bsp],
         out_shape=[big,big,sd((B,D,T),F32),sd((2,D,D),F32),sd((D,1),F32)],
         scratch_shapes=[pltpu.VMEM((GW,T),BF)]*3+[pltpu.VMEM((LM,T),BF)],
@@ -285,47 +295,55 @@
         acc=part if acc is None else jnp.where(row>=bounds[d],part,acc)
     return acc
 BLOCK=64
+TALL=128
+WIDTH=256
+SLABS=range(WIDTH//128)
 def taps(ref, base, weight, sign):
     acc=None
     for r in range(8):
-        win=ref[pl.ds(base+r,BLOCK+32),:] if r==0 else ref[pl.ds(base+r,BLOCK+24),:]
+        win=ref[pl.ds(base+r,TALL+32),:] if r==0 else ref[pl.ds(base+r,TALL+24),:]
         for a in range(5 if r==0 else 4):
             o=8*a+r
-            t=weight(o if sign>0 else 2*HALF-o)*win[8*a:8*a+BLOCK]
+            t=weight(o if sign>0 else 2*HALF-o)*win[8*a:8*a+TALL]
             acc=t if acc is None else acc+t
     return acc
 
+def cut(h): return slice(h*128,(h+1)*128)
 def conv_fwd_kernel(bounds_ref, x_ref, wv_ref, w_ref, v_ref, out_ref, pad_ref, res_ref):
     b=pl.program_id(0)
     bounds=[bounds_ref[b,d] for d in range(DOCS+1)]
     length=v_ref.shape[1]; total=length+GAP*(DOCS+1)
-    pad_ref[0:HALF,:]=jnp.zeros((HALF,128),F32); pad_ref[HALF+total:,:]=jnp.zeros((pad_ref.shape[0]-HALF-total,128),F32)
     for lo in range(0,length,256):
         v_ref[0,lo:lo+256,:]=nt(x_ref[0,lo:lo+256,:],wv_ref[...])+w_ref[KW+1:KW+2,:]
-    spread(pad_ref, lambda lo,n: v_ref[0,lo:lo+n,:], bounds, length, BLOCK)
+    for h in SLABS:
+        pad_ref[h,0:HALF,:]=jnp.zeros((HALF,128),F32)
+        pad_ref[h,HALF+total:,:]=jnp.zeros((pad_ref.shape[1]-HALF-total,128),F32)
+        spread(pad_ref.at[h], lambda lo,n: v_ref[0,lo:lo+n,cut(h)], bounds, length, BLOCK)
     def block(i,c):
-        base=pl.multiple_of(i*BLOCK,BLOCK)
-        res_ref[pl.ds(base,BLOCK),:]=taps(pad_ref, base, lambda s: w_ref[s:s+1,:], 1)
+        base=pl.multiple_of(i*TALL,TALL)
+        for h in SLABS:
+            res_ref[h,pl.ds(base,TALL),:]=taps(pad_ref.at[h], base, lambda s: w_ref[s:s+1,cut(h)], 1)
         return c
-    lax.fori_loop(0,-(-total//BLOCK),block,0)
-    for lo in range(0,length,BLOCK):
-        out_ref[0,lo:lo+BLOCK,:]=collect(res_ref,bounds,lo,BLOCK)
+    lax.fori_loop(0,-(-total//TALL),block,0)
+    for h in SLABS:
+        for lo in range(0,length,BLOCK):
+            out_ref[0,lo:lo+BLOCK,cut(h)]=collect(res_ref.at[h],bounds,lo,BLOCK)
 def padded_rows(length):
     total=length+GAP*(DOCS+1)
-    return -(-total//BLOCK)*BLOCK
+    return -(-total//TALL)*TALL
 
 def conv_fwd(bounds, x, w_v, w):
     B,L,D=x.shape
     rows=padded_rows(L)
-    slab=pl.BlockSpec((1,L,128),lambda b,c,_:(b,0,c)); big=jax.ShapeDtypeStruct((B,L,D),F32)
-    return pl.pallas_call(conv_fwd_kernel,grid_spec=pltpu.PrefetchScalarGridSpec(num_scalar_prefetch=1,grid=(B,D//128),
-        in_specs=[pl.BlockSpec((1,L,D),lambda b,c,_:(b,0,0)),pl.BlockSpec((128,D),lambda b,c,_:(c,0)),
-            pl.BlockSpec((SMALL,128),lambda b,c,_:(0,c))],
+    slab=pl.BlockSpec((1,L,WIDTH),lambda b,c,_:(b,0,c)); big=jax.ShapeDtypeStruct((B,L,D),F32)
+    return pl.pallas_call(conv_fwd_kernel,grid_spec=pltpu.PrefetchScalarGridSpec(num_scalar_prefetch=1,grid=(B,D//WIDTH),
+        in_specs=[pl.BlockSpec((1,L,D),lambda b,c,_:(b,0,0)),pl.BlockSpec((WIDTH,D),lambda b,c,_:(c,0)),
+            pl.BlockSpec((SMALL,WIDTH),lambda b,c,_:(0,c))],
         out_specs=[slab,slab],
-        scratch_shapes=[pltpu.VMEM((rows+2*HALF+8,128),F32),pltpu.VMEM((rows,128),F32)]),
+        scratch_shapes=[pltpu.VMEM((WIDTH//128,rows+2*HALF+8,128),F32),pltpu.VMEM((WIDTH//128,rows,128),F32)]),
         out_shape=[big,big],
         compiler_params=pltpu.CompilerParams(vmem_limit_bytes=60*2**20))(bounds,x,w_v,w)
-def conv_bwd_kernel(bounds_ref, v_ref, al_ref, wo_ref, w_ref, x_ref, att_ref, more_ref, *refs):
+def conv_bwd_kernel(bounds_ref, v_ref, al_ref, wo_ref, w_ref, x_ref, att_ref, q_ref, sums_ref, su_ref, *refs):
     dv_ref, gv_ref, vpad_ref, gpad_ref, res_ref, acc_ref, g_ref, sum_ref = refs[-8:]
     b=pl.program_id(1)
     bounds=[bounds_ref[b,d] for d in range(DOCS+1)]
@@ -368,23 +386,29 @@
         rows=[jnp.sum(acc_ref[s],axis=0,keepdims=True) for s in range(KW)]
         side=jnp.concatenate(rows+[jnp.zeros((128-KW,128),F32)],axis=0).T
         lane=lax.broadcasted_iota(jnp.int32,(128,128),1)
-        gv_ref[:,depth:]=more_ref[...]+side+jnp.where(lane==KW,sum_ref[:,:1],0.0)
+        lines=su_ref.shape[1]
+        side=side+jnp.where(lane==KW,sum_ref[:,:1],0.0)+jnp.where(lane==KW+1,q_ref[...],0.0)
+        early=sums_ref[...].T
+        for i in range(6): side=side+jnp.where(lane==KW+2+i,early[:,i:i+1],0.0)
+        for i in range(lines): side=side+jnp.where(lane==KW+8+i,su_ref[:,i:i+1],0.0)
+        gv_ref[:,depth:]=side
 def conv_bwd(bounds, v, al, w_o, w, x, att, more, before, slabs, at):
     B,L,D=v.shape
     rows=padded_rows(L)
     sd=jax.ShapeDtypeStruct
     seq=pl.BlockSpec((1,L,D),lambda c,b,_:(b,0,0))
     feats=pl.BlockSpec((1,128,L),lambda c,b,_:(b,at+c,0))
-    alias={9:0,10:1} if before else {}
+    alias={11:0,12:1} if before else {}
     return pl.pallas_call(conv_bwd_kernel,grid_spec=pltpu.PrefetchScalarGridSpec(num_scalar_prefetch=1,grid=(slabs,B),
         in_specs=[pl.BlockSpec((1,L,128),lambda c,b,_:(b,0,at+c)),seq,
             pl.BlockSpec((D,128),lambda c,b,_:(0,at+c)),pl.BlockSpec((SMALL,128),lambda c,b,_:(0,at+c)),
-            seq,feats,pl.BlockSpec((128,128),lambda c,b,_:(at+c,0))]+[pl.BlockSpec(memory_space=pl.ANY)]*len(before),
+            seq,feats,pl.BlockSpec((128,1),lambda c,b,_:(at+c,0)),pl.BlockSpec((8,128),lambda c,b,_:(0,at+c)),
+            pl.BlockSpec((128,more[2].shape[1]),lambda c,b,_:(at+c,0))]+[pl.BlockSpec(memory_space=pl.ANY)]*len(before),
         out_specs=[feats,pl.BlockSpec((128,D+128),lambda c,b,_:(at+c,0))],
         scratch_shapes=[pltpu.VMEM((rows+2*HALF+8,128),F32)]*2+[pltpu.VMEM((rows,128),F32),pltpu.VMEM((KW,8,128),F32),
             pltpu.VMEM((L,128),F32),pltpu.VMEM((128,128),F32)]),
         out_shape=[sd((B,D,L),BF),sd((D,D+128),F32)],input_output_aliases={i-1:o for i,o in alias.items()},
-        compiler_params=pltpu.CompilerParams(vmem_limit_bytes=60*2**20))(bounds,v,al,w_o,w,x,att,more,*before)
+        compiler_params=pltpu.CompilerParams(vmem_limit_bytes=60*2**20))(bounds,v,al,w_o,w,x,att,*more,*before)
 
 def gelu_parts(x):
     size=jnp.abs(x)
@@ -400,51 +424,78 @@
 def norm_back(up,n,r,g):
     e=up*g
     return r*(e-jnp.mean(e,axis=-1,keepdims=True)-n*jnp.mean(e*n,axis=-1,keepdims=True))
-def ffn_kernel(chunks, ctx_ref,x_ref,cot_ref,wo_ref,wu_ref,wd_ref,vec_ref,bu_ref,
+def ffn_kernel(chunks, parts, ctx_ref,x_ref,cot_ref,wo_ref,wu_ref,wd_ref,vec_ref,bu_ref,
                out_ref,normed_ref,hidden_ref,down_ref,up_ref,one_ref,att_ref,sums_ref,sumu_ref,slope_ref):
-    width=wu_ref.shape[0]//chunks
+    wu=wu_ref[...].reshape(-1,wu_ref.shape[-1]); width=wu.shape[0]//chunks
+    size=x_ref.shape[0]//parts
     @pl.when(pl.program_id(0)==0)
     def _():
         sums_ref[...]=jnp.zeros_like(sums_ref); sumu_ref[...]=jnp.zeros_like(sumu_ref)
     v=lambda i: vec_ref[i:i+1,:]
     b_o,g1,s1,b_d,g2,s2=[v(KW+i) for i in range(2,8)]
-    n1,r1=norm(x_ref[...].astype(F32)+(nt(ctx_ref[...],wo_ref[...])+b_o))
-    normed=n1*g1+s1
-    low=normed.astype(BF); normed_ref[...]=low
-    down=None
-    for k in range(chunks):
-        part=slice(k*width,(k+1)*width)
-        pre=nt(low,wu_ref[part,:])+bu_ref[:,part]
-        dist,slope=gelu_parts(pre)
-        slope_ref[:,part]=dist+slope
-        hid=(pre*dist).astype(BF); hidden_ref[:,part]=hid
-        add=nt(hid,wd_ref[k]); down=add if down is None else down+add
-    n2,r2=norm(normed+(down+b_d))
-    out_ref[...]=(n2*g2+s2).astype(BF)
-    cot=cot_ref[...].astype(F32)
-    g_two=norm_back(cot,n2,r2,g2)
-    low2=g_two.astype(BF); down_ref[...]=low2
-    back=g_two
-    for k in range(chunks):
-        part=slice(k*width,(k+1)*width)
-        hg=nn(low2,wd_ref[k])
-        upl=(hg*slope_ref[:,part]).astype(BF); up_ref[:,part]=upl
-        sumu_ref[:,part]+=jnp.sum(upl.astype(F32),axis=0,keepdims=True)
-        back=back+nn(upl,wu_ref[part,:])
-    g_one=norm_back(back,n1,r1,g1)
-    one_ref[...]=g_one
-    al=g_one.astype(BF); att_ref[...]=al
-    s=lambda a: jnp.sum(a,axis=0,keepdims=True)
-    sums_ref[...]+=jnp.concatenate([s(al.astype(F32)),s(back*n1),s(back),s(low2.astype(F32)),s(cot*n2),s(cot),jnp.zeros((2,n1.shape[1]),F32)],axis=0)
-def ffn(ctx,x,cot,wo,wu,wd,vec,bu,block=512):
+    total=lambda a: jnp.sum(a,axis=0,keepdims=True)
+    def steps(at):
+        rows=slice(at*size,(at+1)*size); st={}
+        def attend(): st["one"]=nt(ctx_ref[rows,:],wo_ref[...])
+        def norm_one():
+            st["n1"],st["r1"]=norm(x_ref[rows,:].astype(F32)+(st["one"]+b_o))
+            st["normed"]=st["n1"]*g1+s1
+            st["low"]=st["normed"].astype(BF); normed_ref[rows,:]=st["low"]
+        def up(k):
+            def go():
+                if k>0:
+                    add=nt(st["hid"],wd_ref[k-1]); st["down"]=add if k==1 else st["down"]+add
+                if k<chunks: st["pre"]=nt(st["low"],wu[k*width:(k+1)*width,:])
+            return go
+        def gelu(k):
+            part=slice(k*width,(k+1)*width)
+            def go():
+                pre=st["pre"]+bu_ref[:,part]
+                dist,slope=gelu_parts(pre)
+                slope_ref[rows,part]=dist+slope
+                st["hid"]=(pre*dist).astype(BF); hidden_ref[rows,part]=st["hid"]
+            return go
+        def norm_two():
+            n2,r2=norm(st["normed"]+(st["down"]+b_d))
+            out_ref[rows,:]=(n2*g2+s2).astype(BF)
+            cot=cot_ref[rows,:].astype(F32)
+            st["back"]=norm_back(cot,n2,r2,g2)
+            st["low2"]=st["back"].astype(BF); down_ref[rows,:]=st["low2"]
+            sums_ref[3:6,:]+=jnp.concatenate([total(st["low2"].astype(F32)),total(cot*n2),total(cot)],axis=0)
+        def back(k):
+            def go():
+                if k>0: st["back"]=st["back"]+nn(st["upl"],wu[(k-1)*width:k*width,:])
+                if k<chunks: st["hg"]=nn(st["low2"],wd_ref[k])
+            return go
+        def scale(k):
+            part=slice(k*width,(k+1)*width)
+            def go():
+                upl=(st["hg"]*slope_ref[rows,part]).astype(BF); up_ref[rows,part]=upl; st["upl"]=upl
+                sumu_ref[:,part]+=total(upl.astype(F32))
+            return go
+        def norm_last():
+            g_one=norm_back(st["back"],st["n1"],st["r1"],g1)
+            one_ref[rows,:]=g_one
+            al=g_one.astype(BF); att_ref[rows,:]=al
+            sums_ref[0:3,:]+=jnp.concatenate([total(al.astype(F32)),total(st["back"]*st["n1"]),total(st["back"])],axis=0)
+        out=[attend,norm_one]
+        for k in range(chunks): out+=[up(k),gelu(k)]
+        out+=[up(chunks),norm_two]
+        for k in range(chunks): out+=[back(k),scale(k)]
+        return out+[back(chunks),norm_last]
+    lists=[steps(at) for at in range(parts)]
+    for i in range(len(lists[0])+parts-1):
+        for at in range(parts):
+            if 0<=i-at<len(lists[at]): lists[at][i-at]()
+def ffn(ctx,x,cot,wo,wu,wd,vec,bu,block=512,parts=2):
     chunks=wd.shape[0]
-    T,D=x.shape; F=wu.shape[0]
+    T,D=x.shape; F=bu.shape[1]
     row=lambda w: pl.BlockSpec((block,w),lambda i:(i,0))
     full=lambda a: pl.BlockSpec(a.shape,lambda i:(0,)*a.ndim,pipeline_mode=pl.Buffered(1))
     keep=lambda r,w: pl.BlockSpec((r,w),lambda i:(0,0))
     sd=jax.ShapeDtypeStruct
-    return pl.pallas_call(functools.partial(ffn_kernel,chunks),grid=(T//block,),
-        in_specs=[row(D),row(D),row(D),full(wo),full(wu),full(wd),pl.BlockSpec((SMALL,D),lambda i:(0,0)),full(bu)],
+    return pl.pallas_call(functools.partial(ffn_kernel,chunks,parts),grid=(T//block,),
+        in_specs=[row(D),row(D),row(D),full(wo),pl.BlockSpec((wu.shape[0],F//wu.shape[0],D),lambda i:(0,0,0),pipeline_mode=pl.Buffered(1)),full(wd),pl.BlockSpec((SMALL,D),lambda i:(0,0)),full(bu)],
         out_specs=[row(D),row(D),row(F),row(D),row(F),row(D),row(D),keep(8,D),keep(1,F)],
         out_shape=[sd((T,D),BF),sd((T,D),BF),sd((T,F),BF),sd((T,D),BF),sd((T,F),BF),sd((T,D),F32),sd((T,D),BF),sd((8,D),F32),sd((1,F),F32)],
         scratch_shapes=[pltpu.VMEM((block,F),F32)],
@@ -580,9 +631,11 @@
     tokens = batch_rows * sequence_length
     lines = b_up.shape[0] // own
     vectors = (b_query, b_value, b_out, gain_one, shift_one, b_down, gain_two, shift_two)
-    small = jnp.concatenate(
-        [conv_weight] + [vector[None] for vector in vectors] + [b_up.reshape(own, lines).T]
-    )
+    flat = 0
+    for place, vector in enumerate(vectors + (b_up,)):
+        before = place * own
+        flat = flat + jnp.pad(vector, (before, (8 + lines) * own - before - vector.shape[0]))
+    small = jnp.concatenate([conv_weight, flat.reshape(8 + lines, own)])
     small = jnp.pad(small.T, ((0, 0), (0, 128 - small.shape[0])))
     passed = []
     w_q = gather_rows(w_query.T, 1).reshape(feature_width, feature_width)
@@ -591,16 +644,17 @@
     gathered_v = gathered_v.reshape(feature_width, feature_width + 128)
     w_v = gathered_v[:, :feature_width]
     small = gathered_v[:, feature_width:]
-    b_u = small[:, KW + 8 : KW + 8 + lines].reshape(1, -1).astype(F32)
+    b_u = jnp.moveaxis(small[:, KW + 8 : KW + 8 + lines].reshape(group_count, own, lines), 1, 2)
+    b_u = b_u.reshape(1, -1).astype(F32)
     small = small.astype(F32).T
     ff_count = w_down.shape[0] // feature_width
+    w_out, w_up, w_down, _ = lax.optimization_barrier((w_out, w_up, w_down, passed[2]))
     shard = jnp.concatenate(
-        [w_out.T, w_up.T] + [w_down[i * feature_width : (i + 1) * feature_width].T for i in range(ff_count)]
+        [w_up.T, w_out.T] + [w_down[i * feature_width : (i + 1) * feature_width].T for i in range(ff_count)]
     )
-    shard, _ = lax.optimization_barrier((shard, passed[2]))
     gathered = lax.all_gather(shard, ("wide", "narrow"), axis=0)
-    w_o = gathered[:, :own].reshape(feature_width, feature_width)
-    w_u = gathered[:, own : own * (1 + lines)].reshape(-1, feature_width)
+    w_o = gathered[:, own * lines : own * (1 + lines)].reshape(feature_width, feature_width)
+    w_u = gathered if own * lines % 16 == 0 else gathered[:, : own * lines].reshape(1, -1, feature_width)
     w_d = jnp.moveaxis(
         gathered[:, own * (1 + lines) :].reshape(group_count, ff_count, own, feature_width), 0, 1
     ).reshape(ff_count, feature_width, feature_width)
@@ -625,27 +679,18 @@
     dq, dk, dv, grad_qk, sum_q = att_bwd(
         inputs, att_low, w_plain, q, k, v, k1, k3, inv, stash, landmarks, tok_landmark
     )
-    more = jnp.concatenate(
-        [
-            jnp.zeros((feature_width, KW + 1), F32),
-            sum_q,
-            sums[:6].T,
-            sums_up.reshape(feature_width, lines),
-            jnp.zeros((feature_width, 128 - KW - 8 - lines), F32),
-        ],
-        axis=1,
-    )
-    moving = scatter_step(scatter_start(grad_qk, own), 1, 0)
+    more = (sum_q, sums, sums_up.reshape(feature_width, lines))
+    moving = scatter_start(grad_qk, own)
     calls, before = 3, ()
     slabs = feature_width // 128 // calls
     for call in range(calls):
-        moved = scatter_step(moving, 1, 1 + call)
+        moved = scatter_step(moving, 1, call)
         before = conv_bwd(
             bounds, value_rows, att_low, w_o, small, inputs, dv, more, before, slabs, call * slabs
         )
         before, att_low, moving = lax.optimization_barrier((tuple(before), att_low, moved))
     dv, grad_v = before
-    share_qk = scatter_rest(moving, 1, 1 + calls)
+    share_qk = scatter_rest(moving, 1, calls)
     share_v = scatter_rest(scatter_start(grad_v, own), 0, 0)
     input_grad = grad_one.reshape(inputs.shape)
     for grad, weight in zip((dq, dk, dv), (w_q, w_k, w_v)):

time: 462 us -> 438 us (0.948)
  Pallas kernels: 303 us -> 281 us
  local copies, waits for them, and re-layouts: 47.4 us -> 32.8 us
  matrix products: 15.5 us -> 20.9 us
    pallas_call x1, Pallas kernels: 54.5 us -> 45.3 us  [att_bwd(): pl.pallas_call(att_bwd_kernel, grid=(G, B), in_specs=[seq((T, D)), seq((T...]
    pallas_call x1, Pallas kernels: 35 us -> 27.3 us  [conv_fwd(): pl.pallas_call(conv_fwd_kernel, grid_spec=pltpu.PrefetchScalarGridSpec(nu...]
    broadcast_in_dim x10 -> x0, local copies, waits for them, and re-layouts: 6.79 us -> none  [the longest x8 5.98 us: shards(): vector[None]]
    dot_general x3, matrix products: 12.3 us -> 17.6 us  [shards(): jnp.einsum('bot,oi->bti', grad, weight, preferred_element_type=F32)]
  transfers between devices with their start and end apart: 27 -> 27, of which waited for: 12 -> 12; matrix products, arithmetic and copies ran while one was open for 11% -> 10% of each run, Pallas kernels for 43% -> 41%
where the time goes in v5:
time: 438 us; the launch traced here: 432 us
  Pallas kernels  281 us (64%)
  waiting for transfers between devices  35.8 us (8%)
  local copies, waits for them, and re-layouts  32.8 us (7%)
  starting transfers between devices  32.5 us (7%)
  matrix products  20.9 us (5%)
  between operations  15.2 us (3%)
  other arithmetic  14.1 us (3%)
    pallas_call x1, Pallas kernels, ffn(): pl.pallas_call(functools.partial(ffn_kernel, chunks, parts), grid=(T // b...  69.8 us
    pallas_call x3, Pallas kernels, conv_bwd(): pl.pallas_call(conv_bwd_kernel, grid_spec=pltpu.PrefetchScalarGridSpec(nu...  65.9 us
    pallas_call x1, Pallas kernels, att_bwd(): pl.pallas_call(att_bwd_kernel, grid=(G, B), in_specs=[seq((T, D)), seq((T...  45.3 us
    pallas_call x1, Pallas kernels, att_fwd(): pl.pallas_call(att_fwd_kernel, grid=(G, B), in_specs=[seq((T, D)), seq((L...  39.7 us
    ppermute x25, waiting for transfers between devices, exchange(): lax.ppermute(values, axis, [(i, i ^ stride) for i in range(lax.axis_size(...  35.8 us
    pallas_call x1, Pallas kernels, weight_grads(): pl.pallas_call(functools.partial(weight_kernel, own), grid=(halves, T //...  33.2 us
    ppermute x25, starting transfers between devices, exchange(): lax.ppermute(values, axis, [(i, i ^ stride) for i in range(lax.axis_size(...  32.4 us
    pallas_call x1, Pallas kernels, conv_fwd(): pl.pallas_call(conv_fwd_kernel, grid_spec=pltpu.PrefetchScalarGridSpec(nu...  27.3 us
  transfers between devices with their start and end apart: 27, of which 12 were waited for; matrix products, arithmetic and copies ran while one was open for 10% of the time, Pallas kernels for 41%

profile of v5, /device:TPU:0, one launch (start us, length us, event | category | flops | bytes accessed | tf_op | source)
XLA Modules:
  0.0 432.3 jit_solution(2851878298720479253)
XLA Ops:
  9.9 4.0 collective-permute-start.10
  13.9 2.5 collective-permute-done.10
  18.7 3.0 collective-permute-done.11
  27.4 2.6 collective-permute-start
  31.3 3.3 convolution_divide_fusion.mean_ref
  40.2 2.5 collective-permute-done.6
  50.1 3.6 collective-permute-done.2
  58.6 4.0 collective-permute-done.3
  62.7 5.4 %collective-permute-done.13 = bf16[2,2,1,2,1,24,896]{6,5,4,3,2,1,0:T(8,128)(2,1)S(1)} collective-permute-done((bf16[2,2,1,2,1,24,896]{6,5,4,3,2,1,0:T(8,128)(2,1)S(1)}, bf16[2,2,1,2,1,24,896]{6,5,4,3,2,1,0:T(8,128)(2,1)S(1)}, u32[]{:S(2)}, u32[]{:S(2)}) %collective-permute-start.13) | collective-permute-done | bytes 344096 | tf_op jit(solution)/shard_map/ppermute | solution.py:565
  74.4 27.3 %shard_map.331 = (f32[2,1024,768]{2,1,0:T(8,128)}, f32[2,1024,768]{2,1,0:T(8,128)}) custom-call(s32[2,5]{1,0:T(2,128)} %copy.84.bounds_ref, bf16[2,1024,768]{2,1,0:T(8,128)(2,1)} %x_ref.11, bf16[768,768]{1,0:T(8,128)(2,1)} %slice.123.wv_ref, f32[128,768]{1,0:T(8,128)} %convert_bitcast_fusion.w_ref.vec_ref), custom_call_target="tpu_custom_call" | custom-call | tf_op jit(solution)/shard_map/pallas_call | solution.py:339
  101.7 39.7 %shard_map.332 = (bf16[2,768,1024]{2,1,0:T(8,128)(2,1)}, bf16[2,768,1024]{2,1,0:T(8,128)(2,1)}, bf16[2,768,1024]{2,1,0:T(8,128)(2,1)}, bf16[2,768,1024]{2,1,0:T(...) custom-call(bf16[2,1024,768]{2,1,0:T(8,128)(2,1)} %x_ref.11, ...), custom_call_target="tpu_custom_call" | custom-call | tf_op jit(solution)/shard_map/pallas_call | solution.py:154
  141.4 2.6 slice.126
  148.9 69.8 %shard_map.333 = (bf16[2048,768]{1,0:T(8,128)(2,1)}, bf16[2048,768]{1,0:T(8,128)(2,1)}, bf16[2048,3072]{1,0:T(8,128)(2,1)}, bf16[2048,768]{1,0:T(8,128)(2,1)}, b...) custom-call(bf16[2048,768]{1,0:T(8,128)(2,1)} %bitcast.118, ...), custom_call_target="tpu_custom_call" | custom-call | tf_op jit(solution)/shard_map/pallas_call | solution.py:497
  218.7 33.2 %shard_map.338 = bf16[32,224,768]{2,1,0:T(8,128)(2,1)} custom-call(bf16[2048,3072]{1,0:T(8,128)(2,1)} %get-tuple-element.104.up_ref, bf16[2048,768]{1,0:T(8,128)(2,1)} %get-tuple-element.105.normed_ref, bf16[2048,3072]{1,0:T(8,128)(2,1)} %get-tuple-element.106.hidden_ref, bf16[2048,768]{1,0:T(8,128)(2,1)} %get-tuple-element.107.down_ref, ...), custom_call_target="tpu_custom_call" | custom-call | tf_op jit(solution)/shard_map/pallas_call | solution.py:539
  254.6 45.3 %shard_map.334 = (bf16[2,768,1024]{2,1,0:T(8,128)(2,1)}, bf16[2,768,1024]{2,1,0:T(8,128)(2,1)}, f32[2,768,1024]{2,1,0:T(8,128)}, f32[2,768,768]{2,1,0:T(8,128)}, f32[768,1]{1,0:T(8,128)}) custom-call(bf16[2,1024,768]{2,1,0:T(8,128)(2,1)} %x_ref.11, bf16[2,1024,768]{2,1,0:T(8,128)(2,1)} %bitcast.102, bf16[768,768]{1,0:T(8,128)(2,1)} %copy.90.wo_ref, ...), custom_call_target="tpu_custom_call" | custom-call | tf_op jit(solution)/shard_map/pallas_call | solution.py:260
  304.7 21.7 %shard_map.335 = (bf16[2,768,1024]{2,1,0:T(8,128)(2,1)}, f32[768,896]{1,0:T(8,128)}) custom-call(s32[2,5]{1,0:T(2,128)} %copy.84.bounds_ref, f32[2,1024,768]{2,1,0:T(8,128)} %get-tuple-element.81.v_ref, bf16[2,1024,768]{2,1,0:T(8,128)(2,1)} %bitcast.103, bf16[768,768]{1,0:T(8,128)(2,1)} %bitcast.107, f32[128,768]{1,0:T(8,128)} %convert_bitcast_fusion.w_ref.vec_ref, ...), custom_call_target="tpu_custom_call" | custom-call | tf_op jit(solution)/shard_map/pallas_call | solution.py:402
  328.7 21.9 %shard_map.336 = (bf16[2,768,1024]{2,1,0:T(8,128)(2,1)}, f32[768,896]{1,0:T(8,128)}) custom-call(s32[2,5]{1,0:T(2,128)} %copy.84.bounds_ref, f32[2,1024,768]{2,1,0:T(8,128)} %get-tuple-element.81.v_ref, bf16[2,1024,768]{2,1,0:T(8,128)(2,1)} %bitcast.104, bf16[768,768]{1,0:T(8,128)(2,1)} %bitcast.108, ...), custom_call_target="tpu_custom_call", output_to_operand_aliasing={{0}: (10, {}), {1}: (11, {})} | custom-call | tf_op jit(solution)/shard_map/pallas_call | solution.py:402
  350.6 2.6 collective-permute-done.16
  354.6 7.3 %fusion.8 = f32[2,1024,768]{2,1,0:T(8,128)} fusion(bf16[2,768,1024]{2,1,0:T(8,128)(2,1)} %get-tuple-element.79, bf16[768,768,1]{1,0,2:T(8,128)(2,1)S(1)} %bitcast.132), kind=kOutput, calls=%fused_computation.104 | convolution fusion | flops 2415919104 | bytes 10616832 | tf_op jit(solution)/shard_map/bot,oi->bti/dot_general | solution.py:697
  361.8 22.2 %shard_map.337 = (bf16[2,768,1024]{2,1,0:T(8,128)(2,1)}, f32[768,896]{1,0:T(8,128)}) custom-call(s32[2,5]{1,0:T(2,128)} %copy.84.bounds_ref, f32[2,1024,768]{2,1,0:T(8,128)} %get-tuple-element.81.v_ref, bf16[2,1024,768]{2,1,0:T(8,128)(2,1)} %bitcast.105, bf16[768,768]{1,0:T(8,128)(2,1)} %bitcast.109, ...), custom_call_target="tpu_custom_call", output_to_operand_aliasing={{0}: (10, {}), {1}: (11, {})} | custom-call | tf_op jit(solution)/shard_map/pallas_call | solution.py:402
  387.9 2.7 fusion
  392.1 7.6 %add_add_fusion = f32[2,1024,768]{2,1,0:T(8,128)} fusion(f32[2,1024,768]{2,1,0:T(8,128)S(1)} %fusion, f32[2,1024,768]{2,1,0:T(8,128)S(1)} %bitcast.128, f32[2,1024,768]{2,1,0:T(8,128)S(1)} %bitcast.130, bf16[2,768,1024]{2,1,0:T(8,128)(2,1)} %get-tuple-element.80, bf16[768,768,1]{1,0,2:T(8,128)(2,1)S(1)} %bitcast.121), kind=kOutput, calls=%fused_computation | convolution fusion | flops 2420637696 | bytes 29491200 | tf_op jit(solution)/shard_map/bot,oi->bti/dot_general | solution.py:697
  399.7 2.4 collective-permute-done.21
  405.1 3.4 collective-permute-done.22
  (171 shorter events, 76.5 us)
Async XLA Ops:
  7.2 134.1 %all-gather.3.cloned.1.call-start = ((), (), s32[]{:S(2)}) async-start(), calls=%async_computation.2 | async-start | bytes 10948608 | tf_op jit(solution)/shard_map/all_gather | solution.py:655
  9.9 6.5 %collective-permute-start.10 = (bf16[1,1,1,1,1,24,896]{6,5,4,3,2,1,0:T(8,128)(2,1)S(1)}, bf16[1,1,1,1,1,24,896]{6,5,4,3,2,1,0:T(8,128)(2,1)S(1)}, u32[]{:S(2)}, u32[]{:S(2)}) collective-permute-start(bf16[1,1,1,1,1,24,896]{6,5,4,3,2,1,0:T(8,128)(2,1)S(1)} %fusion.5), channel_id=1, source_target_pairs={{0,16},{4,20},{8,24},{12,28},{16,0},{20,4},{24,8},{28,12},{1,17},{... | collective-permute-start | bytes 129032 | tf_op jit(solution)/shard_map/ppermute | solution.py:565
  27.4 393.6 %reduce-scatter.2.cloned.1.call-start = ((), (), s32[]{:S(2)}) async-start(), calls=%async_computation.1 | async-start | bytes 11354112 | tf_op jit(solution)/shard_map/reduce_scatter | solution.py:676
  27.4 9.4 %collective-permute-start = (bf16[1,1,1,1,1,24,768]{6,5,4,3,2,1,0:T(8,128)(2,1)}, bf16[1,1,1,1,1,24,768]{6,5,4,3,2,1,0:T(8,128)(2,1)S(1)}, u32[]{:S(2)}, u32[]{:S(2)}) collective-permute-start(bf16[1,1,1,1,1,24,768]{6,5,4,3,2,1,0:T(8,128)(2,1)} %bitcast.142), channel_id=1, source_target_pairs={{0,16},{4,20},{8,24},{12,28},{16,0},{20,4},{24,8},{28,12},{1,17},{... | collective-permute-start | bytes 110600 | tf_op jit(solution)/shard_map/ppermute | solution.py:565
  30.0 6.8 %collective-permute-start.5 = (bf16[1,1,1,1,1,24,768]{6,5,4,3,2,1,0:T(8,128)(2,1)}, bf16[1,1,1,1,1,24,768]{6,5,4,3,2,1,0:T(8,128)(2,1)S(1)}, u32[]{:S(2)}, u32[]{:S(2)}) collective-permute-start(bf16[1,1,1,1,1,24,768]{6,5,4,3,2,1,0:T(8,128)(2,1)} %bitcast.141), channel_id=1, source_target_pairs={{0,16},{4,20},{8,24},{12,28},{16,0},{20,4},{24,8},{28,12},{1,17},{... | collective-permute-start | bytes 110600 | tf_op jit(solution)/shard_map/ppermute | solution.py:565
  36.9 5.8 %collective-permute-start.6 = (bf16[2,1,1,1,1,24,768]{6,5,4,3,2,1,0:T(8,128)(2,1)S(1)}, bf16[2,1,1,1,1,24,768]{6,5,4,3,2,1,0:T(8,128)(2,1)S(1)}, u32[]{:S(2)}, u32[]{:S(2)}) collective-permute-start(bf16[2,1,1,1,1,24,768]{6,5,4,3,2,1,0:T(8,128)(2,1)S(1)} %pad_maximum_fusion.14), channel_id=1, source_target_pairs={{0,2},{1,3},{2,0},{3,1},{4,6},{5,7},{6,4},{7,5},{8,10},{9,11},{10,... | collective-permute-start | bytes 221192 | tf_op jit(solution)/shard_map/ppermute | solution.py:565
  38.7 6.0 %collective-permute-start.1 = (bf16[2,1,1,1,1,24,768]{6,5,4,3,2,1,0:T(8,128)(2,1)S(1)}, bf16[2,1,1,1,1,24,768]{6,5,4,3,2,1,0:T(8,128)(2,1)S(1)}, u32[]{:S(2)}, u32[]{:S(2)}) collective-permute-start(bf16[2,1,1,1,1,24,768]{6,5,4,3,2,1,0:T(8,128)(2,1)S(1)} %pad_maximum_fusion.13), channel_id=1, source_target_pairs={{0,4},{4,0},{8,12},{12,8},{16,20},{20,16},{24,28},{28,24},{1,5},{5... | collective-permute-start | bytes 221192 | tf_op jit(solution)/shard_map/ppermute | solution.py:565
  42.7 5.2 %collective-permute-start.7 = (bf16[2,1,1,2,1,24,768]{6,5,4,3,2,1,0:T(8,128)(2,1)S(1)}, bf16[2,1,1,2,1,24,768]{6,5,4,3,2,1,0:T(8,128)(2,1)S(1)}, u32[]{:S(2)}, u32[]{:S(2)}) collective-permute-start(bf16[2,1,1,2,1,24,768]{6,5,4,3,2,1,0:T(8,128)(2,1)S(1)} %pad_maximum_fusion.11), channel_id=1, source_target_pairs={{0,4},{4,0},{8,12},{12,8},{16,20},{20,16},{24,28},{28,24},{1,5},{5... | collective-permute-start | bytes 442376 | tf_op jit(solution)/shard_map/ppermute | solution.py:565
  44.8 8.9 %collective-permute-start.2 = (bf16[2,1,2,1,1,24,768]{6,5,4,3,2,1,0:T(8,128)(2,1)S(1)}, bf16[2,1,2,1,1,24,768]{6,5,4,3,2,1,0:T(8,128)(2,1)S(1)}, u32[]{:S(2)}, u32[]{:S(2)}) collective-permute-start(bf16[2,1,2,1,1,24,768]{6,5,4,3,2,1,0:T(8,128)(2,1)S(1)} %pad_maximum_fusion.10), channel_id=1, source_target_pairs={{0,8},{4,12},{8,0},{12,4},{16,24},{20,28},{24,16},{28,20},{1,9},{5... | collective-permute-start | bytes 442376 | tf_op jit(solution)/shard_map/ppermute | solution.py:565
  46.4 9.1 %collective-permute-start.12 = (bf16[2,2,1,1,1,24,896]{6,5,4,3,2,1,0:T(8,128)(2,1)S(1)}, bf16[2,2,1,1,1,24,896]{6,5,4,3,2,1,0:T(8,128)(2,1)S(1)}, u32[]{:S(2)}, u32[]{:S(2)}) collective-permute-start(bf16[2,2,1,1,1,24,896]{6,5,4,3,2,1,0:T(8,128)(2,1)S(1)} %pad_maximum_fusion.9), channel_id=1, source_target_pairs={{0,2},{1,3},{2,0},{3,1},{4,6},{5,7},{6,4},{7,5},{8,10},{9,11},{10,... | collective-permute-start | bytes 516104 | tf_op jit(solution)/shard_map/ppermute | solution.py:565
  48.0 10.4 %collective-permute-start.8 = (bf16[2,1,2,2,1,24,768]{6,5,4,3,2,1,0:T(8,128)(2,1)S(1)}, bf16[2,1,2,2,1,24,768]{6,5,4,3,2,1,0:T(8,128)(2,1)S(1)}, u32[]{:S(2)}, u32[]{:S(2)}) collective-permute-start(bf16[2,1,2,2,1,24,768]{6,5,4,3,2,1,0:T(8,128)(2,1)S(1)} %pad_maximum_fusion.8), channel_id=1, source_target_pairs={{0,8},{4,12},{8,0},{12,4},{16,24},{20,28},{24,16},{28,20},{1,9},{5... | collective-permute-start | bytes 884744 | tf_op jit(solution)/shard_map/ppermute | solution.py:565
  53.8 8.8 %collective-permute-start.3 = (bf16[2,2,2,1,1,24,768]{6,5,4,3,2,1,0:T(8,128)(2,1)S(1)}, bf16[2,2,2,1,1,24,768]{6,5,4,3,2,1,0:T(8,128)(2,1)S(1)}, u32[]{:S(2)}, u32[]{:S(2)}) collective-permute-start(bf16[2,2,2,1,1,24,768]{6,5,4,3,2,1,0:T(8,128)(2,1)S(1)} %pad_maximum_fusion.7), channel_id=1, source_target_pairs={{0,2},{1,3},{2,0},{3,1},{4,6},{5,7},{6,4},{7,5},{8,10},{9,11},{10,... | collective-permute-start | bytes 884744 | tf_op jit(solution)/shard_map/ppermute | solution.py:565
  55.6 12.5 %collective-permute-start.13 = (bf16[2,2,1,2,1,24,896]{6,5,4,3,2,1,0:T(8,128)(2,1)S(1)}, bf16[2,2,1,2,1,24,896]{6,5,4,3,2,1,0:T(8,128)(2,1)S(1)}, u32[]{:S(2)}, u32[]{:S(2)}) collective-permute-start(bf16[2,2,1,2,1,24,896]{6,5,4,3,2,1,0:T(8,128)(2,1)S(1)} %pad_maximum_fusion.6), channel_id=1, source_target_pairs={{0,4},{4,0},{8,12},{12,8},{16,20},{20,16},{24,28},{28,24},{1,5},{5... | collective-permute-start | bytes 1032200 | tf_op jit(solution)/shard_map/ppermute | solution.py:565
  58.5 9.9 %collective-permute-start.9 = (bf16[2,2,2,2,1,24,768]{6,5,4,3,2,1,0:T(8,128)(2,1)S(1)}, bf16[2,2,2,2,1,24,768]{6,5,4,3,2,1,0:T(8,128)(2,1)S(1)}, u32[]{:S(2)}, u32[]{:S(2)}) collective-permute-start(bf16[2,2,2,2,1,24,768]{6,5,4,3,2,1,0:T(8,128)(2,1)S(1)} %pad_maximum_fusion.5), channel_id=1, source_target_pairs={{0,1},{1,0},{2,3},{3,2},{4,5},{5,4},{6,7},{7,6},{8,9},{9,8},{10,11... | collective-permute-start | bytes 1769480 | tf_op jit(solution)/shard_map/ppermute | solution.py:565
  62.7 6.9 %collective-permute-start.4 = (bf16[2,2,2,2,1,24,768]{6,5,4,3,2,1,0:T(8,128)(2,1)S(1)}, bf16[2,2,2,2,1,24,768]{6,5,4,3,2,1,0:T(8,128)(2,1)S(1)}, u32[]{:S(2)}, u32[]{:S(2)}) collective-permute-start(bf16[2,2,2,2,1,24,768]{6,5,4,3,2,1,0:T(8,128)(2,1)S(1)} %pad_maximum_fusion.4), channel_id=1, source_target_pairs={{0,1},{1,0},{2,3},{3,2},{4,5},{5,4},{6,7},{7,6},{8,9},{9,8},{10,11... | collective-permute-start | bytes 1769480 | tf_op jit(solution)/shard_map/ppermute | solution.py:565
  301.7 24.7 %collective-permute-start.15 = (bf16[2,2,2,2,2,1,24,768]{7,6,5,4,3,2,1,0:T(8,128)(2,1)S(1)}, bf16[2,2,2,2,2,1,24,768]{7,6,5,4,3,2,1,0:T(8,128)(2,1)S(1)}, u32[]{:S(2)}, u32[]{:S(2)}) collective-permute-start(bf16[2,2,2,2,2,1,24,768]{7,6,5,4,3,2,1,0:T(8,128)(2,1)S(1)} %dynamic-slice_convert_fusion), channel_id=1, source_target_pairs={{0,1},{1,0},{2,3},{3,2},{4,5},{5,4},{6,7},{7,6},{8,9},{9,8},{10,11... | collective-permute-start | bytes 3538952 | tf_op jit(solution)/shard_map/ppermute | solution.py:565
  328.6 24.7 %collective-permute-start.16 = (bf16[2,2,2,2,1,1,24,768]{7,6,5,4,3,2,1,0:T(8,128)(2,1)S(1)}, bf16[2,2,2,2,1,1,24,768]{7,6,5,4,3,2,1,0:T(8,128)(2,1)}, u32[]{:S(2)}, u32[]{:S(2)}) collective-permute-start(bf16[2,2,2,2,1,1,24,768]{7,6,5,4,3,2,1,0:T(8,128)(2,1)S(1)} %dynamic-slice_convert_fusion.2), channel_id=1, source_target_pairs={{0,2},{1,3},{2,0},{3,1},{4,6},{5,7},{6,4},{7,5},{8,10},{9,11},{10,... | collective-permute-start | bytes 1769480 | tf_op jit(solution)/shard_map/ppermute | solution.py:565
  354.5 29.6 %collective-permute-start.17 = (bf16[2,2,1,2,1,1,24,768]{7,6,5,4,3,2,1,0:T(8,128)(2,1)S(1)}, bf16[2,2,1,2,1,1,24,768]{7,6,5,4,3,2,1,0:T(8,128)(2,1)S(1)}, u32[]{:S(2)}, u32[]{:S(2)}) collective-permute-start(bf16[2,2,1,2,1,1,24,768]{7,6,5,4,3,2,1,0:T(8,128)(2,1)S(1)} %dynamic-slice_convert_fusion.4), channel_id=1, source_target_pairs={{0,8},{4,12},{8,0},{12,4},{16,24},{20,28},{24,16},{28,20},{1,9},{5... | collective-permute-start | bytes 884744 | tf_op jit(solution)/shard_map/ppermute | solution.py:565
  385.7 4.9 %collective-permute-start.20 = (bf16[2,2,2,2,1,24,896]{6,5,4,3,2,1,0:T(8,128)(2,1)S(1)}, bf16[2,2,2,2,1,24,896]{6,5,4,3,2,1,0:T(8,128)(2,1)S(1)}, u32[]{:S(2)}, u32[]{:S(2)}) collective-permute-start(bf16[2,2,2,2,1,24,896]{6,5,4,3,2,1,0:T(8,128)(2,1)S(1)} %dynamic-slice_convert_fusion.1), channel_id=1, source_target_pairs={{0,1},{1,0},{2,3},{3,2},{4,5},{5,4},{6,7},{7,6},{8,9},{9,8},{10,11... | collective-permute-start | bytes 2064392 | tf_op jit(solution)/shard_map/ppermute | solution.py:565
  385.9 17.4 %collective-permute-start.18 = (bf16[2,2,1,1,1,1,24,768]{7,6,5,4,3,2,1,0:T(8,128)(2,1)S(1)}, bf16[2,2,1,1,1,1,24,768]{7,6,5,4,3,2,1,0:T(8,128)(2,1)S(1)}, u32[]{:S(2)}, u32[]{:S(2)}) collective-permute-start(bf16[2,2,1,1,1,1,24,768]{7,6,5,4,3,2,1,0:T(8,128)(2,1)S(1)} %dynamic-slice_convert_fusion.6), channel_id=1, source_target_pairs={{0,4},{4,0},{8,12},{12,8},{16,20},{20,16},{24,28},{28,24},{1,5},{5... | collective-permute-start | bytes 442376 | tf_op jit(solution)/shard_map/ppermute | solution.py:565
  390.9 11.3 %collective-permute-start.21 = (bf16[2,2,1,2,1,24,896]{6,5,4,3,2,1,0:T(8,128)(2,1)S(1)}, bf16[2,2,1,2,1,24,896]{6,5,4,3,2,1,0:T(8,128)(2,1)S(1)}, u32[]{:S(2)}, u32[]{:S(2)}) collective-permute-start(bf16[2,2,1,2,1,24,896]{6,5,4,3,2,1,0:T(8,128)(2,1)S(1)} %dynamic-slice_convert_fusion.3), channel_id=1, source_target_pairs={{0,4},{4,0},{8,12},{12,8},{16,20},{20,16},{24,28},{28,24},{1,5},{5... | collective-permute-start | bytes 1032200 | tf_op jit(solution)/shard_map/ppermute | solution.py:565
  402.3 6.2 %collective-permute-start.22 = (bf16[2,2,1,1,1,24,896]{6,5,4,3,2,1,0:T(8,128)(2,1)S(1)}, bf16[2,2,1,1,1,24,896]{6,5,4,3,2,1,0:T(8,128)(2,1)S(1)}, u32[]{:S(2)}, u32[]{:S(2)}) collective-permute-start(bf16[2,2,1,1,1,24,896]{6,5,4,3,2,1,0:T(8,128)(2,1)S(1)} %dynamic-slice_convert_fusion.5), channel_id=1, source_target_pairs={{0,2},{1,3},{2,0},{3,1},{4,6},{5,7},{6,4},{7,5},{8,10},{9,11},{10,... | collective-permute-start | bytes 516104 | tf_op jit(solution)/shard_map/ppermute | solution.py:565
  403.4 7.3 %collective-permute-start.19 = (bf16[2,1,1,1,1,1,24,768]{7,6,5,4,3,2,1,0:T(8,128)(2,1)S(1)}, bf16[2,1,1,1,1,1,24,768]{7,6,5,4,3,2,1,0:T(8,128)(2,1)S(1)}, u32[]{:S(2)}, u32[]{:S(2)}) collective-permute-start(bf16[2,1,1,1,1,1,24,768]{7,6,5,4,3,2,1,0:T(8,128)(2,1)S(1)} %dynamic-slice_convert_fusion.8), channel_id=1, source_target_pairs={{0,16},{4,20},{8,24},{12,28},{16,0},{20,4},{24,8},{28,12},{1,17},{... | collective-permute-start | bytes 221192 | tf_op jit(solution)/shard_map/ppermute | solution.py:565
  413.2 5.0 %collective-permute-start.24 = (bf16[1,1,1,1,1,24,896]{6,5,4,3,2,1,0:T(8,128)(2,1)S(1)}, bf16[1,1,1,1,1,24,896]{6,5,4,3,2,1,0:T(8,128)(2,1)S(1)}, u32[]{:S(2)}, u32[]{:S(2)}) collective-permute-start(bf16[1,1,1,1,1,24,896]{6,5,4,3,2,1,0:T(8,128)(2,1)S(1)} %dynamic-slice_convert_fusion.9), channel_id=1, source_target_pairs={{0,16},{4,20},{8,24},{12,28},{16,0},{20,4},{24,8},{28,12},{1,17},{... | collective-permute-start | bytes 129032 | tf_op jit(solution)/shard_map/ppermute | solution.py:565
  (20 other events, 270.5 us)
Sparse Core Ops, SparseCore 0:
  27.5 92.4 all-gather.2
  252.0 153.9 reduce-scatter.1

commit v6 on v5

--- a/solution.py
+++ b/solution.py
@@ -266,27 +266,28 @@
             x,al,wo,q,k,v,k1,k3,inv,stash,small,tok[:,None,:])
 
 HALF=16; DOCS=4; GAP=16
-def spread(dst, get, bounds, length, step):
+def spread(places, bounds, length, step):
     total=length+GAP*(DOCS+1)
     ids=lax.broadcasted_iota(jnp.int32,(step,128),0)
     for p0 in range(0,total,step):
         size=min(step,total-p0)
-        acc=None
+        sums=[None]*len(places)
         for d in range(DOCS):
             s0=p0-GAP*(d+1)
             lo=max(s0,0); hi=min(s0+size,length)
             if hi<=lo: continue
             row=ids[:hi-lo]+lo
             inside=(row>=bounds[d])&(row<bounds[d+1])
-            part=jnp.where(inside,get(lo,hi-lo),0.0)
-            pads=[]
-            if lo>s0: pads.append(jnp.zeros((lo-s0,128),F32))
-            pads.append(part)
-            if s0+size>hi: pads.append(jnp.zeros((s0+size-hi,128),F32))
-            part=jnp.concatenate(pads,0) if len(pads)>1 else part
-            acc=part if acc is None else acc+part
-        if acc is None: acc=jnp.zeros((size,128),F32)
-        dst[HALF+p0:HALF+p0+size,:]=acc
+            for i,(_,get) in enumerate(places):
+                part=jnp.where(inside,get(lo,hi-lo),0.0)
+                pads=[]
+                if lo>s0: pads.append(jnp.zeros((lo-s0,128),F32))
+                pads.append(part)
+                if s0+size>hi: pads.append(jnp.zeros((s0+size-hi,128),F32))
+                part=jnp.concatenate(pads,0) if len(pads)>1 else part
+                sums[i]=part if sums[i] is None else sums[i]+part
+        for i,(dst,_) in enumerate(places):
+            dst[HALF+p0:HALF+p0+size,:]=jnp.zeros((size,128),F32) if sums[i] is None else sums[i]
 def collect(src, bounds, lo, size):
     row=lax.broadcasted_iota(jnp.int32,(size,128),0)+lo
     acc=None
@@ -318,7 +319,7 @@
     for h in SLABS:
         pad_ref[h,0:HALF,:]=jnp.zeros((HALF,128),F32)
         pad_ref[h,HALF+total:,:]=jnp.zeros((pad_ref.shape[1]-HALF-total,128),F32)
-        spread(pad_ref.at[h], lambda lo,n: v_ref[0,lo:lo+n,cut(h)], bounds, length, BLOCK)
+    spread([(pad_ref.at[h], lambda lo,n,h=h: v_ref[0,lo:lo+n,cut(h)]) for h in SLABS], bounds, length, BLOCK)
     def block(i,c):
         base=pl.multiple_of(i*TALL,TALL)
         for h in SLABS:
@@ -353,8 +354,7 @@
     for ref in (vpad_ref,gpad_ref):
         ref[0:HALF,:]=jnp.zeros((HALF,128),F32)
         ref[HALF+total:,:]=jnp.zeros((ref.shape[0]-HALF-total,128),F32)
-    spread(vpad_ref, lambda lo,n: v_ref[0,lo:lo+n,:], bounds, length, BLOCK)
-    spread(gpad_ref, lambda lo,n: g_ref[lo:lo+n,:], bounds, length, BLOCK)
+    spread([(vpad_ref, lambda lo,n: v_ref[0,lo:lo+n,:]), (gpad_ref, lambda lo,n: g_ref[lo:lo+n,:])], bounds, length, BLOCK)
     @pl.when(b==0)
     def _():
         acc_ref[...]=jnp.zeros_like(acc_ref); gv_ref[...]=jnp.zeros_like(gv_ref); sum_ref[...]=jnp.zeros_like(sum_ref)
@@ -424,8 +424,10 @@
 def norm_back(up,n,r,g):
     e=up*g
     return r*(e-jnp.mean(e,axis=-1,keepdims=True)-n*jnp.mean(e*n,axis=-1,keepdims=True))
-def ffn_kernel(chunks, parts, ctx_ref,x_ref,cot_ref,wo_ref,wu_ref,wd_ref,vec_ref,bu_ref,
-               out_ref,normed_ref,hidden_ref,down_ref,up_ref,one_ref,att_ref,sums_ref,sumu_ref,slope_ref):
+def ffn_kernel(chunks, parts, ctx_ref,x_ref,cot_ref,wo_ref,wu_ref,*refs):
+    wd_ref=refs[:chunks]
+    (vec_ref,bu_ref,
+               out_ref,normed_ref,hidden_ref,down_ref,up_ref,one_ref,att_ref,sums_ref,sumu_ref,slope_ref)=refs[chunks:]
     wu=wu_ref[...].reshape(-1,wu_ref.shape[-1]); width=wu.shape[0]//chunks
     size=x_ref.shape[0]//parts
     @pl.when(pl.program_id(0)==0)
@@ -444,7 +446,7 @@
         def up(k):
             def go():
                 if k>0:
-                    add=nt(st["hid"],wd_ref[k-1]); st["down"]=add if k==1 else st["down"]+add
+                    add=nt(st["hid"],wd_ref[k-1][...]); st["down"]=add if k==1 else st["down"]+add
                 if k<chunks: st["pre"]=nt(st["low"],wu[k*width:(k+1)*width,:])
             return go
         def gelu(k):
@@ -465,7 +467,7 @@
         def back(k):
             def go():
                 if k>0: st["back"]=st["back"]+nn(st["upl"],wu[(k-1)*width:k*width,:])
-                if k<chunks: st["hg"]=nn(st["low2"],wd_ref[k])
+                if k<chunks: st["hg"]=nn(st["low2"],wd_ref[k][...])
             return go
         def scale(k):
             part=slice(k*width,(k+1)*width)
@@ -488,19 +490,19 @@
         for at in range(parts):
             if 0<=i-at<len(lists[at]): lists[at][i-at]()
 def ffn(ctx,x,cot,wo,wu,wd,vec,bu,block=512,parts=2):
-    chunks=wd.shape[0]
+    chunks=len(wd)
     T,D=x.shape; F=bu.shape[1]
     row=lambda w: pl.BlockSpec((block,w),lambda i:(i,0))
     full=lambda a: pl.BlockSpec(a.shape,lambda i:(0,)*a.ndim,pipeline_mode=pl.Buffered(1))
     keep=lambda r,w: pl.BlockSpec((r,w),lambda i:(0,0))
     sd=jax.ShapeDtypeStruct
     return pl.pallas_call(functools.partial(ffn_kernel,chunks,parts),grid=(T//block,),
-        in_specs=[row(D),row(D),row(D),full(wo),pl.BlockSpec((wu.shape[0],F//wu.shape[0],D),lambda i:(0,0,0),pipeline_mode=pl.Buffered(1)),full(wd),pl.BlockSpec((SMALL,D),lambda i:(0,0)),full(bu)],
+        in_specs=[row(D),row(D),row(D),full(wo),pl.BlockSpec((wu.shape[0],F//wu.shape[0],D),lambda i:(0,0,0),pipeline_mode=pl.Buffered(1)),*[full(a) for a in wd],pl.BlockSpec((SMALL,D),lambda i:(0,0)),full(bu)],
         out_specs=[row(D),row(D),row(F),row(D),row(F),row(D),row(D),keep(8,D),keep(1,F)],
         out_shape=[sd((T,D),BF),sd((T,D),BF),sd((T,F),BF),sd((T,D),BF),sd((T,F),BF),sd((T,D),F32),sd((T,D),BF),sd((8,D),F32),sd((1,F),F32)],
         scratch_shapes=[pltpu.VMEM((block,F),F32)],
         compiler_params=pltpu.CompilerParams(vmem_limit_bytes=60*2**20,dimension_semantics=("arbitrary",)),
-    )(ctx,x,cot,wo,wu,wd,vec,bu)
+    )(ctx,x,cot,wo,wu,*wd,vec,bu)
 
 
 def across_rows(left_side, right_side):
@@ -569,18 +571,21 @@
     return (lax.axis_index(axis) // stride) % 2
 
 
-def gather_rows(shard, number, passed=None):
+def gather_rows(shards):
     places = digits()
-    held = shard.reshape((1,) * len(places) + shard.shape)
-    for dim in link_order(number)[::-1]:
-        if passed is not None:
-            passed.append(held)
-        mine = digit_of(*places[dim])
-        got = exchange(held, *places[dim])
-        first = jnp.where(mine == 0, held, got)
-        second = jnp.where(mine == 0, got, held)
-        held = jnp.concatenate([first, second], dim)
-    return held.reshape((-1,) + shard.shape)
+    held = [shard.reshape((1,) * len(places) + shard.shape) for shard in shards]
+    passed = []
+    for step in range(len(places)):
+        for number, values in enumerate(held):
+            dim = link_order(number)[::-1][step]
+            mine = digit_of(*places[dim])
+            got = exchange(values, *places[dim])
+            first = jnp.where(mine == 0, values, got)
+            second = jnp.where(mine == 0, got, values)
+            held[number] = jnp.concatenate([first, second], dim)
+        held = list(lax.optimization_barrier(tuple(held)))
+        passed.append(held[0])
+    return [values.reshape((-1,) + values.shape[-2:]) for values in held], passed
 
 
 def scatter_start(whole, own):
@@ -637,10 +642,11 @@
         flat = flat + jnp.pad(vector, (before, (8 + lines) * own - before - vector.shape[0]))
     small = jnp.concatenate([conv_weight, flat.reshape(8 + lines, own)])
     small = jnp.pad(small.T, ((0, 0), (0, 128 - small.shape[0])))
-    passed = []
-    w_q = gather_rows(w_query.T, 1).reshape(feature_width, feature_width)
-    w_k = gather_rows(w_key.T, 2).reshape(feature_width, feature_width)
-    gathered_v = gather_rows(jnp.concatenate([w_value.T, small], axis=1), 0, passed)
+    (gathered_v, w_q, w_k), passed = gather_rows(
+        [jnp.concatenate([w_value.T, small], axis=1), w_query.T, w_key.T]
+    )
+    w_q = w_q.reshape(feature_width, feature_width)
+    w_k = w_k.reshape(feature_width, feature_width)
     gathered_v = gathered_v.reshape(feature_width, feature_width + 128)
     w_v = gathered_v[:, :feature_width]
     small = gathered_v[:, feature_width:]
@@ -648,16 +654,17 @@
     b_u = b_u.reshape(1, -1).astype(F32)
     small = small.astype(F32).T
     ff_count = w_down.shape[0] // feature_width
-    w_out, w_up, w_down, _ = lax.optimization_barrier((w_out, w_up, w_down, passed[2]))
+    w_out, w_up, w_down, _ = lax.optimization_barrier((w_out, w_up, w_down, passed[0]))
     shard = jnp.concatenate(
         [w_up.T, w_out.T] + [w_down[i * feature_width : (i + 1) * feature_width].T for i in range(ff_count)]
     )
     gathered = lax.all_gather(shard, ("wide", "narrow"), axis=0)
     w_o = gathered[:, own * lines : own * (1 + lines)].reshape(feature_width, feature_width)
     w_u = gathered if own * lines % 16 == 0 else gathered[:, : own * lines].reshape(1, -1, feature_width)
-    w_d = jnp.moveaxis(
-        gathered[:, own * (1 + lines) :].reshape(group_count, ff_count, own, feature_width), 0, 1
-    ).reshape(ff_count, feature_width, feature_width)
+    w_d = [
+        gathered[:, own * (1 + lines + i) : own * (2 + lines + i)].reshape(feature_width, feature_width)
+        for i in range(ff_count)
+    ]
     member = tok_landmark[:, None, :] == jnp.arange(LM)[None, :, None]
     means = jnp.einsum("bjt,bti->bji", member.astype(BF), inputs, preferred_element_type=F32)
     means = means / jnp.sum(member, axis=2)[..., None].astype(F32)
@@ -689,7 +696,7 @@
             bounds, value_rows, att_low, w_o, small, inputs, dv, more, before, slabs, call * slabs
         )
         before, att_low, moving = lax.optimization_barrier((tuple(before), att_low, moved))
-    dv, grad_v = before
+    (dv, grad_v), dq, dk = lax.optimization_barrier((before, dq, dk))
     share_qk = scatter_rest(moving, 1, calls)
     share_v = scatter_rest(scatter_start(grad_v, own), 0, 0)
     input_grad = grad_one.reshape(inputs.shape)

time: 438 us -> 430 us (0.982)
  matrix products: 20.9 us -> 13.6 us
  other arithmetic: 14.1 us -> 20.4 us
  waiting for transfers between devices: 35.8 us -> 30.8 us
    dot_general x3, matrix products: 17.6 us -> 12.3 us  [shards(): jnp.einsum('bot,oi->bti', grad, weight, preferred_element_type=F32)]
    ppermute x25, waiting for transfers between devices: 35.8 us -> 30.8 us  [exchange(): lax.ppermute(values, axis, [(i, i ^ stride) for i in range(lax.axis_size(...]
  transfers between devices with their start and end apart: 27 -> 27, of which waited for: 12 -> 11; matrix products, arithmetic and copies ran while one was open for 10% -> 11% of each run, Pallas kernels for 41% -> 42%
where the time goes in v6:
time: 430 us; the launch traced here: 424 us
  Pallas kernels  281 us (65%)
  local copies, waits for them, and re-layouts  32.6 us (8%)
  waiting for transfers between devices  30.8 us (7%)
  starting transfers between devices  30.6 us (7%)
  other arithmetic  20.4 us (5%)
  between operations  15 us (3%)
  matrix products  13.6 us (3%)
    pallas_call x1, Pallas kernels, ffn(): pl.pallas_call(functools.partial(ffn_kernel, chunks, parts), grid=(T // b...  69.7 us
    pallas_call x3, Pallas kernels, conv_bwd(): pl.pallas_call(conv_bwd_kernel, grid_spec=pltpu.PrefetchScalarGridSpec(nu...  65.5 us
    pallas_call x1, Pallas kernels, att_bwd(): pl.pallas_call(att_bwd_kernel, grid=(G, B), in_specs=[seq((T, D)), seq((T...  45.3 us
    pallas_call x1, Pallas kernels, att_fwd(): pl.pallas_call(att_fwd_kernel, grid=(G, B), in_specs=[seq((T, D)), seq((L...  39.8 us
    pallas_call x1, Pallas kernels, weight_grads(): pl.pallas_call(functools.partial(weight_kernel, own), grid=(halves, T //...  33.2 us
    ppermute x25, waiting for transfers between devices, exchange(): lax.ppermute(values, axis, [(i, i ^ stride) for i in range(lax.axis_size(...  30.8 us
    ppermute x25, starting transfers between devices, exchange(): lax.ppermute(values, axis, [(i, i ^ stride) for i in range(lax.axis_size(...  30.5 us
    pallas_call x1, Pallas kernels, conv_fwd(): pl.pallas_call(conv_fwd_kernel, grid_spec=pltpu.PrefetchScalarGridSpec(nu...  27.3 us
  transfers between devices with their start and end apart: 27, of which 11 were waited for; matrix products, arithmetic and copies ran while one was open for 11% of the time, Pallas kernels for 42%

profile of v6, /device:TPU:0, one launch (start us, length us, event | category | flops | bytes accessed | tf_op | source)
XLA Modules:
  0.0 423.8 jit_solution(17556564966908936295)
XLA Ops:
  7.2 4.1 collective-permute-start.1
  14.0 2.8 collective-permute-start
  30.3 3.3 collective-permute-done.4
  36.3 5.2 %collective-permute-done.8 = bf16[2,1,1,2,1,24,768]{6,5,4,3,2,1,0:T(8,128)(2,1)S(1)} collective-permute-done((bf16[2,1,1,2,1,24,768]{6,5,4,3,2,1,0:T(8,128)(2,1)S(1)}, bf16[2,1,1,2,1,24,768]{6,5,4,3,2,1,0:T(8,128)(2,1)S(1)}, u32[]{:S(2)}, u32[]{:S(2)}) %collective-permute-start.8) | collective-permute-done | bytes 147488 | tf_op jit(solution)/shard_map/ppermute | solution.py:567
  41.5 3.7 collective-permute-done.7
  48.4 5.7 %collective-permute-done.11 = bf16[2,1,2,2,1,24,768]{6,5,4,3,2,1,0:T(8,128)(2,1)S(1)} collective-permute-done((bf16[2,1,2,2,1,24,768]{6,5,4,3,2,1,0:T(8,128)(2,1)S(1)}, bf16[2,1,2,2,1,24,768]{6,5,4,3,2,1,0:T(8,128)(2,1)S(1)}, u32[]{:S(2)}, u32[]{:S(2)}) %collective-permute-start.11) | collective-permute-done | bytes 294944 | tf_op jit(solution)/shard_map/ppermute | solution.py:567
  68.4 27.3 %shard_map.331 = (f32[2,1024,768]{2,1,0:T(8,128)}, f32[2,1024,768]{2,1,0:T(8,128)}) custom-call(s32[2,5]{1,0:T(2,128)} %copy.81.bounds_ref, bf16[2,1024,768]{2,1,0:T(8,128)(2,1)} %x_ref.11, bf16[768,768]{1,0:T(8,128)(2,1)} %slice.135.wv_ref, f32[128,768]{1,0:T(8,128)} %convert_bitcast_fusion.w_ref.vec_ref.refs_4_), custom_call_target="tpu_custom_call" | custom-call | tf_op jit(solution)/shard_map/pallas_call | solution.py:340
  95.7 39.8 %shard_map.332 = (bf16[2,768,1024]{2,1,0:T(8,128)(2,1)}, bf16[2,768,1024]{2,1,0:T(8,128)(2,1)}, bf16[2,768,1024]{2,1,0:T(8,128)(2,1)}, bf16[2,768,1024]{2,1,0:T(...) custom-call(bf16[2,1024,768]{2,1,0:T(8,128)(2,1)} %x_ref.11, ...), custom_call_target="tpu_custom_call" | custom-call | tf_op jit(solution)/shard_map/pallas_call | solution.py:154
  135.5 5.3 %fusion.7 = (bf16[32,24,768]{2,1,0:T(8,128)(2,1)}, bf16[32,24,768]{2,1,0:T(8,128)(2,1)}, bf16[32,24,768]{2,1,0:T(8,128)(2,1)}, bf16[32,24,768]{2,1,0:T(8,128)(2,1)}, bf16[32,24,768]{2,1,0:T(8,128)(2,1)}) fusion(bf16[32,216,768]{2,1,0:T(8,128)(2,1)} %bitcast.111), kind=kLoop, calls=%fused_computation.103 | loop fusion | bytes 11796480 | tf_op jit(solution)/shard_map/slice | solution.py:665
  140.8 69.7 %shard_map.333 = (bf16[2048,768]{1,0:T(8,128)(2,1)}, bf16[2048,768]{1,0:T(8,128)(2,1)}, bf16[2048,3072]{1,0:T(8,128)(2,1)}, bf16[2048,768]{1,0:T(8,128)(2,1)}, b...) custom-call(bf16[2048,768]{1,0:T(8,128)(2,1)} %bitcast.115, ...), custom_call_target="tpu_custom_call" | custom-call | tf_op jit(solution)/shard_map/pallas_call | solution.py:499
  210.4 33.2 %shard_map.338 = bf16[32,224,768]{2,1,0:T(8,128)(2,1)} custom-call(bf16[2048,3072]{1,0:T(8,128)(2,1)} %get-tuple-element.142.up_ref, bf16[2048,768]{1,0:T(8,128)(2,1)} %get-tuple-element.143.normed_ref, bf16[2048,3072]{1,0:T(8,128)(2,1)} %get-tuple-element.144.hidden_ref, bf16[2048,768]{1,0:T(8,128)(2,1)} %get-tuple-element.145.down_ref, ...), custom_call_target="tpu_custom_call" | custom-call | tf_op jit(solution)/shard_map/pallas_call | solution.py:541
  246.4 45.3 %shard_map.334 = (bf16[2,768,1024]{2,1,0:T(8,128)(2,1)}, bf16[2,768,1024]{2,1,0:T(8,128)(2,1)}, f32[2,768,1024]{2,1,0:T(8,128)}, f32[2,768,768]{2,1,0:T(8,128)}, f32[768,1]{1,0:T(8,128)}) custom-call(bf16[2,1024,768]{2,1,0:T(8,128)(2,1)} %x_ref.11, bf16[2,1024,768]{2,1,0:T(8,128)(2,1)} %bitcast.102, bf16[768,768]{1,0:T(8,128)(2,1)} %copy.86.wo_ref, ...), custom_call_target="tpu_custom_call" | custom-call | tf_op jit(solution)/shard_map/pallas_call | solution.py:260
  296.4 21.8 %shard_map.335 = (bf16[2,768,1024]{2,1,0:T(8,128)(2,1)}, f32[768,896]{1,0:T(8,128)}) custom-call(s32[2,5]{1,0:T(2,128)} %copy.81.bounds_ref, f32[2,1024,768]{2,1,0:T(8,128)} %get-tuple-element.104.v_ref, bf16[2,1024,768]{2,1,0:T(8,128)(2,1)} %bitcast.103, bf16[768,768]{1,0:T(8,128)(2,1)} %bitcast.107, f32[128,768]{1,0:T(8,128)} %convert_bitcast_fusion.w_ref.vec_ref.refs_4_, ...), custom_call_target="tpu_custom_call" | custom-call | tf_op jit(solution)/shard_map/pallas_call | solution.py:402
  318.2 2.4 convert_add_fusion
  322.9 22.0 %shard_map.336 = (bf16[2,768,1024]{2,1,0:T(8,128)(2,1)}, f32[768,896]{1,0:T(8,128)}) custom-call(s32[2,5]{1,0:T(2,128)} %copy.81.bounds_ref, f32[2,1024,768]{2,1,0:T(8,128)} %get-tuple-element.104.v_ref, bf16[2,1024,768]{2,1,0:T(8,128)(2,1)} %bitcast.104, bf16[768,768]{1,0:T(8,128)(2,1)} %bitcast.108, ...), custom_call_target="tpu_custom_call", output_to_operand_aliasing={{0}: (10, {}), {1}: (11, {})} | custom-call | tf_op jit(solution)/shard_map/pallas_call | solution.py:402
  348.2 21.8 %shard_map.337 = (bf16[2,768,1024]{2,1,0:T(8,128)(2,1)}, f32[768,896]{1,0:T(8,128)}) custom-call(s32[2,5]{1,0:T(2,128)} %copy.81.bounds_ref, f32[2,1024,768]{2,1,0:T(8,128)} %get-tuple-element.104.v_ref, bf16[2,1024,768]{2,1,0:T(8,128)(2,1)} %bitcast.105, bf16[768,768]{1,0:T(8,128)(2,1)} %bitcast.109, ...), custom_call_target="tpu_custom_call", output_to_operand_aliasing={{0}: (10, {}), {1}: (11, {})} | custom-call | tf_op jit(solution)/shard_map/pallas_call | solution.py:402
  374.1 4.8 %fusion.8 = f32[2,1024,768]{2,1,0:T(8,128)S(1)} fusion(bf16[2,768,1024]{2,1,0:T(8,128)(2,1)} %get-tuple-element.137, bf16[768,768,1]{1,0,2:T(8,128)(2,1)S(1)} %bitcast.131), kind=kOutput, calls=%fused_computation.104 | convolution fusion | flops 2415919104 | bytes 10616832 | tf_op jit(solution)/shard_map/bot,oi->bti/dot_general | solution.py:704
  379.0 2.8 fusion.9
  384.1 4.8 %add_add_fusion = f32[2,1024,768]{2,1,0:T(8,128)} fusion(f32[2,1024,768]{2,1,0:T(8,128)S(1)} %fusion.9, f32[2,1024,768]{2,1,0:T(8,128)S(1)} %bitcast.123, f32[2,1024,768]{2,1,0:T(8,128)S(1)} %fusion.8, bf16[2,768,1024]{2,1,0:T(8,128)(2,1)S(1)} %copy-done.2, bf16[768,896]{1,0:T(8,128)(2,1)S(1)} %bitcast.120), kind=kOutput, calls=%fused_computation | convolution fusion | flops 2420637696 | bytes 29491200 | tf_op jit(solution)/shard_map/bot,oi->bti/dot_general | solution.py:704
  388.9 4.3 %collective-permute-done.21 = bf16[2,2,1,2,1,24,896]{6,5,4,3,2,1,0:T(8,128)(2,1)} collective-permute-done((bf16[2,2,1,2,1,24,896]{6,5,4,3,2,1,0:T(8,128)(2,1)}, bf16[2,2,1,2,1,24,896]{6,5,4,3,2,1,0:T(8,128)(2,1)}, u32[]{:S(2)}, u32[]{:S(2)}) %collective-permute-start.21) | collective-permute-done | bytes 344096 | tf_op jit(solution)/shard_map/ppermute | solution.py:567
  395.8 2.5 collective-permute-start.19
  400.2 1.8 collective-permute-start.23
  402.3 2.4 collective-permute-done.23
  404.8 2.7 collective-permute-start.24
  (166 shorter events, 69.6 us)
Async XLA Ops:
  7.2 128.3 %all-gather.3.cloned.1.call-start = ((), (), s32[]{:S(2)}) async-start(), calls=%async_computation.2 | async-start | bytes 10948608 | tf_op jit(solution)/shard_map/all_gather | solution.py:661
  7.2 9.6 %collective-permute-start.1 = (bf16[1,1,1,1,1,24,768]{6,5,4,3,2,1,0:T(8,128)(2,1)}, bf16[1,1,1,1,1,24,768]{6,5,4,3,2,1,0:T(8,128)(2,1)S(1)}, u32[]{:S(2)}, u32[]{:S(2)}) collective-permute-start(bf16[1,1,1,1,1,24,768]{6,5,4,3,2,1,0:T(8,128)(2,1)} %bitcast.141), channel_id=1, source_target_pairs={{0,16},{4,20},{8,24},{12,28},{16,0},{20,4},{24,8},{28,12},{1,17},{... | collective-permute-start | bytes 110600 | tf_op jit(solution)/shard_map/ppermute | solution.py:567
  11.3 5.5 %collective-permute-start.2 = (bf16[1,1,1,1,1,24,768]{6,5,4,3,2,1,0:T(8,128)(2,1)}, bf16[1,1,1,1,1,24,768]{6,5,4,3,2,1,0:T(8,128)(2,1)S(1)}, u32[]{:S(2)}, u32[]{:S(2)}) collective-permute-start(bf16[1,1,1,1,1,24,768]{6,5,4,3,2,1,0:T(8,128)(2,1)} %bitcast.140), channel_id=1, source_target_pairs={{0,16},{4,20},{8,24},{12,28},{16,0},{20,4},{24,8},{28,12},{1,17},{... | collective-permute-start | bytes 110600 | tf_op jit(solution)/shard_map/ppermute | solution.py:567
  14.0 5.0 %collective-permute-start = (bf16[1,1,1,1,1,24,896]{6,5,4,3,2,1,0:T(8,128)(2,1)S(1)}, bf16[1,1,1,1,1,24,896]{6,5,4,3,2,1,0:T(8,128)(2,1)S(1)}, u32[]{:S(2)}, u32[]{:S(2)}) collective-permute-start(bf16[1,1,1,1,1,24,896]{6,5,4,3,2,1,0:T(8,128)(2,1)S(1)} %fusion.4), channel_id=1, source_target_pairs={{0,16},{4,20},{8,24},{12,28},{16,0},{20,4},{24,8},{28,12},{1,17},{... | collective-permute-start | bytes 129032 | tf_op jit(solution)/shard_map/ppermute | solution.py:567
  25.4 387.1 %reduce-scatter.2.cloned.1.call-start = ((), (), s32[]{:S(2)}) async-start(), calls=%async_computation.1 | async-start | bytes 11354112 | tf_op jit(solution)/shard_map/reduce_scatter | solution.py:683
  25.4 4.9 %collective-permute-start.5 = (bf16[2,1,1,1,1,24,768]{6,5,4,3,2,1,0:T(8,128)(2,1)S(1)}, bf16[2,1,1,1,1,24,768]{6,5,4,3,2,1,0:T(8,128)(2,1)S(1)}, u32[]{:S(2)}, u32[]{:S(2)}) collective-permute-start(bf16[2,1,1,1,1,24,768]{6,5,4,3,2,1,0:T(8,128)(2,1)S(1)} %pad_maximum_fusion.14), channel_id=1, source_target_pairs={{0,2},{1,3},{2,0},{3,1},{4,6},{5,7},{6,4},{7,5},{8,10},{9,11},{10,... | collective-permute-start | bytes 221192 | tf_op jit(solution)/shard_map/ppermute | solution.py:567
  27.2 6.5 %collective-permute-start.3 = (bf16[2,1,1,1,1,24,896]{6,5,4,3,2,1,0:T(8,128)(2,1)S(1)}, bf16[2,1,1,1,1,24,896]{6,5,4,3,2,1,0:T(8,128)(2,1)S(1)}, u32[]{:S(2)}, u32[]{:S(2)}) collective-permute-start(bf16[2,1,1,1,1,24,896]{6,5,4,3,2,1,0:T(8,128)(2,1)S(1)} %pad_maximum_fusion.12), channel_id=1, source_target_pairs={{0,8},{4,12},{8,0},{12,4},{16,24},{20,28},{24,16},{28,20},{1,9},{5... | collective-permute-start | bytes 258056 | tf_op jit(solution)/shard_map/ppermute | solution.py:567
  28.8 4.8 %collective-permute-start.4 = (bf16[2,1,1,1,1,24,768]{6,5,4,3,2,1,0:T(8,128)(2,1)S(1)}, bf16[2,1,1,1,1,24,768]{6,5,4,3,2,1,0:T(8,128)(2,1)S(1)}, u32[]{:S(2)}, u32[]{:S(2)}) collective-permute-start(bf16[2,1,1,1,1,24,768]{6,5,4,3,2,1,0:T(8,128)(2,1)S(1)} %pad_maximum_fusion.13), channel_id=1, source_target_pairs={{0,4},{4,0},{8,12},{12,8},{16,20},{20,16},{24,28},{28,24},{1,5},{5... | collective-permute-start | bytes 221192 | tf_op jit(solution)/shard_map/ppermute | solution.py:567
  33.7 7.8 %collective-permute-start.8 = (bf16[2,1,1,2,1,24,768]{6,5,4,3,2,1,0:T(8,128)(2,1)S(1)}, bf16[2,1,1,2,1,24,768]{6,5,4,3,2,1,0:T(8,128)(2,1)S(1)}, u32[]{:S(2)}, u32[]{:S(2)}) collective-permute-start(bf16[2,1,1,2,1,24,768]{6,5,4,3,2,1,0:T(8,128)(2,1)S(1)} %pad_maximum_fusion.11), channel_id=1, source_target_pairs={{0,4},{4,0},{8,12},{12,8},{16,20},{20,16},{24,28},{28,24},{1,5},{5... | collective-permute-start | bytes 442376 | tf_op jit(solution)/shard_map/ppermute | solution.py:567
  35.3 10.0 %collective-permute-start.7 = (bf16[2,1,2,1,1,24,768]{6,5,4,3,2,1,0:T(8,128)(2,1)S(1)}, bf16[2,1,2,1,1,24,768]{6,5,4,3,2,1,0:T(8,128)(2,1)S(1)}, u32[]{:S(2)}, u32[]{:S(2)}) collective-permute-start(bf16[2,1,2,1,1,24,768]{6,5,4,3,2,1,0:T(8,128)(2,1)S(1)} %pad_maximum_fusion.10), channel_id=1, source_target_pairs={{0,8},{4,12},{8,0},{12,4},{16,24},{20,28},{24,16},{28,20},{1,9},{5... | collective-permute-start | bytes 442376 | tf_op jit(solution)/shard_map/ppermute | solution.py:567
  35.8 9.6 %collective-permute-start.6 = (bf16[2,2,1,1,1,24,896]{6,5,4,3,2,1,0:T(8,128)(2,1)S(1)}, bf16[2,2,1,1,1,24,896]{6,5,4,3,2,1,0:T(8,128)(2,1)S(1)}, u32[]{:S(2)}, u32[]{:S(2)}) collective-permute-start(bf16[2,2,1,1,1,24,896]{6,5,4,3,2,1,0:T(8,128)(2,1)S(1)} %pad_maximum_fusion.9), channel_id=1, source_target_pairs={{0,2},{1,3},{2,0},{3,1},{4,6},{5,7},{6,4},{7,5},{8,10},{9,11},{10,... | collective-permute-start | bytes 516104 | tf_op jit(solution)/shard_map/ppermute | solution.py:567
  45.5 8.6 %collective-permute-start.11 = (bf16[2,1,2,2,1,24,768]{6,5,4,3,2,1,0:T(8,128)(2,1)S(1)}, bf16[2,1,2,2,1,24,768]{6,5,4,3,2,1,0:T(8,128)(2,1)S(1)}, u32[]{:S(2)}, u32[]{:S(2)}) collective-permute-start(bf16[2,1,2,2,1,24,768]{6,5,4,3,2,1,0:T(8,128)(2,1)S(1)} %pad_maximum_fusion.8), channel_id=1, source_target_pairs={{0,8},{4,12},{8,0},{12,4},{16,24},{20,28},{24,16},{28,20},{1,9},{5... | collective-permute-start | bytes 884744 | tf_op jit(solution)/shard_map/ppermute | solution.py:567
  46.4 8.6 %collective-permute-start.10 = (bf16[2,2,2,1,1,24,768]{6,5,4,3,2,1,0:T(8,128)(2,1)S(1)}, bf16[2,2,2,1,1,24,768]{6,5,4,3,2,1,0:T(8,128)(2,1)S(1)}, u32[]{:S(2)}, u32[]{:S(2)}) collective-permute-start(bf16[2,2,2,1,1,24,768]{6,5,4,3,2,1,0:T(8,128)(2,1)S(1)} %pad_maximum_fusion.7), channel_id=1, source_target_pairs={{0,2},{1,3},{2,0},{3,1},{4,6},{5,7},{6,4},{7,5},{8,10},{9,11},{10,... | collective-permute-start | bytes 884744 | tf_op jit(solution)/shard_map/ppermute | solution.py:567
  47.1 8.8 %collective-permute-start.9 = (bf16[2,2,1,2,1,24,896]{6,5,4,3,2,1,0:T(8,128)(2,1)S(1)}, bf16[2,2,1,2,1,24,896]{6,5,4,3,2,1,0:T(8,128)(2,1)S(1)}, u32[]{:S(2)}, u32[]{:S(2)}) collective-permute-start(bf16[2,2,1,2,1,24,896]{6,5,4,3,2,1,0:T(8,128)(2,1)S(1)} %pad_maximum_fusion.6), channel_id=1, source_target_pairs={{0,4},{4,0},{8,12},{12,8},{16,20},{20,16},{24,28},{28,24},{1,5},{5... | collective-permute-start | bytes 1032200 | tf_op jit(solution)/shard_map/ppermute | solution.py:567
  293.5 24.7 %collective-permute-start.15 = (bf16[2,2,2,2,2,1,24,768]{7,6,5,4,3,2,1,0:T(8,128)(2,1)S(1)}, bf16[2,2,2,2,2,1,24,768]{7,6,5,4,3,2,1,0:T(8,128)(2,1)}, u32[]{:S(2)}, u32[]{:S(2)}) collective-permute-start(bf16[2,2,2,2,2,1,24,768]{7,6,5,4,3,2,1,0:T(8,128)(2,1)S(1)} %dynamic-slice_convert_fusion), channel_id=1, source_target_pairs={{0,1},{1,0},{2,3},{3,2},{4,5},{5,4},{6,7},{7,6},{8,9},{9,8},{10,11... | collective-permute-start | bytes 3538952 | tf_op jit(solution)/shard_map/ppermute | solution.py:567
  322.1 23.9 %collective-permute-start.16 = (bf16[2,2,2,2,1,1,24,768]{7,6,5,4,3,2,1,0:T(8,128)(2,1)S(1)}, bf16[2,2,2,2,1,1,24,768]{7,6,5,4,3,2,1,0:T(8,128)(2,1)S(1)}, u32[]{:S(2)}, u32[]{:S(2)}) collective-permute-start(bf16[2,2,2,2,1,1,24,768]{7,6,5,4,3,2,1,0:T(8,128)(2,1)S(1)} %dynamic-slice_convert_fusion.2), channel_id=1, source_target_pairs={{0,2},{1,3},{2,0},{3,1},{4,6},{5,7},{6,4},{7,5},{8,10},{9,11},{10,... | collective-permute-start | bytes 1769480 | tf_op jit(solution)/shard_map/ppermute | solution.py:567
  347.5 22.5 %collective-permute-start.17 = (bf16[2,2,1,2,1,1,24,768]{7,6,5,4,3,2,1,0:T(8,128)(2,1)S(1)}, bf16[2,2,1,2,1,1,24,768]{7,6,5,4,3,2,1,0:T(8,128)(2,1)}, u32[]{:S(2)}, u32[]{:S(2)}) collective-permute-start(bf16[2,2,1,2,1,1,24,768]{7,6,5,4,3,2,1,0:T(8,128)(2,1)S(1)} %dynamic-slice_convert_fusion.4), channel_id=1, source_target_pairs={{0,8},{4,12},{8,0},{12,4},{16,24},{20,28},{24,16},{28,20},{1,9},{5... | collective-permute-start | bytes 884744 | tf_op jit(solution)/shard_map/ppermute | solution.py:567
  372.5 9.3 %collective-permute-start.20 = (bf16[2,2,2,2,1,24,896]{6,5,4,3,2,1,0:T(8,128)(2,1)S(1)}, bf16[2,2,2,2,1,24,896]{6,5,4,3,2,1,0:T(8,128)(2,1)S(1)}, u32[]{:S(2)}, u32[]{:S(2)}) collective-permute-start(bf16[2,2,2,2,1,24,896]{6,5,4,3,2,1,0:T(8,128)(2,1)S(1)} %dynamic-slice_convert_fusion.1), channel_id=1, source_target_pairs={{0,1},{1,0},{2,3},{3,2},{4,5},{5,4},{6,7},{7,6},{8,9},{9,8},{10,11... | collective-permute-start | bytes 2064392 | tf_op jit(solution)/shard_map/ppermute | solution.py:567
  372.6 23.2 %collective-permute-start.18 = (bf16[2,2,1,1,1,1,24,768]{7,6,5,4,3,2,1,0:T(8,128)(2,1)S(1)}, bf16[2,2,1,1,1,1,24,768]{7,6,5,4,3,2,1,0:T(8,128)(2,1)S(1)}, u32[]{:S(2)}, u32[]{:S(2)}) collective-permute-start(bf16[2,2,1,1,1,1,24,768]{7,6,5,4,3,2,1,0:T(8,128)(2,1)S(1)} %dynamic-slice_convert_fusion.6), channel_id=1, source_target_pairs={{0,4},{4,0},{8,12},{12,8},{16,20},{20,16},{24,28},{28,24},{1,5},{5... | collective-permute-start | bytes 442376 | tf_op jit(solution)/shard_map/ppermute | solution.py:567
  382.7 10.5 %collective-permute-start.21 = (bf16[2,2,1,2,1,24,896]{6,5,4,3,2,1,0:T(8,128)(2,1)}, bf16[2,2,1,2,1,24,896]{6,5,4,3,2,1,0:T(8,128)(2,1)}, u32[]{:S(2)}, u32[]{:S(2)}) collective-permute-start(bf16[2,2,1,2,1,24,896]{6,5,4,3,2,1,0:T(8,128)(2,1)} %dynamic-slice_convert_fusion.3), channel_id=1, source_target_pairs={{0,4},{4,0},{8,12},{12,8},{16,20},{20,16},{24,28},{28,24},{1,5},{5... | collective-permute-start | bytes 1032200 | tf_op jit(solution)/shard_map/ppermute | solution.py:567
  394.2 5.9 %collective-permute-start.22 = (bf16[2,2,1,1,1,24,896]{6,5,4,3,2,1,0:T(8,128)(2,1)S(1)}, bf16[2,2,1,1,1,24,896]{6,5,4,3,2,1,0:T(8,128)(2,1)S(1)}, u32[]{:S(2)}, u32[]{:S(2)}) collective-permute-start(bf16[2,2,1,1,1,24,896]{6,5,4,3,2,1,0:T(8,128)(2,1)S(1)} %dynamic-slice_convert_fusion.5), channel_id=1, source_target_pairs={{0,2},{1,3},{2,0},{3,1},{4,6},{5,7},{6,4},{7,5},{8,10},{9,11},{10,... | collective-permute-start | bytes 516104 | tf_op jit(solution)/shard_map/ppermute | solution.py:567
  395.8 6.5 %collective-permute-start.19 = (bf16[2,1,1,1,1,1,24,768]{7,6,5,4,3,2,1,0:T(8,128)(2,1)S(1)}, bf16[2,1,1,1,1,1,24,768]{7,6,5,4,3,2,1,0:T(8,128)(2,1)S(1)}, u32[]{:S(2)}, u32[]{:S(2)}) collective-permute-start(bf16[2,1,1,1,1,1,24,768]{7,6,5,4,3,2,1,0:T(8,128)(2,1)S(1)} %dynamic-slice_convert_fusion.8), channel_id=1, source_target_pairs={{0,16},{4,20},{8,24},{12,28},{16,0},{20,4},{24,8},{28,12},{1,17},{... | collective-permute-start | bytes 221192 | tf_op jit(solution)/shard_map/ppermute | solution.py:567
  400.2 4.6 %collective-permute-start.23 = (bf16[2,1,1,1,1,24,896]{6,5,4,3,2,1,0:T(8,128)(2,1)S(1)}, bf16[2,1,1,1,1,24,896]{6,5,4,3,2,1,0:T(8,128)(2,1)S(1)}, u32[]{:S(2)}, u32[]{:S(2)}) collective-permute-start(bf16[2,1,1,1,1,24,896]{6,5,4,3,2,1,0:T(8,128)(2,1)S(1)} %dynamic-slice_convert_fusion.7), channel_id=1, source_target_pairs={{0,8},{4,12},{8,0},{12,4},{16,24},{20,28},{24,16},{28,20},{1,9},{5... | collective-permute-start | bytes 258056 | tf_op jit(solution)/shard_map/ppermute | solution.py:567
  404.8 5.0 %collective-permute-start.24 = (bf16[1,1,1,1,1,24,896]{6,5,4,3,2,1,0:T(8,128)(2,1)S(1)}, bf16[1,1,1,1,1,24,896]{6,5,4,3,2,1,0:T(8,128)(2,1)S(1)}, u32[]{:S(2)}, u32[]{:S(2)}) collective-permute-start(bf16[1,1,1,1,1,24,896]{6,5,4,3,2,1,0:T(8,128)(2,1)S(1)} %dynamic-slice_convert_fusion.9), channel_id=1, source_target_pairs={{0,16},{4,20},{8,24},{12,28},{16,0},{20,4},{24,8},{28,12},{1,17},{... | collective-permute-start | bytes 129032 | tf_op jit(solution)/shard_map/ppermute | solution.py:567
  (19 other events, 105.3 us)
Sparse Core Ops, SparseCore 0:
  25.5 91.2 all-gather.2
  243.8 151.8 reduce-scatter.1

commit v7 on v6

--- a/solution.py
+++ b/solution.py
@@ -680,7 +680,7 @@
         context, rows_low, cotangent.reshape(tokens, feature_width), w_o, w_u, w_d, small, b_u
     )
     grads = weight_grads(own, up_low, normed, hidden, down_low, att_low, context)
-    share = lax.psum_scatter(grads, ("wide", "narrow"), scatter_dimension=0, tiled=True)[0].astype(F32)
+    share = lax.psum_scatter(grads, ("wide", "narrow"), scatter_dimension=0, tiled=True)[0]
     w_plain = w_o.T
     att_low = att_low.reshape(inputs.shape)
     dq, dk, dv, grad_qk, sum_q = att_bwd(
@@ -696,13 +696,24 @@
             bounds, value_rows, att_low, w_o, small, inputs, dv, more, before, slabs, call * slabs
         )
         before, att_low, moving = lax.optimization_barrier((tuple(before), att_low, moved))
-    (dv, grad_v), dq, dk = lax.optimization_barrier((before, dq, dk))
-    share_qk = scatter_rest(moving, 1, calls)
-    share_v = scatter_rest(scatter_start(grad_v, own), 0, 0)
+    dv, grad_v = before
     input_grad = grad_one.reshape(inputs.shape)
-    for grad, weight in zip((dq, dk, dv), (w_q, w_k, w_v)):
-        input_grad = input_grad + jnp.einsum("bot,oi->bti", grad, weight, preferred_element_type=F32)
+    moved = scatter_start(grad_v, own)
+    turns = [(dq, w_q), (dk, w_k), (dv, w_v)]
+    for number in range(len(digits())):
+        moved = scatter_step(moved, 0, number)
+        if calls + number < len(digits()):
+            moving = scatter_step(moving, 1, calls + number)
+        if number < len(turns):
+            grad, weight = turns[number]
+            moved, moving, grad, input_grad = lax.optimization_barrier((moved, moving, grad, input_grad))
+            input_grad = input_grad + jnp.einsum("bot,oi->bti", grad, weight, preferred_element_type=F32)
+        elif number == len(digits()) - 2:
+            moved, share, input_grad = lax.optimization_barrier((moved, share, input_grad))
+    share_qk = moving.reshape(moving.shape[:1] + moving.shape[-2:])
+    share_v = moved.reshape(moved.shape[-2:])
     late = share_v[:, feature_width:]
+    share = share.astype(F32)
     share_down = share[own * lines : 2 * own * lines].reshape(ff_count, own, feature_width)
     share_out = share[2 * own * lines : 2 * own * lines + own]
     return (

time: 430 us -> 439 us (1.021)
  other arithmetic: 20.4 us -> 29 us
    add x0 -> x3, other arithmetic: none -> 8.55 us  [shards(): input_grad + jnp.einsum('bot,oi->bti', grad, weight, preferred_element_ty...]
  transfers between devices with their start and end apart: 27 -> 27, of which waited for: 11 -> 10; matrix products, arithmetic and copies ran while one was open for 11% -> 14% of each run, Pallas kernels for 42% -> 41%
where the time goes in v7:
time: 439 us; the launch traced here: 433 us
  Pallas kernels  281 us (64%)
  local copies, waits for them, and re-layouts  33 us (8%)
  starting transfers between devices  32.6 us (7%)
  other arithmetic  29 us (7%)
  waiting for transfers between devices  28.6 us (7%)
  between operations  14.8 us (3%)
  matrix products  14.4 us (3%)
    pallas_call x1, Pallas kernels, ffn(): pl.pallas_call(functools.partial(ffn_kernel, chunks, parts), grid=(T // b...  69.7 us
    pallas_call x3, Pallas kernels, conv_bwd(): pl.pallas_call(conv_bwd_kernel, grid_spec=pltpu.PrefetchScalarGridSpec(nu...  65.7 us
    pallas_call x1, Pallas kernels, att_bwd(): pl.pallas_call(att_bwd_kernel, grid=(G, B), in_specs=[seq((T, D)), seq((T...  45.3 us
    pallas_call x1, Pallas kernels, att_fwd(): pl.pallas_call(att_fwd_kernel, grid=(G, B), in_specs=[seq((T, D)), seq((L...  39.6 us
    pallas_call x1, Pallas kernels, weight_grads(): pl.pallas_call(functools.partial(weight_kernel, own), grid=(halves, T //...  33.2 us
    ppermute x25, starting transfers between devices, exchange(): lax.ppermute(values, axis, [(i, i ^ stride) for i in range(lax.axis_size(...  32.5 us
    ppermute x25, waiting for transfers between devices, exchange(): lax.ppermute(values, axis, [(i, i ^ stride) for i in range(lax.axis_size(...  28.5 us
    pallas_call x1, Pallas kernels, conv_fwd(): pl.pallas_call(conv_fwd_kernel, grid_spec=pltpu.PrefetchScalarGridSpec(nu...  27.4 us
  transfers between devices with their start and end apart: 27, of which 10 were waited for; matrix products, arithmetic and copies ran while one was open for 14% of the time, Pallas kernels for 41%

profile of v7, /device:TPU:0, one launch (start us, length us, event | category | flops | bytes accessed | tf_op | source)
XLA Modules:
  0.0 433.3 jit_solution(355991160354255082)
XLA Ops:
  7.2 4.1 collective-permute-start.2
  14.0 2.8 collective-permute-start
  30.3 3.1 collective-permute-done.5
  35.8 3.0 collective-permute-done.7
  38.8 5.3 %collective-permute-done.8 = bf16[2,1,1,2,1,24,768]{6,5,4,3,2,1,0:T(8,128)(2,1)S(1)} collective-permute-done((bf16[2,1,1,2,1,24,768]{6,5,4,3,2,1,0:T(8,128)(2,1)S(1)}, bf16[2,1,1,2,1,24,768]{6,5,4,3,2,1,0:T(8,128)(2,1)S(1)}, u32[]{:S(2)}, u32[]{:S(2)}) %collective-permute-start.8) | collective-permute-done | bytes 147488 | tf_op jit(solution)/shard_map/ppermute | solution.py:567
  47.5 3.6 collective-permute-done.10
  67.0 27.4 %shard_map.331 = (f32[2,1024,768]{2,1,0:T(8,128)}, f32[2,1024,768]{2,1,0:T(8,128)}) custom-call(s32[2,5]{1,0:T(2,128)} %copy.81.bounds_ref, bf16[2,1024,768]{2,1,0:T(8,128)(2,1)} %x_ref.11, bf16[768,768]{1,0:T(8,128)(2,1)} %slice.126.wv_ref, f32[128,768]{1,0:T(8,128)} %convert_bitcast_fusion.w_ref.vec_ref.refs_4_), custom_call_target="tpu_custom_call" | custom-call | tf_op jit(solution)/shard_map/pallas_call | solution.py:340
  94.4 39.6 %shard_map.332 = (bf16[2,768,1024]{2,1,0:T(8,128)(2,1)}, bf16[2,768,1024]{2,1,0:T(8,128)(2,1)}, bf16[2,768,1024]{2,1,0:T(8,128)(2,1)}, bf16[2,768,1024]{2,1,0:T(...) custom-call(bf16[2,1024,768]{2,1,0:T(8,128)(2,1)} %x_ref.11, ...), custom_call_target="tpu_custom_call" | custom-call | tf_op jit(solution)/shard_map/pallas_call | solution.py:154
  134.0 5.3 %fusion.8 = (bf16[32,24,768]{2,1,0:T(8,128)(2,1)}, bf16[32,24,768]{2,1,0:T(8,128)(2,1)}, bf16[32,24,768]{2,1,0:T(8,128)(2,1)}, bf16[32,24,768]{2,1,0:T(8,128)(2,1)}, bf16[32,24,768]{2,1,0:T(8,128)(2,1)}) fusion(bf16[32,216,768]{2,1,0:T(8,128)(2,1)} %bitcast.108), kind=kLoop, calls=%fused_computation.103 | loop fusion | bytes 11796480 | tf_op jit(solution)/shard_map/slice | solution.py:665
  139.4 69.7 %shard_map.333 = (bf16[2048,768]{1,0:T(8,128)(2,1)}, bf16[2048,768]{1,0:T(8,128)(2,1)}, bf16[2048,3072]{1,0:T(8,128)(2,1)}, bf16[2048,768]{1,0:T(8,128)(2,1)}, b...) custom-call(bf16[2048,768]{1,0:T(8,128)(2,1)} %bitcast.112, ...), custom_call_target="tpu_custom_call" | custom-call | tf_op jit(solution)/shard_map/pallas_call | solution.py:499
  209.1 33.2 %shard_map.338 = bf16[32,224,768]{2,1,0:T(8,128)(2,1)} custom-call(bf16[2048,3072]{1,0:T(8,128)(2,1)} %get-tuple-element.158.up_ref, bf16[2048,768]{1,0:T(8,128)(2,1)} %get-tuple-element.159.normed_ref, bf16[2048,3072]{1,0:T(8,128)(2,1)} %get-tuple-element.160.hidden_ref, bf16[2048,768]{1,0:T(8,128)(2,1)} %get-tuple-element.161.down_ref, ...), custom_call_target="tpu_custom_call" | custom-call | tf_op jit(solution)/shard_map/pallas_call | solution.py:541
  245.0 45.3 %shard_map.334 = (bf16[2,768,1024]{2,1,0:T(8,128)(2,1)}, bf16[2,768,1024]{2,1,0:T(8,128)(2,1)}, f32[2,768,1024]{2,1,0:T(8,128)}, f32[2,768,768]{2,1,0:T(8,128)}, f32[768,1]{1,0:T(8,128)}) custom-call(bf16[2,1024,768]{2,1,0:T(8,128)(2,1)} %x_ref.11, bf16[2,1024,768]{2,1,0:T(8,128)(2,1)} %bitcast.99, bf16[768,768]{1,0:T(8,128)(2,1)} %copy.86.wo_ref, ...), custom_call_target="tpu_custom_call" | custom-call | tf_op jit(solution)/shard_map/pallas_call | solution.py:260
  295.0 21.9 %shard_map.335 = (bf16[2,768,1024]{2,1,0:T(8,128)(2,1)}, f32[768,896]{1,0:T(8,128)}) custom-call(s32[2,5]{1,0:T(2,128)} %copy.81.bounds_ref, f32[2,1024,768]{2,1,0:T(8,128)} %get-tuple-element.114.v_ref, bf16[2,1024,768]{2,1,0:T(8,128)(2,1)} %bitcast.100, bf16[768,768]{1,0:T(8,128)(2,1)} %bitcast.104, f32[128,768]{1,0:T(8,128)} %convert_bitcast_fusion.w_ref.vec_ref.refs_4_, ...), custom_call_target="tpu_custom_call" | custom-call | tf_op jit(solution)/shard_map/pallas_call | solution.py:402
  320.6 21.9 %shard_map.336 = (bf16[2,768,1024]{2,1,0:T(8,128)(2,1)}, f32[768,896]{1,0:T(8,128)}) custom-call(s32[2,5]{1,0:T(2,128)} %copy.81.bounds_ref, f32[2,1024,768]{2,1,0:T(8,128)} %get-tuple-element.114.v_ref, bf16[2,1024,768]{2,1,0:T(8,128)(2,1)} %bitcast.101, bf16[768,768]{1,0:T(8,128)(2,1)} %bitcast.105, ...), custom_call_target="tpu_custom_call", output_to_operand_aliasing={{0}: (10, {}), {1}: (11, {})} | custom-call | tf_op jit(solution)/shard_map/pallas_call | solution.py:402
  347.1 21.9 %shard_map.337 = (bf16[2,768,1024]{2,1,0:T(8,128)(2,1)}, f32[768,896]{1,0:T(8,128)}) custom-call(s32[2,5]{1,0:T(2,128)} %copy.81.bounds_ref, f32[2,1024,768]{2,1,0:T(8,128)} %get-tuple-element.114.v_ref, bf16[2,1024,768]{2,1,0:T(8,128)(2,1)} %bitcast.102, bf16[768,768]{1,0:T(8,128)(2,1)} %bitcast.106, ...), custom_call_target="tpu_custom_call", output_to_operand_aliasing={{0}: (10, {}), {1}: (11, {})} | custom-call | tf_op jit(solution)/shard_map/pallas_call | solution.py:402
  374.8 5.1 %collective-permute-done.19 = bf16[2,2,1,1,1,1,24,768]{7,6,5,4,3,2,1,0:T(8,128)(2,1)S(1)} collective-permute-done((bf16[2,2,1,1,1,1,24,768]{7,6,5,4,3,2,1,0:T(8,128)(2,1)}, bf16[2,2,1,1,1,1,24,768]{7,6,5,4,3,2,1,0:T(8,128)(2,1)S(1)}, u32[]{:S(2)}, u32[]{:S(2)}) %collective-permute-start.19) | collective-permute-done | bytes 147488 | tf_op jit(solution)/shard_map/ppermute | solution.py:567
  383.5 2.6 collective-permute-start.21
  386.1 2.7 fusion.9
  389.7 3.0 collective-permute-done.21
  396.5 7.6 %fusion.10 = f32[2,1024,768]{2,1,0:T(8,128)} fusion(bf16[2,768,1024]{2,1,0:T(8,128)(2,1)} %get-tuple-element.156, bf16[768,768,1]{1,0,2:T(8,128)(2,1)} %bitcast.126), kind=kOutput, calls=%fused_computation.105 | convolution fusion | flops 2415919104 | bytes 10616832 | tf_op jit(solution)/shard_map/bot,oi->bti/dot_general | solution.py:710
  404.1 4.3 add.203
  409.9 2.7 fusion
  413.3 3.5 add.205
  416.9 2.6 collective-permute-start.24
  (177 shorter events, 76.3 us)
Async XLA Ops:
  7.2 126.8 %all-gather.3.cloned.1.call-start = ((), (), s32[]{:S(2)}) async-start(), calls=%async_computation.2 | async-start | bytes 10948608 | tf_op jit(solution)/shard_map/all_gather | solution.py:661
  7.2 9.6 %collective-permute-start.2 = (bf16[1,1,1,1,1,24,768]{6,5,4,3,2,1,0:T(8,128)(2,1)}, bf16[1,1,1,1,1,24,768]{6,5,4,3,2,1,0:T(8,128)(2,1)S(1)}, u32[]{:S(2)}, u32[]{:S(2)}) collective-permute-start(bf16[1,1,1,1,1,24,768]{6,5,4,3,2,1,0:T(8,128)(2,1)} %bitcast.139), channel_id=1, source_target_pairs={{0,16},{4,20},{8,24},{12,28},{16,0},{20,4},{24,8},{28,12},{1,17},{... | collective-permute-start | bytes 110600 | tf_op jit(solution)/shard_map/ppermute | solution.py:567
  11.3 5.5 %collective-permute-start.1 = (bf16[1,1,1,1,1,24,768]{6,5,4,3,2,1,0:T(8,128)(2,1)}, bf16[1,1,1,1,1,24,768]{6,5,4,3,2,1,0:T(8,128)(2,1)S(1)}, u32[]{:S(2)}, u32[]{:S(2)}) collective-permute-start(bf16[1,1,1,1,1,24,768]{6,5,4,3,2,1,0:T(8,128)(2,1)} %bitcast.140), channel_id=1, source_target_pairs={{0,16},{4,20},{8,24},{12,28},{16,0},{20,4},{24,8},{28,12},{1,17},{... | collective-permute-start | bytes 110600 | tf_op jit(solution)/shard_map/ppermute | solution.py:567
  14.0 5.0 %collective-permute-start = (bf16[1,1,1,1,1,24,896]{6,5,4,3,2,1,0:T(8,128)(2,1)S(1)}, bf16[1,1,1,1,1,24,896]{6,5,4,3,2,1,0:T(8,128)(2,1)S(1)}, u32[]{:S(2)}, u32[]{:S(2)}) collective-permute-start(bf16[1,1,1,1,1,24,896]{6,5,4,3,2,1,0:T(8,128)(2,1)S(1)} %fusion.5), channel_id=1, source_target_pairs={{0,16},{4,20},{8,24},{12,28},{16,0},{20,4},{24,8},{28,12},{1,17},{... | collective-permute-start | bytes 129032 | tf_op jit(solution)/shard_map/ppermute | solution.py:567
  25.4 391.5 %reduce-scatter.2.cloned.1.call-start = ((), (), s32[]{:S(2)}) async-start(), calls=%async_computation.1 | async-start | bytes 11354112 | tf_op jit(solution)/shard_map/reduce_scatter | solution.py:683
  25.4 4.9 %collective-permute-start.4 = (bf16[2,1,1,1,1,24,768]{6,5,4,3,2,1,0:T(8,128)(2,1)S(1)}, bf16[2,1,1,1,1,24,768]{6,5,4,3,2,1,0:T(8,128)(2,1)S(1)}, u32[]{:S(2)}, u32[]{:S(2)}) collective-permute-start(bf16[2,1,1,1,1,24,768]{6,5,4,3,2,1,0:T(8,128)(2,1)S(1)} %pad_maximum_fusion.13), channel_id=1, source_target_pairs={{0,4},{4,0},{8,12},{12,8},{16,20},{20,16},{24,28},{28,24},{1,5},{5... | collective-permute-start | bytes 221192 | tf_op jit(solution)/shard_map/ppermute | solution.py:567
  27.2 6.3 %collective-permute-start.3 = (bf16[2,1,1,1,1,24,896]{6,5,4,3,2,1,0:T(8,128)(2,1)S(1)}, bf16[2,1,1,1,1,24,896]{6,5,4,3,2,1,0:T(8,128)(2,1)S(1)}, u32[]{:S(2)}, u32[]{:S(2)}) collective-permute-start(bf16[2,1,1,1,1,24,896]{6,5,4,3,2,1,0:T(8,128)(2,1)S(1)} %pad_maximum_fusion.12), channel_id=1, source_target_pairs={{0,8},{4,12},{8,0},{12,4},{16,24},{20,28},{24,16},{28,20},{1,9},{5... | collective-permute-start | bytes 258056 | tf_op jit(solution)/shard_map/ppermute | solution.py:567
  28.8 4.7 %collective-permute-start.5 = (bf16[2,1,1,1,1,24,768]{6,5,4,3,2,1,0:T(8,128)(2,1)S(1)}, bf16[2,1,1,1,1,24,768]{6,5,4,3,2,1,0:T(8,128)(2,1)S(1)}, u32[]{:S(2)}, u32[]{:S(2)}) collective-permute-start(bf16[2,1,1,1,1,24,768]{6,5,4,3,2,1,0:T(8,128)(2,1)S(1)} %pad_maximum_fusion.14), channel_id=1, source_target_pairs={{0,2},{1,3},{2,0},{3,1},{4,6},{5,7},{6,4},{7,5},{8,10},{9,11},{10,... | collective-permute-start | bytes 221192 | tf_op jit(solution)/shard_map/ppermute | solution.py:567
  33.6 5.2 %collective-permute-start.7 = (bf16[2,1,2,1,1,24,768]{6,5,4,3,2,1,0:T(8,128)(2,1)S(1)}, bf16[2,1,2,1,1,24,768]{6,5,4,3,2,1,0:T(8,128)(2,1)S(1)}, u32[]{:S(2)}, u32[]{:S(2)}) collective-permute-start(bf16[2,1,2,1,1,24,768]{6,5,4,3,2,1,0:T(8,128)(2,1)S(1)} %pad_maximum_fusion.10), channel_id=1, source_target_pairs={{0,8},{4,12},{8,0},{12,4},{16,24},{20,28},{24,16},{28,20},{1,9},{5... | collective-permute-start | bytes 442376 | tf_op jit(solution)/shard_map/ppermute | solution.py:567
  33.7 10.4 %collective-permute-start.6 = (bf16[2,2,1,1,1,24,896]{6,5,4,3,2,1,0:T(8,128)(2,1)S(1)}, bf16[2,2,1,1,1,24,896]{6,5,4,3,2,1,0:T(8,128)(2,1)S(1)}, u32[]{:S(2)}, u32[]{:S(2)}) collective-permute-start(bf16[2,2,1,1,1,24,896]{6,5,4,3,2,1,0:T(8,128)(2,1)S(1)} %pad_maximum_fusion.9), channel_id=1, source_target_pairs={{0,2},{1,3},{2,0},{3,1},{4,6},{5,7},{6,4},{7,5},{8,10},{9,11},{10,... | collective-permute-start | bytes 516104 | tf_op jit(solution)/shard_map/ppermute | solution.py:567
  35.3 8.8 %collective-permute-start.8 = (bf16[2,1,1,2,1,24,768]{6,5,4,3,2,1,0:T(8,128)(2,1)S(1)}, bf16[2,1,1,2,1,24,768]{6,5,4,3,2,1,0:T(8,128)(2,1)S(1)}, u32[]{:S(2)}, u32[]{:S(2)}) collective-permute-start(bf16[2,1,1,2,1,24,768]{6,5,4,3,2,1,0:T(8,128)(2,1)S(1)} %pad_maximum_fusion.11), channel_id=1, source_target_pairs={{0,4},{4,0},{8,12},{12,8},{16,20},{20,16},{24,28},{28,24},{1,5},{5... | collective-permute-start | bytes 442376 | tf_op jit(solution)/shard_map/ppermute | solution.py:567
  44.3 6.8 %collective-permute-start.10 = (bf16[2,2,2,1,1,24,768]{6,5,4,3,2,1,0:T(8,128)(2,1)S(1)}, bf16[2,2,2,1,1,24,768]{6,5,4,3,2,1,0:T(8,128)(2,1)S(1)}, u32[]{:S(2)}, u32[]{:S(2)}) collective-permute-start(bf16[2,2,2,1,1,24,768]{6,5,4,3,2,1,0:T(8,128)(2,1)S(1)} %pad_maximum_fusion.7), channel_id=1, source_target_pairs={{0,2},{1,3},{2,0},{3,1},{4,6},{5,7},{6,4},{7,5},{8,10},{9,11},{10,... | collective-permute-start | bytes 884744 | tf_op jit(solution)/shard_map/ppermute | solution.py:567
  44.9 9.6 %collective-permute-start.9 = (bf16[2,2,1,2,1,24,896]{6,5,4,3,2,1,0:T(8,128)(2,1)S(1)}, bf16[2,2,1,2,1,24,896]{6,5,4,3,2,1,0:T(8,128)(2,1)S(1)}, u32[]{:S(2)}, u32[]{:S(2)}) collective-permute-start(bf16[2,2,1,2,1,24,896]{6,5,4,3,2,1,0:T(8,128)(2,1)S(1)} %pad_maximum_fusion.6), channel_id=1, source_target_pairs={{0,4},{4,0},{8,12},{12,8},{16,20},{20,16},{24,28},{28,24},{1,5},{5... | collective-permute-start | bytes 1032200 | tf_op jit(solution)/shard_map/ppermute | solution.py:567
  45.1 8.4 %collective-permute-start.11 = (bf16[2,1,2,2,1,24,768]{6,5,4,3,2,1,0:T(8,128)(2,1)S(1)}, bf16[2,1,2,2,1,24,768]{6,5,4,3,2,1,0:T(8,128)(2,1)S(1)}, u32[]{:S(2)}, u32[]{:S(2)}) collective-permute-start(bf16[2,1,2,2,1,24,768]{6,5,4,3,2,1,0:T(8,128)(2,1)S(1)} %pad_maximum_fusion.8), channel_id=1, source_target_pairs={{0,8},{4,12},{8,0},{12,4},{16,24},{20,28},{24,16},{28,20},{1,9},{5... | collective-permute-start | bytes 884744 | tf_op jit(solution)/shard_map/ppermute | solution.py:567
  292.1 24.8 %collective-permute-start.15 = (bf16[2,2,2,2,2,1,24,768]{7,6,5,4,3,2,1,0:T(8,128)(2,1)S(1)}, bf16[2,2,2,2,2,1,24,768]{7,6,5,4,3,2,1,0:T(8,128)(2,1)S(1)}, u32[]{:S(2)}, u32[]{:S(2)}) collective-permute-start(bf16[2,2,2,2,2,1,24,768]{7,6,5,4,3,2,1,0:T(8,128)(2,1)S(1)} %dynamic-slice_convert_fusion), channel_id=1, source_target_pairs={{0,1},{1,0},{2,3},{3,2},{4,5},{5,4},{6,7},{7,6},{8,9},{9,8},{10,11... | collective-permute-start | bytes 3538952 | tf_op jit(solution)/shard_map/ppermute | solution.py:567
  319.0 25.3 %collective-permute-start.16 = (bf16[2,2,2,2,1,1,24,768]{7,6,5,4,3,2,1,0:T(8,128)(2,1)S(1)}, bf16[2,2,2,2,1,1,24,768]{7,6,5,4,3,2,1,0:T(8,128)(2,1)S(1)}, u32[]{:S(2)}, u32[]{:S(2)}) collective-permute-start(bf16[2,2,2,2,1,1,24,768]{7,6,5,4,3,2,1,0:T(8,128)(2,1)S(1)} %dynamic-slice_convert_fusion.2), channel_id=1, source_target_pairs={{0,2},{1,3},{2,0},{3,1},{4,6},{5,7},{6,4},{7,5},{8,10},{9,11},{10,... | collective-permute-start | bytes 1769480 | tf_op jit(solution)/shard_map/ppermute | solution.py:567
  345.5 23.5 %collective-permute-start.17 = (bf16[2,2,1,2,1,1,24,768]{7,6,5,4,3,2,1,0:T(8,128)(2,1)S(1)}, bf16[2,2,1,2,1,1,24,768]{7,6,5,4,3,2,1,0:T(8,128)(2,1)}, u32[]{:S(2)}, u32[]{:S(2)}) collective-permute-start(bf16[2,2,1,2,1,1,24,768]{7,6,5,4,3,2,1,0:T(8,128)(2,1)S(1)} %dynamic-slice_convert_fusion.4), channel_id=1, source_target_pairs={{0,8},{4,12},{8,0},{12,4},{16,24},{20,28},{24,16},{28,20},{1,9},{5... | collective-permute-start | bytes 884744 | tf_op jit(solution)/shard_map/ppermute | solution.py:567
  372.7 7.2 %collective-permute-start.18 = (bf16[2,2,2,2,1,24,896]{6,5,4,3,2,1,0:T(8,128)(2,1)}, bf16[2,2,2,2,1,24,896]{6,5,4,3,2,1,0:T(8,128)(2,1)}, u32[]{:S(2)}, u32[]{:S(2)}) collective-permute-start(bf16[2,2,2,2,1,24,896]{6,5,4,3,2,1,0:T(8,128)(2,1)} %dynamic-slice_convert_fusion.1), channel_id=1, source_target_pairs={{0,1},{1,0},{2,3},{3,2},{4,5},{5,4},{6,7},{7,6},{8,9},{9,8},{10,11... | collective-permute-start | bytes 2064392 | tf_op jit(solution)/shard_map/ppermute | solution.py:567
  373.4 6.5 %collective-permute-start.19 = (bf16[2,2,1,1,1,1,24,768]{7,6,5,4,3,2,1,0:T(8,128)(2,1)}, bf16[2,2,1,1,1,1,24,768]{7,6,5,4,3,2,1,0:T(8,128)(2,1)S(1)}, u32[]{:S(2)}, u32[]{:S(2)}) collective-permute-start(bf16[2,2,1,1,1,1,24,768]{7,6,5,4,3,2,1,0:T(8,128)(2,1)} %dynamic-slice_convert_fusion.6), channel_id=1, source_target_pairs={{0,4},{4,0},{8,12},{12,8},{16,20},{20,16},{24,28},{28,24},{1,5},{5... | collective-permute-start | bytes 442376 | tf_op jit(solution)/shard_map/ppermute | solution.py:567
  382.1 11.5 %collective-permute-start.20 = (bf16[2,2,1,2,1,24,896]{6,5,4,3,2,1,0:T(8,128)(2,1)}, bf16[2,2,1,2,1,24,896]{6,5,4,3,2,1,0:T(8,128)(2,1)}, u32[]{:S(2)}, u32[]{:S(2)}) collective-permute-start(bf16[2,2,1,2,1,24,896]{6,5,4,3,2,1,0:T(8,128)(2,1)} %dynamic-slice_convert_fusion.3), channel_id=1, source_target_pairs={{0,4},{4,0},{8,12},{12,8},{16,20},{20,16},{24,28},{28,24},{1,5},{5... | collective-permute-start | bytes 1032200 | tf_op jit(solution)/shard_map/ppermute | solution.py:567
  383.5 9.2 %collective-permute-start.21 = (bf16[2,1,1,1,1,1,24,768]{7,6,5,4,3,2,1,0:T(8,128)(2,1)S(1)}, bf16[2,1,1,1,1,1,24,768]{7,6,5,4,3,2,1,0:T(8,128)(2,1)S(1)}, u32[]{:S(2)}, u32[]{:S(2)}) collective-permute-start(bf16[2,1,1,1,1,1,24,768]{7,6,5,4,3,2,1,0:T(8,128)(2,1)S(1)} %dynamic-slice_convert_fusion.8), channel_id=1, source_target_pairs={{0,16},{4,20},{8,24},{12,28},{16,0},{20,4},{24,8},{28,12},{1,17},{... | collective-permute-start | bytes 221192 | tf_op jit(solution)/shard_map/ppermute | solution.py:567
  395.0 13.4 %collective-permute-start.22 = (bf16[2,2,1,1,1,24,896]{6,5,4,3,2,1,0:T(8,128)(2,1)S(1)}, bf16[2,2,1,1,1,24,896]{6,5,4,3,2,1,0:T(8,128)(2,1)S(1)}, u32[]{:S(2)}, u32[]{:S(2)}) collective-permute-start(bf16[2,2,1,1,1,24,896]{6,5,4,3,2,1,0:T(8,128)(2,1)S(1)} %dynamic-slice_convert_fusion.5), channel_id=1, source_target_pairs={{0,2},{1,3},{2,0},{3,1},{4,6},{5,7},{6,4},{7,5},{8,10},{9,11},{10,... | collective-permute-start | bytes 516104 | tf_op jit(solution)/shard_map/ppermute | solution.py:567
  408.4 8.4 %collective-permute-start.23 = (bf16[2,1,1,1,1,24,896]{6,5,4,3,2,1,0:T(8,128)(2,1)S(1)}, bf16[2,1,1,1,1,24,896]{6,5,4,3,2,1,0:T(8,128)(2,1)S(1)}, u32[]{:S(2)}, u32[]{:S(2)}) collective-permute-start(bf16[2,1,1,1,1,24,896]{6,5,4,3,2,1,0:T(8,128)(2,1)S(1)} %dynamic-slice_convert_fusion.7), channel_id=1, source_target_pairs={{0,8},{4,12},{8,0},{12,4},{16,24},{20,28},{24,16},{28,20},{1,9},{5... | collective-permute-start | bytes 258056 | tf_op jit(solution)/shard_map/ppermute | solution.py:567
  416.9 6.6 %collective-permute-start.24 = (bf16[1,1,1,1,1,24,896]{6,5,4,3,2,1,0:T(8,128)(2,1)S(1)}, bf16[1,1,1,1,1,24,896]{6,5,4,3,2,1,0:T(8,128)(2,1)S(1)}, u32[]{:S(2)}, u32[]{:S(2)}) collective-permute-start(bf16[1,1,1,1,1,24,896]{6,5,4,3,2,1,0:T(8,128)(2,1)S(1)} %dynamic-slice_convert_fusion.9), channel_id=1, source_target_pairs={{0,16},{4,20},{8,24},{12,28},{16,0},{20,4},{24,8},{28,12},{1,17},{... | collective-permute-start | bytes 129032 | tf_op jit(solution)/shard_map/ppermute | solution.py:567
  (23 other events, 184.1 us)
Sparse Core Ops, SparseCore 0:
  25.5 91.3 all-gather.2
  242.4 155.2 reduce-scatter.1

commit v8 on v7

--- a/solution.py
+++ b/solution.py
@@ -571,7 +571,7 @@
     return (lax.axis_index(axis) // stride) % 2
 
 
-def gather_rows(shards):
+def gather_rows(shards, others):
     places = digits()
     held = [shard.reshape((1,) * len(places) + shard.shape) for shard in shards]
     passed = []
@@ -583,9 +583,12 @@
             first = jnp.where(mine == 0, values, got)
             second = jnp.where(mine == 0, got, values)
             held[number] = jnp.concatenate([first, second], dim)
-        held = list(lax.optimization_barrier(tuple(held)))
+        if step == 2:
+            held, others = lax.optimization_barrier((held, others))
+        else:
+            held = lax.optimization_barrier(held)
         passed.append(held[0])
-    return [values.reshape((-1,) + values.shape[-2:]) for values in held], passed
+    return [values.reshape((-1,) + values.shape[-2:]) for values in held], passed, others
 
 
 def scatter_start(whole, own):
@@ -642,8 +645,13 @@
         flat = flat + jnp.pad(vector, (before, (8 + lines) * own - before - vector.shape[0]))
     small = jnp.concatenate([conv_weight, flat.reshape(8 + lines, own)])
     small = jnp.pad(small.T, ((0, 0), (0, 128 - small.shape[0])))
-    (gathered_v, w_q, w_k), passed = gather_rows(
-        [jnp.concatenate([w_value.T, small], axis=1), w_query.T, w_key.T]
+    member = tok_landmark[:, None, :] == jnp.arange(LM)[None, :, None]
+    means = jnp.einsum("bjt,bti->bji", member.astype(BF), inputs, preferred_element_type=F32)
+    means = means / jnp.sum(member, axis=2)[..., None].astype(F32)
+    doc = jnp.sum(jnp.where(member, landmark_doc[:, :, None], 0), axis=1)
+    bounds = jnp.sum(doc[:, None, :] < jnp.arange(DOCS + 1)[None, :, None], axis=2).astype(jnp.int32)
+    (gathered_v, w_q, w_k), passed, (means, bounds) = gather_rows(
+        [jnp.concatenate([w_value.T, small], axis=1), w_query.T, w_key.T], (means, bounds)
     )
     w_q = w_q.reshape(feature_width, feature_width)
     w_k = w_k.reshape(feature_width, feature_width)
@@ -665,11 +673,6 @@
         gathered[:, own * (1 + lines + i) : own * (2 + lines + i)].reshape(feature_width, feature_width)
         for i in range(ff_count)
     ]
-    member = tok_landmark[:, None, :] == jnp.arange(LM)[None, :, None]
-    means = jnp.einsum("bjt,bti->bji", member.astype(BF), inputs, preferred_element_type=F32)
-    means = means / jnp.sum(member, axis=2)[..., None].astype(F32)
-    doc = jnp.sum(jnp.where(member, landmark_doc[:, :, None], 0), axis=1)
-    bounds = jnp.sum(doc[:, None, :] < jnp.arange(DOCS + 1)[None, :, None], axis=2).astype(jnp.int32)
     rows_low = inputs.reshape(tokens, feature_width)
     value_rows, conv_part = conv_fwd(bounds, inputs, w_v, small)
     q, k, v, k1, k3, inv, stash, landmarks, context = att_fwd(
@@ -697,17 +700,25 @@
         )
         before, att_low, moving = lax.optimization_barrier((tuple(before), att_low, moved))
     dv, grad_v = before
-    input_grad = grad_one.reshape(inputs.shape)
     moved = scatter_start(grad_v, own)
-    turns = [(dq, w_q), (dk, w_k), (dv, w_v)]
+
+    def through(grad, weight):
+        return jnp.einsum("bot,oi->bti", grad, weight, preferred_element_type=F32)
+
+    parts = ()
     for number in range(len(digits())):
         moved = scatter_step(moved, 0, number)
         if calls + number < len(digits()):
             moving = scatter_step(moving, 1, calls + number)
-        if number < len(turns):
-            grad, weight = turns[number]
-            moved, moving, grad, input_grad = lax.optimization_barrier((moved, moving, grad, input_grad))
-            input_grad = input_grad + jnp.einsum("bot,oi->bti", grad, weight, preferred_element_type=F32)
+        if number == 0:
+            moved, moving, dq = lax.optimization_barrier((moved, moving, dq))
+            parts = (through(dq, w_q),)
+        elif number == 1:
+            moved, moving, dk, parts = lax.optimization_barrier((moved, moving, dk, parts))
+            parts = parts + (through(dk, w_k),)
+        elif number == 2:
+            moved, dv, parts = lax.optimization_barrier((moved, dv, parts))
+            input_grad = grad_one.reshape(inputs.shape) + parts[0] + parts[1] + through(dv, w_v)
         elif number == len(digits()) - 2:
             moved, share, input_grad = lax.optimization_barrier((moved, share, input_grad))
     share_qk = moving.reshape(moving.shape[:1] + moving.shape[-2:])

time: 439 us -> 424 us (0.966)
  other arithmetic: 29 us -> 19.1 us
    add x3 -> x0, other arithmetic: 8.55 us -> none  [shards(): input_grad + jnp.einsum('bot,oi->bti', grad, weight, preferred_element_ty...]
  transfers between devices with their start and end apart: 27 -> 27, of which waited for: 10 -> 11; matrix products, arithmetic and copies ran while one was open for 14% -> 11% of each run, Pallas kernels for 41% -> 43%
where the time goes in v8:
time: 424 us; the launch traced here: 418 us
  Pallas kernels  281 us (66%)
  local copies, waits for them, and re-layouts  32.3 us (8%)
  starting transfers between devices  29.9 us (7%)
  waiting for transfers between devices  29 us (7%)
  other arithmetic  19.1 us (5%)
  between operations  15 us (4%)
  matrix products  12.3 us (3%)
    pallas_call x1, Pallas kernels, ffn(): pl.pallas_call(functools.partial(ffn_kernel, chunks, parts), grid=(T // b...  69.7 us
    pallas_call x3, Pallas kernels, conv_bwd(): pl.pallas_call(conv_bwd_kernel, grid_spec=pltpu.PrefetchScalarGridSpec(nu...  65.5 us
    pallas_call x1, Pallas kernels, att_bwd(): pl.pallas_call(att_bwd_kernel, grid=(G, B), in_specs=[seq((T, D)), seq((T...  45.2 us
    pallas_call x1, Pallas kernels, att_fwd(): pl.pallas_call(att_fwd_kernel, grid=(G, B), in_specs=[seq((T, D)), seq((L...  39.8 us
    pallas_call x1, Pallas kernels, weight_grads(): pl.pallas_call(functools.partial(weight_kernel, own), grid=(halves, T //...  33.2 us
    ppermute x25, starting transfers between devices, exchange(): lax.ppermute(values, axis, [(i, i ^ stride) for i in range(lax.axis_size(...  29.8 us
    ppermute x25, waiting for transfers between devices, exchange(): lax.ppermute(values, axis, [(i, i ^ stride) for i in range(lax.axis_size(...  28.9 us
    pallas_call x1, Pallas kernels, conv_fwd(): pl.pallas_call(conv_fwd_kernel, grid_spec=pltpu.PrefetchScalarGridSpec(nu...  27.4 us
  transfers between devices with their start and end apart: 27, of which 11 were waited for; matrix products, arithmetic and copies ran while one was open for 11% of the time, Pallas kernels for 43%

profile of v8, /device:TPU:0, one launch (start us, length us, event | category | flops | bytes accessed | tf_op | source)
XLA Modules:
  0.0 418.2 jit_solution(1792750740696748050)
XLA Ops:
  7.3 4.1 collective-permute-start.2
  14.0 2.8 collective-permute-start
  32.9 1.9 collective-permute-done.5
  36.3 2.0 convolution_divide_fusion.mean_ref
  40.7 2.9 collective-permute-done.7
  48.2 4.3 %collective-permute-done.10 = bf16[2,2,2,1,1,24,768]{6,5,4,3,2,1,0:T(8,128)(2,1)S(1)} collective-permute-done((bf16[2,2,2,1,1,24,768]{6,5,4,3,2,1,0:T(8,128)(2,1)S(1)}, bf16[2,2,2,1,1,24,768]{6,5,4,3,2,1,0:T(8,128)(2,1)S(1)}, u32[]{:S(2)}, u32[]{:S(2)}) %collective-permute-start.10) | collective-permute-done | bytes 294944 | tf_op jit(solution)/shard_map/ppermute | solution.py:567
  52.6 3.1 collective-permute-done.11
  64.6 27.4 %shard_map.331 = (f32[2,1024,768]{2,1,0:T(8,128)}, f32[2,1024,768]{2,1,0:T(8,128)}) custom-call(s32[2,5]{1,0:T(2,128)} %copy.81.bounds_ref, bf16[2,1024,768]{2,1,0:T(8,128)(2,1)} %x_ref.11, bf16[768,768]{1,0:T(8,128)(2,1)} %slice.126.wv_ref, f32[128,768]{1,0:T(8,128)} %convert_bitcast_fusion.w_ref.vec_ref.refs_4_), custom_call_target="tpu_custom_call" | custom-call | tf_op jit(solution)/shard_map/pallas_call | solution.py:340
  92.0 39.8 %shard_map.332 = (bf16[2,768,1024]{2,1,0:T(8,128)(2,1)}, bf16[2,768,1024]{2,1,0:T(8,128)(2,1)}, bf16[2,768,1024]{2,1,0:T(8,128)(2,1)}, bf16[2,768,1024]{2,1,0:T(...) custom-call(bf16[2,1024,768]{2,1,0:T(8,128)(2,1)} %x_ref.11, ...), custom_call_target="tpu_custom_call" | custom-call | tf_op jit(solution)/shard_map/pallas_call | solution.py:154
  131.8 5.4 %fusion.10 = (bf16[32,24,768]{2,1,0:T(8,128)(2,1)}, bf16[32,24,768]{2,1,0:T(8,128)(2,1)}, bf16[32,24,768]{2,1,0:T(8,128)(2,1)}, bf16[32,24,768]{2,1,0:T(8,128)(2,1)}, bf16[32,24,768]{2,1,0:T(8,128)(2,1)}) fusion(bf16[32,216,768]{2,1,0:T(8,128)(2,1)} %bitcast.110), kind=kLoop, calls=%fused_computation.104 | loop fusion | bytes 11796480 | tf_op jit(solution)/shard_map/slice | solution.py:673
  137.2 69.7 %shard_map.333 = (bf16[2048,768]{1,0:T(8,128)(2,1)}, bf16[2048,768]{1,0:T(8,128)(2,1)}, bf16[2048,3072]{1,0:T(8,128)(2,1)}, bf16[2048,768]{1,0:T(8,128)(2,1)}, b...) custom-call(bf16[2048,768]{1,0:T(8,128)(2,1)} %bitcast.114, ...), custom_call_target="tpu_custom_call" | custom-call | tf_op jit(solution)/shard_map/pallas_call | solution.py:499
  206.8 33.2 %shard_map.338 = bf16[32,224,768]{2,1,0:T(8,128)(2,1)} custom-call(bf16[2048,3072]{1,0:T(8,128)(2,1)} %get-tuple-element.158.up_ref, bf16[2048,768]{1,0:T(8,128)(2,1)} %get-tuple-element.159.normed_ref, bf16[2048,3072]{1,0:T(8,128)(2,1)} %get-tuple-element.160.hidden_ref, bf16[2048,768]{1,0:T(8,128)(2,1)} %get-tuple-element.161.down_ref, ...), custom_call_target="tpu_custom_call" | custom-call | tf_op jit(solution)/shard_map/pallas_call | solution.py:541
  242.8 45.2 %shard_map.334 = (bf16[2,768,1024]{2,1,0:T(8,128)(2,1)}, bf16[2,768,1024]{2,1,0:T(8,128)(2,1)}, f32[2,768,1024]{2,1,0:T(8,128)}, f32[2,768,768]{2,1,0:T(8,128)}, f32[768,1]{1,0:T(8,128)}) custom-call(bf16[2,1024,768]{2,1,0:T(8,128)(2,1)} %x_ref.11, bf16[2,1024,768]{2,1,0:T(8,128)(2,1)} %bitcast.101, bf16[768,768]{1,0:T(8,128)(2,1)} %copy.86.wo_ref, ...), custom_call_target="tpu_custom_call" | custom-call | tf_op jit(solution)/shard_map/pallas_call | solution.py:260
  292.6 21.8 %shard_map.335 = (bf16[2,768,1024]{2,1,0:T(8,128)(2,1)}, f32[768,896]{1,0:T(8,128)}) custom-call(s32[2,5]{1,0:T(2,128)} %copy.81.bounds_ref, f32[2,1024,768]{2,1,0:T(8,128)} %get-tuple-element.117.v_ref, bf16[2,1024,768]{2,1,0:T(8,128)(2,1)} %bitcast.102, bf16[768,768]{1,0:T(8,128)(2,1)} %bitcast.106, f32[128,768]{1,0:T(8,128)} %convert_bitcast_fusion.w_ref.vec_ref.refs_4_, ...), custom_call_target="tpu_custom_call" | custom-call | tf_op jit(solution)/shard_map/pallas_call | solution.py:402
  314.4 2.0 convert_add_fusion
  318.1 21.9 %shard_map.336 = (bf16[2,768,1024]{2,1,0:T(8,128)(2,1)}, f32[768,896]{1,0:T(8,128)}) custom-call(s32[2,5]{1,0:T(2,128)} %copy.81.bounds_ref, f32[2,1024,768]{2,1,0:T(8,128)} %get-tuple-element.117.v_ref, bf16[2,1024,768]{2,1,0:T(8,128)(2,1)} %bitcast.103, bf16[768,768]{1,0:T(8,128)(2,1)} %bitcast.107, ...), custom_call_target="tpu_custom_call", output_to_operand_aliasing={{0}: (10, {}), {1}: (11, {})} | custom-call | tf_op jit(solution)/shard_map/pallas_call | solution.py:402
  344.2 21.8 %shard_map.337 = (bf16[2,768,1024]{2,1,0:T(8,128)(2,1)}, f32[768,896]{1,0:T(8,128)}) custom-call(s32[2,5]{1,0:T(2,128)} %copy.81.bounds_ref, f32[2,1024,768]{2,1,0:T(8,128)} %get-tuple-element.117.v_ref, bf16[2,1024,768]{2,1,0:T(8,128)(2,1)} %bitcast.104, bf16[768,768]{1,0:T(8,128)(2,1)} %bitcast.108, ...), custom_call_target="tpu_custom_call", output_to_operand_aliasing={{0}: (10, {}), {1}: (11, {})} | custom-call | tf_op jit(solution)/shard_map/pallas_call | solution.py:402
  367.3 2.3 dynamic-slice_convert_fusion.1
  371.5 5.2 %collective-permute-done.19 = bf16[2,2,1,1,1,1,24,768]{7,6,5,4,3,2,1,0:T(8,128)(2,1)S(1)} collective-permute-done((bf16[2,2,1,1,1,1,24,768]{7,6,5,4,3,2,1,0:T(8,128)(2,1)}, bf16[2,2,1,1,1,1,24,768]{7,6,5,4,3,2,1,0:T(8,128)(2,1)S(1)}, u32[]{:S(2)}, u32[]{:S(2)}) %collective-permute-start.19) | collective-permute-done | bytes 147488 | tf_op jit(solution)/shard_map/ppermute | solution.py:567
  379.4 2.3 collective-permute-start.21
  381.8 2.7 fusion.11
  384.4 4.1 collective-permute-done.21
  391.7 2.8 fusion.12
  397.5 4.8 %add_add_fusion = f32[2,1024,768]{2,1,0:T(8,128)} fusion(f32[2,1024,768]{2,1,0:T(8,128)S(1)} %fusion.12, f32[2,1024,768]{2,1,0:T(8,128)S(1)} %bitcast.122, f32[2,1024,768]{2,1,0:T(8,128)S(1)} %fusion.11, bf16[2,768,1024]{2,1,0:T(8,128)(2,1)S(1)} %copy-done.2, bf16[768,896]{1,0:T(8,128)(2,1)S(1)} %bitcast.119), kind=kOutput, calls=%fused_computation | convolution fusion | flops 2420637696 | bytes 29491200 | tf_op jit(solution)/shard_map/bot,oi->bti/dot_general | solution.py:706
  (168 shorter events, 69.8 us)
Async XLA Ops:
  7.2 124.6 %all-gather.3.cloned.1.call-start = ((), (), s32[]{:S(2)}) async-start(), calls=%async_computation.2 | async-start | bytes 10948608 | tf_op jit(solution)/shard_map/all_gather | solution.py:669
  7.3 9.6 %collective-permute-start.2 = (bf16[1,1,1,1,1,24,768]{6,5,4,3,2,1,0:T(8,128)(2,1)}, bf16[1,1,1,1,1,24,768]{6,5,4,3,2,1,0:T(8,128)(2,1)S(1)}, u32[]{:S(2)}, u32[]{:S(2)}) collective-permute-start(bf16[1,1,1,1,1,24,768]{6,5,4,3,2,1,0:T(8,128)(2,1)} %bitcast.141), channel_id=1, source_target_pairs={{0,16},{4,20},{8,24},{12,28},{16,0},{20,4},{24,8},{28,12},{1,17},{... | collective-permute-start | bytes 110600 | tf_op jit(solution)/shard_map/ppermute | solution.py:567
  11.4 5.5 %collective-permute-start.1 = (bf16[1,1,1,1,1,24,768]{6,5,4,3,2,1,0:T(8,128)(2,1)}, bf16[1,1,1,1,1,24,768]{6,5,4,3,2,1,0:T(8,128)(2,1)S(1)}, u32[]{:S(2)}, u32[]{:S(2)}) collective-permute-start(bf16[1,1,1,1,1,24,768]{6,5,4,3,2,1,0:T(8,128)(2,1)} %bitcast.142), channel_id=1, source_target_pairs={{0,16},{4,20},{8,24},{12,28},{16,0},{20,4},{24,8},{28,12},{1,17},{... | collective-permute-start | bytes 110600 | tf_op jit(solution)/shard_map/ppermute | solution.py:567
  14.0 5.0 %collective-permute-start = (bf16[1,1,1,1,1,24,896]{6,5,4,3,2,1,0:T(8,128)(2,1)S(1)}, bf16[1,1,1,1,1,24,896]{6,5,4,3,2,1,0:T(8,128)(2,1)S(1)}, u32[]{:S(2)}, u32[]{:S(2)}) collective-permute-start(bf16[1,1,1,1,1,24,896]{6,5,4,3,2,1,0:T(8,128)(2,1)S(1)} %fusion.5), channel_id=1, source_target_pairs={{0,16},{4,20},{8,24},{12,28},{16,0},{20,4},{24,8},{28,12},{1,17},{... | collective-permute-start | bytes 129032 | tf_op jit(solution)/shard_map/ppermute | solution.py:567
  26.0 376.3 %reduce-scatter.2.cloned.1.call-start = ((), (), s32[]{:S(2)}) async-start(), calls=%async_computation.1 | async-start | bytes 11354112 | tf_op jit(solution)/shard_map/reduce_scatter | solution.py:686
  26.1 5.8 %collective-permute-start.4 = (bf16[2,1,1,1,1,24,768]{6,5,4,3,2,1,0:T(8,128)(2,1)}, bf16[2,1,1,1,1,24,768]{6,5,4,3,2,1,0:T(8,128)(2,1)S(1)}, u32[]{:S(2)}, u32[]{:S(2)}) collective-permute-start(bf16[2,1,1,1,1,24,768]{6,5,4,3,2,1,0:T(8,128)(2,1)} %pad_maximum_fusion.13), channel_id=1, source_target_pairs={{0,4},{4,0},{8,12},{12,8},{16,20},{20,16},{24,28},{28,24},{1,5},{5... | collective-permute-start | bytes 221192 | tf_op jit(solution)/shard_map/ppermute | solution.py:567
  28.8 6.0 %collective-permute-start.3 = (bf16[2,1,1,1,1,24,896]{6,5,4,3,2,1,0:T(8,128)(2,1)}, bf16[2,1,1,1,1,24,896]{6,5,4,3,2,1,0:T(8,128)(2,1)S(1)}, u32[]{:S(2)}, u32[]{:S(2)}) collective-permute-start(bf16[2,1,1,1,1,24,896]{6,5,4,3,2,1,0:T(8,128)(2,1)} %pad_maximum_fusion.12), channel_id=1, source_target_pairs={{0,8},{4,12},{8,0},{12,4},{16,24},{20,28},{24,16},{28,20},{1,9},{5... | collective-permute-start | bytes 258056 | tf_op jit(solution)/shard_map/ppermute | solution.py:567
  30.4 4.4 %collective-permute-start.5 = (bf16[2,1,1,1,1,24,768]{6,5,4,3,2,1,0:T(8,128)(2,1)S(1)}, bf16[2,1,1,1,1,24,768]{6,5,4,3,2,1,0:T(8,128)(2,1)S(1)}, u32[]{:S(2)}, u32[]{:S(2)}) collective-permute-start(bf16[2,1,1,1,1,24,768]{6,5,4,3,2,1,0:T(8,128)(2,1)S(1)} %pad_maximum_fusion.14), channel_id=1, source_target_pairs={{0,2},{1,3},{2,0},{3,1},{4,6},{5,7},{6,4},{7,5},{8,10},{9,11},{10,... | collective-permute-start | bytes 221192 | tf_op jit(solution)/shard_map/ppermute | solution.py:567
  35.8 7.7 %collective-permute-start.7 = (bf16[2,1,2,1,1,24,768]{6,5,4,3,2,1,0:T(8,128)(2,1)S(1)}, bf16[2,1,2,1,1,24,768]{6,5,4,3,2,1,0:T(8,128)(2,1)S(1)}, u32[]{:S(2)}, u32[]{:S(2)}) collective-permute-start(bf16[2,1,2,1,1,24,768]{6,5,4,3,2,1,0:T(8,128)(2,1)S(1)} %pad_maximum_fusion.10), channel_id=1, source_target_pairs={{0,8},{4,12},{8,0},{12,4},{16,24},{20,28},{24,16},{28,20},{1,9},{5... | collective-permute-start | bytes 442376 | tf_op jit(solution)/shard_map/ppermute | solution.py:567
  38.5 6.8 %collective-permute-start.6 = (bf16[2,2,1,1,1,24,896]{6,5,4,3,2,1,0:T(8,128)(2,1)S(1)}, bf16[2,2,1,1,1,24,896]{6,5,4,3,2,1,0:T(8,128)(2,1)S(1)}, u32[]{:S(2)}, u32[]{:S(2)}) collective-permute-start(bf16[2,2,1,1,1,24,896]{6,5,4,3,2,1,0:T(8,128)(2,1)S(1)} %pad_maximum_fusion.9), channel_id=1, source_target_pairs={{0,2},{1,3},{2,0},{3,1},{4,6},{5,7},{6,4},{7,5},{8,10},{9,11},{10,... | collective-permute-start | bytes 516104 | tf_op jit(solution)/shard_map/ppermute | solution.py:567
  40.1 5.1 %collective-permute-start.8 = (bf16[2,1,1,2,1,24,768]{6,5,4,3,2,1,0:T(8,128)(2,1)S(1)}, bf16[2,1,1,2,1,24,768]{6,5,4,3,2,1,0:T(8,128)(2,1)S(1)}, u32[]{:S(2)}, u32[]{:S(2)}) collective-permute-start(bf16[2,1,1,2,1,24,768]{6,5,4,3,2,1,0:T(8,128)(2,1)S(1)} %pad_maximum_fusion.11), channel_id=1, source_target_pairs={{0,4},{4,0},{8,12},{12,8},{16,20},{20,16},{24,28},{28,24},{1,5},{5... | collective-permute-start | bytes 442376 | tf_op jit(solution)/shard_map/ppermute | solution.py:567
  45.5 7.0 %collective-permute-start.10 = (bf16[2,2,2,1,1,24,768]{6,5,4,3,2,1,0:T(8,128)(2,1)S(1)}, bf16[2,2,2,1,1,24,768]{6,5,4,3,2,1,0:T(8,128)(2,1)S(1)}, u32[]{:S(2)}, u32[]{:S(2)}) collective-permute-start(bf16[2,2,2,1,1,24,768]{6,5,4,3,2,1,0:T(8,128)(2,1)S(1)} %pad_maximum_fusion.7), channel_id=1, source_target_pairs={{0,2},{1,3},{2,0},{3,1},{4,6},{5,7},{6,4},{7,5},{8,10},{9,11},{10,... | collective-permute-start | bytes 884744 | tf_op jit(solution)/shard_map/ppermute | solution.py:567
  46.1 9.8 %collective-permute-start.9 = (bf16[2,2,1,2,1,24,896]{6,5,4,3,2,1,0:T(8,128)(2,1)S(1)}, bf16[2,2,1,2,1,24,896]{6,5,4,3,2,1,0:T(8,128)(2,1)S(1)}, u32[]{:S(2)}, u32[]{:S(2)}) collective-permute-start(bf16[2,2,1,2,1,24,896]{6,5,4,3,2,1,0:T(8,128)(2,1)S(1)} %pad_maximum_fusion.6), channel_id=1, source_target_pairs={{0,4},{4,0},{8,12},{12,8},{16,20},{20,16},{24,28},{28,24},{1,5},{5... | collective-permute-start | bytes 1032200 | tf_op jit(solution)/shard_map/ppermute | solution.py:567
  46.4 9.3 %collective-permute-start.11 = (bf16[2,1,2,2,1,24,768]{6,5,4,3,2,1,0:T(8,128)(2,1)S(1)}, bf16[2,1,2,2,1,24,768]{6,5,4,3,2,1,0:T(8,128)(2,1)S(1)}, u32[]{:S(2)}, u32[]{:S(2)}) collective-permute-start(bf16[2,1,2,2,1,24,768]{6,5,4,3,2,1,0:T(8,128)(2,1)S(1)} %pad_maximum_fusion.8), channel_id=1, source_target_pairs={{0,8},{4,12},{8,0},{12,4},{16,24},{20,28},{24,16},{28,20},{1,9},{5... | collective-permute-start | bytes 884744 | tf_op jit(solution)/shard_map/ppermute | solution.py:567
  289.8 24.6 %collective-permute-start.15 = (bf16[2,2,2,2,2,1,24,768]{7,6,5,4,3,2,1,0:T(8,128)(2,1)S(1)}, bf16[2,2,2,2,2,1,24,768]{7,6,5,4,3,2,1,0:T(8,128)(2,1)S(1)}, u32[]{:S(2)}, u32[]{:S(2)}) collective-permute-start(bf16[2,2,2,2,2,1,24,768]{7,6,5,4,3,2,1,0:T(8,128)(2,1)S(1)} %dynamic-slice_convert_fusion), channel_id=1, source_target_pairs={{0,1},{1,0},{2,3},{3,2},{4,5},{5,4},{6,7},{7,6},{8,9},{9,8},{10,11... | collective-permute-start | bytes 3538952 | tf_op jit(solution)/shard_map/ppermute | solution.py:567
  316.5 25.3 %collective-permute-start.16 = (bf16[2,2,2,2,1,1,24,768]{7,6,5,4,3,2,1,0:T(8,128)(2,1)S(1)}, bf16[2,2,2,2,1,1,24,768]{7,6,5,4,3,2,1,0:T(8,128)(2,1)S(1)}, u32[]{:S(2)}, u32[]{:S(2)}) collective-permute-start(bf16[2,2,2,2,1,1,24,768]{7,6,5,4,3,2,1,0:T(8,128)(2,1)S(1)} %dynamic-slice_convert_fusion.2), channel_id=1, source_target_pairs={{0,2},{1,3},{2,0},{3,1},{4,6},{5,7},{6,4},{7,5},{8,10},{9,11},{10,... | collective-permute-start | bytes 1769480 | tf_op jit(solution)/shard_map/ppermute | solution.py:567
  343.0 22.9 %collective-permute-start.17 = (bf16[2,2,1,2,1,1,24,768]{7,6,5,4,3,2,1,0:T(8,128)(2,1)S(1)}, bf16[2,2,1,2,1,1,24,768]{7,6,5,4,3,2,1,0:T(8,128)(2,1)}, u32[]{:S(2)}, u32[]{:S(2)}) collective-permute-start(bf16[2,2,1,2,1,1,24,768]{7,6,5,4,3,2,1,0:T(8,128)(2,1)S(1)} %dynamic-slice_convert_fusion.4), channel_id=1, source_target_pairs={{0,8},{4,12},{8,0},{12,4},{16,24},{20,28},{24,16},{28,20},{1,9},{5... | collective-permute-start | bytes 884744 | tf_op jit(solution)/shard_map/ppermute | solution.py:567
  369.6 7.2 %collective-permute-start.18 = (bf16[2,2,2,2,1,24,896]{6,5,4,3,2,1,0:T(8,128)(2,1)}, bf16[2,2,2,2,1,24,896]{6,5,4,3,2,1,0:T(8,128)(2,1)}, u32[]{:S(2)}, u32[]{:S(2)}) collective-permute-start(bf16[2,2,2,2,1,24,896]{6,5,4,3,2,1,0:T(8,128)(2,1)} %dynamic-slice_convert_fusion.1), channel_id=1, source_target_pairs={{0,1},{1,0},{2,3},{3,2},{4,5},{5,4},{6,7},{7,6},{8,9},{9,8},{10,11... | collective-permute-start | bytes 2064392 | tf_op jit(solution)/shard_map/ppermute | solution.py:567
  370.3 6.5 %collective-permute-start.19 = (bf16[2,2,1,1,1,1,24,768]{7,6,5,4,3,2,1,0:T(8,128)(2,1)}, bf16[2,2,1,1,1,1,24,768]{7,6,5,4,3,2,1,0:T(8,128)(2,1)S(1)}, u32[]{:S(2)}, u32[]{:S(2)}) collective-permute-start(bf16[2,2,1,1,1,1,24,768]{7,6,5,4,3,2,1,0:T(8,128)(2,1)} %dynamic-slice_convert_fusion.6), channel_id=1, source_target_pairs={{0,4},{4,0},{8,12},{12,8},{16,20},{20,16},{24,28},{28,24},{1,5},{5... | collective-permute-start | bytes 442376 | tf_op jit(solution)/shard_map/ppermute | solution.py:567
  378.1 12.2 %collective-permute-start.20 = (bf16[2,2,1,2,1,24,896]{6,5,4,3,2,1,0:T(8,128)(2,1)S(1)}, bf16[2,2,1,2,1,24,896]{6,5,4,3,2,1,0:T(8,128)(2,1)S(1)}, u32[]{:S(2)}, u32[]{:S(2)}) collective-permute-start(bf16[2,2,1,2,1,24,896]{6,5,4,3,2,1,0:T(8,128)(2,1)S(1)} %dynamic-slice_convert_fusion.3), channel_id=1, source_target_pairs={{0,4},{4,0},{8,12},{12,8},{16,20},{20,16},{24,28},{28,24},{1,5},{5... | collective-permute-start | bytes 1032200 | tf_op jit(solution)/shard_map/ppermute | solution.py:567
  379.4 9.1 %collective-permute-start.21 = (bf16[2,1,1,1,1,1,24,768]{7,6,5,4,3,2,1,0:T(8,128)(2,1)S(1)}, bf16[2,1,1,1,1,1,24,768]{7,6,5,4,3,2,1,0:T(8,128)(2,1)S(1)}, u32[]{:S(2)}, u32[]{:S(2)}) collective-permute-start(bf16[2,1,1,1,1,1,24,768]{7,6,5,4,3,2,1,0:T(8,128)(2,1)S(1)} %dynamic-slice_convert_fusion.8), channel_id=1, source_target_pairs={{0,16},{4,20},{8,24},{12,28},{16,0},{20,4},{24,8},{28,12},{1,17},{... | collective-permute-start | bytes 221192 | tf_op jit(solution)/shard_map/ppermute | solution.py:567
  390.4 6.2 %collective-permute-start.22 = (bf16[2,2,1,1,1,24,896]{6,5,4,3,2,1,0:T(8,128)(2,1)S(1)}, bf16[2,2,1,1,1,24,896]{6,5,4,3,2,1,0:T(8,128)(2,1)S(1)}, u32[]{:S(2)}, u32[]{:S(2)}) collective-permute-start(bf16[2,2,1,1,1,24,896]{6,5,4,3,2,1,0:T(8,128)(2,1)S(1)} %dynamic-slice_convert_fusion.5), channel_id=1, source_target_pairs={{0,2},{1,3},{2,0},{3,1},{4,6},{5,7},{6,4},{7,5},{8,10},{9,11},{10,... | collective-permute-start | bytes 516104 | tf_op jit(solution)/shard_map/ppermute | solution.py:567
  396.7 5.6 %collective-permute-start.23 = (bf16[2,1,1,1,1,24,896]{6,5,4,3,2,1,0:T(8,128)(2,1)S(1)}, bf16[2,1,1,1,1,24,896]{6,5,4,3,2,1,0:T(8,128)(2,1)S(1)}, u32[]{:S(2)}, u32[]{:S(2)}) collective-permute-start(bf16[2,1,1,1,1,24,896]{6,5,4,3,2,1,0:T(8,128)(2,1)S(1)} %dynamic-slice_convert_fusion.7), channel_id=1, source_target_pairs={{0,8},{4,12},{8,0},{12,4},{16,24},{20,28},{24,16},{28,20},{1,9},{5... | collective-permute-start | bytes 258056 | tf_op jit(solution)/shard_map/ppermute | solution.py:567
  402.4 5.9 %collective-permute-start.24 = (bf16[1,1,1,1,1,24,896]{6,5,4,3,2,1,0:T(8,128)(2,1)S(1)}, bf16[1,1,1,1,1,24,896]{6,5,4,3,2,1,0:T(8,128)(2,1)S(1)}, u32[]{:S(2)}, u32[]{:S(2)}) collective-permute-start(bf16[1,1,1,1,1,24,896]{6,5,4,3,2,1,0:T(8,128)(2,1)S(1)} %dynamic-slice_convert_fusion.9), channel_id=1, source_target_pairs={{0,16},{4,20},{8,24},{12,28},{16,0},{20,4},{24,8},{28,12},{1,17},{... | collective-permute-start | bytes 129032 | tf_op jit(solution)/shard_map/ppermute | solution.py:567
  (20 other events, 202.6 us)
Sparse Core Ops, SparseCore 0:
  26.1 90.2 all-gather.2
  240.2 154.8 reduce-scatter.1

commit v9 on v8

--- a/solution.py
+++ b/solution.py
@@ -691,7 +691,7 @@
     )
     more = (sum_q, sums, sums_up.reshape(feature_width, lines))
     moving = scatter_start(grad_qk, own)
-    calls, before = 3, ()
+    calls, before = 2, ()
     slabs = feature_width // 128 // calls
     for call in range(calls):
         moved = scatter_step(moving, 1, call)

time: 424 us -> 425 us (level)
  waiting for transfers between devices: 29 us -> 36.6 us
    ppermute x25, waiting for transfers between devices: 28.9 us -> 36.6 us  [exchange(): lax.ppermute(values, axis, [(i, i ^ stride) for i in range(lax.axis_size(...]
    pallas_call x3 -> x2, Pallas kernels: 65.5 us -> 61.4 us  [conv_bwd(): pl.pallas_call(conv_bwd_kernel, grid_spec=pltpu.PrefetchScalarGridSpec(nu...]
  transfers between devices with their start and end apart: 27 -> 27, of which waited for: 11 -> 9; matrix products, arithmetic and copies ran while one was open for 11% -> 11% of each run, Pallas kernels for 43% -> 41%
where the time goes in v9:
time: 425 us; the launch traced here: 419 us
  Pallas kernels  277 us (65%)
  waiting for transfers between devices  36.6 us (9%)
  local copies, waits for them, and re-layouts  31.8 us (7%)
  starting transfers between devices  26.2 us (6%)
  other arithmetic  20.8 us (5%)
  between operations  15.1 us (4%)
  matrix products  12.2 us (3%)
    pallas_call x1, Pallas kernels, ffn(): pl.pallas_call(functools.partial(ffn_kernel, chunks, parts), grid=(T // b...  69.7 us
    pallas_call x2, Pallas kernels, conv_bwd(): pl.pallas_call(conv_bwd_kernel, grid_spec=pltpu.PrefetchScalarGridSpec(nu...  61.4 us
    pallas_call x1, Pallas kernels, att_bwd(): pl.pallas_call(att_bwd_kernel, grid=(G, B), in_specs=[seq((T, D)), seq((T...  45.2 us
    pallas_call x1, Pallas kernels, att_fwd(): pl.pallas_call(att_fwd_kernel, grid=(G, B), in_specs=[seq((T, D)), seq((L...  39.8 us
    ppermute x25, waiting for transfers between devices, exchange(): lax.ppermute(values, axis, [(i, i ^ stride) for i in range(lax.axis_size(...  36.6 us
    pallas_call x1, Pallas kernels, weight_grads(): pl.pallas_call(functools.partial(weight_kernel, own), grid=(halves, T //...  33.3 us
    pallas_call x1, Pallas kernels, conv_fwd(): pl.pallas_call(conv_fwd_kernel, grid_spec=pltpu.PrefetchScalarGridSpec(nu...  27.3 us
    ppermute x25, starting transfers between devices, exchange(): lax.ppermute(values, axis, [(i, i ^ stride) for i in range(lax.axis_size(...  26.1 us
  transfers between devices with their start and end apart: 27, of which 9 were waited for; matrix products, arithmetic and copies ran while one was open for 11% of the time, Pallas kernels for 41%

profile of v9, /device:TPU:0, one launch (start us, length us, event | category | flops | bytes accessed | tf_op | source)
XLA Modules:
  0.0 419.4 jit_solution(17774493995610574142)
XLA Ops:
  7.3 4.1 collective-permute-start.2
  14.0 2.8 collective-permute-start
  32.9 1.9 collective-permute-done.5
  36.3 2.1 convolution_divide_fusion.mean_ref
  40.6 2.9 collective-permute-done.7
  48.1 4.3 %collective-permute-done.10 = bf16[2,2,2,1,1,24,768]{6,5,4,3,2,1,0:T(8,128)(2,1)S(1)} collective-permute-done((bf16[2,2,2,1,1,24,768]{6,5,4,3,2,1,0:T(8,128)(2,1)S(1)}, bf16[2,2,2,1,1,24,768]{6,5,4,3,2,1,0:T(8,128)(2,1)S(1)}, u32[]{:S(2)}, u32[]{:S(2)}) %collective-permute-start.10) | collective-permute-done | bytes 294944 | tf_op jit(solution)/shard_map/ppermute | solution.py:567
  52.5 3.1 collective-permute-done.11
  64.6 27.3 %shard_map.331 = (f32[2,1024,768]{2,1,0:T(8,128)}, f32[2,1024,768]{2,1,0:T(8,128)}) custom-call(s32[2,5]{1,0:T(2,128)} %copy.78.bounds_ref, bf16[2,1024,768]{2,1,0:T(8,128)(2,1)} %x_ref.9, bf16[768,768]{1,0:T(8,128)(2,1)} %slice.126.wv_ref, f32[128,768]{1,0:T(8,128)} %convert_bitcast_fusion.w_ref.vec_ref.refs_4_), custom_call_target="tpu_custom_call" | custom-call | tf_op jit(solution)/shard_map/pallas_call | solution.py:340
  91.8 39.8 %shard_map.332 = (bf16[2,768,1024]{2,1,0:T(8,128)(2,1)}, bf16[2,768,1024]{2,1,0:T(8,128)(2,1)}, bf16[2,768,1024]{2,1,0:T(8,128)(2,1)}, bf16[2,768,1024]{2,1,0:T(...) custom-call(bf16[2,1024,768]{2,1,0:T(8,128)(2,1)} %x_ref.9, ...), custom_call_target="tpu_custom_call" | custom-call | tf_op jit(solution)/shard_map/pallas_call | solution.py:154
  131.6 5.3 %fusion.10 = (bf16[32,24,768]{2,1,0:T(8,128)(2,1)}, bf16[32,24,768]{2,1,0:T(8,128)(2,1)}, bf16[32,24,768]{2,1,0:T(8,128)(2,1)}, bf16[32,24,768]{2,1,0:T(8,128)(2,1)}, bf16[32,24,768]{2,1,0:T(8,128)(2,1)}) fusion(bf16[32,216,768]{2,1,0:T(8,128)(2,1)} %bitcast.108), kind=kLoop, calls=%fused_computation.104 | loop fusion | bytes 11796480 | tf_op jit(solution)/shard_map/slice | solution.py:673
  136.9 69.7 %shard_map.333 = (bf16[2048,768]{1,0:T(8,128)(2,1)}, bf16[2048,768]{1,0:T(8,128)(2,1)}, bf16[2048,3072]{1,0:T(8,128)(2,1)}, bf16[2048,768]{1,0:T(8,128)(2,1)}, b...) custom-call(bf16[2048,768]{1,0:T(8,128)(2,1)} %bitcast.110, ...), custom_call_target="tpu_custom_call" | custom-call | tf_op jit(solution)/shard_map/pallas_call | solution.py:499
  206.6 33.3 %shard_map.337 = bf16[32,224,768]{2,1,0:T(8,128)(2,1)} custom-call(bf16[2048,3072]{1,0:T(8,128)(2,1)} %get-tuple-element.146.up_ref, bf16[2048,768]{1,0:T(8,128)(2,1)} %get-tuple-element.147.normed_ref, bf16[2048,3072]{1,0:T(8,128)(2,1)} %get-tuple-element.148.hidden_ref, bf16[2048,768]{1,0:T(8,128)(2,1)} %get-tuple-element.149.down_ref, ...), custom_call_target="tpu_custom_call" | custom-call | tf_op jit(solution)/shard_map/pallas_call | solution.py:541
  242.7 45.2 %shard_map.334 = (bf16[2,768,1024]{2,1,0:T(8,128)(2,1)}, bf16[2,768,1024]{2,1,0:T(8,128)(2,1)}, f32[2,768,1024]{2,1,0:T(8,128)}, f32[2,768,768]{2,1,0:T(8,128)}, f32[768,1]{1,0:T(8,128)}) custom-call(bf16[2,1024,768]{2,1,0:T(8,128)(2,1)} %x_ref.9, bf16[2,1024,768]{2,1,0:T(8,128)(2,1)} %bitcast.101, bf16[768,768]{1,0:T(8,128)(2,1)} %copy.83.wo_ref, ...), custom_call_target="tpu_custom_call" | custom-call | tf_op jit(solution)/shard_map/pallas_call | solution.py:260
  292.5 30.7 %shard_map.335 = (bf16[2,768,1024]{2,1,0:T(8,128)(2,1)}, f32[768,896]{1,0:T(8,128)}) custom-call(s32[2,5]{1,0:T(2,128)} %copy.78.bounds_ref, f32[2,1024,768]{2,1,0:T(8,128)} %get-tuple-element.111.v_ref, bf16[2,1024,768]{2,1,0:T(8,128)(2,1)} %bitcast.102, bf16[768,768]{1,0:T(8,128)(2,1)} %bitcast.105, f32[128,768]{1,0:T(8,128)} %convert_bitcast_fusion.w_ref.vec_ref.refs_4_, ...), custom_call_target="tpu_custom_call" | custom-call | tf_op jit(solution)/shard_map/pallas_call | solution.py:402
  323.2 2.5 convert_add_fusion
  328.9 30.7 %shard_map.336 = (bf16[2,768,1024]{2,1,0:T(8,128)(2,1)}, f32[768,896]{1,0:T(8,128)}) custom-call(s32[2,5]{1,0:T(2,128)} %copy.78.bounds_ref, f32[2,1024,768]{2,1,0:T(8,128)} %get-tuple-element.111.v_ref, bf16[2,1024,768]{2,1,0:T(8,128)(2,1)} %bitcast.103, bf16[768,768]{1,0:T(8,128)(2,1)} %bitcast.106, ...), custom_call_target="tpu_custom_call", output_to_operand_aliasing={{0}: (10, {}), {1}: (11, {})} | custom-call | tf_op jit(solution)/shard_map/pallas_call | solution.py:402
  361.1 2.3 dynamic-slice_convert_fusion.1
  364.3 11.1 %collective-permute-done.18 = bf16[2,2,1,2,1,1,24,768]{7,6,5,4,3,2,1,0:T(8,128)(2,1)} collective-permute-done((bf16[2,2,1,2,1,1,24,768]{7,6,5,4,3,2,1,0:T(8,128)(2,1)S(1)}, bf16[2,2,1,2,1,1,24,768]{7,6,5,4,3,2,1,0:T(8,128)(2,1)}, u32[]{:S(2)}, u32[]{:S(2)}) %collective-permute-start.18) | collective-permute-done | bytes 294944 | tf_op jit(solution)/shard_map/ppermute | solution.py:567
  380.2 2.7 fusion.11
  382.9 8.1 %collective-permute-done.20 = bf16[2,2,1,1,1,1,24,768]{7,6,5,4,3,2,1,0:T(8,128)(2,1)S(1)} collective-permute-done((bf16[2,2,1,1,1,1,24,768]{7,6,5,4,3,2,1,0:T(8,128)(2,1)S(1)}, bf16[2,2,1,1,1,1,24,768]{7,6,5,4,3,2,1,0:T(8,128)(2,1)S(1)}, u32[]{:S(2)}, u32[]{:S(2)}) %collective-permute-start.20) | collective-permute-done | bytes 147488 | tf_op jit(solution)/shard_map/ppermute | solution.py:567
  391.8 2.7 fusion.12
  394.5 2.8 collective-permute-done.23
  398.1 4.8 %add_add_fusion = f32[2,1024,768]{2,1,0:T(8,128)} fusion(f32[2,1024,768]{2,1,0:T(8,128)S(1)} %fusion.12, f32[2,1024,768]{2,1,0:T(8,128)S(1)} %bitcast.120, f32[2,1024,768]{2,1,0:T(8,128)S(1)} %fusion.11, bf16[2,768,1024]{2,1,0:T(8,128)(2,1)S(1)} %copy-done.2, bf16[768,896]{1,0:T(8,128)(2,1)S(1)} %bitcast.115), kind=kOutput, calls=%fused_computation | convolution fusion | flops 2420637696 | bytes 29491200 | tf_op jit(solution)/shard_map/bot,oi->bti/dot_general | solution.py:706
  403.0 2.4 collective-permute-start.24
  (161 shorter events, 62.0 us)
Async XLA Ops:
  7.2 124.4 %all-gather.3.cloned.1.call-start = ((), (), s32[]{:S(2)}) async-start(), calls=%async_computation.2 | async-start | bytes 10948608 | tf_op jit(solution)/shard_map/all_gather | solution.py:669
  7.3 9.6 %collective-permute-start.2 = (bf16[1,1,1,1,1,24,768]{6,5,4,3,2,1,0:T(8,128)(2,1)}, bf16[1,1,1,1,1,24,768]{6,5,4,3,2,1,0:T(8,128)(2,1)S(1)}, u32[]{:S(2)}, u32[]{:S(2)}) collective-permute-start(bf16[1,1,1,1,1,24,768]{6,5,4,3,2,1,0:T(8,128)(2,1)} %bitcast.139), channel_id=1, source_target_pairs={{0,16},{4,20},{8,24},{12,28},{16,0},{20,4},{24,8},{28,12},{1,17},{... | collective-permute-start | bytes 110600 | tf_op jit(solution)/shard_map/ppermute | solution.py:567
  11.4 5.5 %collective-permute-start.1 = (bf16[1,1,1,1,1,24,768]{6,5,4,3,2,1,0:T(8,128)(2,1)}, bf16[1,1,1,1,1,24,768]{6,5,4,3,2,1,0:T(8,128)(2,1)S(1)}, u32[]{:S(2)}, u32[]{:S(2)}) collective-permute-start(bf16[1,1,1,1,1,24,768]{6,5,4,3,2,1,0:T(8,128)(2,1)} %bitcast.140), channel_id=1, source_target_pairs={{0,16},{4,20},{8,24},{12,28},{16,0},{20,4},{24,8},{28,12},{1,17},{... | collective-permute-start | bytes 110600 | tf_op jit(solution)/shard_map/ppermute | solution.py:567
  14.0 5.0 %collective-permute-start = (bf16[1,1,1,1,1,24,896]{6,5,4,3,2,1,0:T(8,128)(2,1)S(1)}, bf16[1,1,1,1,1,24,896]{6,5,4,3,2,1,0:T(8,128)(2,1)S(1)}, u32[]{:S(2)}, u32[]{:S(2)}) collective-permute-start(bf16[1,1,1,1,1,24,896]{6,5,4,3,2,1,0:T(8,128)(2,1)S(1)} %fusion.5), channel_id=1, source_target_pairs={{0,16},{4,20},{8,24},{12,28},{16,0},{20,4},{24,8},{28,12},{1,17},{... | collective-permute-start | bytes 129032 | tf_op jit(solution)/shard_map/ppermute | solution.py:567
  26.0 377.0 %reduce-scatter.2.cloned.1.call-start = ((), (), s32[]{:S(2)}) async-start(), calls=%async_computation.1 | async-start | bytes 11354112 | tf_op jit(solution)/shard_map/reduce_scatter | solution.py:686
  26.1 5.8 %collective-permute-start.4 = (bf16[2,1,1,1,1,24,768]{6,5,4,3,2,1,0:T(8,128)(2,1)}, bf16[2,1,1,1,1,24,768]{6,5,4,3,2,1,0:T(8,128)(2,1)S(1)}, u32[]{:S(2)}, u32[]{:S(2)}) collective-permute-start(bf16[2,1,1,1,1,24,768]{6,5,4,3,2,1,0:T(8,128)(2,1)} %pad_maximum_fusion.13), channel_id=1, source_target_pairs={{0,4},{4,0},{8,12},{12,8},{16,20},{20,16},{24,28},{28,24},{1,5},{5... | collective-permute-start | bytes 221192 | tf_op jit(solution)/shard_map/ppermute | solution.py:567
  28.8 6.0 %collective-permute-start.3 = (bf16[2,1,1,1,1,24,896]{6,5,4,3,2,1,0:T(8,128)(2,1)}, bf16[2,1,1,1,1,24,896]{6,5,4,3,2,1,0:T(8,128)(2,1)S(1)}, u32[]{:S(2)}, u32[]{:S(2)}) collective-permute-start(bf16[2,1,1,1,1,24,896]{6,5,4,3,2,1,0:T(8,128)(2,1)} %pad_maximum_fusion.12), channel_id=1, source_target_pairs={{0,8},{4,12},{8,0},{12,4},{16,24},{20,28},{24,16},{28,20},{1,9},{5... | collective-permute-start | bytes 258056 | tf_op jit(solution)/shard_map/ppermute | solution.py:567
  30.4 4.4 %collective-permute-start.5 = (bf16[2,1,1,1,1,24,768]{6,5,4,3,2,1,0:T(8,128)(2,1)S(1)}, bf16[2,1,1,1,1,24,768]{6,5,4,3,2,1,0:T(8,128)(2,1)S(1)}, u32[]{:S(2)}, u32[]{:S(2)}) collective-permute-start(bf16[2,1,1,1,1,24,768]{6,5,4,3,2,1,0:T(8,128)(2,1)S(1)} %pad_maximum_fusion.14), channel_id=1, source_target_pairs={{0,2},{1,3},{2,0},{3,1},{4,6},{5,7},{6,4},{7,5},{8,10},{9,11},{10,... | collective-permute-start | bytes 221192 | tf_op jit(solution)/shard_map/ppermute | solution.py:567
  35.8 7.7 %collective-permute-start.7 = (bf16[2,1,2,1,1,24,768]{6,5,4,3,2,1,0:T(8,128)(2,1)S(1)}, bf16[2,1,2,1,1,24,768]{6,5,4,3,2,1,0:T(8,128)(2,1)S(1)}, u32[]{:S(2)}, u32[]{:S(2)}) collective-permute-start(bf16[2,1,2,1,1,24,768]{6,5,4,3,2,1,0:T(8,128)(2,1)S(1)} %pad_maximum_fusion.10), channel_id=1, source_target_pairs={{0,8},{4,12},{8,0},{12,4},{16,24},{20,28},{24,16},{28,20},{1,9},{5... | collective-permute-start | bytes 442376 | tf_op jit(solution)/shard_map/ppermute | solution.py:567
  38.5 6.8 %collective-permute-start.6 = (bf16[2,2,1,1,1,24,896]{6,5,4,3,2,1,0:T(8,128)(2,1)S(1)}, bf16[2,2,1,1,1,24,896]{6,5,4,3,2,1,0:T(8,128)(2,1)S(1)}, u32[]{:S(2)}, u32[]{:S(2)}) collective-permute-start(bf16[2,2,1,1,1,24,896]{6,5,4,3,2,1,0:T(8,128)(2,1)S(1)} %pad_maximum_fusion.9), channel_id=1, source_target_pairs={{0,2},{1,3},{2,0},{3,1},{4,6},{5,7},{6,4},{7,5},{8,10},{9,11},{10,... | collective-permute-start | bytes 516104 | tf_op jit(solution)/shard_map/ppermute | solution.py:567
  40.1 5.1 %collective-permute-start.8 = (bf16[2,1,1,2,1,24,768]{6,5,4,3,2,1,0:T(8,128)(2,1)S(1)}, bf16[2,1,1,2,1,24,768]{6,5,4,3,2,1,0:T(8,128)(2,1)S(1)}, u32[]{:S(2)}, u32[]{:S(2)}) collective-permute-start(bf16[2,1,1,2,1,24,768]{6,5,4,3,2,1,0:T(8,128)(2,1)S(1)} %pad_maximum_fusion.11), channel_id=1, source_target_pairs={{0,4},{4,0},{8,12},{12,8},{16,20},{20,16},{24,28},{28,24},{1,5},{5... | collective-permute-start | bytes 442376 | tf_op jit(solution)/shard_map/ppermute | solution.py:567
  45.5 6.9 %collective-permute-start.10 = (bf16[2,2,2,1,1,24,768]{6,5,4,3,2,1,0:T(8,128)(2,1)S(1)}, bf16[2,2,2,1,1,24,768]{6,5,4,3,2,1,0:T(8,128)(2,1)S(1)}, u32[]{:S(2)}, u32[]{:S(2)}) collective-permute-start(bf16[2,2,2,1,1,24,768]{6,5,4,3,2,1,0:T(8,128)(2,1)S(1)} %pad_maximum_fusion.7), channel_id=1, source_target_pairs={{0,2},{1,3},{2,0},{3,1},{4,6},{5,7},{6,4},{7,5},{8,10},{9,11},{10,... | collective-permute-start | bytes 884744 | tf_op jit(solution)/shard_map/ppermute | solution.py:567
  46.0 9.8 %collective-permute-start.9 = (bf16[2,2,1,2,1,24,896]{6,5,4,3,2,1,0:T(8,128)(2,1)S(1)}, bf16[2,2,1,2,1,24,896]{6,5,4,3,2,1,0:T(8,128)(2,1)S(1)}, u32[]{:S(2)}, u32[]{:S(2)}) collective-permute-start(bf16[2,2,1,2,1,24,896]{6,5,4,3,2,1,0:T(8,128)(2,1)S(1)} %pad_maximum_fusion.6), channel_id=1, source_target_pairs={{0,4},{4,0},{8,12},{12,8},{16,20},{20,16},{24,28},{28,24},{1,5},{5... | collective-permute-start | bytes 1032200 | tf_op jit(solution)/shard_map/ppermute | solution.py:567
  46.4 9.3 %collective-permute-start.11 = (bf16[2,1,2,2,1,24,768]{6,5,4,3,2,1,0:T(8,128)(2,1)S(1)}, bf16[2,1,2,2,1,24,768]{6,5,4,3,2,1,0:T(8,128)(2,1)S(1)}, u32[]{:S(2)}, u32[]{:S(2)}) collective-permute-start(bf16[2,1,2,2,1,24,768]{6,5,4,3,2,1,0:T(8,128)(2,1)S(1)} %pad_maximum_fusion.8), channel_id=1, source_target_pairs={{0,8},{4,12},{8,0},{12,4},{16,24},{20,28},{24,16},{28,20},{1,9},{5... | collective-permute-start | bytes 884744 | tf_op jit(solution)/shard_map/ppermute | solution.py:567
  289.6 33.6 %collective-permute-start.15 = (bf16[2,2,2,2,2,1,24,768]{7,6,5,4,3,2,1,0:T(8,128)(2,1)S(1)}, bf16[2,2,2,2,2,1,24,768]{7,6,5,4,3,2,1,0:T(8,128)(2,1)}, u32[]{:S(2)}, u32[]{:S(2)}) collective-permute-start(bf16[2,2,2,2,2,1,24,768]{7,6,5,4,3,2,1,0:T(8,128)(2,1)S(1)} %dynamic-slice_convert_fusion), channel_id=1, source_target_pairs={{0,1},{1,0},{2,3},{3,2},{4,5},{5,4},{6,7},{7,6},{8,9},{9,8},{10,11... | collective-permute-start | bytes 3538952 | tf_op jit(solution)/shard_map/ppermute | solution.py:567
  327.3 32.3 %collective-permute-start.16 = (bf16[2,2,2,2,1,1,24,768]{7,6,5,4,3,2,1,0:T(8,128)(2,1)S(1)}, bf16[2,2,2,2,1,1,24,768]{7,6,5,4,3,2,1,0:T(8,128)(2,1)S(1)}, u32[]{:S(2)}, u32[]{:S(2)}) collective-permute-start(bf16[2,2,2,2,1,1,24,768]{7,6,5,4,3,2,1,0:T(8,128)(2,1)S(1)} %dynamic-slice_convert_fusion.2), channel_id=1, source_target_pairs={{0,2},{1,3},{2,0},{3,1},{4,6},{5,7},{6,4},{7,5},{8,10},{9,11},{10,... | collective-permute-start | bytes 1769480 | tf_op jit(solution)/shard_map/ppermute | solution.py:567
  363.4 13.1 %collective-permute-start.17 = (bf16[2,2,2,2,1,24,896]{6,5,4,3,2,1,0:T(8,128)(2,1)}, bf16[2,2,2,2,1,24,896]{6,5,4,3,2,1,0:T(8,128)(2,1)S(1)}, u32[]{:S(2)}, u32[]{:S(2)}) collective-permute-start(bf16[2,2,2,2,1,24,896]{6,5,4,3,2,1,0:T(8,128)(2,1)} %dynamic-slice_convert_fusion.1), channel_id=1, source_target_pairs={{0,1},{1,0},{2,3},{3,2},{4,5},{5,4},{6,7},{7,6},{8,9},{9,8},{10,11... | collective-permute-start | bytes 2064392 | tf_op jit(solution)/shard_map/ppermute | solution.py:567
  363.4 12.0 %collective-permute-start.18 = (bf16[2,2,1,2,1,1,24,768]{7,6,5,4,3,2,1,0:T(8,128)(2,1)S(1)}, bf16[2,2,1,2,1,1,24,768]{7,6,5,4,3,2,1,0:T(8,128)(2,1)}, u32[]{:S(2)}, u32[]{:S(2)}) collective-permute-start(bf16[2,2,1,2,1,1,24,768]{7,6,5,4,3,2,1,0:T(8,128)(2,1)S(1)} %dynamic-slice_convert_fusion.4), channel_id=1, source_target_pairs={{0,8},{4,12},{8,0},{12,4},{16,24},{20,28},{24,16},{28,20},{1,9},{5... | collective-permute-start | bytes 884744 | tf_op jit(solution)/shard_map/ppermute | solution.py:567
  378.0 13.0 %collective-permute-start.19 = (bf16[2,2,1,2,1,24,896]{6,5,4,3,2,1,0:T(8,128)(2,1)S(1)}, bf16[2,2,1,2,1,24,896]{6,5,4,3,2,1,0:T(8,128)(2,1)S(1)}, u32[]{:S(2)}, u32[]{:S(2)}) collective-permute-start(bf16[2,2,1,2,1,24,896]{6,5,4,3,2,1,0:T(8,128)(2,1)S(1)} %dynamic-slice_convert_fusion.3), channel_id=1, source_target_pairs={{0,4},{4,0},{8,12},{12,8},{16,20},{20,16},{24,28},{28,24},{1,5},{5... | collective-permute-start | bytes 1032200 | tf_op jit(solution)/shard_map/ppermute | solution.py:567
  379.7 11.3 %collective-permute-start.20 = (bf16[2,2,1,1,1,1,24,768]{7,6,5,4,3,2,1,0:T(8,128)(2,1)S(1)}, bf16[2,2,1,1,1,1,24,768]{7,6,5,4,3,2,1,0:T(8,128)(2,1)S(1)}, u32[]{:S(2)}, u32[]{:S(2)}) collective-permute-start(bf16[2,2,1,1,1,1,24,768]{7,6,5,4,3,2,1,0:T(8,128)(2,1)S(1)} %dynamic-slice_convert_fusion.6), channel_id=1, source_target_pairs={{0,4},{4,0},{8,12},{12,8},{16,20},{20,16},{24,28},{28,24},{1,5},{5... | collective-permute-start | bytes 442376 | tf_op jit(solution)/shard_map/ppermute | solution.py:567
  391.1 6.8 %collective-permute-start.21 = (bf16[2,2,1,1,1,24,896]{6,5,4,3,2,1,0:T(8,128)(2,1)S(1)}, bf16[2,2,1,1,1,24,896]{6,5,4,3,2,1,0:T(8,128)(2,1)S(1)}, u32[]{:S(2)}, u32[]{:S(2)}) collective-permute-start(bf16[2,2,1,1,1,24,896]{6,5,4,3,2,1,0:T(8,128)(2,1)S(1)} %dynamic-slice_convert_fusion.5), channel_id=1, source_target_pairs={{0,2},{1,3},{2,0},{3,1},{4,6},{5,7},{6,4},{7,5},{8,10},{9,11},{10,... | collective-permute-start | bytes 516104 | tf_op jit(solution)/shard_map/ppermute | solution.py:567
  391.2 6.1 %collective-permute-start.23 = (bf16[2,1,1,1,1,1,24,768]{7,6,5,4,3,2,1,0:T(8,128)(2,1)S(1)}, bf16[2,1,1,1,1,1,24,768]{7,6,5,4,3,2,1,0:T(8,128)(2,1)S(1)}, u32[]{:S(2)}, u32[]{:S(2)}) collective-permute-start(bf16[2,1,1,1,1,1,24,768]{7,6,5,4,3,2,1,0:T(8,128)(2,1)S(1)} %dynamic-slice_convert_fusion.8), channel_id=1, source_target_pairs={{0,16},{4,20},{8,24},{12,28},{16,0},{20,4},{24,8},{28,12},{1,17},{... | collective-permute-start | bytes 221192 | tf_op jit(solution)/shard_map/ppermute | solution.py:567
  398.0 4.9 %collective-permute-start.22 = (bf16[2,1,1,1,1,24,896]{6,5,4,3,2,1,0:T(8,128)(2,1)S(1)}, bf16[2,1,1,1,1,24,896]{6,5,4,3,2,1,0:T(8,128)(2,1)S(1)}, u32[]{:S(2)}, u32[]{:S(2)}) collective-permute-start(bf16[2,1,1,1,1,24,896]{6,5,4,3,2,1,0:T(8,128)(2,1)S(1)} %dynamic-slice_convert_fusion.7), channel_id=1, source_target_pairs={{0,8},{4,12},{8,0},{12,4},{16,24},{20,28},{24,16},{28,20},{1,9},{5... | collective-permute-start | bytes 258056 | tf_op jit(solution)/shard_map/ppermute | solution.py:567
  403.0 6.4 %collective-permute-start.24 = (bf16[1,1,1,1,1,24,896]{6,5,4,3,2,1,0:T(8,128)(2,1)S(1)}, bf16[1,1,1,1,1,24,896]{6,5,4,3,2,1,0:T(8,128)(2,1)S(1)}, u32[]{:S(2)}, u32[]{:S(2)}) collective-permute-start(bf16[1,1,1,1,1,24,896]{6,5,4,3,2,1,0:T(8,128)(2,1)S(1)} %dynamic-slice_convert_fusion.9), channel_id=1, source_target_pairs={{0,16},{4,20},{8,24},{12,28},{16,0},{20,4},{24,8},{28,12},{1,17},{... | collective-permute-start | bytes 129032 | tf_op jit(solution)/shard_map/ppermute | solution.py:567
  (17 other events, 169.5 us)
Sparse Core Ops, SparseCore 0:
  26.1 90.2 all-gather.2
  240.1 143.5 reduce-scatter.1
